TPU v7x, 32 devices: a whole 2x2x4 slice. The times are simulated.
32 devices in a mesh: task: 4 (over y, x), space: 8 (over z, core).
Axes of the slice: x: 2, y: 2, z: 4, core: 2. Of those that a mesh axis runs over, the one named last changes fastest.
Arguments:
- features: bfloat16 [16, 128, 2048], P('space'), may hold values from -6 to 6
- row_width: int32 [16], replicated, may hold values from 32 to 128, as said below
- w_reduce: bfloat16 [2048, 512], replicated, may hold values from -0.125 to 0.125
- w_dilated: bfloat16 [512, 9, 512], replicated, may hold values from -0.09375 to 0.09375
- w_expand: bfloat16 [512, 2048], replicated, may hold values from -0.25 to 0.25
- trunk_gain: float32 [3072], replicated, may hold values from 0.5 to 1.5
- trunk_shift: float32 [3072], replicated, may hold values from -3 to 3
- branch_weight: bfloat16 [4, 2048, 512], P('task', 'space'), may hold values from -0.125 to 0.125
- rate_weight: bfloat16 [4, 2048, 6912], P('task', 'space'), may hold values from -0.046875 to 0.046875
- proj_weight: bfloat16 [4, 1280, 256], P('task'), may hold values from -0.15625 to 0.15625
- head_gain: float32 [4, 1280], P('task'), may hold values from 0.5 to 1.5
- head_shift: float32 [4, 1280], P('task'), may hold values from -3 to 3
- head_cot: bfloat16 [4, 16, 128, 256], P('task', 'space'), may hold values from -20 to 20
Outputs:
- head_out: bfloat16 [4, 16, 128, 256], P('task', 'space')
- features_grad: bfloat16 [16, 128, 2048], P('space')
- w_reduce_grad: float32 [2048, 512], P('space')
- w_dilated_grad: float32 [512, 9, 512], P('space')
- w_expand_grad: float32 [512, 2048], P('space')
- trunk_gain_grad: float32 [3072], replicated
- trunk_shift_grad: float32 [3072], replicated
- batch_stats: float32 [2, 3072], replicated
- branch_grad: float32 [4, 2048, 512], P('task', 'space')
- rate_grad: float32 [4, 2048, 6912], P('task', 'space')
- proj_grad: float32 [4, 1280, 256], P('task')
- head_gain_grad: float32 [4, 1280], P('task')
- head_shift_grad: float32 [4, 1280], P('task')
- task_weight: float32 [4], replicated
Inputs may be any that keep to these rules, and one draw needn't show every extreme that they name: Columns 0 to row_width[r] - 1 of canvas row r are image, the rest padding; row 0 holds 32 columns and the last row is full.
All inputs are finite; a program needn't handle non-finite values.
Results may differ from a plain program's by a relative error of at most 0.02.
Values may be sent and summed in bfloat16 or wider, within the bound.
A program may use at most 384 MiB of HBM per device.

v0:
```python
import jax
import jax.numpy as jnp
from jax import lax
from jax.sharding import PartitionSpec as P

CONV_DILATION = 2
RATE = 12


NORM_EPS = 1e-05
GRAM_EPS = 1e-06
PRECISE = lax.Precision.HIGHEST


def with_halo(block, sides, width):
    for axis, dim in sides:
        count = lax.axis_size(axis)
        forward = [(i, i + 1) for i in range(count - 1)]
        backward = [(target, source) for source, target in forward]
        low = lax.ppermute(
            lax.slice_in_dim(block, block.shape[dim] - width, None, axis=dim), axis, forward
        )
        high = lax.ppermute(lax.slice_in_dim(block, 0, width, axis=dim), axis, backward)
        block = jnp.concatenate([low, block, high], axis=dim)
    return block


def from_behind(shard, axis, by):
    count = lax.axis_size(axis)
    pairs = [(i, i + by) for i in range(count) if 0 <= i + by < count]
    return lax.ppermute(shard, axis, pairs)


def small_solve(matrix, target):
    size_n = matrix.shape[0]
    rows_list = [matrix[number] for number in range(size_n)]
    values = [target[number] for number in range(size_n)]
    for pivot_row in range(size_n):
        for lower_row in range(pivot_row + 1, size_n):
            factor = rows_list[lower_row][pivot_row] / rows_list[pivot_row][pivot_row]
            rows_list[lower_row] = rows_list[lower_row] - factor * rows_list[pivot_row]
            values[lower_row] = values[lower_row] - factor * values[pivot_row]
    answer = [None] * size_n
    for pivot_row in reversed(range(size_n)):
        running = values[pivot_row]
        for later_row in range(pivot_row + 1, size_n):
            running = running - rows_list[pivot_row][later_row] * answer[later_row]
        answer[pivot_row] = running / rows_list[pivot_row][pivot_row]
    return jnp.stack(answer)


def imtl_weights(gram_matrix):
    grad_norms = jnp.sqrt(jnp.diagonal(gram_matrix) + GRAM_EPS)
    projections = gram_matrix / grad_norms[None, :]
    system = projections[0, 0] - projections[0:1, 1:] - projections[1:, 0:1] + projections[1:, 1:]
    target = projections[0, 0] - projections[0, 1:]
    other_weights = small_solve(jnp.transpose(system), target)
    return jnp.concatenate([(1.0 - jnp.sum(other_weights))[None], other_weights])


def gelu_back(value, upstream):
    return jax.vjp(jax.nn.gelu, value)[1](upstream)[0]


def channel_sums(members):
    return lax.psum(members, "space")


def norm_values(hidden, first_total, second_total, gain_vec, shift_vec, pixel_count):
    mean_value = first_total / pixel_count
    variance = second_total / pixel_count - mean_value * mean_value
    inv_std = lax.rsqrt(variance + NORM_EPS)
    scaled = (hidden - mean_value) * inv_std
    return (gain_vec * scaled + shift_vec, scaled, inv_std, mean_value, variance)


def norm_forward(hidden, gain_vec, shift_vec, valid_mask, pixel_count):
    totals = channel_sums(
        (jnp.sum(hidden * valid_mask, axis=0), jnp.sum(hidden * hidden * valid_mask, axis=0))
    )
    return norm_values(hidden, totals[0], totals[1], gain_vec, shift_vec, pixel_count)


def norm_finish(
    upstream, scaled, inv_std, gain_vec, gain_grad, shift_grad, valid_mask, pixel_count
):
    return (
        valid_mask
        * gain_vec
        * inv_std
        * (upstream - shift_grad / pixel_count - scaled * gain_grad / pixel_count)
    )


def norm_backward(upstream, scaled, inv_std, gain_vec, valid_mask, pixel_count):
    totals = channel_sums(
        (jnp.sum(upstream * valid_mask, axis=0), jnp.sum(upstream * scaled * valid_mask, axis=0))
    )
    hidden_grad = norm_finish(
        upstream, scaled, inv_std, gain_vec, totals[1], totals[0], valid_mask, pixel_count
    )
    return (hidden_grad, totals[1], totals[0])


def band_rim(strip_image):
    return with_halo(strip_image, (("space", 0),), CONV_DILATION)


def far_rows(strip_image, bands_away, upward):
    if bands_away >= lax.axis_size("space"):
        return jnp.zeros_like(strip_image)
    if upward:
        return from_behind(strip_image, "space", bands_away)
    return from_behind(strip_image, "space", -bands_away)


def trunk_taps(padded, reach_cells, rows_count, cols_count, flipped):
    col_padded = jnp.pad(padded, ((0, 0), (reach_cells, reach_cells), (0, 0)))
    pieces = []
    for row_tap in range(3):
        for col_tap in range(3):
            row_from = (2 - row_tap) * reach_cells if flipped else row_tap * reach_cells
            col_from = (2 - col_tap) * reach_cells if flipped else col_tap * reach_cells
            pieces.append(
                col_padded[
                    row_from : row_from + rows_count, col_from : col_from + cols_count
                ].reshape(rows_count * cols_count, -1)
            )
    return jnp.stack(pieces, axis=1)


def per_device(
    features,
    row_width,
    w_reduce,
    w_dilated,
    w_expand,
    trunk_gain,
    trunk_shift,
    branch_weight,
    rate_weight,
    proj_weight,
    head_gain,
    head_shift,
    head_cot,
):
    band_rows, cols_count, in_width = features.shape
    pixels = band_rows * cols_count
    middle_width = w_reduce.shape[1]
    head_width = proj_weight.shape[2]
    first_row = lax.axis_index("space") * band_rows
    widths = lax.dynamic_slice_in_dim(row_width, first_row, band_rows)
    valid_mask = (
        (jnp.arange(cols_count)[None, :] < widths[:, None]).astype(jnp.float32).reshape(pixels, 1)
    )
    pixel_count = jnp.sum(row_width).astype(jnp.float32)
    inputs = features.reshape(pixels, in_width)
    gain_one, shift_one = (trunk_gain[:middle_width], trunk_shift[:middle_width])
    gain_two, shift_two = (
        trunk_gain[middle_width : 2 * middle_width],
        trunk_shift[middle_width : 2 * middle_width],
    )
    gain_three, shift_three = (trunk_gain[2 * middle_width :], trunk_shift[2 * middle_width :])
    hidden_one = jnp.dot(inputs, w_reduce, preferred_element_type=jnp.float32)
    stats_one = norm_forward(hidden_one, gain_one, shift_one, valid_mask, pixel_count)
    first_active = (jax.nn.gelu(stats_one[0]) * valid_mask).astype(jnp.bfloat16)
    patches = trunk_taps(
        band_rim(first_active.reshape(band_rows, cols_count, middle_width)),
        CONV_DILATION,
        band_rows,
        cols_count,
        False,
    )
    hidden_two = jnp.einsum("pti,ito->po", patches, w_dilated, preferred_element_type=jnp.float32)
    stats_two = norm_forward(hidden_two, gain_two, shift_two, valid_mask, pixel_count)
    active_two = (jax.nn.gelu(stats_two[0]) * valid_mask).astype(jnp.bfloat16)
    hidden_three = jnp.dot(active_two, w_expand, preferred_element_type=jnp.float32)
    stats_three = norm_forward(hidden_three, gain_three, shift_three, valid_mask, pixel_count)
    before_act = stats_three[0] + inputs.astype(jnp.float32)
    shared = (jax.nn.gelu(before_act) * valid_mask).astype(jnp.bfloat16)
    proj_local = proj_weight[0]
    gain_local = head_gain[0]
    shift_local = head_shift[0]
    joined_weight = jnp.concatenate([branch_weight[0], rate_weight[0]], axis=1)
    pixel_sum = jnp.dot(
        valid_mask.reshape(1, pixels).astype(jnp.bfloat16),
        shared,
        preferred_element_type=jnp.float32,
    )[0]
    shared_image = shared.reshape(band_rows, cols_count, in_width)
    padded_sources = []
    for level in (1, 2, 3):
        reach = level * RATE
        bands_away = reach // band_rows
        triple = (
            far_rows(shared_image, bands_away, True),
            shared_image,
            far_rows(shared_image, bands_away, False),
        )
        padded_sources.append(
            [jnp.pad(source, ((0, 0), (reach, reach), (0, 0))) for source in triple]
        )
    zero_rows = jnp.zeros((pixels, head_width), jnp.float32)
    start_totals = (
        zero_rows,
        jnp.zeros((1, head_width), jnp.float32),
        zero_rows,
        zero_rows,
        zero_rows,
    )
    all_weights = lax.all_gather(joined_weight, "space", axis=0, tiled=True)
    width_now = all_weights.shape[0]
    one_acc = jnp.dot(shared, all_weights[:, :head_width], preferred_element_type=jnp.float32)
    pool_cols = pixel_sum[None]
    pool_acc = jnp.dot(
        pool_cols,
        all_weights[:, head_width : 2 * head_width].astype(jnp.float32),
        precision=PRECISE,
        preferred_element_type=jnp.float32,
    )
    rate_accs = []
    for fold_level_index in range(3):
        fold_reach = (fold_level_index + 1) * RATE
        running = start_totals[2 + fold_level_index]
        for fold_row_tap in range(3):
            fold_source = padded_sources[fold_level_index][fold_row_tap]
            for fold_col_tap in range(3):
                window = fold_source[
                    :, fold_col_tap * fold_reach : fold_col_tap * fold_reach + cols_count
                ].reshape(pixels, width_now)
                column = (2 + 9 * fold_level_index + 3 * fold_row_tap + fold_col_tap) * head_width
                running = running + jnp.dot(
                    window,
                    all_weights[:, column : column + head_width],
                    preferred_element_type=jnp.float32,
                )
        rate_accs.append(running)
    pre_both = jnp.concatenate([one_acc, rate_accs[0], rate_accs[1], rate_accs[2]], axis=1)
    gain_both, shift_both = (gain_local[: 4 * head_width], shift_local[: 4 * head_width])
    totals = channel_sums(
        (
            jnp.sum(pre_both * valid_mask, axis=0),
            jnp.sum(pre_both * pre_both * valid_mask, axis=0),
            pool_acc[0],
        )
    )
    stats_both = norm_values(pre_both, totals[0], totals[1], gain_both, shift_both, pixel_count)
    pooled = totals[2][None] / pixel_count
    active_both = (jax.nn.gelu(stats_both[0]) * valid_mask).astype(jnp.bfloat16)
    active_pool = jax.nn.gelu(pooled).astype(jnp.bfloat16)
    joined = jnp.concatenate(
        [active_both, (active_pool.astype(jnp.float32) * valid_mask).astype(jnp.bfloat16)], axis=1
    )
    projected = jnp.dot(joined, proj_local, preferred_element_type=jnp.float32)
    gain_proj = gain_local[4 * head_width :]
    stats_proj = norm_forward(
        projected, gain_proj, shift_local[4 * head_width :], valid_mask, pixel_count
    )
    head_result = (jax.nn.gelu(stats_proj[0]) * valid_mask).astype(jnp.bfloat16)
    cot_rows = head_cot[0].reshape(pixels, head_width).astype(jnp.float32)
    proj_upstream = gelu_back(stats_proj[0], cot_rows * valid_mask)
    proj_hidden, proj_gain_grad, proj_shift_grad = norm_backward(
        proj_upstream, stats_proj[1], stats_proj[2], gain_proj, valid_mask, pixel_count
    )
    proj_low = proj_hidden.astype(jnp.bfloat16)
    joined_grad = lax.dot_general(
        proj_low, proj_local, (((1,), (1,)), ((), ())), preferred_element_type=jnp.float32
    )
    proj_term = lax.dot_general(
        joined, proj_low, (((0,), (0,)), ((), ())), preferred_element_type=jnp.float32
    )
    both_upstream = gelu_back(stats_both[0], joined_grad[:, : 4 * head_width] * valid_mask)
    pool_total = jnp.sum(joined_grad[:, 4 * head_width :] * valid_mask, axis=0)
    back_totals = channel_sums(
        (
            proj_term,
            pool_total,
            jnp.sum(both_upstream * valid_mask, axis=0),
            jnp.sum(both_upstream * stats_both[1] * valid_mask, axis=0),
        )
    )
    pool_grad = gelu_back(pooled, back_totals[1][None]).astype(jnp.bfloat16)
    both_grad = norm_finish(
        both_upstream,
        stats_both[1],
        stats_both[2],
        gain_both,
        back_totals[3],
        back_totals[2],
        valid_mask,
        pixel_count,
    ).astype(jnp.bfloat16)
    tap_grads = []
    for level_index in range(3):
        reach = (level_index + 1) * RATE
        bands_away = reach // band_rows
        rate_image = both_grad[
            :, (1 + level_index) * head_width : (2 + level_index) * head_width
        ].reshape(band_rows, cols_count, head_width)
        back_sources = [
            jnp.pad(source, ((0, 0), (reach, reach), (0, 0)))
            for source in (
                far_rows(rate_image, bands_away, False),
                rate_image,
                far_rows(rate_image, bands_away, True),
            )
        ]
        for row_tap in range(3):
            for col_tap in range(3):
                tap_grads.append(
                    back_sources[row_tap][
                        :, (2 - col_tap) * reach : (2 - col_tap) * reach + cols_count
                    ].reshape(pixels, head_width)
                )
    right_side = jnp.concatenate([both_grad[:, :head_width]] + tap_grads, axis=1)
    used_rows = jnp.concatenate(
        [all_weights[:, :head_width], all_weights[:, 2 * head_width :]], axis=1
    )
    main_part = lax.dot_general(
        right_side, used_rows, (((1,), (1,)), ((), ())), preferred_element_type=jnp.float32
    )
    pool_part = lax.dot_general(
        pool_grad,
        all_weights[:, head_width : 2 * head_width],
        (((1,), (1,)), ((), ())),
        preferred_element_type=jnp.float32,
    )
    shared_grad = (main_part + valid_mask * pool_part / pixel_count).astype(jnp.bfloat16)
    head_term = lax.dot_general(
        shared, right_side, (((0,), (0,)), ((), ())), preferred_element_type=jnp.float32
    )
    pool_term = pixel_sum[:, None] * pool_grad.astype(jnp.float32) / pixel_count
    head_term = jnp.concatenate(
        [head_term[:, :head_width], pool_term, head_term[:, head_width:]], axis=1
    )
    all_grads = lax.all_gather(shared_grad[None], "task", axis=0, tiled=True)
    flat_grads = all_grads.reshape(all_grads.shape[0], -1)
    gram_matrix = lax.psum(
        lax.dot_general(
            flat_grads, flat_grads, (((1,), (1,)), ((), ())), preferred_element_type=jnp.float32
        ),
        "space",
    )
    task_weight = imtl_weights(gram_matrix)
    mixed_grad = task_weight[0] * all_grads[0].astype(jnp.float32)
    for task_index in range(1, all_grads.shape[0]):
        mixed_grad = mixed_grad + task_weight[task_index] * all_grads[task_index].astype(
            jnp.float32
        )
    combined = mixed_grad.astype(jnp.bfloat16)
    gate_grad = gelu_back(before_act, combined.astype(jnp.float32) * valid_mask)
    hidden_grad_three, gain_grad_three, shift_grad_three = norm_backward(
        gate_grad, stats_three[1], stats_three[2], gain_three, valid_mask, pixel_count
    )
    low_three = hidden_grad_three.astype(jnp.bfloat16)
    expand_term = lax.dot_general(
        active_two, low_three, (((0,), (0,)), ((), ())), preferred_element_type=jnp.float32
    )
    active_grad_two = lax.dot_general(
        low_three, w_expand, (((1,), (1,)), ((), ())), preferred_element_type=jnp.float32
    )
    upstream_two = gelu_back(stats_two[0], active_grad_two * valid_mask)
    hidden_grad_two, gain_grad_two, shift_grad_two = norm_backward(
        upstream_two, stats_two[1], stats_two[2], gain_two, valid_mask, pixel_count
    )
    low_two = hidden_grad_two.astype(jnp.bfloat16)
    dilated_term = jnp.einsum("pti,po->ito", patches, low_two, preferred_element_type=jnp.float32)
    back_patches = trunk_taps(
        band_rim(low_two.reshape(band_rows, cols_count, middle_width)),
        CONV_DILATION,
        band_rows,
        cols_count,
        True,
    )
    active_grad_one = jnp.einsum(
        "pto,ito->pi", back_patches, w_dilated, preferred_element_type=jnp.float32
    )
    upstream_one = gelu_back(stats_one[0], active_grad_one * valid_mask)
    hidden_grad_one, gain_grad_one, shift_grad_one = norm_backward(
        upstream_one, stats_one[1], stats_one[2], gain_one, valid_mask, pixel_count
    )
    low_one = hidden_grad_one.astype(jnp.bfloat16)
    reduce_term = lax.dot_general(
        inputs, low_one, (((0,), (0,)), ((), ())), preferred_element_type=jnp.float32
    )
    input_grad = (
        lax.dot_general(
            low_one, w_reduce, (((1,), (1,)), ((), ())), preferred_element_type=jnp.float32
        )
        + gate_grad
    )
    reduced = (
        lax.psum_scatter(head_term, "space", scatter_dimension=0, tiled=True),
        lax.psum_scatter(reduce_term, "space", scatter_dimension=0, tiled=True),
        lax.psum_scatter(dilated_term, "space", scatter_dimension=0, tiled=True),
        lax.psum_scatter(expand_term, "space", scatter_dimension=0, tiled=True),
    )
    means = jnp.concatenate([stats_one[3], stats_two[3], stats_three[3]])
    variances = (
        jnp.concatenate([stats_one[4], stats_two[4], stats_three[4]])
        * pixel_count
        / (pixel_count - 1.0)
    )
    batch_stats = jnp.stack([means, variances])
    head_gain_grad = jnp.concatenate([back_totals[3], proj_gain_grad])[None]
    head_shift_grad = jnp.concatenate([back_totals[2], proj_shift_grad])[None]
    return (
        head_result.reshape(1, band_rows, cols_count, head_width),
        input_grad.reshape(band_rows, cols_count, in_width).astype(jnp.bfloat16),
        reduced[1],
        reduced[2],
        reduced[3],
        jnp.concatenate([gain_grad_one, gain_grad_two, gain_grad_three]),
        jnp.concatenate([shift_grad_one, shift_grad_two, shift_grad_three]),
        batch_stats,
        reduced[0][:, : 2 * head_width][None],
        reduced[0][:, 2 * head_width :][None],
        back_totals[0][None],
        head_gain_grad,
        head_shift_grad,
        task_weight,
    )


def solution(mesh):
    return jax.shard_map(
        per_device,
        mesh=mesh,
        in_specs=(
            P("space", None, None),
            P(),
            P(),
            P(),
            P(),
            P(),
            P(),
            P("task", "space", None),
            P("task", "space", None),
            P("task", None, None),
            P("task", None),
            P("task", None),
            P("task", "space", None, None),
        ),
        out_specs=(
            P("task", "space", None, None),
            P("space", None, None),
            P("space", None),
            P("space", None, None),
            P("space", None),
            P(),
            P(),
            P(),
            P("task", "space", None),
            P("task", "space", None),
            P("task", None, None),
            P("task", None),
            P("task", None),
            P(),
        ),
        check_vma=False,
    )
```

profile of v0, /device:TPU:13, one launch (start us, length us, event | category | flops | bytes accessed | tf_op | source)
XLA Modules:
  0.0 1591.6 jit_solution(11085551254530966808)
XLA Ops:
  16.8 10.2 all-reduce.25
  35.7 11.2 collective-permute-done.1
  49.6 26.7 %all-reduce.24 = (f32[512]{0:T(512)S(1)}, f32[512]{0:T(512)S(1)}) all-reduce(f32[512]{0:T(512)S(1)} %get-tuple-element.69, f32[512]{0:T(512)S(1)} %get-tuple-element.68), channel_id=1, replica_groups=mesh['task'=4,'space'=8] {'space'}, use_global_device_ids=true, to_apply=%region_8.9 | all-reduce | flops 1024 | bytes 8192 | tf_op jit(solution)/shard_map/psum | solution.py:66
  79.3 34.0 %all-reduce.23 = (f32[2048]{0:T(1024)S(1)}, f32[2048]{0:T(1024)S(1)}) all-reduce(f32[2048]{0:T(1024)S(1)} %get-tuple-element.59, f32[2048]{0:T(1024)S(1)} %get-tuple-element.58), channel_id=1, replica_groups=mesh['task'=4,'space'=8] {'space'}, use_global_device_ids=true, to_apply=%region_12.13 | all-reduce | flops 4096 | bytes 32768 | tf_op jit(solution)/shard_map/psum | solution.py:66
  139.1 160.4 %all-gather.4.cloned.1.call-done = bf16[2048,7424]{1,0:T(8,128)(2,1)} async-done(((bf16[256,7424]{1,0:T(8,128)(2,1)}), bf16[2048,7424]{1,0:T(8,128)(2,1)}) %all-gather.4.cloned.1.call-update) | async-done | bytes 30408720 | tf_op jit(solution)/shard_map/all_gather | solution.py:211
  340.2 12.7 all-reduce.22
  359.7 14.7 all-reduce.21
  378.3 14.2 all-reduce.20
  400.4 14.0 all-reduce.19
  422.9 19.6 %slice.570 = bf16[2048,6912]{1,0:T(8,128)(2,1)} slice(bf16[2048,7424]{1,0:T(8,128)(2,1)} %all-gather.4.cloned.1.call-done), slice={[0:2048], [512:7424]} | slice | bytes 56623104 | tf_op jit(solution)/shard_map/slice | solution.py:317
  469.5 14.5 fusion.9
  484.3 60.8 %all-gather.6.cloned.1.call-done = bf16[1024,2048]{1,0:T(8,128)(2,1)} async-done(((bf16[256,2048]{1,0:T(8,128)(2,1)}), bf16[1024,2048]{1,0:T(8,128)(2,1)}) %all-gather.6.cloned.1.call-update) | async-done | bytes 4194320 | tf_op jit(solution)/shard_map/all_gather | solution.py:336
  545.1 12.7 fusion.30
  590.3 26.7 %all-reduce.18 = (f32[2048]{0:T(1024)S(1)}, f32[2048]{0:T(1024)S(1)}) all-reduce(f32[2048]{0:T(1024)S(1)} %get-tuple-element.57, f32[2048]{0:T(1024)S(1)} %get-tuple-element.56), channel_id=1, replica_groups=mesh['task'=4,'space'=8] {'space'}, use_global_device_ids=true, to_apply=%region_36.37 | all-reduce | flops 4096 | bytes 32768 | tf_op jit(solution)/shard_map/psum | solution.py:66
  621.4 15.7 all-reduce.17
  652.2 14.2 all-reduce.16
  676.0 16.7 %copy.63 = f32[512,9,512]{2,1,0:T(8,128)} copy(f32[512,9,512]{0,2,1:T(8,128)} %convolution_bitcast_fusion) | data formatting | bytes 18874368 | tf_op jit(solution)/shard_map/pti,po->ito/transpose | solution.py:367
  695.1 23.0 %fusion.144 = f32[2048,7168]{1,0:T(8,128)} fusion(bf16[256,2048]{1,0:T(8,128)(2,1)S(1)} %copy-done.4, bf16[256,7168]{0,1:T(8,128)(2,1)} %bitcast_dynamic-update-slice_fusion.5), kind=kOutput, calls=%fused_computation.346 | convolution fusion | flops 7516192768 | bytes 63438848 | tf_op jit(solution)/shard_map/dot_general | solution.py:329
  718.1 37.8 %slice.583 = f32[2048,6912]{1,0:T(8,128)} slice(f32[2048,7168]{1,0:T(8,128)} %fusion.144), slice={[0:2048], [256:7168]} | slice | bytes 113246208 | tf_op jit(solution)/shard_map/slice | solution.py:334
  757.5 40.6 %pad_maximum_fusion = f32[2048,7424]{1,0:T(8,128)} fusion(f32[2048,6912]{1,0:T(8,128)} %slice.583, f32[2048,256]{1,0:T(8,128)} %multiply_divide_fusion, f32[2048,256]{1,0:T(8,128)S(1)} %slice-done), kind=kLoop, calls=%fused_computation.1 | loop fusion | flops 30408704 | bytes 121634816 | tf_op jit(solution)/shard_map/concatenate | solution.py:333
  815.9 70.6 %reduce-scatter.7.cloned.1.call-done = f32[64,9,512]{2,1,0:T(8,128)} async-done(((f32[512,9,512]{2,1,0:T(8,128)}), f32[64,9,512]{2,1,0:T(8,128)}) %reduce-scatter.7.cloned.1.call-update) | async-done | bytes 1179664 | tf_op jit(solution)/shard_map/reduce_scatter | solution.py:395
  889.7 578.9 %reduce-scatter.11.cloned.1.call-done = f32[256,7424]{1,0:T(8,128)} async-done(((f32[2048,7424]{1,0:T(8,128)}), f32[256,7424]{1,0:T(8,128)}) %reduce-scatter.11.cloned.1.call-update) | async-done | bytes 7602192 | tf_op jit(solution)/shard_map/reduce_scatter | solution.py:393
  1477.1 52.1 %all-reduce.28.cloned.1.call-done = f32[1,1280,256]{2,1,0:T(8,128)} async-done(((f32[1,1280,256]{2,1,0:T(8,128)}), f32[1,1280,256]{2,1,0:T(8,128)}) %all-reduce.28.cloned.1.call-update) | async-done | bytes 1310736 | tf_op jit(solution)/shard_map/psum | solution.py:66
  1529.2 52.8 %reduce-scatter.9.cloned.1.call-done = f32[64,2048]{1,0:T(8,128)} async-done(((f32[512,2048]{1,0:T(8,128)}), f32[64,2048]{1,0:T(8,128)}) %reduce-scatter.9.cloned.1.call-update) | async-done | bytes 524304 | tf_op jit(solution)/shard_map/reduce_scatter | solution.py:396
  (410 shorter events, 229.4 us)
Async XLA Ops:
  7.2 69.7 %copy-start = (bf16[512,2048]{1,0:T(8,128)(2,1)S(1)}, bf16[512,2048]{1,0:T(8,128)(2,1)}, u32[]{:S(2)}) copy-start(bf16[512,2048]{1,0:T(8,128)(2,1)} %param.17) | copy-start | bytes 6291460
  7.2 292.3 %all-gather.4.cloned.1.call-start = ((), (), s32[]{:S(2)}) async-start(), calls=%async_computation.4 | async-start | bytes 34209792 | tf_op jit(solution)/shard_map/all_gather | solution.py:211
  11.6 533.5 %all-gather.6.cloned.1.call-start = ((), (), s32[]{:S(2)}) async-start(), calls=%async_computation.10 | async-start | bytes 5242880 | tf_op jit(solution)/shard_map/all_gather | solution.py:336
  27.6 49.3 %copy-start.57 = (f32[512]{0:T(512)}, f32[512]{0:T(512)S(1)}, u32[]{:S(2)}) copy-start(f32[512]{0:T(512)S(1)} %get-tuple-element.159) | copy-start | bytes 6148
  27.6 49.3 %copy-start.66 = (f32[512]{0:T(512)}, f32[512]{0:T(512)S(1)}, u32[]{:S(2)}) copy-start(f32[512]{0:T(512)S(1)} %get-tuple-element.189) | copy-start | bytes 6148
  27.9 19.0 %collective-permute-start.1 = (bf16[2,128,512]{2,1,0:T(8,128)(2,1)S(1)}, bf16[2,128,512]{2,1,0:T(8,128)(2,1)S(1)}, u32[]{:S(2)}, u32[]{:S(2)}) collective-permute-start(bf16[2,128,512]{2,1,0:T(8,128)(2,1)S(1)} %bitcast.302), channel_id=1, source_target_pairs={{1,0},{2,1},{3,2},{4,3},{5,4},{6,5},{7,6},{9,8},{10,9},{11,10},{12... | collective-permute-start | bytes 786440 | tf_op jit(solution)/shard_map/ppermute | solution.py:23
  33.8 13.2 collective-permute-start
  35.7 78.2 %copy-start.59 = (f32[2048]{0:T(1024)}, f32[2048]{0:T(1024)S(1)}, u32[]{:S(2)}) copy-start(f32[2048]{0:T(1024)S(1)} %slice.422) | copy-start | bytes 24580
  35.7 78.1 %copy-start.47 = (f32[2048]{0:T(1024)}, f32[2048]{0:T(1024)S(1)}, u32[]{:S(2)}) copy-start(f32[2048]{0:T(1024)S(1)} %slice.411) | copy-start | bytes 24580
  116.9 220.5 %copy-start.3 = (bf16[256,2048]{1,0:T(8,128)(2,1)}, bf16[256,2048]{1,0:T(8,128)(2,1)S(1)}, u32[]{:S(2)}) copy-start(bf16[256,2048]{1,0:T(8,128)(2,1)S(1)} %multiply_convert_fusion.1) | copy-start | bytes 3145732
  116.9 15.3 collective-permute-start.3
  121.1 14.7 collective-permute-start.2
  359.7 40.0 %copy-start.35 = (f32[256,256]{0,1:T(8,128)}, f32[256,256]{0,1:T(8,128)S(1)}, u32[]{:S(2)}) copy-start(f32[256,256]{0,1:T(8,128)S(1)} %get-tuple-element.185) | copy-start | bytes 786436
  418.7 24.1 %collective-permute-start.4 = (bf16[2,128,256]{1,0,2:T(2,128)(2,1)S(1)}, bf16[2,128,256]{1,0,2:T(2,128)(2,1)S(1)}, u32[]{:S(2)}, u32[]{:S(2)}) collective-permute-start(bf16[2,128,256]{1,0,2:T(2,128)(2,1)S(1)} %reshape.413), channel_id=1, source_target_pairs={{6,0},{7,1},{14,8},{15,9},{22,16},{23,17},{30,24},{31,25}} | collective-permute-start | bytes 393224 | tf_op jit(solution)/shard_map/ppermute | solution.py:31
  419.4 27.9 %collective-permute-start.5 = (bf16[2,128,256]{1,0,2:T(2,128)(2,1)S(1)}, bf16[2,128,256]{1,0,2:T(2,128)(2,1)S(1)}, u32[]{:S(2)}, u32[]{:S(2)}) collective-permute-start(bf16[2,128,256]{1,0,2:T(2,128)(2,1)S(1)} %reshape.413), channel_id=1, source_target_pairs={{0,6},{1,7},{8,14},{9,15},{16,22},{17,23},{24,30},{25,31}} | collective-permute-start | bytes 393224 | tf_op jit(solution)/shard_map/ppermute | solution.py:31
  484.1 329.8 %reduce-scatter.5.cloned.1.call-start = ((), (), s32[]{:S(2)}) async-start(), calls=%async_computation.5 | async-start | bytes 4718592 | tf_op jit(solution)/shard_map/reduce_scatter | solution.py:394
  545.1 39.3 %copy-start.60 = (f32[2048]{0:T(1024)S(1)}, f32[2048]{0:T(1024)}, u32[]{:S(2)}) copy-start(f32[2048]{0:T(1024)} %copy-done.59) | copy-start | bytes 24580
  637.4 7.7 collective-permute-start.7
  639.9 6.5 collective-permute-start.6
  669.2 217.2 %reduce-scatter.7.cloned.1.call-start = ((), (), s32[]{:S(2)}) async-start(), calls=%async_computation.6 | async-start | bytes 18874368 | tf_op jit(solution)/shard_map/reduce_scatter | solution.py:395
  692.8 775.9 %reduce-scatter.11.cloned.1.call-start = ((), (), s32[]{:S(2)}) async-start(), calls=%async_computation.8 | async-start | bytes 68419584 | tf_op jit(solution)/shard_map/reduce_scatter | solution.py:393
  798.2 731.0 %all-reduce.28.cloned.1.call-start = ((), (), s32[]{:S(2)}) async-start(), calls=%async_computation.9 | async-start | bytes 2621440 | tf_op jit(solution)/shard_map/psum | solution.py:66
  802.0 780.0 %reduce-scatter.9.cloned.1.call-start = ((), (), s32[]{:S(2)}) async-start(), calls=%async_computation.7 | async-start | bytes 4718592 | tf_op jit(solution)/shard_map/reduce_scatter | solution.py:396
  1470.5 113.9 %copy-start.1 = (bf16[512,2048]{1,0:T(8,128)(2,1)S(1)}, bf16[512,2048]{1,0:T(8,128)(2,1)}, u32[]{:S(2)}) copy-start(bf16[512,2048]{1,0:T(8,128)(2,1)} %param.17) | copy-start | bytes 6291460
  (90 other events, 747.6 us)
Sparse Core Ops, SparseCore 0:
  11.7 287.8 all-gather.3
  484.2 60.8 all-gather.5
  669.4 48.4 reduce-scatter.4
  720.0 166.3 reduce-scatter.6
  888.7 579.9 reduce-scatter.10
  1471.6 57.5 all-reduce.27
  1532.2 49.7 reduce-scatter.8
where the time goes:
time: 1600 us; the launch traced here: 1590 us
  waiting for transfers between devices  990 us (62%)
  blocking collectives  193 us (12%)
  local copies, waits for them, and re-layouts  152 us (10%)
  matrix products  128 us (8%)
  other arithmetic  82.3 us (5%)
  between operations  27.3 us (2%)
  starting transfers between devices  18.7 us (1%)
    reduce_scatter x1, waiting for transfers between devices, per_device(): lax.psum_scatter(head_term, 'space', scatter_dimension=0, tiled=True)  579 us
    psum x10, blocking collectives, channel_sums(): return lax.psum(members, 'space')  183 us
    all_gather x1, waiting for transfers between devices, per_device(): all_weights = lax.all_gather(joined_weight, 'space', axis=0, tiled=True)  160 us
    reduce_scatter x1, waiting for transfers between devices, per_device(): lax.psum_scatter(dilated_term, 'space', scatter_dimension=0, tiled=True)  70.6 us
    all_gather x1, waiting for transfers between devices, per_device(): all_grads = lax.all_gather(shared_grad[None], 'task', axis=0, tiled=True)  60.8 us
    reduce_scatter x1, waiting for transfers between devices, per_device(): lax.psum_scatter(expand_term, 'space', scatter_dimension=0, tiled=True)  52.8 us
    psum x1, waiting for transfers between devices, channel_sums(): return lax.psum(members, 'space')  52.1 us
    concatenate x1, other arithmetic, per_device(): jnp.concatenate([head_term[:, :head_width], pool_term, head_term[:, head_...  40.6 us
  transfers between devices with their start and end apart: 15, of which 9 were waited for; matrix products, arithmetic and copies ran while one was open for 13% of the time, Pallas kernels for 0%

commit v1 on v0

--- a/solution.py
+++ b/solution.py
@@ -1,6 +1,10 @@
+import functools
+
 import jax
 import jax.numpy as jnp
 from jax import lax
+from jax.experimental import pallas as pl
+from jax.experimental.pallas import tpu as pltpu
 from jax.sharding import PartitionSpec as P
 
 CONV_DILATION = 2
@@ -422,9 +426,634 @@
     )
 
 
+MESH_ID = pl.DeviceIdType.MESH
+LANE = 128
+
+
+def meet_bands(place, count):
+    barrier = pltpu.get_barrier_semaphore()
+    for step in range(1, count):
+        pl.semaphore_signal(
+            barrier,
+            inc=1,
+            device_id={"space": lax.rem(place + step, count)},
+            device_id_type=MESH_ID,
+        )
+    pl.semaphore_wait(barrier, count - 1)
+
+
+def sum_kernel(count, own_ref, out_ref, landing, send_sem, recv_sem):
+    place = lax.axis_index("space")
+    meet_bands(place, count)
+    copies = []
+    for step in range(1, count):
+        copy = pltpu.make_async_remote_copy(
+            own_ref,
+            landing.at[step],
+            send_sem.at[step],
+            recv_sem.at[step],
+            device_id={"space": lax.rem(place + step, count)},
+            device_id_type=MESH_ID,
+        )
+        copy.start()
+        copies.append(copy)
+    total = own_ref[...]
+    for step in range(1, count):
+        copies[step - 1].wait_recv()
+        total = total + landing[step]
+    out_ref[...] = total
+    for copy in copies:
+        copy.wait_send()
+
+
+def gather_kernel(count, own_ref, out_ref, send_sem, recv_sem, local_sem):
+    place = lax.axis_index("space")
+    chips = count // 2
+    chip = place // 2
+    core = lax.rem(place, 2)
+    twin = chip * 2 + 1 - core
+    meet_bands(place, count)
+    copies = []
+    for step in range(1, chips):
+        copy = pltpu.make_async_remote_copy(
+            own_ref,
+            out_ref.at[place],
+            send_sem.at[step],
+            recv_sem.at[step],
+            device_id={"space": lax.rem(chip + step, chips) * 2 + core},
+            device_id_type=MESH_ID,
+        )
+        copy.start()
+        copies.append(copy)
+    to_twin = pltpu.make_async_remote_copy(
+        own_ref,
+        out_ref.at[place],
+        send_sem.at[0],
+        recv_sem.at[0],
+        device_id={"space": twin},
+        device_id_type=MESH_ID,
+    )
+    to_twin.start()
+    here = pltpu.make_async_copy(own_ref, out_ref.at[place], local_sem)
+    here.start()
+    passed = []
+    for step in range(1, chips):
+        copies[step - 1].wait_recv()
+        source = lax.rem(chip + chips - step, chips) * 2 + core
+        copy = pltpu.make_async_remote_copy(
+            out_ref.at[source],
+            out_ref.at[source],
+            send_sem.at[chips - 1 + step],
+            recv_sem.at[chips - 1 + step],
+            device_id={"space": twin},
+            device_id_type=MESH_ID,
+        )
+        copy.start()
+        passed.append(copy)
+    to_twin.wait()
+    for copy in passed:
+        copy.wait()
+    for copy in copies:
+        copy.wait_send()
+    here.wait()
+
+
+def swap_kernel(count, own_ref, out_ref, send_sem, recv_sem, local_sem):
+    place = lax.axis_index("space")
+    meet_bands(place, count)
+    copies = []
+    for step in range(1, count):
+        target = lax.rem(place + step, count)
+        copy = pltpu.make_async_remote_copy(
+            own_ref.at[target],
+            out_ref.at[place],
+            send_sem.at[step],
+            recv_sem.at[step],
+            device_id={"space": target},
+            device_id_type=MESH_ID,
+        )
+        copy.start()
+        copies.append(copy)
+    here = pltpu.make_async_copy(own_ref.at[place], out_ref.at[place], local_sem)
+    here.start()
+    for copy in copies:
+        copy.wait()
+    here.wait()
+
+
+def scatter_kernel(count, own_ref, out_ref, twin_land, paired, landing, send_sem, recv_sem):
+    place = lax.axis_index("space")
+    chips = count // 2
+    chip = place // 2
+    core = lax.rem(place, 2)
+    twin = chip * 2 + 1 - core
+    meet_bands(place, count)
+    from_twin = []
+    for step in range(chips):
+        other = lax.rem(chip + step, chips)
+        copy = pltpu.make_async_remote_copy(
+            own_ref.at[other * 2 + 1 - core],
+            twin_land.at[step],
+            send_sem.at[step],
+            recv_sem.at[step],
+            device_id={"space": twin},
+            device_id_type=MESH_ID,
+        )
+        from_twin.append(copy)
+    order = list(range(1, chips)) + [0]
+    for step in order:
+        from_twin[step].start()
+    sent = []
+    for step in order:
+        from_twin[step].wait_recv()
+        other = lax.rem(chip + step, chips)
+        pair = own_ref[other * 2 + core].astype(jnp.float32) + twin_land[step].astype(jnp.float32)
+        if step == 0:
+            out_ref[...] = pair
+            continue
+        paired[step] = pair.astype(paired.dtype)
+        copy = pltpu.make_async_remote_copy(
+            paired.at[step],
+            landing.at[step],
+            send_sem.at[chips + step],
+            recv_sem.at[chips + step],
+            device_id={"space": other * 2 + core},
+            device_id_type=MESH_ID,
+        )
+        copy.start()
+        sent.append(copy)
+    for step in range(1, chips):
+        sent[step - 1].wait_recv()
+        out_ref[...] += landing[step].astype(jnp.float32)
+    for copy in sent:
+        copy.wait_send()
+    for copy in from_twin:
+        copy.wait_send()
+
+
+def tasks_kernel(count, own_ref, out_ref, send_sem, recv_sem, local_sem):
+    place = lax.axis_index("task")
+    barrier = pltpu.get_barrier_semaphore()
+    for step in range(1, count):
+        pl.semaphore_signal(
+            barrier,
+            inc=1,
+            device_id={"task": lax.rem(place + step, count)},
+            device_id_type=MESH_ID,
+        )
+    pl.semaphore_wait(barrier, count - 1)
+    copies = []
+    for step in range(1, count):
+        copy = pltpu.make_async_remote_copy(
+            own_ref,
+            out_ref.at[place],
+            send_sem.at[step],
+            recv_sem.at[step],
+            device_id={"task": lax.rem(place + step, count)},
+            device_id_type=MESH_ID,
+        )
+        copy.start()
+        copies.append(copy)
+    here = pltpu.make_async_copy(own_ref, out_ref.at[place], local_sem)
+    here.start()
+    for copy in copies:
+        copy.wait()
+    here.wait()
+
+
+class Links:
+    def __init__(self):
+        self.bands = lax.axis_size("space")
+        self.tasks = lax.axis_size("task")
+        self.used = 0
+
+    def call(self, kernel, out, scratch, operand, label):
+        self.used += 1
+        in_vmem = pl.BlockSpec(memory_space=pltpu.VMEM)
+        return pl.pallas_call(
+            kernel,
+            name=label,
+            out_shape=out,
+            in_specs=[in_vmem],
+            out_specs=in_vmem,
+            scratch_shapes=scratch,
+            compiler_params=pltpu.CompilerParams(
+                collective_id=self.used - 1, has_side_effects=True, vmem_limit_bytes=48 << 20
+            ),
+        )(operand)
+
+    def sums(self, members, label):
+        sizes = [member.size for member in members]
+        flat = jnp.concatenate([member.reshape(-1) for member in members])
+        tile = 8 * LANE
+        padded = -(-flat.size // tile) * tile
+        block = jnp.pad(flat, (0, padded - flat.size)).reshape(-1, LANE)
+        sems = pltpu.SemaphoreType.DMA((self.bands,))
+        total = self.call(
+            functools.partial(sum_kernel, self.bands),
+            jax.ShapeDtypeStruct(block.shape, block.dtype),
+            [pltpu.VMEM((self.bands,) + block.shape, block.dtype), sems, sems],
+            block,
+            label,
+        ).reshape(-1)
+        out = []
+        start = 0
+        for member, size in zip(members, sizes):
+            out.append(total[start : start + size].reshape(member.shape))
+            start += size
+        return out
+
+    def gather(self, block, label):
+        sems = pltpu.SemaphoreType.DMA((self.bands,))
+        return self.call(
+            functools.partial(gather_kernel, self.bands),
+            jax.ShapeDtypeStruct((self.bands,) + block.shape, block.dtype),
+            [sems, sems, pltpu.SemaphoreType.DMA],
+            block,
+            label,
+        )
+
+    def swap(self, blocks, label):
+        sems = pltpu.SemaphoreType.DMA((self.bands,))
+        return self.call(
+            functools.partial(swap_kernel, self.bands),
+            jax.ShapeDtypeStruct(blocks.shape, blocks.dtype),
+            [sems, sems, pltpu.SemaphoreType.DMA],
+            blocks,
+            label,
+        )
+
+    def scatter(self, blocks, label):
+        sems = pltpu.SemaphoreType.DMA((self.bands,))
+        half = (self.bands // 2,) + blocks.shape[1:]
+        return self.call(
+            functools.partial(scatter_kernel, self.bands),
+            jax.ShapeDtypeStruct(blocks.shape[1:], jnp.float32),
+            [pltpu.VMEM(half, blocks.dtype)] * 3 + [sems, sems],
+            blocks,
+            label,
+        )
+
+    def over_tasks(self, block, label):
+        sems = pltpu.SemaphoreType.DMA((self.tasks,))
+        return self.call(
+            functools.partial(tasks_kernel, self.tasks),
+            jax.ShapeDtypeStruct((self.tasks,) + block.shape, block.dtype),
+            [sems, sems, pltpu.SemaphoreType.DMA],
+            block,
+            label,
+        )
+
+
+def norm_scale(totals, pixel_count):
+    mean_value = totals[0] / pixel_count
+    variance = totals[1] / pixel_count - mean_value * mean_value
+    return mean_value, variance, lax.rsqrt(variance + NORM_EPS)
+
+
+def masked_sums(hidden, valid_mask):
+    kept = hidden * valid_mask
+    return [jnp.sum(kept, axis=0), jnp.sum(hidden * kept, axis=0)]
+
+
+def shift_columns(image, by):
+    if by == 0:
+        return image
+    cols = image.shape[1]
+    if by > 0:
+        return jnp.pad(image[:, by:], ((0, 0), (0, by), (0, 0)))
+    return jnp.pad(image[:, : cols + by], ((0, 0), (-by, 0), (0, 0)))
+
+
+def live_taps(rows, cols):
+    taps = []
+    for level in (1, 2, 3):
+        for row_tap in range(3):
+            for col_tap in range(3):
+                down, right = (row_tap - 1) * level * RATE, (col_tap - 1) * level * RATE
+                if abs(down) < rows and abs(right) < cols:
+                    taps.append((level, row_tap, col_tap, down, right))
+    return taps
+
+
+def per_device_slices(
+    features,
+    row_width,
+    w_reduce,
+    w_dilated,
+    w_expand,
+    trunk_gain,
+    trunk_shift,
+    branch_weight,
+    rate_weight,
+    proj_weight,
+    head_gain,
+    head_shift,
+    head_cot,
+):
+    links = Links()
+    bands, tasks = links.bands, links.tasks
+    low = jnp.bfloat16
+    wide = jnp.float32
+    band_rows, cols_count, in_width = features.shape
+    rows_count = band_rows * bands
+    pixels = band_rows * cols_count
+    all_pixels = pixels * bands
+    middle_width = w_reduce.shape[1]
+    head_width = proj_weight.shape[2]
+    slice_width = in_width // bands
+    band = lax.axis_index("space")
+    task = lax.axis_index("task")
+    widths = lax.dynamic_slice_in_dim(row_width, band * band_rows, band_rows)
+
+    def mask_of(some_widths):
+        return (
+            (jnp.arange(cols_count)[None, :] < some_widths[:, None]).astype(wide).reshape(-1, 1)
+        )
+
+    valid_mask = mask_of(widths)
+    all_mask = mask_of(row_width)
+    pixel_count = jnp.sum(row_width).astype(wide)
+    inputs = features.reshape(pixels, in_width)
+    gains = [
+        trunk_gain[:middle_width],
+        trunk_gain[middle_width : 2 * middle_width],
+        trunk_gain[2 * middle_width :],
+    ]
+    shifts = [
+        trunk_shift[:middle_width],
+        trunk_shift[middle_width : 2 * middle_width],
+        trunk_shift[2 * middle_width :],
+    ]
+
+    def norm(hidden, totals, gain_vec, shift_vec):
+        mean_value, variance, inv_std = norm_scale(totals, pixel_count)
+        scaled = (hidden - mean_value) * inv_std
+        return gain_vec * scaled + shift_vec, scaled, inv_std, mean_value, variance
+
+    hidden_one = jnp.dot(inputs, w_reduce, preferred_element_type=wide)
+    stats_one = norm(
+        hidden_one, links.sums(masked_sums(hidden_one, valid_mask), "sums_one"), gains[0], shifts[0]
+    )
+    first_active = (jax.nn.gelu(stats_one[0]) * valid_mask).astype(low)
+    patches = trunk_taps(
+        band_rim(first_active.reshape(band_rows, cols_count, middle_width)),
+        CONV_DILATION,
+        band_rows,
+        cols_count,
+        False,
+    )
+    hidden_two = jnp.einsum("pti,ito->po", patches, w_dilated, preferred_element_type=wide)
+    stats_two = norm(
+        hidden_two, links.sums(masked_sums(hidden_two, valid_mask), "sums_two"), gains[1], shifts[1]
+    )
+    active_two = (jax.nn.gelu(stats_two[0]) * valid_mask).astype(low)
+    hidden_three = jnp.dot(active_two, w_expand, preferred_element_type=wide)
+    stats_three = norm(
+        hidden_three,
+        links.sums(masked_sums(hidden_three, valid_mask), "sums_three"),
+        gains[2],
+        shifts[2],
+    )
+    before_act = stats_three[0] + inputs.astype(wide)
+    shared = (jax.nn.gelu(before_act) * valid_mask).astype(low)
+
+    shared_slice = links.swap(
+        shared.reshape(pixels, bands, slice_width).transpose(1, 0, 2), "swap_shared"
+    ).reshape(all_pixels, slice_width)
+    pixel_sum = jnp.sum(shared_slice.astype(wide), axis=0)
+    branch_local = branch_weight[0]
+    rate_local = rate_weight[0]
+    proj_local = proj_weight[0]
+    gain_local = head_gain[0]
+    shift_local = head_shift[0]
+
+    def rate_columns(level, row_tap, col_tap):
+        start = (9 * (level - 1) + 3 * row_tap + col_tap) * head_width
+        return slice(start, start + head_width)
+
+    taps = live_taps(rows_count, cols_count)
+    shared_image = shared_slice.reshape(rows_count, cols_count, slice_width)
+    pre_parts = [
+        jnp.dot(shared_slice, branch_local[:, :head_width], preferred_element_type=wide).reshape(
+            rows_count, cols_count, head_width
+        )
+    ]
+    for level in (1, 2, 3):
+        total = jnp.zeros((rows_count, cols_count, head_width), wide)
+        for number, row_tap, col_tap, down, right in taps:
+            if number != level:
+                continue
+            first, last = max(0, -down), rows_count - max(0, down)
+            window = shift_columns(shared_image[first + down : last + down], right)
+            term = jnp.dot(
+                window.reshape(-1, slice_width),
+                rate_local[:, rate_columns(level, row_tap, col_tap)],
+                preferred_element_type=wide,
+            ).reshape(last - first, cols_count, head_width)
+            total = total + jnp.pad(term, ((first, rows_count - last), (0, 0), (0, 0)))
+        pre_parts.append(total)
+    pre_terms = jnp.concatenate(pre_parts, axis=2).astype(low)
+    pre_both = links.scatter(pre_terms.reshape(bands, pixels, 4 * head_width), "scatter_pre")
+    pool_term = jnp.dot(
+        pixel_sum[None],
+        branch_local[:, head_width:].astype(wide),
+        precision=PRECISE,
+        preferred_element_type=wide,
+    )
+    totals = links.sums(masked_sums(pre_both, valid_mask) + [pool_term], "sums_both")
+    gain_both, shift_both = (gain_local[: 4 * head_width], shift_local[: 4 * head_width])
+    stats_both = norm(pre_both, totals, gain_both, shift_both)
+    pooled = totals[2] / pixel_count
+    active_both = (jax.nn.gelu(stats_both[0]) * valid_mask).astype(low)
+    active_pool = jax.nn.gelu(pooled).astype(low)
+    joined = jnp.concatenate(
+        [active_both, (active_pool.astype(wide) * valid_mask).astype(low)], axis=1
+    )
+    projected = jnp.dot(joined, proj_local, preferred_element_type=wide)
+    gain_proj = gain_local[4 * head_width :]
+    stats_proj = norm(
+        projected,
+        links.sums(masked_sums(projected, valid_mask), "sums_proj"),
+        gain_proj,
+        shift_local[4 * head_width :],
+    )
+    head_result = (jax.nn.gelu(stats_proj[0]) * valid_mask).astype(low)
+    cot_rows = head_cot[0].reshape(pixels, head_width).astype(wide)
+
+    def back_sums(upstream, scaled):
+        kept = upstream * valid_mask
+        return [jnp.sum(kept, axis=0), jnp.sum(kept * scaled, axis=0)]
+
+    def finish(upstream, stats, gain_vec, sums):
+        return norm_finish(
+            upstream, stats[1], stats[2], gain_vec, sums[1], sums[0], valid_mask, pixel_count
+        ).astype(low)
+
+    proj_upstream = gelu_back(stats_proj[0], cot_rows * valid_mask)
+    proj_sums = links.sums(back_sums(proj_upstream, stats_proj[1]), "back_proj")
+    proj_low = finish(proj_upstream, stats_proj, gain_proj, proj_sums)
+    joined_grad = lax.dot_general(
+        proj_low, proj_local, (((1,), (1,)), ((), ())), preferred_element_type=wide
+    )
+    proj_term = lax.dot_general(
+        joined, proj_low, (((0,), (0,)), ((), ())), preferred_element_type=wide
+    )
+    both_upstream = gelu_back(stats_both[0], joined_grad[:, : 4 * head_width] * valid_mask)
+    pool_total = jnp.sum(joined_grad[:, 4 * head_width :] * valid_mask, axis=0)
+    both_sums = links.sums(back_sums(both_upstream, stats_both[1]) + [pool_total], "back_both")
+    pool_grad = gelu_back(pooled, both_sums[2][None]).astype(low)
+    both_grad = finish(both_upstream, stats_both, gain_both, both_sums)
+    proj_grad = lax.psum(proj_term, "space")
+
+    both_all = links.gather(both_grad, "gather_both").reshape(
+        rows_count, cols_count, 4 * head_width
+    )
+    turned = shared_slice.T
+
+    def shared_back(first, last, grad_rows, weights):
+        flat = grad_rows.reshape(-1, head_width)
+        part = lax.dot_general(
+            flat, weights, (((1,), (1,)), ((), ())), preferred_element_type=wide
+        ).reshape(last - first, cols_count, slice_width)
+        grad = jnp.dot(
+            turned[:, first * cols_count : last * cols_count], flat, preferred_element_type=wide
+        )
+        return jnp.pad(part, ((first, rows_count - last), (0, 0), (0, 0))), grad
+
+    slice_grad, one_grad = shared_back(
+        0, rows_count, both_all[:, :, :head_width], branch_local[:, :head_width]
+    )
+    rate_grads = {}
+    for level, row_tap, col_tap, down, right in taps:
+        image = both_all[:, :, level * head_width : (level + 1) * head_width]
+        first, last = max(0, down), rows_count - max(0, -down)
+        window = shift_columns(image[first - down : last - down], -right)
+        part, grad = shared_back(
+            first, last, window, rate_local[:, rate_columns(level, row_tap, col_tap)]
+        )
+        slice_grad = slice_grad + part
+        rate_grads[level, row_tap, col_tap] = grad
+    nothing = jnp.zeros((slice_width, head_width), wide)
+    rate_grad = jnp.concatenate(
+        [
+            rate_grads.get((level, row_tap, col_tap), nothing)
+            for level in (1, 2, 3)
+            for row_tap in range(3)
+            for col_tap in range(3)
+        ],
+        axis=1,
+    )
+    pool_weight_grad = pixel_sum[:, None] * pool_grad.astype(wide) / pixel_count
+    branch_grad = jnp.concatenate([one_grad, pool_weight_grad], axis=1)
+    pool_part = lax.dot_general(
+        pool_grad,
+        branch_local[:, head_width:],
+        (((1,), (1,)), ((), ())),
+        preferred_element_type=wide,
+    )
+    shared_grad = (
+        slice_grad.reshape(all_pixels, slice_width) + all_mask * pool_part / pixel_count
+    ).astype(low)
+
+    all_grads = links.over_tasks(shared_grad, "tasks_grads")
+    flat_grads = all_grads.reshape(tasks, -1)
+    gram_part = lax.dot_general(
+        flat_grads, flat_grads, (((1,), (1,)), ((), ())), preferred_element_type=wide
+    )
+    gram_matrix = links.sums([gram_part], "sums_gram")[0]
+    task_weight = imtl_weights(gram_matrix)
+    mixed_grad = task_weight[0] * all_grads[0].astype(wide)
+    for task_index in range(1, tasks):
+        mixed_grad = mixed_grad + task_weight[task_index] * all_grads[task_index].astype(wide)
+    combined = (
+        links.swap(mixed_grad.astype(low).reshape(bands, pixels, slice_width), "swap_combined")
+        .transpose(1, 0, 2)
+        .reshape(pixels, in_width)
+    )
+
+    gate_grad = gelu_back(before_act, combined.astype(wide) * valid_mask)
+    sums_three = links.sums(back_sums(gate_grad, stats_three[1]), "back_three")
+    low_three = finish(gate_grad, stats_three, gains[2], sums_three)
+    active_grad_two = lax.dot_general(
+        low_three, w_expand, (((1,), (1,)), ((), ())), preferred_element_type=wide
+    )
+    upstream_two = gelu_back(stats_two[0], active_grad_two * valid_mask)
+    sums_two = links.sums(back_sums(upstream_two, stats_two[1]), "back_two")
+    low_two = finish(upstream_two, stats_two, gains[1], sums_two)
+    back_patches = trunk_taps(
+        band_rim(low_two.reshape(band_rows, cols_count, middle_width)),
+        CONV_DILATION,
+        band_rows,
+        cols_count,
+        True,
+    )
+    active_grad_one = jnp.einsum("pto,ito->pi", back_patches, w_dilated, preferred_element_type=wide)
+    upstream_one = gelu_back(stats_one[0], active_grad_one * valid_mask)
+    sums_one = links.sums(back_sums(upstream_one, stats_one[1]), "back_one")
+    low_one = finish(upstream_one, stats_one, gains[0], sums_one)
+    input_grad = (
+        lax.dot_general(low_one, w_reduce, (((1,), (1,)), ((), ())), preferred_element_type=wide)
+        + gate_grad
+    ).astype(low)
+
+    def share(low_grad):
+        width = low_grad.shape[1] // tasks
+        return lax.dynamic_slice_in_dim(low_grad, task * width, width, axis=1)
+
+    def against(left_side, right_side):
+        return lax.dot_general(
+            left_side, right_side, (((0,), (0,)), ((), ())), preferred_element_type=wide
+        ).astype(low)
+
+    narrow = middle_width // tasks
+    wide_share = in_width // tasks
+    expand_term = against(active_two, share(low_three)).reshape(bands, -1, narrow)
+    reduce_term = against(inputs, share(low_one)).reshape(bands, -1, narrow)
+    dilated_term = against(
+        patches.transpose(0, 2, 1).reshape(pixels, -1), share(low_two)
+    ).reshape(bands, -1, narrow)
+    terms = jnp.concatenate([expand_term, reduce_term, dilated_term], axis=1)
+    shares = links.over_tasks(
+        links.scatter(terms, "scatter_trunk").astype(low), "tasks_trunk"
+    ).astype(wide)
+    cut_one = expand_term.shape[1]
+    cut_two = cut_one + reduce_term.shape[1]
+    w_expand_grad = (
+        shares[:, :cut_one].reshape(tasks, -1, wide_share).transpose(1, 0, 2).reshape(-1, in_width)
+    )
+    w_reduce_grad = shares[:, cut_one:cut_two].transpose(1, 0, 2).reshape(-1, middle_width)
+    w_dilated_grad = (
+        shares[:, cut_two:].transpose(1, 0, 2).reshape(-1, 9, middle_width)
+    )
+    means = jnp.concatenate([stats_one[3], stats_two[3], stats_three[3]])
+    variances = (
+        jnp.concatenate([stats_one[4], stats_two[4], stats_three[4]])
+        * pixel_count
+        / (pixel_count - 1.0)
+    )
+    return (
+        head_result.reshape(1, band_rows, cols_count, head_width),
+        input_grad.reshape(band_rows, cols_count, in_width),
+        w_reduce_grad,
+        w_dilated_grad,
+        w_expand_grad,
+        jnp.concatenate([sums_one[1], sums_two[1], sums_three[1]]),
+        jnp.concatenate([sums_one[0], sums_two[0], sums_three[0]]),
+        jnp.stack([means, variances]),
+        branch_grad[None],
+        rate_grad[None],
+        proj_grad[None],
+        jnp.concatenate([both_sums[1], proj_sums[1]])[None],
+        jnp.concatenate([both_sums[0], proj_sums[0]])[None],
+        task_weight,
+    )
+
+
 def solution(mesh):
+    body = per_device_slices if mesh.shape["space"] == 8 else per_device
     return jax.shard_map(
-        per_device,
+        body,
         mesh=mesh,
         in_specs=(
             P("space", None, None),

time: 1600 us -> 551 us (0.34)
  waiting for transfers between devices: 990 us -> 1.89 us
  Pallas kernels: 0 us -> 316 us
  blocking collectives: 193 us -> 0 us
  local copies, waits for them, and re-layouts: 152 us -> 82.8 us
  matrix products: 128 us -> 67.3 us
  other arithmetic: 82.3 us -> 32.5 us
    reduce_scatter x4 -> x0, waiting for transfers between devices: 702 us -> none  [the longest x1 579 us: per_device(): lax.psum_scatter(head_term, 'space', scatter_dimension=0, tiled=True)]
    pallas_call x0 -> x18, Pallas kernels: none -> 316 us  [call(): pl.pallas_call(kernel, name=label, out_shape=out, in_specs=[in_vmem], out...]
    all_gather x2 -> x0, waiting for transfers between devices: 221 us -> none  [the longest x1 160 us: per_device(): all_weights = lax.all_gather(joined_weight, 'space', axis=0, tiled=True)]
    psum x11 -> x0, blocking collectives: 193 us -> none  [the longest x10 183 us: channel_sums(): return lax.psum(members, 'space')]
    slice x28, local copies, waits for them, and re-layouts: 80.2 us -> 11.3 us  [the longest x1 4.47 us: per_device_slices(): image = both_all[:, :, level * head_width:(level + 1) * head_width]]
    dot_general x46 -> x57, matrix products: 128 us -> 60.1 us  [the longest x13 16.8 us: shared_back(): lax.dot_general(flat, weights, (((1,), (1,)), ((), ())), preferred_elemen...]
    psum x1, waiting for transfers between devices: 52.1 us -> 0.01 us  [per_device_slices(): proj_grad = lax.psum(proj_term, 'space')]
    concatenate x7 -> x13, other arithmetic: 46.1 us -> 3.79 us  [the longest x1 1.57 us: per_device_slices(): terms = jnp.concatenate([expand_term, reduce_term, dilated_term], axis=1)]
  transfers between devices with their start and end apart: 15 -> 5, of which waited for: 9 -> 1; matrix products, arithmetic and copies ran while one was open for 13% -> 12% of each run, Pallas kernels for 0% -> 10%
where the time goes in v1:
time: 551 us; the launch traced here: 540 us
  Pallas kernels  316 us (57%)
  local copies, waits for them, and re-layouts  82.8 us (15%)
  matrix products  67.3 us (12%)
  other arithmetic  32.5 us (6%)
  between operations  28.5 us (5%)
  starting transfers between devices  10.8 us (2%)
    pallas_call x18, Pallas kernels, call(): pl.pallas_call(kernel, name=label, out_shape=out, in_specs=[in_vmem], out...  316 us
    unnamed x248, local copies, waits for them, and re-layouts  22.7 us
    dot_general x13, matrix products, shared_back(): lax.dot_general(flat, weights, (((1,), (1,)), ((), ())), preferred_elemen...  16.8 us
  transfers between devices with their start and end apart: 5, of which 1 were waited for; matrix products, arithmetic and copies ran while one was open for 12% of the time, Pallas kernels for 10%

profile of v1, /device:TPU:13, one launch (start us, length us, event | category | flops | bytes accessed | tf_op | source)
XLA Modules:
  0.0 539.9 jit_solution(2596235181609567715)
XLA Ops:
  12.2 6.1 %sums_one.1 = f32[8,128]{1,0:T(8,128)S(1)} custom-call(f32[8,128]{1,0:T(8,128)S(1)} %pad_maximum_fusion.13.own_ref), custom_call_target="tpu_custom_call" | custom-call | tf_op jit(solution)/shard_map/sums_one/pallas_call | solution.py:633
  37.5 4.6 sums_two.1
  43.8 6.9 %sums_three.1 = f32[32,128]{1,0:T(8,128)S(1)} custom-call(f32[32,128]{1,0:T(8,128)S(1)} %pad_maximum_fusion.6.own_ref), custom_call_target="tpu_custom_call" | custom-call | tf_op jit(solution)/shard_map/sums_three/pallas_call | solution.py:633
  57.9 26.4 %swap_shared.1 = bf16[8,256,256]{2,1,0:T(8,128)(2,1)S(1)} custom-call(bf16[8,256,256]{2,1,0:T(8,128)(2,1)S(1)} %bitcast.421), custom_call_target="tpu_custom_call" | custom-call | tf_op jit(solution)/shard_map/swap_shared/pallas_call | solution.py:633
  95.0 50.8 %scatter_pre.1 = f32[256,1024]{1,0:T(8,128)S(1)} custom-call(bf16[8,256,1024]{2,1,0:T(8,128)(2,1)S(1)} %pad_maximum_fusion.own_ref), custom_call_target="tpu_custom_call" | custom-call | tf_op jit(solution)/shard_map/scatter_pre/pallas_call | solution.py:633
  146.3 6.1 %sums_both.1 = f32[24,128]{1,0:T(8,128)S(1)} custom-call(f32[24,128]{1,0:T(8,128)S(1)} %fusion.107.own_ref), custom_call_target="tpu_custom_call" | custom-call | tf_op jit(solution)/shard_map/sums_both/pallas_call | solution.py:633
  153.5 6.1 %sums_proj.1 = f32[8,128]{1,0:T(8,128)S(1)} custom-call(f32[8,128]{1,0:T(8,128)S(1)} %fusion.112.own_ref), custom_call_target="tpu_custom_call" | custom-call | tf_op jit(solution)/shard_map/sums_proj/pallas_call | solution.py:633
  160.6 5.8 %back_proj.1 = f32[8,128]{1,0:T(8,128)S(1)} custom-call(f32[8,128]{1,0:T(8,128)S(1)} %fusion.111.own_ref), custom_call_target="tpu_custom_call" | custom-call | tf_op jit(solution)/shard_map/back_proj/pallas_call | solution.py:633
  168.6 6.2 %back_both.1 = f32[24,128]{1,0:T(8,128)S(1)} custom-call(f32[24,128]{1,0:T(8,128)S(1)} %fusion.106.own_ref), custom_call_target="tpu_custom_call" | custom-call | tf_op jit(solution)/shard_map/back_both/pallas_call | solution.py:633
  175.8 51.3 %gather_both.1 = bf16[8,256,1024]{2,1,0:T(8,128)(2,1)S(1)} custom-call(bf16[256,1024]{1,0:T(8,128)(2,1)S(1)} %multiply_convert_fusion.2.own_ref), custom_call_target="tpu_custom_call" | custom-call | tf_op jit(solution)/shard_map/gather_both/pallas_call | solution.py:633
  247.4 4.7 add_add_fusion
  252.5 48.7 %tasks_grads.1 = bf16[4,2048,256]{2,1,0:T(8,128)(2,1)S(1)} custom-call(bf16[2048,256]{1,0:T(8,128)(2,1)S(1)} %fusion.11.own_ref), custom_call_target="tpu_custom_call" | custom-call | tf_op jit(solution)/shard_map/tasks_grads/pallas_call | solution.py:633
  303.2 6.3 %fusion.14 = f32[4,4]{1,0:T(4,128)S(1)} fusion(bf16[4,2048,256]{2,1,0:T(8,128)(2,1)S(1)} %tasks_grads.1), kind=kOutput, calls=%fused_computation.66 | convolution fusion | flops 16777216 | bytes 4194368 | tf_op jit(solution)/shard_map/dot_general | solution.py:961
  309.5 6.3 %sums_gram.1 = f32[8,128]{1,0:T(8,128)S(1)} custom-call(f32[8,128]{1,0:T(8,128)S(1)} %pad_bitcast_fusion.own_ref), custom_call_target="tpu_custom_call" | custom-call | tf_op jit(solution)/shard_map/sums_gram/pallas_call | solution.py:633
  332.3 4.5 fusion.168
  356.4 26.5 %swap_combined.1 = bf16[8,256,256]{2,1,0:T(8,128)(2,1)S(1)} custom-call(bf16[8,256,256]{2,1,0:T(8,128)(2,1)S(1)} %bitcast.420), custom_call_target="tpu_custom_call" | custom-call | tf_op jit(solution)/shard_map/swap_combined/pallas_call | solution.py:633
  390.2 4.4 multiply_reduce_fusion.2
  394.6 6.4 %back_three.1 = f32[32,128]{1,0:T(8,128)S(1)} custom-call(f32[32,128]{1,0:T(8,128)S(1)} %pad_maximum_fusion.7.own_ref), custom_call_target="tpu_custom_call" | custom-call | tf_op jit(solution)/shard_map/back_three/pallas_call | solution.py:633
  403.4 5.9 %back_two.1 = f32[8,128]{1,0:T(8,128)S(1)} custom-call(f32[8,128]{1,0:T(8,128)S(1)} %pad_maximum_fusion.15.own_ref), custom_call_target="tpu_custom_call" | custom-call | tf_op jit(solution)/shard_map/back_two/pallas_call | solution.py:633
  432.0 7.9 %copy.62 = bf16[256,512,9]{0,2,1:T(8,128)(2,1)} copy(bf16[256,512,9]{1,0,2:T(8,128)(2,1)} %bitcast.474) | data formatting | bytes 4718592 | tf_op jit(solution)/shard_map/transpose | solution.py:1014
  439.9 5.7 %reshape.754 = bf16[256,4608]{0,1:T(8,128)(2,1)} reshape(bf16[256,512,9]{0,2,1:T(8,128)(2,1)} %copy.62) | data formatting | bytes 4718592 | tf_op jit(solution)/shard_map/reshape | solution.py:1014
  458.3 6.2 %back_one.1 = f32[8,128]{1,0:T(8,128)S(1)} custom-call(f32[8,128]{1,0:T(8,128)S(1)} %pad_maximum_fusion.16.own_ref), custom_call_target="tpu_custom_call" | custom-call | tf_op jit(solution)/shard_map/back_one/pallas_call | solution.py:633
  466.9 30.4 %scatter_trunk.1 = f32[1088,128]{1,0:T(8,128)S(1)} custom-call(bf16[8,1088,128]{2,1,0:T(8,128)(2,1)S(1)} %pad_maximum_fusion.1.own_ref), custom_call_target="tpu_custom_call" | custom-call | tf_op jit(solution)/shard_map/scatter_trunk/pallas_call | solution.py:633
  497.4 15.6 %tasks_trunk.1 = bf16[4,1088,128]{2,1,0:T(8,128)(2,1)S(1)} custom-call(bf16[1088,128]{1,0:T(8,128)(2,1)S(1)} %convert_element_type.253.own_ref), custom_call_target="tpu_custom_call" | custom-call | tf_op jit(solution)/shard_map/tasks_trunk/pallas_call | solution.py:633
  (459 shorter events, 161.8 us)
Async XLA Ops:
  7.2 35.5 %copy-start = (bf16[512,2048]{1,0:T(8,128)(2,1)S(1)}, bf16[512,2048]{1,0:T(8,128)(2,1)}, u32[]{:S(2)}) copy-start(bf16[512,2048]{1,0:T(8,128)(2,1)} %param.17) | copy-start | bytes 6291460
  7.2 523.0 %all-reduce.41.cloned.1.call-start = ((), (), s32[]{:S(2)}) async-start(), calls=%async_computation | async-start | bytes 2621440 | tf_op jit(solution)/shard_map/psum | solution.py:907
  9.5 17.0 %copy-start.100 = (f32[1,1280]{1,0:T(1,128)S(1)}, f32[1,1280]{1,0:T(1,128)}, u32[]{:S(2)}) copy-start(f32[1,1280]{1,0:T(1,128)} %param.23) | copy-start | bytes 15364
  9.5 17.7 %copy-start.101 = (f32[1,1280]{1,0:T(1,128)S(1)}, f32[1,1280]{1,0:T(1,128)}, u32[]{:S(2)}) copy-start(f32[1,1280]{1,0:T(1,128)} %param.24) | copy-start | bytes 15364
  9.5 19.3 %copy-start.108 = (s32[16]{0:T(128)S(1)}, s32[16]{0:T(128)}, u32[]{:S(2)}) copy-start(s32[16]{0:T(128)} %param.14) | copy-start | bytes 196
  12.2 17.3 %copy-start.21 = (f32[256,512]{1,0:T(8,128)}, f32[256,512]{1,0:T(8,128)S(1)}, u32[]{:S(2)}) copy-start(f32[256,512]{1,0:T(8,128)S(1)} %get-tuple-element.132) | copy-start | bytes 1572868
  19.6 23.1 %copy-start.94 = (f32[512]{0:T(512)}, f32[512]{0:T(512)S(1)}, u32[]{:S(2)}) copy-start(f32[512]{0:T(512)S(1)} %get-tuple-element.139) | copy-start | bytes 6148
  19.7 23.1 %copy-start.106 = (f32[512]{0:T(512)}, f32[512]{0:T(512)S(1)}, u32[]{:S(2)}) copy-start(f32[512]{0:T(512)S(1)} %get-tuple-element.112) | copy-start | bytes 6148
  20.6 8.9 %collective-permute-start = (bf16[2,128,512]{2,1,0:T(8,128)(2,1)}, bf16[2,128,512]{2,1,0:T(8,128)(2,1)S(1)}, u32[]{:S(2)}, u32[]{:S(2)}) collective-permute-start(bf16[2,128,512]{2,1,0:T(8,128)(2,1)} %bitcast.8), channel_id=1, source_target_pairs={{0,1},{1,2},{2,3},{3,4},{4,5},{5,6},{6,7},{8,9},{9,10},{10,11},{11... | collective-permute-start | bytes 786440 | tf_op jit(solution)/shard_map/ppermute | solution.py:24
  24.1 8.0 %collective-permute-start.1 = (bf16[2,128,512]{2,1,0:T(8,128)(2,1)}, bf16[2,128,512]{2,1,0:T(8,128)(2,1)}, u32[]{:S(2)}, u32[]{:S(2)}) collective-permute-start(bf16[2,128,512]{2,1,0:T(8,128)(2,1)} %bitcast.8), channel_id=1, source_target_pairs={{1,0},{2,1},{3,2},{4,3},{5,4},{6,5},{7,6},{9,8},{10,9},{11,10},{12... | collective-permute-start | bytes 786440 | tf_op jit(solution)/shard_map/ppermute | solution.py:27
  26.5 24.8 %copy-start.59 = (f32[2048]{0:T(1024)}, f32[2048]{0:T(1024)S(1)}, u32[]{:S(2)}) copy-start(f32[2048]{0:T(1024)S(1)} %slice.494) | copy-start | bytes 24580
  26.5 24.8 %copy-start.63 = (f32[2048]{0:T(1024)}, f32[2048]{0:T(1024)S(1)}, u32[]{:S(2)}) copy-start(f32[2048]{0:T(1024)S(1)} %slice.511) | copy-start | bytes 24580
  89.2 56.8 %copy-start.83 = (f32[256]{0:T(256)}, f32[256]{0:T(256)S(1)}, u32[]{:S(2)}) copy-start(f32[256]{0:T(256)S(1)} %convert_reduce_fusion) | copy-start | bytes 3076
  95.0 57.6 %copy-start.67 = (f32[1,1024]{1,0:T(1,128)S(1)}, f32[1,1024]{1,0:T(1,128)}, u32[]{:S(2)}) copy-start(f32[1,1024]{1,0:T(1,128)} %slice.545) | copy-start | bytes 12292
  175.5 51.7 %copy-start.68 = (f32[1024]{0:T(1024)}, f32[1024]{0:T(1024)S(1)}, u32[]{:S(2)}) copy-start(f32[1024]{0:T(1024)S(1)} %get-tuple-element.109) | copy-start | bytes 12292
  228.3 19.1 %copy-start.19 = (bf16[16,92,256]{2,1,0:T(8,128)(2,1)}, bf16[16,92,256]{2,1,0:T(8,128)(2,1)S(1)}, u32[]{:S(2)}) copy-start(bf16[16,92,256]{2,1,0:T(8,128)(2,1)S(1)} %get-tuple-element.71) | copy-start | bytes 2260996
  228.5 16.6 %copy-start.42 = (bf16[4,116,256]{2,1,0:T(8,128)(2,1)}, bf16[4,116,256]{2,1,0:T(8,128)(2,1)S(1)}, u32[]{:S(2)}) copy-start(bf16[4,116,256]{2,1,0:T(8,128)(2,1)S(1)} %get-tuple-element.73) | copy-start | bytes 712708
  228.5 17.7 %copy-start.40 = (bf16[4,116,256]{2,1,0:T(8,128)(2,1)}, bf16[4,116,256]{2,1,0:T(8,128)(2,1)S(1)}, u32[]{:S(2)}) copy-start(bf16[4,116,256]{2,1,0:T(8,128)(2,1)S(1)} %get-tuple-element.76) | copy-start | bytes 712708
  303.1 20.9 %copy-start.86 = (f32[1,256]{1,0:T(1,128)S(1)}, f32[1,256]{1,0:T(1,128)}, u32[]{:S(2)}) copy-start(f32[1,256]{1,0:T(1,128)} %slice.492) | copy-start | bytes 3076
  303.1 20.9 %copy-start.88 = (f32[256]{0:T(256)S(1)}, f32[256]{0:T(256)}, u32[]{:S(2)}) copy-start(f32[256]{0:T(256)} %copy-done.87) | copy-start | bytes 3076
  303.1 20.9 %copy-start.90 = (f32[256]{0:T(256)S(1)}, f32[256]{0:T(256)}, u32[]{:S(2)}) copy-start(f32[256]{0:T(256)} %copy-done.89) | copy-start | bytes 3076
  303.1 21.0 %copy-start.92 = (f32[256]{0:T(256)S(1)}, f32[256]{0:T(256)}, u32[]{:S(2)}) copy-start(f32[256]{0:T(256)} %copy-done.91) | copy-start | bytes 3076
  409.6 43.0 %collective-permute-start.2 = (bf16[2,128,512]{2,1,0:T(8,128)(2,1)S(1)}, bf16[2,128,512]{2,1,0:T(8,128)(2,1)}, u32[]{:S(2)}, u32[]{:S(2)}) collective-permute-start(bf16[2,128,512]{2,1,0:T(8,128)(2,1)S(1)} %bitcast.475), channel_id=1, source_target_pairs={{0,1},{1,2},{2,3},{3,4},{4,5},{5,6},{6,7},{8,9},{9,10},{10,11},{11... | collective-permute-start | bytes 786440 | tf_op jit(solution)/shard_map/ppermute | solution.py:24
  413.0 39.6 %collective-permute-start.3 = (bf16[2,128,512]{2,1,0:T(8,128)(2,1)S(1)}, bf16[2,128,512]{2,1,0:T(8,128)(2,1)}, u32[]{:S(2)}, u32[]{:S(2)}) collective-permute-start(bf16[2,128,512]{2,1,0:T(8,128)(2,1)S(1)} %bitcast.476), channel_id=1, source_target_pairs={{1,0},{2,1},{3,2},{4,3},{5,4},{6,5},{7,6},{9,8},{10,9},{11,10},{12... | collective-permute-start | bytes 786440 | tf_op jit(solution)/shard_map/ppermute | solution.py:27
  (95 other events, 508.1 us)
Sparse Core Ops, SparseCore 0:
  415.2 59.8 all-reduce.40

commit v2 on v1

--- a/solution.py
+++ b/solution.py
@@ -705,6 +705,1299 @@
         )
 
 
+GELU_A = 0.7978845608028654
+GELU_B = 0.044715
+
+
+def gelu_of(value):
+    return 0.5 * value * (1.0 + jnp.tanh(GELU_A * (value + GELU_B * value * value * value)))
+
+
+def gelu_slope(value):
+    square = value * value
+    bend = jnp.tanh(GELU_A * value * (1.0 + GELU_B * square))
+    return 0.5 * (1.0 + bend) + 0.5 * value * (1.0 - bend * bend) * (
+        GELU_A * (1.0 + 3.0 * GELU_B * square)
+    )
+
+
+def dot_nn(left_side, right_side):
+    return jnp.dot(left_side, right_side, preferred_element_type=jnp.float32)
+
+
+def dot_nt(left_side, right_side):
+    return lax.dot_general(
+        left_side, right_side, (((1,), (1,)), ((), ())), preferred_element_type=jnp.float32
+    )
+
+
+def shift_pixels(value, by, cols):
+    if by == 0:
+        return value
+    rows = value.shape[0]
+    column = lax.rem(lax.broadcasted_iota(jnp.int32, value.shape, 0), cols) + by
+    rolled = pltpu.roll(value, (-by) % rows, 0)
+    return jnp.where((column >= 0) & (column < cols), rolled, 0.0)
+
+
+class Post:
+    def __init__(self, send_sem, recv_sem):
+        self.send_sem, self.recv_sem = send_sem, recv_sem
+        self.used = 0
+        self.sent = []
+
+    def copy(self, source, target, device):
+        made = pltpu.make_async_remote_copy(
+            source,
+            target,
+            self.send_sem.at[self.used],
+            self.recv_sem.at[self.used],
+            device_id=device,
+            device_id_type=MESH_ID,
+        )
+        self.used += 1
+        return made
+
+    def push(self, source, target, device):
+        made = self.copy(source, target, device)
+        made.start()
+        self.sent.append(made)
+        return made
+
+    def close(self):
+        for made in self.sent:
+            made.wait_send()
+
+
+class Place:
+    def __init__(self, tasks, bands):
+        self.tasks, self.bands, self.chips = tasks, bands, bands // 2
+        self.task = lax.axis_index("task")
+        self.band = lax.axis_index("space")
+        self.chip = self.band // 2
+        self.core = lax.rem(self.band, 2)
+        self.twin = {"space": self.chip * 2 + 1 - self.core}
+        low, high = lax.rem(self.task, 2), self.task // 2
+        self.other_tasks = [(1 - high) * 2 + 1 - low, high * 2 + 1 - low, (1 - high) * 2 + low]
+        self.other_bands = [lax.rem(self.band + step, bands) for step in range(1, bands)]
+
+    def meet(self, with_tasks, with_bands):
+        barrier = pltpu.get_barrier_semaphore()
+        greeted = []
+        if with_tasks:
+            greeted += [{"task": task} for task in self.other_tasks]
+        if with_bands:
+            greeted += [{"space": band} for band in self.other_bands]
+        for device in greeted:
+            pl.semaphore_signal(barrier, inc=1, device_id=device, device_id_type=MESH_ID)
+        pl.semaphore_wait(barrier, len(greeted))
+
+    def sum_over(self, post, axis, own_ref, land_ref):
+        mine = self.task if axis == "task" else self.band
+        others = self.other_tasks if axis == "task" else self.other_bands
+        copies = [post.push(own_ref, land_ref.at[mine], {axis: other}) for other in others]
+        land_ref[pl.ds(mine, 1)] = own_ref[...][None]
+        for made in copies:
+            made.wait_recv()
+        total = land_ref[0]
+        for slot in range(1, len(others) + 1):
+            total = total + land_ref[slot]
+        return total
+
+
+def trunk_back_kernel(
+    sizes,
+    sg_ref,
+    h3_ref,
+    x_ref,
+    v3_ref,
+    h2_ref,
+    v2_ref,
+    h1_ref,
+    v1_ref,
+    a1_ref,
+    a2_ref,
+    mask_ref,
+    inv_ref,
+    we_hbm,
+    wd_hbm,
+    wr_hbm,
+    pt_ref,
+    tw_out,
+    ig_out,
+    rg_out,
+    dg_out,
+    eg_out,
+    s3_out,
+    s2_out,
+    s1_out,
+    pg_out,
+    we,
+    wd,
+    wr,
+    h3q,
+    xq,
+    xg,
+    gram_own,
+    gram_land,
+    gram_mid,
+    gram_land_b,
+    comb,
+    comb_land,
+    gate,
+    scaled,
+    gate_low,
+    gate_band,
+    st3,
+    st3_land,
+    st3_mid,
+    st3_land_b,
+    l3,
+    l3x,
+    st2,
+    st2_land,
+    st2_mid,
+    st2_land_b,
+    l2,
+    l2_halo,
+    ag1,
+    st1,
+    st1_land,
+    l1,
+    xt,
+    a1t,
+    a2t,
+    e_term,
+    e_twin,
+    e_land,
+    e_share,
+    e_tasks,
+    d_term,
+    d_twin,
+    d_land,
+    d_share,
+    d_tasks,
+    r_term,
+    r_twin,
+    r_land,
+    r_share,
+    r_tasks,
+    p_twin,
+    p_land,
+    p_all,
+    send_sem,
+    recv_sem,
+    local_sem,
+):
+    tasks, bands, cols, quarter, mid, wide, piece = sizes
+    low = jnp.bfloat16
+    f32 = jnp.float32
+    at = Place(tasks, bands)
+    post = Post(send_sem, recv_sem)
+    task, band = at.task, at.band
+    my_rows = pl.ds(pl.multiple_of(task * quarter, quarter), quarter)
+    loads = [
+        pltpu.make_async_copy(h3_ref.at[my_rows], h3q, local_sem.at[0]),
+        pltpu.make_async_copy(x_ref.at[my_rows], xq, local_sem.at[1]),
+        pltpu.make_async_copy(we_hbm, we, local_sem.at[2]),
+        pltpu.make_async_copy(wd_hbm, wd, local_sem.at[3]),
+        pltpu.make_async_copy(wr_hbm, wr, local_sem.at[4]),
+    ]
+    for load in loads:
+        load.start()
+    at.meet(True, True)
+
+    grads_in = []
+    for other in at.other_tasks:
+        theirs = pl.ds(pl.multiple_of(other * quarter, quarter), quarter)
+        grads_in.append(post.push(sg_ref.at[:, theirs], xg.at[task], {"task": other}))
+    own_copy = pltpu.make_async_copy(sg_ref.at[:, my_rows], xg.at[task], local_sem.at[5])
+    own_copy.start()
+
+    p_pair = [
+        post.push(pt_ref.at[2 * number + 1 - at.core], p_twin.at[number], at.twin)
+        for number in range(at.chips)
+    ]
+
+    for number in range(3):
+        a1t[number] = a1_ref[number].T
+    a2t[...] = a2_ref[...].T
+
+    def turn_inputs(number, carry):
+        lanes = pl.ds(pl.multiple_of(number * piece, piece), piece)
+        xt[lanes, :] = x_ref[:, lanes].T
+        return carry
+
+    lax.fori_loop(0, wide // piece, turn_inputs, 0)
+    for made in p_pair:
+        made.wait_recv()
+    p_in = []
+    for step in range(1, at.chips):
+        other = lax.rem(at.chip + step, at.chips)
+        both = pt_ref[2 * other + at.core].astype(f32) + p_twin[other].astype(f32)
+        p_twin[other] = both.astype(low)
+        p_in.append(
+            post.push(p_twin.at[other], p_land.at[at.chip], {"space": other * 2 + at.core})
+        )
+    own_copy.wait()
+    for made in grads_in:
+        made.wait_recv()
+
+    pairs = [(a, b) for a in range(tasks) for b in range(a, tasks)]
+
+    def gram_step(number, totals):
+        grads = [xg[a, number].astype(f32) for a in range(tasks)]
+        out = []
+        for (a, b), total in zip(pairs, totals):
+            product = grads[a] * grads[b]
+            product = product.reshape(quarter // 8, 8, piece).sum(axis=0)
+            for start in range(0, piece, LANE):
+                total = total + product[:, start : start + LANE]
+            out.append(total)
+        return tuple(out)
+
+    totals = lax.fori_loop(
+        0, bands, gram_step, tuple(jnp.zeros((8, LANE), f32) for _ in pairs)
+    )
+    gram_own[...] = jnp.zeros_like(gram_own)
+    for number, total in enumerate(totals):
+        gram_own[number : number + 1] = jnp.sum(total, axis=0, keepdims=True)
+    p_total = pt_ref[band].astype(f32) + p_twin[at.chip].astype(f32)
+    for made in p_in:
+        made.wait_recv()
+    for step in range(1, at.chips):
+        p_total = p_total + p_land[lax.rem(at.chip + step, at.chips)].astype(f32)
+    p_all[pl.ds(band, 1)] = p_total.astype(low)[None]
+    p_block = p_all.at[band]
+    p_near = post.push(p_block, p_block, at.twin)
+    p_far = [
+        post.push(
+            p_block,
+            p_block,
+            {"space": lax.rem(at.chip + step, at.chips) * 2 + at.core},
+        )
+        for step in range(1, at.chips)
+    ]
+    gram_mid[...] = at.sum_over(post, "task", gram_own, gram_land)
+    gram_sum = at.sum_over(post, "space", gram_mid, gram_land_b)
+    gram_sum = jnp.broadcast_to(jnp.sum(gram_sum, axis=1, keepdims=True), gram_sum.shape)
+    gram = [[None] * tasks for _ in range(tasks)]
+    for number, (a, b) in enumerate(pairs):
+        gram[a][b] = gram[b][a] = gram_sum[number : number + 1]
+    norms = [jnp.sqrt(gram[a][a] + GRAM_EPS) for a in range(tasks)]
+    cos = [[gram[a][b] / norms[b] for b in range(tasks)] for a in range(tasks)]
+    rows_list = [
+        [cos[0][0] - cos[0][l] - cos[k][0] + cos[k][l] for k in range(1, tasks)]
+        for l in range(1, tasks)
+    ]
+    values = [cos[0][0] - cos[0][l] for l in range(1, tasks)]
+    count = tasks - 1
+    for pivot in range(count):
+        for lower in range(pivot + 1, count):
+            factor = rows_list[lower][pivot] / rows_list[pivot][pivot]
+            rows_list[lower] = [
+                under - factor * over for under, over in zip(rows_list[lower], rows_list[pivot])
+            ]
+            values[lower] = values[lower] - factor * values[pivot]
+    answer = [None] * count
+    for pivot in reversed(range(count)):
+        running = values[pivot]
+        for later in range(pivot + 1, count):
+            running = running - rows_list[pivot][later] * answer[later]
+        answer[pivot] = running / rows_list[pivot][pivot]
+    rest = answer[0]
+    for value in answer[1:]:
+        rest = rest + value
+    task_weight = [1.0 - rest] + answer
+    for number in range(tasks):
+        tw_out[number : number + 1] = task_weight[number]
+    weights = [jnp.concatenate([value] * (piece // LANE), axis=1) for value in task_weight]
+
+    def mixed(number):
+        total = weights[0] * xg[0, number].astype(f32)
+        for a in range(1, tasks):
+            total = total + weights[a] * xg[a, number].astype(f32)
+        return total.astype(low)
+
+    comb_in = []
+    for other in at.other_bands:
+        comb[other] = mixed(other)
+        comb_in.append(post.push(comb.at[other], comb_land.at[band], {"space": other}))
+    comb_land[pl.ds(band, 1)] = mixed(band)[None]
+    for load in loads[:2]:
+        load.wait()
+    for made in comb_in:
+        made.wait_recv()
+
+    mask_quarter = mask_ref[my_rows]
+    mask_piece = jnp.concatenate([mask_quarter] * (piece // LANE), axis=1)
+    inv_count = inv_ref[0:1]
+    inv_piece = jnp.concatenate([inv_count] * (piece // LANE), axis=1)
+    per_row = st3.shape[1] // piece
+    half = st3.shape[0] // 2
+
+    def gate_step(number, carry):
+        lanes = pl.ds(pl.multiple_of(number * piece, piece), piece)
+        hat = (h3q[:, lanes] - v3_ref[0:1, lanes]) * v3_ref[1:2, lanes]
+        before = v3_ref[2:3, lanes] * hat + v3_ref[3:4, lanes] + xq[:, lanes].astype(f32)
+        grad = gelu_slope(before) * comb_land[number].astype(f32) * mask_piece
+        gate[number] = grad
+        scaled[number] = hat
+        gate_low[number] = grad.astype(low)
+        row = number // per_row
+        spot = pl.ds(pl.multiple_of(lax.rem(number, per_row) * piece, piece), piece)
+        st3[pl.ds(row, 1), spot] = jnp.sum(grad, axis=0, keepdims=True)
+        st3[pl.ds(half + row, 1), spot] = jnp.sum(grad * hat, axis=0, keepdims=True)
+        return carry
+
+    lax.fori_loop(0, bands, gate_step, 0)
+    st3_mid[...] = at.sum_over(post, "task", st3, st3_land)
+    gate_in = [
+        post.push(gate_low, gate_band.at[task], {"task": other}) for other in at.other_tasks
+    ]
+    gate_band[pl.ds(task, 1)] = gate_low[...][None]
+    s3_out[...] = at.sum_over(post, "space", st3_mid, st3_land_b)
+
+    def third_step(number, carry):
+        lanes = pl.ds(pl.multiple_of(number * piece, piece), piece)
+        row = number // per_row
+        spot = pl.ds(pl.multiple_of(lax.rem(number, per_row) * piece, piece), piece)
+        shift_grad = s3_out[pl.ds(row, 1), spot] * inv_piece
+        gain_grad = s3_out[pl.ds(half + row, 1), spot] * inv_piece
+        l3[number] = (
+            mask_piece
+            * (v3_ref[2:3, lanes] * v3_ref[1:2, lanes])
+            * (gate[number] - shift_grad - scaled[number] * gain_grad)
+        ).astype(low)
+        return carry
+
+    lax.fori_loop(0, bands, third_step, 0)
+    per_task = bands // tasks
+    l3_in = []
+    for other in at.other_tasks:
+        l3_in.append(
+            post.push(l3.at[pl.ds(other * per_task, per_task)], l3x.at[task], {"task": other})
+        )
+    l3x[pl.ds(task, 1)] = l3[pl.ds(task * per_task, per_task)][None]
+    loads[2].wait()
+
+    def expand_step(number, total):
+        lanes = pl.ds(pl.multiple_of(number * piece, piece), piece)
+        return total + dot_nt(l3[number], we[:, lanes])
+
+    ag2 = lax.fori_loop(0, bands, expand_step, jnp.zeros((quarter, mid), f32))
+
+    mask_mid = jnp.concatenate([mask_quarter] * (mid // LANE), axis=1)
+    inv_mid = jnp.concatenate([inv_count] * (mid // LANE), axis=1)
+    hat = (h2_ref[my_rows] - v2_ref[0:1]) * v2_ref[1:2]
+    grad = gelu_slope(v2_ref[2:3] * hat + v2_ref[3:4]) * ag2 * mask_mid
+    spread = mid // LANE
+
+    def put_sums(target, first, second):
+        for number in range(spread):
+            lanes = slice(number * LANE, (number + 1) * LANE)
+            target[number : number + 1] = first[:, lanes]
+            target[spread + number : spread + number + 1] = second[:, lanes]
+
+    def get_sums(total):
+        return [
+            jnp.concatenate([total[base + k : base + k + 1] for k in range(spread)], axis=1)
+            for base in (0, spread)
+        ]
+
+    put_sums(
+        st2, jnp.sum(grad, axis=0, keepdims=True), jnp.sum(grad * hat, axis=0, keepdims=True)
+    )
+    st2_mid[...] = at.sum_over(post, "task", st2, st2_land)
+    s2_out[...] = at.sum_over(post, "space", st2_mid, st2_land_b)
+    shift_grad, gain_grad = get_sums(s2_out[...])
+    l2[my_rows] = (
+        mask_mid
+        * (v2_ref[2:3] * v2_ref[1:2])
+        * (grad - shift_grad * inv_mid - hat * (gain_grad * inv_mid))
+    ).astype(low)
+    l2_in = [post.push(l2.at[my_rows], l2.at[my_rows], {"task": other}) for other in at.other_tasks]
+    for made in l2_in:
+        made.wait_recv()
+    has_above, has_below = band > 0, band < bands - 1
+    up = post.copy(l2, l2_halo.at[1], {"space": lax.rem(band + bands - 1, bands)})
+    down = post.copy(l2, l2_halo.at[0], {"space": lax.rem(band + 1, bands)})
+
+    @pl.when(has_above)
+    def _():
+        up.start()
+
+    @pl.when(has_below)
+    def _():
+        down.start()
+
+    @pl.when(jnp.logical_not(has_above))
+    def _():
+        l2_halo[0] = jnp.zeros_like(l2)
+
+    @pl.when(jnp.logical_not(has_below))
+    def _():
+        l2_halo[1] = jnp.zeros_like(l2)
+
+    p_passed = []
+    for step, made in enumerate(p_far, start=1):
+        made.wait_recv()
+        block = p_all.at[lax.rem(at.chip + at.chips - step, at.chips) * 2 + at.core]
+        p_passed.append(post.push(block, block, at.twin))
+    loads[3].wait()
+    halves = [slice(start, start + piece) for start in range(0, mid, piece)]
+    for lanes in halves:
+        total = None
+        for col_tap in range(3):
+            part = shift_pixels(
+                dot_nt(l2[...], wd[3 + col_tap, lanes, :]), -CONV_DILATION * (col_tap - 1), cols
+            )
+            total = part if total is None else total + part
+        ag1[:, lanes] = total
+
+    for made in l3_in:
+        made.wait_recv()
+    share_e = [
+        jnp.concatenate([l3x[a, number] for a in range(tasks)], axis=0)
+        for number in range(per_task)
+    ]
+    for number in range(per_task):
+        part = dot_nn(a2t[...], share_e[number]).astype(low)
+        per_band = part.shape[0] // bands
+        for target in range(bands):
+            e_term[target % 2, target // 2, :, number * piece : (number + 1) * piece] = part[
+                target * per_band : (target + 1) * per_band
+            ]
+
+    def to_twin(term, landing):
+        return post.push(term.at[1 - at.core], landing, at.twin)
+
+    e_pair = to_twin(e_term, e_twin)
+    narrow = mid // tasks
+    my_lanes = pl.ds(pl.multiple_of(task * narrow, narrow), narrow)
+
+    @pl.when(has_below)
+    def _():
+        up.wait_recv()
+
+    @pl.when(has_above)
+    def _():
+        down.wait_recv()
+
+    for lanes in halves:
+        total = None
+        for col_tap in range(3):
+            part = dot_nt(l2_halo[1], wd[col_tap, lanes, :]) + dot_nt(
+                l2_halo[0], wd[6 + col_tap, lanes, :]
+            )
+            part = shift_pixels(part, -CONV_DILATION * (col_tap - 1), cols)
+            total = part if total is None else total + part
+        ag1[:, lanes] += total
+
+    pixels = ag1.shape[0]
+    chunk = pixels // 8
+
+    def first_rows(number):
+        return pl.ds(pl.multiple_of(number * chunk, chunk), chunk)
+
+    def first_step(number, sums):
+        rows = first_rows(number)
+        hat = (h1_ref[rows] - v1_ref[0:1]) * v1_ref[1:2]
+        keep = jnp.concatenate([mask_ref[rows]] * spread, axis=1)
+        grad = gelu_slope(v1_ref[2:3] * hat + v1_ref[3:4]) * ag1[rows] * keep
+        ag1[rows] = grad
+        return (
+            sums[0] + jnp.sum(grad, axis=0, keepdims=True),
+            sums[1] + jnp.sum(grad * hat, axis=0, keepdims=True),
+        )
+
+    nothing = jnp.zeros((1, mid), f32)
+    first, second = lax.fori_loop(0, 8, first_step, (nothing, nothing))
+    put_sums(st1, first, second)
+    s1_out[...] = at.sum_over(post, "space", st1, st1_land)
+    shift_grad, gain_grad = get_sums(s1_out[...])
+    shift_grad, gain_grad = shift_grad * inv_mid, gain_grad * inv_mid
+
+    def first_finish(number, carry):
+        rows = first_rows(number)
+        hat = (h1_ref[rows] - v1_ref[0:1]) * v1_ref[1:2]
+        keep = jnp.concatenate([mask_ref[rows]] * spread, axis=1)
+        l1[rows] = (
+            keep * (v1_ref[2:3] * v1_ref[1:2]) * (ag1[rows] - shift_grad - hat * gain_grad)
+        ).astype(low)
+        return carry
+
+    lax.fori_loop(0, 8, first_finish, 0)
+
+    share_r = l1[:, my_lanes]
+    per_band_r = wide // bands
+
+    def reduce_step(number, carry):
+        rows = pl.ds(pl.multiple_of(number * per_band_r, per_band_r), per_band_r)
+        r_term[lax.rem(number, 2), number // 2] = dot_nn(xt[rows, :], share_r).astype(low)
+        return carry
+
+    lax.fori_loop(0, bands, reduce_step, 0)
+    r_pair = to_twin(r_term, r_twin)
+    share_d = l2[:, my_lanes].astype(f32)
+    for col_tap in range(3):
+        moved = shift_pixels(share_d, -CONV_DILATION * (col_tap - 1), cols).astype(low)
+        for row_tap in range(3):
+            part = dot_nn(a1t[row_tap], moved).astype(low)
+            per_band = part.shape[0] // bands
+            for target in range(bands):
+                d_term[target % 2, target // 2, 3 * row_tap + col_tap] = part[
+                    target * per_band : (target + 1) * per_band
+                ]
+
+    def along(pair, term, twin, landing):
+        pair.wait_recv()
+        arrivals = []
+        for step in range(1, at.chips):
+            other = lax.rem(at.chip + step, at.chips)
+            both = term[at.core, other].astype(f32) + twin[other].astype(f32)
+            twin[other] = both.astype(low)
+            arrivals.append(
+                post.push(twin.at[other], landing.at[at.chip], {"space": other * 2 + at.core})
+            )
+        return arrivals
+
+    def settle(arrivals, term, twin, landing):
+        total = term[at.core, at.chip].astype(f32) + twin[at.chip].astype(f32)
+        for made in arrivals:
+            made.wait_recv()
+        for step in range(1, at.chips):
+            total = total + landing[lax.rem(at.chip + step, at.chips)].astype(f32)
+        return total.astype(low)
+
+    def to_tasks(share, landing):
+        arrivals = [post.push(share, landing.at[task], {"task": other}) for other in at.other_tasks]
+        landing[pl.ds(task, 1)] = share[...][None]
+        return arrivals
+
+    r_in = along(r_pair, r_term, r_twin, r_land)
+    e_in = along(e_pair, e_term, e_twin, e_land)
+    d_pair = to_twin(d_term, d_twin)
+    r_share[...] = settle(r_in, r_term, r_twin, r_land)
+    r_back = to_tasks(r_share, r_tasks)
+    d_in = along(d_pair, d_term, d_twin, d_land)
+    e_share[...] = settle(e_in, e_term, e_twin, e_land)
+    e_back = to_tasks(e_share, e_tasks)
+
+    loads[4].wait()
+    for made in gate_in:
+        made.wait_recv()
+
+    def input_step(number, carry):
+        lanes = pl.ds(pl.multiple_of(number * piece, piece), piece)
+        gates = jnp.concatenate([gate_band[a, number] for a in range(tasks)], axis=0).astype(f32)
+        ig_out[:, lanes] = (dot_nt(l1[...], wr[lanes, :]) + gates).astype(low)
+        return carry
+
+    lax.fori_loop(0, bands, input_step, 0)
+    d_share[...] = settle(d_in, d_term, d_twin, d_land)
+    d_back = to_tasks(d_share, d_tasks)
+    for made in [p_near] + p_passed:
+        made.wait_recv()
+    pg_out[...] = p_all[...].astype(f32)
+    for made in r_back:
+        made.wait_recv()
+    for a in range(tasks):
+        rg_out[:, a * narrow : (a + 1) * narrow] = r_tasks[a].astype(f32)
+    for made in e_back:
+        made.wait_recv()
+    broad = wide // tasks
+    for a in range(tasks):
+        eg_out[:, a * broad : (a + 1) * broad] = e_tasks[a].astype(f32)
+    for made in d_back:
+        made.wait_recv()
+    for a in range(tasks):
+        dg_out[:, :, a * narrow : (a + 1) * narrow] = d_tasks[a].astype(f32)
+    post.close()
+
+    @pl.when(has_above)
+    def _():
+        up.wait_send()
+
+    @pl.when(has_below)
+    def _():
+        down.wait_send()
+
+
+def trunk_back(
+    tasks, bands, cols, collective, sg, h3, x, v3, h2, v2, h1, v1, a1, a2, mask, inv, we, wd, wr, pt
+):
+    low, f32 = jnp.bfloat16, jnp.float32
+    pixels, wide = x.shape
+    mid = a2.shape[1]
+    quarter = pixels // tasks
+    piece = wide // bands
+    narrow, broad = mid // tasks, wide // tasks
+    chips = bands // 2
+    part = mid // bands
+    in_vmem = pl.BlockSpec(memory_space=pltpu.VMEM)
+    anywhere = pl.BlockSpec(memory_space=pl.ANY)
+    shape = jax.ShapeDtypeStruct
+
+    def stats(rows, lanes):
+        return [
+            pltpu.VMEM((rows, lanes), f32),
+            pltpu.VMEM((tasks, rows, lanes), f32),
+            pltpu.VMEM((rows, lanes), f32),
+            pltpu.VMEM((bands, rows, lanes), f32),
+        ]
+
+    def terms(*dims):
+        return [
+            pltpu.VMEM((2, chips) + dims, low),
+            pltpu.VMEM((chips,) + dims, low),
+            pltpu.VMEM((chips,) + dims, low),
+            pltpu.VMEM(dims, low),
+            pltpu.VMEM((tasks,) + dims, low),
+        ]
+
+    stat_wide = 2 * wide // 8
+    scratch = (
+        [
+            pltpu.VMEM(we.shape, low),
+            pltpu.VMEM(wd.shape, low),
+            pltpu.VMEM(wr.shape, low),
+            pltpu.VMEM((quarter, wide), f32),
+            pltpu.VMEM((quarter, wide), low),
+            pltpu.VMEM((tasks, bands, quarter, piece), low),
+        ]
+        + stats(16, LANE)
+        + [
+            pltpu.VMEM((bands, quarter, piece), low),
+            pltpu.VMEM((bands, quarter, piece), low),
+            pltpu.VMEM((bands, quarter, piece), f32),
+            pltpu.VMEM((bands, quarter, piece), f32),
+            pltpu.VMEM((bands, quarter, piece), low),
+            pltpu.VMEM((tasks, bands, quarter, piece), low),
+        ]
+        + stats(8, stat_wide)
+        + [
+            pltpu.VMEM((bands, quarter, piece), low),
+            pltpu.VMEM((tasks, bands // tasks, quarter, piece), low),
+        ]
+        + stats(2 * mid // LANE, LANE)
+        + [
+            pltpu.VMEM((pixels, mid), low),
+            pltpu.VMEM((2, pixels, mid), low),
+            pltpu.VMEM((pixels, mid), f32),
+            pltpu.VMEM((2 * mid // LANE, LANE), f32),
+            pltpu.VMEM((bands, 2 * mid // LANE, LANE), f32),
+            pltpu.VMEM((pixels, mid), low),
+            pltpu.VMEM((wide, pixels), low),
+            pltpu.VMEM((3, mid, pixels), low),
+            pltpu.VMEM((mid, pixels), low),
+        ]
+        + terms(part, broad)
+        + terms(9, part, narrow)
+        + terms(piece, narrow)
+        + [
+            pltpu.VMEM((chips,) + pt.shape[1:], low),
+            pltpu.VMEM((chips,) + pt.shape[1:], low),
+            pltpu.VMEM(pt.shape, low),
+            pltpu.SemaphoreType.DMA((96,)),
+            pltpu.SemaphoreType.DMA((96,)),
+            pltpu.SemaphoreType.DMA((6,)),
+        ]
+    )
+    out_shapes = (
+        shape((8, LANE), f32),
+        shape((pixels, wide), low),
+        shape((piece, mid), f32),
+        shape((9, part, mid), f32),
+        shape((part, wide), f32),
+        shape((8, stat_wide), f32),
+        shape((2 * mid // LANE, LANE), f32),
+        shape((2 * mid // LANE, LANE), f32),
+        shape(pt.shape, f32),
+    )
+    return pl.pallas_call(
+        functools.partial(trunk_back_kernel, (tasks, bands, cols, quarter, mid, wide, piece)),
+        name="trunk_back",
+        out_shape=out_shapes,
+        in_specs=[in_vmem, anywhere, in_vmem] + [in_vmem] * 9 + [anywhere] * 3 + [in_vmem],
+        out_specs=(in_vmem,) * 9,
+        scratch_shapes=scratch,
+        compiler_params=pltpu.CompilerParams(
+            collective_id=collective, has_side_effects=True, vmem_limit_bytes=56 << 20
+        ),
+    )(sg, h3, x, v3, h2, v2, h1, v1, a1, a2, mask, inv, we, wd, wr, pt)
+
+
+def head_kernel(
+    plan,
+    sh_ref,
+    mask_ref,
+    inv_ref,
+    gain_ref,
+    shift_ref,
+    cot_ref,
+    bw_ref,
+    pw_ref,
+    rate_hbm,
+    head_out,
+    sg_out,
+    grads_out,
+    proj_out,
+    pool_out,
+    both_sums_out,
+    proj_sums_out,
+    rate,
+    turned,
+    extra,
+    term,
+    twin_land,
+    right_land,
+    left_land,
+    pre,
+    joined,
+    upstream,
+    st_both,
+    st_both_sum,
+    st_both_land,
+    st_proj,
+    st_proj_sum,
+    st_proj_land,
+    st_pback,
+    st_pback_land,
+    st_back,
+    st_back_land,
+    both_all,
+    moved,
+    grads,
+    back,
+    send_sem,
+    recv_sem,
+    rate_sem,
+):
+    tasks, bands, cols, pixels, width, taps, extras = plan
+    low, f32 = jnp.bfloat16, jnp.float32
+    at = Place(tasks, bands)
+    post = Post(send_sem, recv_sem)
+    chips, chip, core, band = at.chips, at.chip, at.core, at.band
+    last = chips - 1
+    group = 2 * pixels
+    number_of = {tap[:3]: number for number, tap in enumerate(taps)}
+    loads = []
+    for number, (level, row_tap, col_tap, _, _) in enumerate(taps):
+        start = (9 * (level - 1) + 3 * row_tap + col_tap) * width
+        load = pltpu.make_async_copy(
+            rate_hbm.at[:, start : start + width], rate.at[number], rate_sem.at[number]
+        )
+        load.start()
+        loads.append(load)
+    at.meet(False, True)
+    for load in loads:
+        load.wait()
+
+    def rows_of(ref, number):
+        return jnp.concatenate([ref[2 * number], ref[2 * number + 1]], axis=0)
+
+    def right_of(level, col_tap):
+        return (col_tap - 1) * level * RATE
+
+    def forward_taps(source, level, row_tap):
+        total = None
+        for col_tap in range(3):
+            number = number_of.get((level, row_tap, col_tap))
+            if number is None:
+                continue
+            part = shift_pixels(
+                dot_nn(source, rate[number]), right_of(level, col_tap), cols
+            )
+            total = part if total is None else total + part
+        return total
+
+    extra[...] = jnp.zeros_like(extra)
+    for level, target, source, row_tap in extras:
+        extra[level - 1, target] += forward_taps(rows_of(sh_ref, source), level, row_tap)
+
+    def twin_term(number):
+        return pltpu.make_async_remote_copy(
+            term.at[number, 1 - core],
+            twin_land.at[number],
+            send_sem.at[number],
+            recv_sem.at[number],
+            device_id=at.twin,
+            device_id_type=MESH_ID,
+        )
+
+    post.used = chips
+
+    def forward_group(step, carry):
+        number = lax.rem(step, 2) * (last - step // 2) + (1 - lax.rem(step, 2)) * (step // 2)
+        source = rows_of(sh_ref, number)
+
+        def put(branch, value):
+            value = value.astype(low)
+            term[number, 0, branch] = value[:pixels]
+            term[number, 1, branch] = value[pixels:]
+
+        put(0, dot_nn(source, bw_ref[:, :width]))
+        for level in (1, 2, 3):
+            total = forward_taps(source, level, 1)
+            if any(level == entry[0] for entry in extras):
+                total = total + extra[level - 1, number]
+            put(level, total)
+        twin_term(number).start()
+        turned[:, pl.ds(pl.multiple_of(number * group, group), group)] = source.T
+        return carry + jnp.sum(source.astype(f32), axis=0, keepdims=True)
+
+    pixel_sum = lax.fori_loop(0, chips, forward_group, jnp.zeros((1, width), f32))
+
+    def hop(source, landing, device_chip, number):
+        return pltpu.make_async_remote_copy(
+            source,
+            landing,
+            send_sem.at[number],
+            recv_sem.at[number],
+            device_id={"space": device_chip * 2 + core},
+            device_id_type=MESH_ID,
+        )
+
+    base_right, base_left = post.used, post.used + chips
+    post.used += 2 * chips
+    next_chip = lax.rem(chip + 1, chips)
+    prev_chip = lax.rem(chip + last, chips)
+
+    def go_right(number):
+        return hop(twin_land.at[number], right_land.at[number], next_chip, base_right + number)
+
+    def go_left(number):
+        return hop(twin_land.at[number], left_land.at[number], prev_chip, base_left + number)
+
+    def pass_on(number, copy, landing, has_incoming):
+        twin_term(number).wait_recv()
+
+        @pl.when(has_incoming)
+        def _():
+            copy.wait_recv()
+
+            def add(branch, carry):
+                twin_land[number, branch] = (
+                    term[number, core, branch].astype(f32)
+                    + twin_land[number, branch].astype(f32)
+                    + landing[number, branch].astype(f32)
+                ).astype(low)
+                return carry
+
+            lax.fori_loop(0, 4, add, 0)
+
+        @pl.when(jnp.logical_not(has_incoming))
+        def _():
+            def add(branch, carry):
+                twin_land[number, branch] = (
+                    term[number, core, branch].astype(f32) + twin_land[number, branch].astype(f32)
+                ).astype(low)
+                return carry
+
+            lax.fori_loop(0, 4, add, 0)
+
+        copy.start()
+
+    for number in range(last):
+        to_right, to_left = last - number, number
+
+        @pl.when(chip < to_right)
+        def _():
+            pass_on(to_right, go_right(to_right), right_land, chip > 0)
+
+        @pl.when(chip > to_left)
+        def _():
+            pass_on(to_left, go_left(to_left), left_land, chip < last)
+
+    mask_own = mask_ref[pl.ds(pl.multiple_of(band * pixels, pixels), pixels)]
+    mask_own = jnp.concatenate([mask_own] * (width // LANE), axis=1)
+    inv_count = jnp.concatenate([inv_ref[0:1]] * (width // LANE), axis=1)
+    spread = width // LANE
+
+    def put_rows(target, number, value):
+        for part in range(spread):
+            target[pl.ds(number * spread + part, 1), :] = value[:, part * LANE : (part + 1) * LANE]
+
+    def get_rows(target, number):
+        return jnp.concatenate(
+            [target[pl.ds(number * spread + part, 1), :] for part in range(spread)], axis=1
+        )
+
+    def column_sum(value):
+        return jnp.sum(value, axis=0, keepdims=True)
+
+    twin_term(chip).wait_recv()
+
+    @pl.when(chip > 0)
+    def _():
+        go_right(chip).wait_recv()
+
+    @pl.when(chip < last)
+    def _():
+        go_left(chip).wait_recv()
+
+    @pl.when(chip == 0)
+    def _():
+        right_land[0] = jnp.zeros(right_land.shape[1:], low)
+
+    @pl.when(chip == last)
+    def _():
+        left_land[last] = jnp.zeros(left_land.shape[1:], low)
+
+    st_both[...] = jnp.zeros_like(st_both)
+
+    def settle(branch, carry):
+        value = (
+            term[chip, core, branch].astype(f32)
+            + twin_land[chip, branch].astype(f32)
+            + right_land[chip, branch].astype(f32)
+            + left_land[chip, branch].astype(f32)
+        )
+        pre[branch] = value
+        kept = value * mask_own
+        put_rows(st_both, branch, column_sum(kept))
+        put_rows(st_both, 4 + branch, column_sum(kept * value))
+        return carry
+
+    lax.fori_loop(0, 4, settle, 0)
+    high = pixel_sum.astype(low)
+    rest = pixel_sum - high.astype(f32)
+    middle = rest.astype(low)
+    tail = (rest - middle.astype(f32)).astype(low)
+    pieces = jnp.concatenate(
+        [high.astype(f32), middle.astype(f32), tail.astype(f32), jnp.zeros((13, width), f32)],
+        axis=0,
+    ).astype(low)
+    put_rows(st_both, 8, column_sum(dot_nn(pieces, bw_ref[:, width:])))
+    st_both_sum[...] = at.sum_over(post, "space", st_both, st_both_land)
+    pooled = get_rows(st_both_sum, 8) * inv_count
+
+    def lanes_of(number):
+        return pl.ds(pl.multiple_of(number * width, width), width)
+
+    def scale_of(target, first, second):
+        mean_value = get_rows(target, first) * inv_count
+        variance = get_rows(target, second) * inv_count - mean_value * mean_value
+        return mean_value, lax.rsqrt(variance + NORM_EPS)
+
+    def activate(branch, projected):
+        mean_value, inv_std = scale_of(st_both_sum, branch, 4 + branch)
+        hat = (pre[branch] - mean_value) * inv_std
+        pre[branch] = hat
+        normed = gain_ref[:, lanes_of(branch)] * hat + shift_ref[:, lanes_of(branch)]
+        active = (gelu_of(normed) * mask_own).astype(low)
+        joined[branch] = active
+        return projected + dot_nn(active, pw_ref[lanes_of(branch), :])
+
+    joined[4] = (gelu_of(pooled).astype(low).astype(f32) * mask_own).astype(low)
+    projected = dot_nn(joined[4], pw_ref[4 * width : 5 * width, :])
+    projected = lax.fori_loop(0, 4, activate, projected)
+    kept = projected * mask_own
+    st_proj[...] = jnp.zeros_like(st_proj)
+    put_rows(st_proj, 0, column_sum(kept))
+    put_rows(st_proj, 1, column_sum(kept * projected))
+    st_proj_sum[...] = at.sum_over(post, "space", st_proj, st_proj_land)
+    mean_value, inv_std = scale_of(st_proj_sum, 0, 1)
+    hat = (projected - mean_value) * inv_std
+    gain_proj = gain_ref[:, 4 * width : 5 * width]
+    normed = gain_proj * hat + shift_ref[:, 4 * width : 5 * width]
+    proj_up = gelu_slope(normed) * cot_ref[...].astype(f32) * mask_own
+    st_pback[...] = jnp.zeros_like(st_pback)
+    put_rows(st_pback, 0, column_sum(proj_up))
+    put_rows(st_pback, 1, column_sum(proj_up * hat))
+    proj_sums_out[...] = at.sum_over(post, "space", st_pback, st_pback_land)
+    head_out[...] = (gelu_of(normed) * mask_own).astype(low)
+    shift_grad, gain_grad = get_rows(proj_sums_out, 0), get_rows(proj_sums_out, 1)
+    proj_low = (
+        mask_own
+        * (gain_proj * inv_std)
+        * (proj_up - shift_grad * inv_count - hat * (gain_grad * inv_count))
+    ).astype(low)
+    st_back[...] = jnp.zeros_like(st_back)
+
+    def back_step(branch, carry):
+        joined_grad = dot_nt(proj_low, pw_ref[lanes_of(branch), :])
+        hat = pre[branch]
+        normed = gain_ref[:, lanes_of(branch)] * hat + shift_ref[:, lanes_of(branch)]
+        up = gelu_slope(normed) * joined_grad * mask_own
+        upstream[branch] = up
+        put_rows(st_back, branch, column_sum(up))
+        put_rows(st_back, 4 + branch, column_sum(up * hat))
+        return carry
+
+    lax.fori_loop(0, 4, back_step, 0)
+    pool_total = column_sum(dot_nt(proj_low, pw_ref[4 * width : 5 * width, :]) * mask_own)
+    put_rows(st_back, 8, pool_total)
+    both_sums_out[...] = at.sum_over(post, "space", st_back, st_back_land)
+    pool_grad = (gelu_slope(pooled) * get_rows(both_sums_out, 8)).astype(low)
+    pool_out[...] = jnp.broadcast_to(pool_grad.astype(f32), pool_out.shape)
+
+    def both_step(branch, carry):
+        _, inv_std = scale_of(st_both_sum, branch, 4 + branch)
+        shift_grad = get_rows(both_sums_out, branch) * inv_count
+        gain_grad = get_rows(both_sums_out, 4 + branch) * inv_count
+        both_all[band, branch] = (
+            mask_own
+            * (gain_ref[:, lanes_of(branch)] * inv_std)
+            * (upstream[branch] - shift_grad - pre[branch] * gain_grad)
+        ).astype(low)
+        return carry
+
+    lax.fori_loop(0, 4, both_step, 0)
+
+    all_right = post.used
+    all_left = all_right + chips
+    all_twin = all_left + chips
+
+    def send_right(step):
+        block = both_all.at[lax.rem(chip - step + 1 + chips, chips) * 2 + core]
+        return hop(block, block, next_chip, all_right + step)
+
+    def send_left(step):
+        block = both_all.at[lax.rem(chip + step - 1, chips) * 2 + core]
+        return hop(block, block, prev_chip, all_left + step)
+
+    def hand_over(number):
+        block = both_all.at[number * 2 + core]
+        return pltpu.make_async_remote_copy(
+            block,
+            block,
+            send_sem.at[all_twin + number],
+            recv_sem.at[all_twin + number],
+            device_id=at.twin,
+            device_id_type=MESH_ID,
+        )
+
+    def from_left(step):
+        block = both_all.at[lax.rem(chip - step + chips, chips) * 2 + core]
+        return hop(block, block, next_chip, all_right + step)
+
+    def from_right(step):
+        block = both_all.at[lax.rem(chip + step, chips) * 2 + core]
+        return hop(block, block, prev_chip, all_left + step)
+
+    @pl.when(chip < last)
+    def _():
+        send_right(1).start()
+
+    @pl.when(chip > 0)
+    def _():
+        send_left(1).start()
+
+    hand_over(chip).start()
+
+    def proj_step(branch, carry):
+        proj_out[lanes_of(branch), :] = dot_nn(joined[branch].T, proj_low).astype(low)
+        return carry
+
+    lax.fori_loop(0, 5, proj_step, 0)
+    grads[...] = jnp.zeros_like(grads)
+    pool_row = dot_nt(
+        jnp.broadcast_to(pool_grad, (16, width)), bw_ref[:, width:]
+    )[0:1] * inv_count
+    moved_levels = sorted({entry[0] for entry in extras})
+
+    def back_group(step, carry):
+        number = group_at(step)
+        hand_over(number).wait_recv()
+        columns = turned[:, pl.ds(pl.multiple_of(number * group, group), group)]
+
+        def both_of(branch):
+            return jnp.concatenate(
+                [both_all[2 * number, branch], both_all[2 * number + 1, branch]], axis=0
+            )
+
+        part = both_of(0)
+        total = dot_nt(part, bw_ref[:, :width])
+        grads[len(taps)] += dot_nn(columns, part)
+        for level in (1, 2, 3):
+            image = both_of(level).astype(f32)
+            for col_tap in range(3):
+                tap = number_of.get((level, 1, col_tap))
+                if tap is None:
+                    continue
+                part = shift_pixels(image, -right_of(level, col_tap), cols).astype(low)
+                if level in moved_levels:
+                    moved[moved_levels.index(level), number, col_tap] = part
+                total = total + dot_nt(part, rate[tap])
+                grads[tap] += dot_nn(columns, part)
+        back[number] = total
+        return carry
+
+    mirror = chip // 2
+    near = chip * (1 - mirror) + (last - chip) * mirror
+
+    def group_at(step):
+        place = step + near * (1 - 2 * step) * ((last - step) // 2)
+        return place * (1 - mirror) + (last - place) * mirror
+
+    lax.fori_loop(0, 1, back_group, 0)
+    done = 1
+    for step in range(1, chips):
+        @pl.when(chip >= step)
+        def _():
+            from_left(step).wait_recv()
+            if step < last:
+
+                @pl.when(chip < last)
+                def _():
+                    send_right(step + 1).start()
+
+            hand_over(lax.rem(chip - step + chips, chips)).start()
+
+        @pl.when(chip + step <= last)
+        def _():
+            from_right(step).wait_recv()
+            if step < last:
+
+                @pl.when(chip > 0)
+                def _():
+                    send_left(step + 1).start()
+
+            hand_over(lax.rem(chip + step, chips)).start()
+
+        upto = chips if step == last else step + 1 + near
+        lax.fori_loop(done, upto, back_group, 0)
+        done = upto
+
+    for level, target, source, row_tap in extras:
+        columns = turned[:, source * group : (source + 1) * group]
+        total = back[source]
+        for col_tap in range(3):
+            tap = number_of.get((level, row_tap, col_tap))
+            if tap is None:
+                continue
+            part = moved[moved_levels.index(level), target, col_tap]
+            total = total + dot_nt(part, rate[tap])
+            grads[tap] += dot_nn(columns, part)
+        back[source] = total
+
+    def finish_group(number, carry):
+        rows = pl.ds(pl.multiple_of(number * group, group), group)
+        keep = jnp.concatenate([mask_ref[rows]] * spread, axis=1)
+        value = (back[number] + keep * pool_row).astype(low)
+        sg_out[2 * number] = value[:pixels]
+        sg_out[2 * number + 1] = value[pixels:]
+        return carry
+
+    lax.fori_loop(0, chips, finish_group, 0)
+
+    def finish_tap(number, carry):
+        grads_out[number] = grads[number].astype(low)
+        return carry
+
+    lax.fori_loop(0, len(taps) + 1, finish_tap, 0)
+
+    post.close()
+
+    def twin_left(number, carry):
+        twin_term(number).wait_send()
+        hand_over(number).wait_send()
+        return carry
+
+    lax.fori_loop(0, chips, twin_left, 0)
+    for number in range(last):
+        to_right, to_left = last - number, number
+
+        @pl.when(chip < to_right)
+        def _():
+            go_right(to_right).wait_send()
+
+        @pl.when(chip > to_left)
+        def _():
+            go_left(to_left).wait_send()
+
+    for step in range(1, chips):
+
+        @pl.when((chip < last) & (chip - step + 1 >= 0))
+        def _():
+            send_right(step).wait_send()
+
+        @pl.when((chip > 0) & (chip + step - 1 <= last))
+        def _():
+            send_left(step).wait_send()
+
+
+def head(tasks, bands, cols, rows, collective, sh, mask, inv, gain, shift, cot, bw, pw, rate):
+    low, f32 = jnp.bfloat16, jnp.float32
+    pixels, width = sh.shape[1], pw.shape[1]
+    chips = bands // 2
+    group_rows = rows // chips
+    taps = live_taps(rows, cols)
+    extras = []
+    for level in (1, 2, 3):
+        for row_tap in (0, 2):
+            if (level, row_tap, 1) in [tap[:3] for tap in taps]:
+                away = (row_tap - 1) * level * RATE // group_rows
+                extras += [
+                    (level, target, target + away, row_tap)
+                    for target in range(chips)
+                    if 0 <= target + away < chips
+                ]
+    levels = max([entry[0] for entry in extras], default=1)
+    in_vmem = pl.BlockSpec(memory_space=pltpu.VMEM)
+    anywhere = pl.BlockSpec(memory_space=pl.ANY)
+    shape = jax.ShapeDtypeStruct
+    block = (pixels, width)
+    both_rows, proj_rows = -(-9 * width // LANE // 8) * 8, 8
+
+    def stats(count):
+        return [pltpu.VMEM((count, LANE), f32), pltpu.VMEM((bands, count, LANE), f32)]
+
+    scratch = (
+        [
+            pltpu.VMEM((len(taps), sh.shape[2], width), low),
+            pltpu.VMEM((sh.shape[2], bands * pixels), low),
+            pltpu.VMEM((levels, chips, 2 * pixels, width), f32),
+            pltpu.VMEM((chips, 2, 4) + block, low),
+            pltpu.VMEM((chips, 4) + block, low),
+            pltpu.VMEM((chips, 4) + block, low),
+            pltpu.VMEM((chips, 4) + block, low),
+            pltpu.VMEM((4,) + block, f32),
+            pltpu.VMEM((5,) + block, low),
+            pltpu.VMEM((4,) + block, f32),
+        ]
+        + [pltpu.VMEM((both_rows, LANE), f32)]
+        + stats(both_rows)
+        + [pltpu.VMEM((proj_rows, LANE), f32)]
+        + stats(proj_rows)
+        + stats(proj_rows)
+        + stats(both_rows)
+        + [
+            pltpu.VMEM((bands, 4) + block, low),
+            pltpu.VMEM((levels, chips, 3, 2 * pixels, width), low),
+            pltpu.VMEM((len(taps) + 1, sh.shape[2], width), f32),
+            pltpu.VMEM((chips, 2 * pixels, width), f32),
+            pltpu.SemaphoreType.DMA((80,)),
+            pltpu.SemaphoreType.DMA((80,)),
+            pltpu.SemaphoreType.DMA((len(taps),)),
+        ]
+    )
+    out_shapes = (
+        shape(block, low),
+        shape(sh.shape, low),
+        shape((len(taps) + 1, sh.shape[2], width), low),
+        shape(pw.shape, low),
+        shape((8, width), f32),
+        shape((both_rows, LANE), f32),
+        shape((proj_rows, LANE), f32),
+    )
+    return taps, pl.pallas_call(
+        functools.partial(
+            head_kernel, (tasks, bands, cols, pixels, width, tuple(taps), tuple(extras))
+        ),
+        name="head",
+        out_shape=out_shapes,
+        in_specs=[in_vmem] * 8 + [anywhere],
+        out_specs=(in_vmem,) * 7,
+        scratch_shapes=scratch,
+        compiler_params=pltpu.CompilerParams(
+            collective_id=collective, has_side_effects=True, vmem_limit_bytes=60 << 20
+        ),
+    )(sh, mask, inv, gain, shift, cot, bw, pw, rate)
+
+
 def norm_scale(totals, pixel_count):
     mean_value = totals[0] / pixel_count
     variance = totals[1] / pixel_count - mean_value * mean_value
@@ -796,13 +2089,8 @@
         hidden_one, links.sums(masked_sums(hidden_one, valid_mask), "sums_one"), gains[0], shifts[0]
     )
     first_active = (jax.nn.gelu(stats_one[0]) * valid_mask).astype(low)
-    patches = trunk_taps(
-        band_rim(first_active.reshape(band_rows, cols_count, middle_width)),
-        CONV_DILATION,
-        band_rows,
-        cols_count,
-        False,
-    )
+    rim = band_rim(first_active.reshape(band_rows, cols_count, middle_width))
+    patches = trunk_taps(rim, CONV_DILATION, band_rows, cols_count, False)
     hidden_two = jnp.einsum("pti,ito->po", patches, w_dilated, preferred_element_type=wide)
     stats_two = norm(
         hidden_two, links.sums(masked_sums(hidden_two, valid_mask), "sums_two"), gains[1], shifts[1]
@@ -823,208 +2111,101 @@
     ).reshape(all_pixels, slice_width)
     pixel_sum = jnp.sum(shared_slice.astype(wide), axis=0)
     branch_local = branch_weight[0]
-    rate_local = rate_weight[0]
-    proj_local = proj_weight[0]
-    gain_local = head_gain[0]
-    shift_local = head_shift[0]
-
-    def rate_columns(level, row_tap, col_tap):
-        start = (9 * (level - 1) + 3 * row_tap + col_tap) * head_width
-        return slice(start, start + head_width)
-
-    taps = live_taps(rows_count, cols_count)
-    shared_image = shared_slice.reshape(rows_count, cols_count, slice_width)
-    pre_parts = [
-        jnp.dot(shared_slice, branch_local[:, :head_width], preferred_element_type=wide).reshape(
-            rows_count, cols_count, head_width
-        )
-    ]
-    for level in (1, 2, 3):
-        total = jnp.zeros((rows_count, cols_count, head_width), wide)
-        for number, row_tap, col_tap, down, right in taps:
-            if number != level:
-                continue
-            first, last = max(0, -down), rows_count - max(0, down)
-            window = shift_columns(shared_image[first + down : last + down], right)
-            term = jnp.dot(
-                window.reshape(-1, slice_width),
-                rate_local[:, rate_columns(level, row_tap, col_tap)],
-                preferred_element_type=wide,
-            ).reshape(last - first, cols_count, head_width)
-            total = total + jnp.pad(term, ((first, rows_count - last), (0, 0), (0, 0)))
-        pre_parts.append(total)
-    pre_terms = jnp.concatenate(pre_parts, axis=2).astype(low)
-    pre_both = links.scatter(pre_terms.reshape(bands, pixels, 4 * head_width), "scatter_pre")
-    pool_term = jnp.dot(
-        pixel_sum[None],
-        branch_local[:, head_width:].astype(wide),
-        precision=PRECISE,
-        preferred_element_type=wide,
-    )
-    totals = links.sums(masked_sums(pre_both, valid_mask) + [pool_term], "sums_both")
-    gain_both, shift_both = (gain_local[: 4 * head_width], shift_local[: 4 * head_width])
-    stats_both = norm(pre_both, totals, gain_both, shift_both)
-    pooled = totals[2] / pixel_count
-    active_both = (jax.nn.gelu(stats_both[0]) * valid_mask).astype(low)
-    active_pool = jax.nn.gelu(pooled).astype(low)
-    joined = jnp.concatenate(
-        [active_both, (active_pool.astype(wide) * valid_mask).astype(low)], axis=1
-    )
-    projected = jnp.dot(joined, proj_local, preferred_element_type=wide)
-    gain_proj = gain_local[4 * head_width :]
-    stats_proj = norm(
-        projected,
-        links.sums(masked_sums(projected, valid_mask), "sums_proj"),
-        gain_proj,
-        shift_local[4 * head_width :],
-    )
-    head_result = (jax.nn.gelu(stats_proj[0]) * valid_mask).astype(low)
-    cot_rows = head_cot[0].reshape(pixels, head_width).astype(wide)
-
-    def back_sums(upstream, scaled):
-        kept = upstream * valid_mask
-        return [jnp.sum(kept, axis=0), jnp.sum(kept * scaled, axis=0)]
-
-    def finish(upstream, stats, gain_vec, sums):
-        return norm_finish(
-            upstream, stats[1], stats[2], gain_vec, sums[1], sums[0], valid_mask, pixel_count
-        ).astype(low)
-
-    proj_upstream = gelu_back(stats_proj[0], cot_rows * valid_mask)
-    proj_sums = links.sums(back_sums(proj_upstream, stats_proj[1]), "back_proj")
-    proj_low = finish(proj_upstream, stats_proj, gain_proj, proj_sums)
-    joined_grad = lax.dot_general(
-        proj_low, proj_local, (((1,), (1,)), ((), ())), preferred_element_type=wide
-    )
-    proj_term = lax.dot_general(
-        joined, proj_low, (((0,), (0,)), ((), ())), preferred_element_type=wide
-    )
-    both_upstream = gelu_back(stats_both[0], joined_grad[:, : 4 * head_width] * valid_mask)
-    pool_total = jnp.sum(joined_grad[:, 4 * head_width :] * valid_mask, axis=0)
-    both_sums = links.sums(back_sums(both_upstream, stats_both[1]) + [pool_total], "back_both")
-    pool_grad = gelu_back(pooled, both_sums[2][None]).astype(low)
-    both_grad = finish(both_upstream, stats_both, gain_both, both_sums)
-    proj_grad = lax.psum(proj_term, "space")
-
-    both_all = links.gather(both_grad, "gather_both").reshape(
-        rows_count, cols_count, 4 * head_width
-    )
-    turned = shared_slice.T
-
-    def shared_back(first, last, grad_rows, weights):
-        flat = grad_rows.reshape(-1, head_width)
-        part = lax.dot_general(
-            flat, weights, (((1,), (1,)), ((), ())), preferred_element_type=wide
-        ).reshape(last - first, cols_count, slice_width)
-        grad = jnp.dot(
-            turned[:, first * cols_count : last * cols_count], flat, preferred_element_type=wide
-        )
-        return jnp.pad(part, ((first, rows_count - last), (0, 0), (0, 0))), grad
-
-    slice_grad, one_grad = shared_back(
-        0, rows_count, both_all[:, :, :head_width], branch_local[:, :head_width]
-    )
-    rate_grads = {}
-    for level, row_tap, col_tap, down, right in taps:
-        image = both_all[:, :, level * head_width : (level + 1) * head_width]
-        first, last = max(0, down), rows_count - max(0, -down)
-        window = shift_columns(image[first - down : last - down], -right)
-        part, grad = shared_back(
-            first, last, window, rate_local[:, rate_columns(level, row_tap, col_tap)]
-        )
-        slice_grad = slice_grad + part
-        rate_grads[level, row_tap, col_tap] = grad
+    inv_block = jnp.broadcast_to(1.0 / pixel_count, (8, LANE))
+    links.used += 1
+    taps, (
+        head_result,
+        shared_grad,
+        tap_grads,
+        proj_term,
+        pool_rows,
+        both_sums,
+        proj_sums,
+    ) = head(
+        tasks,
+        bands,
+        cols_count,
+        rows_count,
+        links.used - 1,
+        shared_slice.reshape(bands, pixels, slice_width),
+        jnp.broadcast_to(all_mask, (all_pixels, LANE)),
+        inv_block,
+        head_gain,
+        head_shift,
+        head_cot.reshape(pixels, head_width),
+        branch_local,
+        proj_weight[0],
+        rate_weight[0],
+    )
+    pool_weight_grad = pixel_sum[:, None] * pool_rows[0:1] / pixel_count
+    branch_grad = jnp.concatenate([tap_grads[len(taps)].astype(wide), pool_weight_grad], axis=1)
+    place_of = {tap[:3]: number for number, tap in enumerate(taps)}
     nothing = jnp.zeros((slice_width, head_width), wide)
     rate_grad = jnp.concatenate(
         [
-            rate_grads.get((level, row_tap, col_tap), nothing)
+            tap_grads[place_of[level, row_tap, col_tap]].astype(wide)
+            if (level, row_tap, col_tap) in place_of
+            else nothing
             for level in (1, 2, 3)
             for row_tap in range(3)
             for col_tap in range(3)
         ],
         axis=1,
     )
-    pool_weight_grad = pixel_sum[:, None] * pool_grad.astype(wide) / pixel_count
-    branch_grad = jnp.concatenate([one_grad, pool_weight_grad], axis=1)
-    pool_part = lax.dot_general(
-        pool_grad,
-        branch_local[:, head_width:],
-        (((1,), (1,)), ((), ())),
-        preferred_element_type=wide,
-    )
-    shared_grad = (
-        slice_grad.reshape(all_pixels, slice_width) + all_mask * pool_part / pixel_count
-    ).astype(low)
-
-    all_grads = links.over_tasks(shared_grad, "tasks_grads")
-    flat_grads = all_grads.reshape(tasks, -1)
-    gram_part = lax.dot_general(
-        flat_grads, flat_grads, (((1,), (1,)), ((), ())), preferred_element_type=wide
-    )
-    gram_matrix = links.sums([gram_part], "sums_gram")[0]
-    task_weight = imtl_weights(gram_matrix)
-    mixed_grad = task_weight[0] * all_grads[0].astype(wide)
-    for task_index in range(1, tasks):
-        mixed_grad = mixed_grad + task_weight[task_index] * all_grads[task_index].astype(wide)
-    combined = (
-        links.swap(mixed_grad.astype(low).reshape(bands, pixels, slice_width), "swap_combined")
-        .transpose(1, 0, 2)
-        .reshape(pixels, in_width)
-    )
-
-    gate_grad = gelu_back(before_act, combined.astype(wide) * valid_mask)
-    sums_three = links.sums(back_sums(gate_grad, stats_three[1]), "back_three")
-    low_three = finish(gate_grad, stats_three, gains[2], sums_three)
-    active_grad_two = lax.dot_general(
-        low_three, w_expand, (((1,), (1,)), ((), ())), preferred_element_type=wide
-    )
-    upstream_two = gelu_back(stats_two[0], active_grad_two * valid_mask)
-    sums_two = links.sums(back_sums(upstream_two, stats_two[1]), "back_two")
-    low_two = finish(upstream_two, stats_two, gains[1], sums_two)
-    back_patches = trunk_taps(
-        band_rim(low_two.reshape(band_rows, cols_count, middle_width)),
-        CONV_DILATION,
-        band_rows,
+    head_sums = [
+        jnp.concatenate([both, proj])
+        for both, proj in zip(
+            both_sums.reshape(-1)[: 8 * head_width].reshape(2, -1),
+            proj_sums.reshape(-1)[: 2 * head_width].reshape(2, -1),
+        )
+    ]
+
+    def vectors(stats, number):
+        return jnp.concatenate(
+            [
+                jnp.stack([stats[3], stats[2], gains[number], shifts[number]]),
+                jnp.zeros((4, stats[3].size), wide),
+            ]
+        )
+
+    links.used += 1
+    (
+        weight_rows,
+        input_grad,
+        w_reduce_grad,
+        dilated_grad,
+        w_expand_grad,
+        sums_three,
+        sums_two,
+        sums_one,
+        proj_grad,
+    ) = trunk_back(
+        tasks,
+        bands,
         cols_count,
-        True,
-    )
-    active_grad_one = jnp.einsum("pto,ito->pi", back_patches, w_dilated, preferred_element_type=wide)
-    upstream_one = gelu_back(stats_one[0], active_grad_one * valid_mask)
-    sums_one = links.sums(back_sums(upstream_one, stats_one[1]), "back_one")
-    low_one = finish(upstream_one, stats_one, gains[0], sums_one)
-    input_grad = (
-        lax.dot_general(low_one, w_reduce, (((1,), (1,)), ((), ())), preferred_element_type=wide)
-        + gate_grad
-    ).astype(low)
-
-    def share(low_grad):
-        width = low_grad.shape[1] // tasks
-        return lax.dynamic_slice_in_dim(low_grad, task * width, width, axis=1)
-
-    def against(left_side, right_side):
-        return lax.dot_general(
-            left_side, right_side, (((0,), (0,)), ((), ())), preferred_element_type=wide
-        ).astype(low)
-
-    narrow = middle_width // tasks
-    wide_share = in_width // tasks
-    expand_term = against(active_two, share(low_three)).reshape(bands, -1, narrow)
-    reduce_term = against(inputs, share(low_one)).reshape(bands, -1, narrow)
-    dilated_term = against(
-        patches.transpose(0, 2, 1).reshape(pixels, -1), share(low_two)
-    ).reshape(bands, -1, narrow)
-    terms = jnp.concatenate([expand_term, reduce_term, dilated_term], axis=1)
-    shares = links.over_tasks(
-        links.scatter(terms, "scatter_trunk").astype(low), "tasks_trunk"
-    ).astype(wide)
-    cut_one = expand_term.shape[1]
-    cut_two = cut_one + reduce_term.shape[1]
-    w_expand_grad = (
-        shares[:, :cut_one].reshape(tasks, -1, wide_share).transpose(1, 0, 2).reshape(-1, in_width)
-    )
-    w_reduce_grad = shares[:, cut_one:cut_two].transpose(1, 0, 2).reshape(-1, middle_width)
-    w_dilated_grad = (
-        shares[:, cut_two:].transpose(1, 0, 2).reshape(-1, 9, middle_width)
+        links.used - 1,
+        shared_grad,
+        hidden_three,
+        inputs,
+        vectors(stats_three, 2),
+        hidden_two,
+        vectors(stats_two, 1),
+        hidden_one,
+        vectors(stats_one, 0),
+        rim.reshape(3, pixels, middle_width),
+        active_two,
+        jnp.broadcast_to(valid_mask, (pixels, LANE)),
+        inv_block,
+        w_expand,
+        w_dilated.transpose(1, 0, 2),
+        w_reduce,
+        proj_term.reshape(bands, -1, head_width),
+    )
+    proj_grad = proj_grad.reshape(-1, head_width)
+    task_weight = weight_rows[:tasks, 0]
+    w_dilated_grad = dilated_grad.transpose(1, 0, 2)
+    sums_three, sums_two, sums_one = (
+        value.reshape(2, -1) for value in (sums_three, sums_two, sums_one)
     )
     means = jnp.concatenate([stats_one[3], stats_two[3], stats_three[3]])
     variances = (
@@ -1044,8 +2225,8 @@
         branch_grad[None],
         rate_grad[None],
         proj_grad[None],
-        jnp.concatenate([both_sums[1], proj_sums[1]])[None],
-        jnp.concatenate([both_sums[0], proj_sums[0]])[None],
+        head_sums[1][None],
+        head_sums[0][None],
         task_weight,
     )
 

time: 551 us -> 346 us (0.63); the launches traced: 540 us -> 344 us
  matrix products: 67.3 us -> 4.82 us
  local copies, waits for them, and re-layouts: 82.8 us -> 24.8 us
  Pallas kernels: 316 us -> 286 us
  between operations: 28.5 us -> 1.82 us
  other arithmetic: 32.5 us -> 19.4 us
    pallas_call x18 -> x4, Pallas kernels: 316 us -> 46.2 us  [call(): pl.pallas_call(kernel, name=label, out_shape=out, in_specs=[in_vmem], out...]
    pallas_call x0 -> x2, Pallas kernels: none -> 239 us  [the longest x1 122 us: trunk_back(): pl.pallas_call(functools.partial(trunk_back_kernel, (tasks, bands, cols,...]
    dot_general x54 -> x0, matrix products: 55 us -> none  [the longest x13 16.8 us: shared_back(): lax.dot_general(flat, weights, (((1,), (1,)), ((), ())), preferred_elemen...]
    slice x31 -> x2, local copies, waits for them, and re-layouts: 14.9 us -> 2 us  [the longest x1 1.3 us: per_device_slices(): task_weight = weight_rows[:tasks, 0]]
    unnamed x2 -> x16, other arithmetic: 0.26 us -> 12 us
    unnamed x248 -> x60, local copies, waits for them, and re-layouts: 22.7 us -> 11.1 us
    pad x10 -> x0, local copies, waits for them, and re-layouts: 11.1 us -> none  [the longest x5 5.72 us: shift_columns(): return jnp.pad(image[:, by:], ((0, 0), (0, by), (0, 0)))]
    transpose x5 -> x0, local copies, waits for them, and re-layouts: 10.7 us -> none  [the longest x1 7.87 us: per_device_slices(): patches.transpose(0, 2, 1).reshape(pixels, -1)]
  transfers between devices with their start and end apart: 5 -> 2, of which waited for: 1 -> 2; matrix products, arithmetic and copies ran while one was open for 12% -> 0% of each run, Pallas kernels for 10% -> 0%
where the time goes in v2:
time: 346 us; the launch traced here: 344 us
  Pallas kernels  286 us (83%)
  local copies, waits for them, and re-layouts  24.8 us (7%)
  other arithmetic  19.4 us (6%)
  starting transfers between devices  5.56 us (2%)
  matrix products  4.82 us (1%)
    pallas_call x1, Pallas kernels, trunk_back(): pl.pallas_call(functools.partial(trunk_back_kernel, (tasks, bands, cols,...  122 us
    pallas_call x1, Pallas kernels, head(): pl.pallas_call(functools.partial(head_kernel, (tasks, bands, cols, pixels...  117 us
    pallas_call x4, Pallas kernels, call(): pl.pallas_call(kernel, name=label, out_shape=out, in_specs=[in_vmem], out...  46.2 us
    unnamed x16, other arithmetic  12 us
    unnamed x60, local copies, waits for them, and re-layouts  11.1 us
  transfers between devices with their start and end apart: 2, of which 2 were waited for; matrix products, arithmetic and copies ran while one was open for 0% of the time, Pallas kernels for 0%

profile of v2, /device:TPU:13, one launch (start us, length us, event | category | flops | bytes accessed | tf_op | source)
XLA Modules:
  0.0 344.4 jit_solution(16861323521711228512)
XLA Ops:
  0.7 1.3 reduce_sum.74
  4.2 2.7 multiply_reduce_fusion.2
  6.9 6.1 %sums_one.1 = f32[8,128]{1,0:T(8,128)S(1)} custom-call(f32[8,128]{1,0:T(8,128)S(1)} %pad_maximum_fusion.8.own_ref), custom_call_target="tpu_custom_call" | custom-call | tf_op jit(solution)/shard_map/sums_one/pallas_call | solution.py:633
  13.3 2.3 collective-permute-start.1
  15.6 3.3 collective-permute-start
  19.7 1.6 collective-permute-done.1
  24.6 1.1 copy-done.3
  25.7 1.4 multiply_reduce_fusion.1
  27.1 6.7 %sums_two.1 = f32[8,128]{1,0:T(8,128)S(1)} custom-call(f32[8,128]{1,0:T(8,128)S(1)} %pad_maximum_fusion.9.own_ref), custom_call_target="tpu_custom_call" | custom-call | tf_op jit(solution)/shard_map/sums_two/pallas_call | solution.py:633
  35.0 6.8 %sums_three.1 = f32[32,128]{1,0:T(8,128)S(1)} custom-call(f32[32,128]{1,0:T(8,128)S(1)} %pad_maximum_fusion.2.own_ref), custom_call_target="tpu_custom_call" | custom-call | tf_op jit(solution)/shard_map/sums_three/pallas_call | solution.py:633
  41.9 1.3 fusion.9
  43.2 26.6 %swap_shared.1.sh_ref = bf16[8,256,256]{2,1,0:T(8,128)(2,1)S(1)} custom-call(bf16[8,256,256]{2,1,0:T(8,128)(2,1)S(1)} %bitcast.157), custom_call_target="tpu_custom_call" | custom-call | tf_op jit(solution)/shard_map/swap_shared/pallas_call | solution.py:633
  70.7 1.3 broadcast_in_dim.28.mask_ref
  72.1 117.2 %head.1 = (bf16[256,256]{1,0:T(8,128)(2,1)}, bf16[8,256,256]{2,1,0:T(8,128)(2,1)}, bf16[16,256,256]{2,1,0:T(8,128)(2,1)}, bf16[1280,256]{1,0:T(8,128)(2,1)}, f32...) custom-call(bf16[8,256,256]{2,1,0:T(8,128)(2,1)} %copy-done, f32[2048,128]{1,0:T(8,128)} %broadcast_in_dim.28.mask_ref, ...), custom_call_target="tpu_custom_call" | custom-call | tf_op jit(solution)/shard_map/head/pallas_call | solution.py:1986
  189.2 0.9 bitcast_convert_fusion
  190.1 1.6 convert_dynamic-update-slice_fusion.14
  197.2 122.1 %trunk_back.1 = (f32[8,128]{1,0:T(8,128)}, bf16[256,2048]{1,0:T(8,128)(2,1)}, f32[256,512]{1,0:T(8,128)}, f32[9,64,512]{2,1,0:T(8,128)}, f32[64,2048]{1,0:T(8,12...) custom-call(bf16[8,256,256]{2,1,0:T(8,128)(2,1)} %get-tuple-element.31.sg_ref, ...), custom_call_target="tpu_custom_call" | custom-call | tf_op jit(solution)/shard_map/trunk_back/pallas_call | solution.py:1418
  319.4 1.3 slice_reduce_fusion
  328.8 0.9 broadcast_dynamic-update-slice_fusion.1
  331.9 1.3 broadcast_dynamic-update-slice_fusion
  335.4 0.9 broadcast_dynamic-update-slice_fusion.2
  339.8 1.0 copy.66
  341.6 1.0 copy.68
  343.4 1.1 copy.70
  (116 shorter events, 30.8 us)
Async XLA Ops:
  0.6 12.4 %copy-start.19 = (f32[3072]{0:T(1024)S(1)}, f32[3072]{0:T(1024)}, u32[]{:S(2)}) copy-start(f32[3072]{0:T(1024)} %param.18) | copy-start | bytes 36868
  4.2 14.7 %copy-start.18 = (f32[3072]{0:T(1024)S(1)}, f32[3072]{0:T(1024)}, u32[]{:S(2)}) copy-start(f32[3072]{0:T(1024)} %param.19) | copy-start | bytes 36868
  4.2 15.4 %copy-start.20 = (s32[16]{0:T(128)S(1)}, s32[16]{0:T(128)}, u32[]{:S(2)}) copy-start(s32[16]{0:T(128)} %param.14) | copy-start | bytes 196
  6.8 17.4 %copy-start.4 = (f32[256,512]{1,0:T(8,128)}, f32[256,512]{1,0:T(8,128)S(1)}, u32[]{:S(2)}) copy-start(f32[256,512]{1,0:T(8,128)S(1)} %get-tuple-element.84.h1_ref) | copy-start | bytes 1572868
  13.3 8.0 %collective-permute-start.1 = (bf16[2,128,512]{2,1,0:T(8,128)(2,1)S(1)}, bf16[2,128,512]{2,1,0:T(8,128)(2,1)S(1)}, u32[]{:S(2)}, u32[]{:S(2)}) collective-permute-start(bf16[2,128,512]{2,1,0:T(8,128)(2,1)S(1)} %bitcast.175), channel_id=1, source_target_pairs={{1,0},{2,1},{3,2},{4,3},{5,4},{6,5},{7,6},{9,8},{10,9},{11,10},{12... | collective-permute-start | bytes 786440 | tf_op jit(solution)/shard_map/ppermute | solution.py:27
  15.6 6.6 %collective-permute-start = (bf16[2,128,512]{2,1,0:T(8,128)(2,1)S(1)}, bf16[2,128,512]{2,1,0:T(8,128)(2,1)S(1)}, u32[]{:S(2)}, u32[]{:S(2)}) collective-permute-start(bf16[2,128,512]{2,1,0:T(8,128)(2,1)S(1)} %bitcast.176), channel_id=1, source_target_pairs={{0,1},{1,2},{2,3},{3,4},{4,5},{5,6},{6,7},{8,9},{9,10},{10,11},{11... | collective-permute-start | bytes 786440 | tf_op jit(solution)/shard_map/ppermute | solution.py:24
  22.2 0.7 copy-start.13
  23.0 1.5 copy-start.2
  23.0 1.1 copy-start.14
  23.3 2.4 copy-start.3
  25.7 8.4 %copy-start.6 = (bf16[512,2048]{1,0:T(8,128)(2,1)S(1)}, bf16[512,2048]{1,0:T(8,128)(2,1)}, u32[]{:S(2)}) copy-start(bf16[512,2048]{1,0:T(8,128)(2,1)} %we_hbm.1) | copy-start | bytes 6291460
  27.1 7.8 %copy-start.8 = (f32[256,512]{1,0:T(8,128)}, f32[256,512]{1,0:T(8,128)S(1)}, u32[]{:S(2)}) copy-start(f32[256,512]{1,0:T(8,128)S(1)} %get-tuple-element.85.h2_ref) | copy-start | bytes 1572868
  34.2 0.8 copy-start.11
  34.2 7.7 %copy-start.5 = (bf16[2,128,2048]{2,1,0:T(8,128)(2,1)S(1)}, bf16[2,128,2048]{2,1,0:T(8,128)(2,1)}, u32[]{:S(2)}) copy-start(bf16[2,128,2048]{2,1,0:T(8,128)(2,1)} %param.13) | copy-start | bytes 3145732
  35.0 8.3 %copy-start.1 = (f32[256,2048]{1,0:T(8,128)}, f32[256,2048]{1,0:T(8,128)S(1)}, u32[]{:S(2)}) copy-start(f32[256,2048]{1,0:T(8,128)S(1)} %get-tuple-element.86.h3_ref) | copy-start | bytes 6291460
  69.8 2.2 copy-start
  197.2 125.8 %copy-start.7 = (bf16[16,256,256]{2,1,0:T(8,128)(2,1)S(1)}, bf16[16,256,256]{2,1,0:T(8,128)(2,1)}, u32[]{:S(2)}) copy-start(bf16[16,256,256]{2,1,0:T(8,128)(2,1)} %get-tuple-element.40) | copy-start | bytes 6291460
  331.9 7.3 %copy-start.17 = (bf16[256,256]{1,0:T(8,128)(2,1)S(1)}, bf16[256,256]{1,0:T(8,128)(2,1)}, u32[]{:S(2)}) copy-start(bf16[256,256]{1,0:T(8,128)(2,1)} %get-tuple-element.30) | copy-start | bytes 393220
  331.9 7.9 %copy-start.12 = (bf16[256,2048]{1,0:T(8,128)(2,1)S(1)}, bf16[256,2048]{1,0:T(8,128)(2,1)}, u32[]{:S(2)}) copy-start(bf16[256,2048]{1,0:T(8,128)(2,1)} %get-tuple-element.33) | copy-start | bytes 3145732
  335.4 5.4 %copy-start.16 = (f32[256,512]{1,0:T(8,128)S(1)}, f32[256,512]{1,0:T(8,128)}, u32[]{:S(2)}) copy-start(f32[256,512]{1,0:T(8,128)} %get-tuple-element.105) | copy-start | bytes 1572868
  337.0 4.6 %copy-start.10 = (f32[9,64,512]{2,1,0:T(8,128)S(1)}, f32[9,64,512]{2,1,0:T(8,128)}, u32[]{:S(2)}) copy-start(f32[9,64,512]{2,1,0:T(8,128)} %get-tuple-element.35) | copy-start | bytes 3538948
  339.8 2.8 copy-start.15
  340.8 2.6 copy-start.9

commit v3 on v2

--- a/solution.py
+++ b/solution.py
@@ -430,281 +430,6 @@
 LANE = 128
 
 
-def meet_bands(place, count):
-    barrier = pltpu.get_barrier_semaphore()
-    for step in range(1, count):
-        pl.semaphore_signal(
-            barrier,
-            inc=1,
-            device_id={"space": lax.rem(place + step, count)},
-            device_id_type=MESH_ID,
-        )
-    pl.semaphore_wait(barrier, count - 1)
-
-
-def sum_kernel(count, own_ref, out_ref, landing, send_sem, recv_sem):
-    place = lax.axis_index("space")
-    meet_bands(place, count)
-    copies = []
-    for step in range(1, count):
-        copy = pltpu.make_async_remote_copy(
-            own_ref,
-            landing.at[step],
-            send_sem.at[step],
-            recv_sem.at[step],
-            device_id={"space": lax.rem(place + step, count)},
-            device_id_type=MESH_ID,
-        )
-        copy.start()
-        copies.append(copy)
-    total = own_ref[...]
-    for step in range(1, count):
-        copies[step - 1].wait_recv()
-        total = total + landing[step]
-    out_ref[...] = total
-    for copy in copies:
-        copy.wait_send()
-
-
-def gather_kernel(count, own_ref, out_ref, send_sem, recv_sem, local_sem):
-    place = lax.axis_index("space")
-    chips = count // 2
-    chip = place // 2
-    core = lax.rem(place, 2)
-    twin = chip * 2 + 1 - core
-    meet_bands(place, count)
-    copies = []
-    for step in range(1, chips):
-        copy = pltpu.make_async_remote_copy(
-            own_ref,
-            out_ref.at[place],
-            send_sem.at[step],
-            recv_sem.at[step],
-            device_id={"space": lax.rem(chip + step, chips) * 2 + core},
-            device_id_type=MESH_ID,
-        )
-        copy.start()
-        copies.append(copy)
-    to_twin = pltpu.make_async_remote_copy(
-        own_ref,
-        out_ref.at[place],
-        send_sem.at[0],
-        recv_sem.at[0],
-        device_id={"space": twin},
-        device_id_type=MESH_ID,
-    )
-    to_twin.start()
-    here = pltpu.make_async_copy(own_ref, out_ref.at[place], local_sem)
-    here.start()
-    passed = []
-    for step in range(1, chips):
-        copies[step - 1].wait_recv()
-        source = lax.rem(chip + chips - step, chips) * 2 + core
-        copy = pltpu.make_async_remote_copy(
-            out_ref.at[source],
-            out_ref.at[source],
-            send_sem.at[chips - 1 + step],
-            recv_sem.at[chips - 1 + step],
-            device_id={"space": twin},
-            device_id_type=MESH_ID,
-        )
-        copy.start()
-        passed.append(copy)
-    to_twin.wait()
-    for copy in passed:
-        copy.wait()
-    for copy in copies:
-        copy.wait_send()
-    here.wait()
-
-
-def swap_kernel(count, own_ref, out_ref, send_sem, recv_sem, local_sem):
-    place = lax.axis_index("space")
-    meet_bands(place, count)
-    copies = []
-    for step in range(1, count):
-        target = lax.rem(place + step, count)
-        copy = pltpu.make_async_remote_copy(
-            own_ref.at[target],
-            out_ref.at[place],
-            send_sem.at[step],
-            recv_sem.at[step],
-            device_id={"space": target},
-            device_id_type=MESH_ID,
-        )
-        copy.start()
-        copies.append(copy)
-    here = pltpu.make_async_copy(own_ref.at[place], out_ref.at[place], local_sem)
-    here.start()
-    for copy in copies:
-        copy.wait()
-    here.wait()
-
-
-def scatter_kernel(count, own_ref, out_ref, twin_land, paired, landing, send_sem, recv_sem):
-    place = lax.axis_index("space")
-    chips = count // 2
-    chip = place // 2
-    core = lax.rem(place, 2)
-    twin = chip * 2 + 1 - core
-    meet_bands(place, count)
-    from_twin = []
-    for step in range(chips):
-        other = lax.rem(chip + step, chips)
-        copy = pltpu.make_async_remote_copy(
-            own_ref.at[other * 2 + 1 - core],
-            twin_land.at[step],
-            send_sem.at[step],
-            recv_sem.at[step],
-            device_id={"space": twin},
-            device_id_type=MESH_ID,
-        )
-        from_twin.append(copy)
-    order = list(range(1, chips)) + [0]
-    for step in order:
-        from_twin[step].start()
-    sent = []
-    for step in order:
-        from_twin[step].wait_recv()
-        other = lax.rem(chip + step, chips)
-        pair = own_ref[other * 2 + core].astype(jnp.float32) + twin_land[step].astype(jnp.float32)
-        if step == 0:
-            out_ref[...] = pair
-            continue
-        paired[step] = pair.astype(paired.dtype)
-        copy = pltpu.make_async_remote_copy(
-            paired.at[step],
-            landing.at[step],
-            send_sem.at[chips + step],
-            recv_sem.at[chips + step],
-            device_id={"space": other * 2 + core},
-            device_id_type=MESH_ID,
-        )
-        copy.start()
-        sent.append(copy)
-    for step in range(1, chips):
-        sent[step - 1].wait_recv()
-        out_ref[...] += landing[step].astype(jnp.float32)
-    for copy in sent:
-        copy.wait_send()
-    for copy in from_twin:
-        copy.wait_send()
-
-
-def tasks_kernel(count, own_ref, out_ref, send_sem, recv_sem, local_sem):
-    place = lax.axis_index("task")
-    barrier = pltpu.get_barrier_semaphore()
-    for step in range(1, count):
-        pl.semaphore_signal(
-            barrier,
-            inc=1,
-            device_id={"task": lax.rem(place + step, count)},
-            device_id_type=MESH_ID,
-        )
-    pl.semaphore_wait(barrier, count - 1)
-    copies = []
-    for step in range(1, count):
-        copy = pltpu.make_async_remote_copy(
-            own_ref,
-            out_ref.at[place],
-            send_sem.at[step],
-            recv_sem.at[step],
-            device_id={"task": lax.rem(place + step, count)},
-            device_id_type=MESH_ID,
-        )
-        copy.start()
-        copies.append(copy)
-    here = pltpu.make_async_copy(own_ref, out_ref.at[place], local_sem)
-    here.start()
-    for copy in copies:
-        copy.wait()
-    here.wait()
-
-
-class Links:
-    def __init__(self):
-        self.bands = lax.axis_size("space")
-        self.tasks = lax.axis_size("task")
-        self.used = 0
-
-    def call(self, kernel, out, scratch, operand, label):
-        self.used += 1
-        in_vmem = pl.BlockSpec(memory_space=pltpu.VMEM)
-        return pl.pallas_call(
-            kernel,
-            name=label,
-            out_shape=out,
-            in_specs=[in_vmem],
-            out_specs=in_vmem,
-            scratch_shapes=scratch,
-            compiler_params=pltpu.CompilerParams(
-                collective_id=self.used - 1, has_side_effects=True, vmem_limit_bytes=48 << 20
-            ),
-        )(operand)
-
-    def sums(self, members, label):
-        sizes = [member.size for member in members]
-        flat = jnp.concatenate([member.reshape(-1) for member in members])
-        tile = 8 * LANE
-        padded = -(-flat.size // tile) * tile
-        block = jnp.pad(flat, (0, padded - flat.size)).reshape(-1, LANE)
-        sems = pltpu.SemaphoreType.DMA((self.bands,))
-        total = self.call(
-            functools.partial(sum_kernel, self.bands),
-            jax.ShapeDtypeStruct(block.shape, block.dtype),
-            [pltpu.VMEM((self.bands,) + block.shape, block.dtype), sems, sems],
-            block,
-            label,
-        ).reshape(-1)
-        out = []
-        start = 0
-        for member, size in zip(members, sizes):
-            out.append(total[start : start + size].reshape(member.shape))
-            start += size
-        return out
-
-    def gather(self, block, label):
-        sems = pltpu.SemaphoreType.DMA((self.bands,))
-        return self.call(
-            functools.partial(gather_kernel, self.bands),
-            jax.ShapeDtypeStruct((self.bands,) + block.shape, block.dtype),
-            [sems, sems, pltpu.SemaphoreType.DMA],
-            block,
-            label,
-        )
-
-    def swap(self, blocks, label):
-        sems = pltpu.SemaphoreType.DMA((self.bands,))
-        return self.call(
-            functools.partial(swap_kernel, self.bands),
-            jax.ShapeDtypeStruct(blocks.shape, blocks.dtype),
-            [sems, sems, pltpu.SemaphoreType.DMA],
-            blocks,
-            label,
-        )
-
-    def scatter(self, blocks, label):
-        sems = pltpu.SemaphoreType.DMA((self.bands,))
-        half = (self.bands // 2,) + blocks.shape[1:]
-        return self.call(
-            functools.partial(scatter_kernel, self.bands),
-            jax.ShapeDtypeStruct(blocks.shape[1:], jnp.float32),
-            [pltpu.VMEM(half, blocks.dtype)] * 3 + [sems, sems],
-            blocks,
-            label,
-        )
-
-    def over_tasks(self, block, label):
-        sems = pltpu.SemaphoreType.DMA((self.tasks,))
-        return self.call(
-            functools.partial(tasks_kernel, self.tasks),
-            jax.ShapeDtypeStruct((self.tasks,) + block.shape, block.dtype),
-            [sems, sems, pltpu.SemaphoreType.DMA],
-            block,
-            label,
-        )
-
-
 GELU_A = 0.7978845608028654
 GELU_B = 0.044715
 
@@ -738,6 +463,24 @@
     column = lax.rem(lax.broadcasted_iota(jnp.int32, value.shape, 0), cols) + by
     rolled = pltpu.roll(value, (-by) % rows, 0)
     return jnp.where((column >= 0) & (column < cols), rolled, 0.0)
+
+
+def row_mask(widths_ref, first_row, rows, cols):
+    column = lax.broadcasted_iota(jnp.int32, (cols, LANE), 0)
+    return jnp.concatenate(
+        [
+            jnp.where(column < widths_ref[first_row + number], 1.0, 0.0).astype(jnp.float32)
+            for number in range(rows)
+        ],
+        axis=0,
+    )
+
+
+def count_pixels(widths_ref):
+    total = widths_ref[0]
+    for number in range(1, widths_ref.shape[0]):
+        total = total + widths_ref[number]
+    return jnp.full((1, LANE), total.astype(jnp.float32), jnp.float32)
 
 
 class Post:
@@ -792,23 +535,30 @@
             pl.semaphore_signal(barrier, inc=1, device_id=device, device_id_type=MESH_ID)
         pl.semaphore_wait(barrier, len(greeted))
 
-    def sum_over(self, post, axis, own_ref, land_ref):
+    def sum_begin(self, post, axis, own_ref, land_ref):
         mine = self.task if axis == "task" else self.band
         others = self.other_tasks if axis == "task" else self.other_bands
         copies = [post.push(own_ref, land_ref.at[mine], {axis: other}) for other in others]
         land_ref[pl.ds(mine, 1)] = own_ref[...][None]
+        return copies, land_ref
+
+    def sum_end(self, begun):
+        copies, land_ref = begun
         for made in copies:
             made.wait_recv()
         total = land_ref[0]
-        for slot in range(1, len(others) + 1):
+        for slot in range(1, len(copies) + 1):
             total = total + land_ref[slot]
         return total
+
+    def sum_over(self, post, axis, own_ref, land_ref):
+        return self.sum_end(self.sum_begin(post, axis, own_ref, land_ref))
 
 
 def trunk_back_kernel(
     sizes,
     sg_ref,
-    h3_ref,
+    h3q,
     x_ref,
     v3_ref,
     h2_ref,
@@ -817,8 +567,7 @@
     v1_ref,
     a1_ref,
     a2_ref,
-    mask_ref,
-    inv_ref,
+    widths_ref,
     we_hbm,
     wd_hbm,
     wr_hbm,
@@ -835,7 +584,7 @@
     we,
     wd,
     wr,
-    h3q,
+    mask_ref,
     xq,
     xg,
     gram_own,
@@ -897,11 +646,10 @@
     task, band = at.task, at.band
     my_rows = pl.ds(pl.multiple_of(task * quarter, quarter), quarter)
     loads = [
-        pltpu.make_async_copy(h3_ref.at[my_rows], h3q, local_sem.at[0]),
-        pltpu.make_async_copy(x_ref.at[my_rows], xq, local_sem.at[1]),
-        pltpu.make_async_copy(we_hbm, we, local_sem.at[2]),
-        pltpu.make_async_copy(wd_hbm, wd, local_sem.at[3]),
-        pltpu.make_async_copy(wr_hbm, wr, local_sem.at[4]),
+        pltpu.make_async_copy(x_ref.at[my_rows], xq, local_sem.at[0]),
+        pltpu.make_async_copy(we_hbm, we, local_sem.at[1]),
+        pltpu.make_async_copy(wd_hbm, wd, local_sem.at[2]),
+        pltpu.make_async_copy(wr_hbm, wr, local_sem.at[3]),
     ]
     for load in loads:
         load.start()
@@ -911,13 +659,16 @@
     for other in at.other_tasks:
         theirs = pl.ds(pl.multiple_of(other * quarter, quarter), quarter)
         grads_in.append(post.push(sg_ref.at[:, theirs], xg.at[task], {"task": other}))
-    own_copy = pltpu.make_async_copy(sg_ref.at[:, my_rows], xg.at[task], local_sem.at[5])
+    own_copy = pltpu.make_async_copy(sg_ref.at[:, my_rows], xg.at[task], local_sem.at[4])
     own_copy.start()
 
     p_pair = [
         post.push(pt_ref.at[2 * number + 1 - at.core], p_twin.at[number], at.twin)
         for number in range(at.chips)
     ]
+
+    band_rows = x_ref.shape[0] // cols
+    mask_ref[...] = row_mask(widths_ref, band * band_rows, band_rows, cols)
 
     for number in range(3):
         a1t[number] = a1_ref[number].T
@@ -1024,14 +775,13 @@
         comb[other] = mixed(other)
         comb_in.append(post.push(comb.at[other], comb_land.at[band], {"space": other}))
     comb_land[pl.ds(band, 1)] = mixed(band)[None]
-    for load in loads[:2]:
-        load.wait()
+    loads[0].wait()
     for made in comb_in:
         made.wait_recv()
 
     mask_quarter = mask_ref[my_rows]
     mask_piece = jnp.concatenate([mask_quarter] * (piece // LANE), axis=1)
-    inv_count = inv_ref[0:1]
+    inv_count = 1.0 / count_pixels(widths_ref)
     inv_piece = jnp.concatenate([inv_count] * (piece // LANE), axis=1)
     per_row = st3.shape[1] // piece
     half = st3.shape[0] // 2
@@ -1052,10 +802,6 @@
 
     lax.fori_loop(0, bands, gate_step, 0)
     st3_mid[...] = at.sum_over(post, "task", st3, st3_land)
-    gate_in = [
-        post.push(gate_low, gate_band.at[task], {"task": other}) for other in at.other_tasks
-    ]
-    gate_band[pl.ds(task, 1)] = gate_low[...][None]
     s3_out[...] = at.sum_over(post, "space", st3_mid, st3_land_b)
 
     def third_step(number, carry):
@@ -1079,7 +825,7 @@
             post.push(l3.at[pl.ds(other * per_task, per_task)], l3x.at[task], {"task": other})
         )
     l3x[pl.ds(task, 1)] = l3[pl.ds(task * per_task, per_task)][None]
-    loads[2].wait()
+    loads[1].wait()
 
     def expand_step(number, total):
         lanes = pl.ds(pl.multiple_of(number * piece, piece), piece)
@@ -1105,11 +851,61 @@
             for base in (0, spread)
         ]
 
+    def to_twin(term, landing):
+        return post.push(term.at[1 - at.core], landing, at.twin)
+
+    def both_cores(pair, term, twin):
+        pair.wait_recv()
+        for step in range(1, at.chips):
+            other = lax.rem(at.chip + step, at.chips)
+            both = term[at.core, other].astype(f32) + twin[other].astype(f32)
+            twin[other] = both.astype(low)
+
+    def along(twin, landing):
+        return [
+            post.push(
+                twin.at[other], landing.at[at.chip], {"space": other * 2 + at.core}
+            )
+            for other in [lax.rem(at.chip + step, at.chips) for step in range(1, at.chips)]
+        ]
+
+    def settle(arrivals, term, twin, landing):
+        total = term[at.core, at.chip].astype(f32) + twin[at.chip].astype(f32)
+        for made in arrivals:
+            made.wait_recv()
+        for step in range(1, at.chips):
+            total = total + landing[lax.rem(at.chip + step, at.chips)].astype(f32)
+        return total.astype(low)
+
+    def to_tasks(share, landing):
+        arrivals = [post.push(share, landing.at[task], {"task": other}) for other in at.other_tasks]
+        landing[pl.ds(task, 1)] = share[...][None]
+        return arrivals
+
+    def expand_part(number):
+        share = jnp.concatenate([l3x[a, number] for a in range(tasks)], axis=0)
+        part = dot_nn(a2t[...], share).astype(low)
+        per_band = part.shape[0] // bands
+        for target in range(bands):
+            e_term[target % 2, target // 2, :, number * piece : (number + 1) * piece] = part[
+                target * per_band : (target + 1) * per_band
+            ]
+
+    narrow = mid // tasks
+    my_lanes = pl.ds(pl.multiple_of(task * narrow, narrow), narrow)
     put_sums(
         st2, jnp.sum(grad, axis=0, keepdims=True), jnp.sum(grad * hat, axis=0, keepdims=True)
     )
-    st2_mid[...] = at.sum_over(post, "task", st2, st2_land)
-    s2_out[...] = at.sum_over(post, "space", st2_mid, st2_land_b)
+    begun = at.sum_begin(post, "task", st2, st2_land)
+    for made in l3_in:
+        made.wait_recv()
+    expand_part(0)
+    st2_mid[...] = at.sum_end(begun)
+    begun = at.sum_begin(post, "space", st2_mid, st2_land_b)
+    for number in range(1, per_task):
+        expand_part(number)
+    e_pair = to_twin(e_term, e_twin)
+    s2_out[...] = at.sum_end(begun)
     shift_grad, gain_grad = get_sums(s2_out[...])
     l2[my_rows] = (
         mask_mid
@@ -1117,8 +913,14 @@
         * (grad - shift_grad * inv_mid - hat * (gain_grad * inv_mid))
     ).astype(low)
     l2_in = [post.push(l2.at[my_rows], l2.at[my_rows], {"task": other}) for other in at.other_tasks]
+    both_cores(e_pair, e_term, e_twin)
+    e_in = along(e_twin, e_land)
     for made in l2_in:
         made.wait_recv()
+    gate_in = [
+        post.push(gate_low, gate_band.at[task], {"task": other}) for other in at.other_tasks
+    ]
+    gate_band[pl.ds(task, 1)] = gate_low[...][None]
     has_above, has_below = band > 0, band < bands - 1
     up = post.copy(l2, l2_halo.at[1], {"space": lax.rem(band + bands - 1, bands)})
     down = post.copy(l2, l2_halo.at[0], {"space": lax.rem(band + 1, bands)})
@@ -1144,7 +946,7 @@
         made.wait_recv()
         block = p_all.at[lax.rem(at.chip + at.chips - step, at.chips) * 2 + at.core]
         p_passed.append(post.push(block, block, at.twin))
-    loads[3].wait()
+    loads[2].wait()
     halves = [slice(start, start + piece) for start in range(0, mid, piece)]
     for lanes in halves:
         total = None
@@ -1155,26 +957,17 @@
             total = part if total is None else total + part
         ag1[:, lanes] = total
 
-    for made in l3_in:
-        made.wait_recv()
-    share_e = [
-        jnp.concatenate([l3x[a, number] for a in range(tasks)], axis=0)
-        for number in range(per_task)
-    ]
-    for number in range(per_task):
-        part = dot_nn(a2t[...], share_e[number]).astype(low)
-        per_band = part.shape[0] // bands
-        for target in range(bands):
-            e_term[target % 2, target // 2, :, number * piece : (number + 1) * piece] = part[
-                target * per_band : (target + 1) * per_band
-            ]
-
-    def to_twin(term, landing):
-        return post.push(term.at[1 - at.core], landing, at.twin)
-
-    e_pair = to_twin(e_term, e_twin)
-    narrow = mid // tasks
-    my_lanes = pl.ds(pl.multiple_of(task * narrow, narrow), narrow)
+    share_d = l2[:, my_lanes].astype(f32)
+    for col_tap in range(3):
+        moved = shift_pixels(share_d, -CONV_DILATION * (col_tap - 1), cols).astype(low)
+        for row_tap in range(3):
+            part = dot_nn(a1t[row_tap], moved).astype(low)
+            per_band = part.shape[0] // bands
+            for target in range(bands):
+                d_term[target % 2, target // 2, 3 * row_tap + col_tap] = part[
+                    target * per_band : (target + 1) * per_band
+                ]
+    d_pair = to_twin(d_term, d_twin)
 
     @pl.when(has_below)
     def _():
@@ -1214,7 +1007,11 @@
     nothing = jnp.zeros((1, mid), f32)
     first, second = lax.fori_loop(0, 8, first_step, (nothing, nothing))
     put_sums(st1, first, second)
-    s1_out[...] = at.sum_over(post, "space", st1, st1_land)
+    begun = at.sum_begin(post, "space", st1, st1_land)
+    both_cores(d_pair, d_term, d_twin)
+    e_share[...] = settle(e_in, e_term, e_twin, e_land)
+    s1_out[...] = at.sum_end(begun)
+    d_in = along(d_twin, d_land)
     shift_grad, gain_grad = get_sums(s1_out[...])
     shift_grad, gain_grad = shift_grad * inv_mid, gain_grad * inv_mid
 
@@ -1239,52 +1036,11 @@
 
     lax.fori_loop(0, bands, reduce_step, 0)
     r_pair = to_twin(r_term, r_twin)
-    share_d = l2[:, my_lanes].astype(f32)
-    for col_tap in range(3):
-        moved = shift_pixels(share_d, -CONV_DILATION * (col_tap - 1), cols).astype(low)
-        for row_tap in range(3):
-            part = dot_nn(a1t[row_tap], moved).astype(low)
-            per_band = part.shape[0] // bands
-            for target in range(bands):
-                d_term[target % 2, target // 2, 3 * row_tap + col_tap] = part[
-                    target * per_band : (target + 1) * per_band
-                ]
-
-    def along(pair, term, twin, landing):
-        pair.wait_recv()
-        arrivals = []
-        for step in range(1, at.chips):
-            other = lax.rem(at.chip + step, at.chips)
-            both = term[at.core, other].astype(f32) + twin[other].astype(f32)
-            twin[other] = both.astype(low)
-            arrivals.append(
-                post.push(twin.at[other], landing.at[at.chip], {"space": other * 2 + at.core})
-            )
-        return arrivals
-
-    def settle(arrivals, term, twin, landing):
-        total = term[at.core, at.chip].astype(f32) + twin[at.chip].astype(f32)
-        for made in arrivals:
-            made.wait_recv()
-        for step in range(1, at.chips):
-            total = total + landing[lax.rem(at.chip + step, at.chips)].astype(f32)
-        return total.astype(low)
-
-    def to_tasks(share, landing):
-        arrivals = [post.push(share, landing.at[task], {"task": other}) for other in at.other_tasks]
-        landing[pl.ds(task, 1)] = share[...][None]
-        return arrivals
-
-    r_in = along(r_pair, r_term, r_twin, r_land)
-    e_in = along(e_pair, e_term, e_twin, e_land)
-    d_pair = to_twin(d_term, d_twin)
-    r_share[...] = settle(r_in, r_term, r_twin, r_land)
-    r_back = to_tasks(r_share, r_tasks)
-    d_in = along(d_pair, d_term, d_twin, d_land)
-    e_share[...] = settle(e_in, e_term, e_twin, e_land)
     e_back = to_tasks(e_share, e_tasks)
-
-    loads[4].wait()
+    both_cores(r_pair, r_term, r_twin)
+    r_in = along(r_twin, r_land)
+
+    loads[3].wait()
     for made in gate_in:
         made.wait_recv()
 
@@ -1297,13 +1053,11 @@
     lax.fori_loop(0, bands, input_step, 0)
     d_share[...] = settle(d_in, d_term, d_twin, d_land)
     d_back = to_tasks(d_share, d_tasks)
+    r_share[...] = settle(r_in, r_term, r_twin, r_land)
+    r_back = to_tasks(r_share, r_tasks)
     for made in [p_near] + p_passed:
         made.wait_recv()
-    pg_out[...] = p_all[...].astype(f32)
-    for made in r_back:
-        made.wait_recv()
-    for a in range(tasks):
-        rg_out[:, a * narrow : (a + 1) * narrow] = r_tasks[a].astype(f32)
+    pg_out[...] = p_all[...]
     for made in e_back:
         made.wait_recv()
     broad = wide // tasks
@@ -1313,6 +1067,10 @@
         made.wait_recv()
     for a in range(tasks):
         dg_out[:, :, a * narrow : (a + 1) * narrow] = d_tasks[a].astype(f32)
+    for made in r_back:
+        made.wait_recv()
+    for a in range(tasks):
+        rg_out[:, a * narrow : (a + 1) * narrow] = r_tasks[a].astype(f32)
     post.close()
 
     @pl.when(has_above)
@@ -1325,7 +1083,7 @@
 
 
 def trunk_back(
-    tasks, bands, cols, collective, sg, h3, x, v3, h2, v2, h1, v1, a1, a2, mask, inv, we, wd, wr, pt
+    tasks, bands, cols, collective, sg, h3, x, v3, h2, v2, h1, v1, a1, a2, widths, we, wd, wr, pt
 ):
     low, f32 = jnp.bfloat16, jnp.float32
     pixels, wide = x.shape
@@ -1362,7 +1120,7 @@
             pltpu.VMEM(we.shape, low),
             pltpu.VMEM(wd.shape, low),
             pltpu.VMEM(wr.shape, low),
-            pltpu.VMEM((quarter, wide), f32),
+            pltpu.VMEM((pixels, LANE), f32),
             pltpu.VMEM((quarter, wide), low),
             pltpu.VMEM((tasks, bands, quarter, piece), low),
         ]
@@ -1413,26 +1171,28 @@
         shape((8, stat_wide), f32),
         shape((2 * mid // LANE, LANE), f32),
         shape((2 * mid // LANE, LANE), f32),
-        shape(pt.shape, f32),
+        shape(pt.shape, low),
     )
     return pl.pallas_call(
         functools.partial(trunk_back_kernel, (tasks, bands, cols, quarter, mid, wide, piece)),
         name="trunk_back",
         out_shape=out_shapes,
-        in_specs=[in_vmem, anywhere, in_vmem] + [in_vmem] * 9 + [anywhere] * 3 + [in_vmem],
+        in_specs=[in_vmem] * 10
+        + [pl.BlockSpec(memory_space=pltpu.SMEM)]
+        + [anywhere] * 3
+        + [in_vmem],
         out_specs=(in_vmem,) * 9,
         scratch_shapes=scratch,
         compiler_params=pltpu.CompilerParams(
-            collective_id=collective, has_side_effects=True, vmem_limit_bytes=56 << 20
+            collective_id=collective, has_side_effects=True, vmem_limit_bytes=27 << 20
         ),
-    )(sg, h3, x, v3, h2, v2, h1, v1, a1, a2, mask, inv, we, wd, wr, pt)
+    )(sg, h3, x, v3, h2, v2, h1, v1, a1, a2, widths, we, wd, wr, pt)
 
 
 def head_kernel(
     plan,
     sh_ref,
-    mask_ref,
-    inv_ref,
+    widths_ref,
     gain_ref,
     shift_ref,
     cot_ref,
@@ -1443,7 +1203,6 @@
     sg_out,
     grads_out,
     proj_out,
-    pool_out,
     both_sums_out,
     proj_sums_out,
     rate,
@@ -1544,10 +1303,9 @@
                 total = total + extra[level - 1, number]
             put(level, total)
         twin_term(number).start()
-        turned[:, pl.ds(pl.multiple_of(number * group, group), group)] = source.T
-        return carry + jnp.sum(source.astype(f32), axis=0, keepdims=True)
-
-    pixel_sum = lax.fori_loop(0, chips, forward_group, jnp.zeros((1, width), f32))
+        return carry
+
+    lax.fori_loop(0, 2, forward_group, 0)
 
     def hop(source, landing, device_chip, number):
         return pltpu.make_async_remote_copy(
@@ -1570,11 +1328,27 @@
     def go_left(number):
         return hop(twin_land.at[number], left_land.at[number], prev_chip, base_left + number)
 
+    def start_off(number, copy):
+        twin_term(number).wait_recv()
+
+        def add(branch, carry):
+            twin_land[number, branch] = (
+                term[number, core, branch].astype(f32) + twin_land[number, branch].astype(f32)
+            ).astype(low)
+            return carry
+
+        lax.fori_loop(0, 4, add, 0)
+        copy.start()
+
     def pass_on(number, copy, landing, has_incoming):
-        twin_term(number).wait_recv()
+
+        @pl.when(jnp.logical_not(has_incoming))
+        def _():
+            start_off(number, copy)
 
         @pl.when(has_incoming)
         def _():
+            twin_term(number).wait_recv()
             copy.wait_recv()
 
             def add(branch, carry):
@@ -1586,33 +1360,55 @@
                 return carry
 
             lax.fori_loop(0, 4, add, 0)
-
-        @pl.when(jnp.logical_not(has_incoming))
+            copy.start()
+
+    @pl.when(chip == 0)
+    def _():
+        start_off(last, go_right(last))
+
+    @pl.when(chip == last)
+    def _():
+        start_off(0, go_left(0))
+
+    lax.fori_loop(2, chips, forward_group, 0)
+
+    def pass_right(number):
+        there = (chip < number) if number < last else ((chip < number) & (chip > 0))
+
+        @pl.when(there)
         def _():
-            def add(branch, carry):
-                twin_land[number, branch] = (
-                    term[number, core, branch].astype(f32) + twin_land[number, branch].astype(f32)
-                ).astype(low)
-                return carry
-
-            lax.fori_loop(0, 4, add, 0)
-
-        copy.start()
-
-    for number in range(last):
-        to_right, to_left = last - number, number
-
-        @pl.when(chip < to_right)
+            pass_on(number, go_right(number), right_land, chip > 0)
+
+    def pass_left(number):
+        there = (chip > number) if number > 0 else ((chip > number) & (chip < last))
+
+        @pl.when(there)
         def _():
-            pass_on(to_right, go_right(to_right), right_land, chip > 0)
-
-        @pl.when(chip > to_left)
-        def _():
-            pass_on(to_left, go_left(to_left), left_land, chip < last)
-
-    mask_own = mask_ref[pl.ds(pl.multiple_of(band * pixels, pixels), pixels)]
+            pass_on(number, go_left(number), left_land, chip < last)
+
+    def turn_group(number, carry):
+        source = rows_of(sh_ref, number)
+        turned[:, pl.ds(pl.multiple_of(number * group, group), group)] = source.T
+        return carry + jnp.sum(source.astype(f32), axis=0, keepdims=True)
+
+    pixel_sum = lax.fori_loop(0, chips, turn_group, jnp.zeros((1, width), f32))
+
+    @pl.when(chip < chips // 2)
+    def _():
+        for number in range(last):
+            pass_right(last - number)
+            pass_left(number)
+
+    @pl.when(chip >= chips // 2)
+    def _():
+        for number in range(last):
+            pass_left(number)
+            pass_right(last - number)
+
+    band_rows = pixels // cols
+    mask_own = row_mask(widths_ref, band * band_rows, band_rows, cols)
     mask_own = jnp.concatenate([mask_own] * (width // LANE), axis=1)
-    inv_count = jnp.concatenate([inv_ref[0:1]] * (width // LANE), axis=1)
+    inv_count = jnp.concatenate([1.0 / count_pixels(widths_ref)] * (width // LANE), axis=1)
     spread = width // LANE
 
     def put_rows(target, number, value):
@@ -1731,7 +1527,10 @@
     put_rows(st_back, 8, pool_total)
     both_sums_out[...] = at.sum_over(post, "space", st_back, st_back_land)
     pool_grad = (gelu_slope(pooled) * get_rows(both_sums_out, 8)).astype(low)
-    pool_out[...] = jnp.broadcast_to(pool_grad.astype(f32), pool_out.shape)
+    column = jnp.broadcast_to(pixel_sum, (8, width)).T[:, 0:1]
+    grads_out[len(taps) + 1] = (
+        column * (pool_grad.astype(f32) * inv_count)
+    ).astype(low)
 
     def both_step(branch, carry):
         _, inv_std = scale_of(st_both_sum, branch, 4 + branch)
@@ -1874,8 +1673,8 @@
         back[source] = total
 
     def finish_group(number, carry):
-        rows = pl.ds(pl.multiple_of(number * group, group), group)
-        keep = jnp.concatenate([mask_ref[rows]] * spread, axis=1)
+        keep = row_mask(widths_ref, number * 2 * band_rows, 2 * band_rows, cols)
+        keep = jnp.concatenate([keep] * spread, axis=1)
         value = (back[number] + keep * pool_row).astype(low)
         sg_out[2 * number] = value[:pixels]
         sg_out[2 * number + 1] = value[pixels:]
@@ -1919,7 +1718,7 @@
             send_left(step).wait_send()
 
 
-def head(tasks, bands, cols, rows, collective, sh, mask, inv, gain, shift, cot, bw, pw, rate):
+def head(tasks, bands, cols, rows, collective, sh, widths, gain, shift, cot, bw, pw, rate):
     low, f32 = jnp.bfloat16, jnp.float32
     pixels, width = sh.shape[1], pw.shape[1]
     chips = bands // 2
@@ -1977,9 +1776,8 @@
     out_shapes = (
         shape(block, low),
         shape(sh.shape, low),
-        shape((len(taps) + 1, sh.shape[2], width), low),
+        shape((len(taps) + 2, sh.shape[2], width), low),
         shape(pw.shape, low),
-        shape((8, width), f32),
         shape((both_rows, LANE), f32),
         shape((proj_rows, LANE), f32),
     )
@@ -1989,33 +1787,412 @@
         ),
         name="head",
         out_shape=out_shapes,
-        in_specs=[in_vmem] * 8 + [anywhere],
-        out_specs=(in_vmem,) * 7,
+        in_specs=[in_vmem, pl.BlockSpec(memory_space=pltpu.SMEM)] + [in_vmem] * 5 + [anywhere],
+        out_specs=(in_vmem,) * 6,
         scratch_shapes=scratch,
         compiler_params=pltpu.CompilerParams(
-            collective_id=collective, has_side_effects=True, vmem_limit_bytes=60 << 20
+            collective_id=collective, has_side_effects=True, vmem_limit_bytes=36 << 20
         ),
-    )(sh, mask, inv, gain, shift, cot, bw, pw, rate)
-
-
-def norm_scale(totals, pixel_count):
-    mean_value = totals[0] / pixel_count
-    variance = totals[1] / pixel_count - mean_value * mean_value
-    return mean_value, variance, lax.rsqrt(variance + NORM_EPS)
-
-
-def masked_sums(hidden, valid_mask):
-    kept = hidden * valid_mask
-    return [jnp.sum(kept, axis=0), jnp.sum(hidden * kept, axis=0)]
-
-
-def shift_columns(image, by):
-    if by == 0:
-        return image
-    cols = image.shape[1]
-    if by > 0:
-        return jnp.pad(image[:, by:], ((0, 0), (0, by), (0, 0)))
-    return jnp.pad(image[:, : cols + by], ((0, 0), (-by, 0), (0, 0)))
+    )(sh, widths, gain, shift, cot, bw, pw, rate)
+
+
+def trunk_kernel(
+    sizes,
+    x_hbm,
+    widths_ref,
+    gain_ref,
+    shift_ref,
+    wr_hbm,
+    wd_hbm,
+    we_hbm,
+    sh_out,
+    rim,
+    h1,
+    h2,
+    a2,
+    h3q,
+    v1,
+    v2,
+    v3,
+    stats_out,
+    x,
+    wr,
+    wd,
+    we,
+    h3,
+    blocks,
+    mask_own,
+    st1,
+    st1_land,
+    st2,
+    st2_land,
+    st3,
+    st3_land,
+    send_sem,
+    recv_sem,
+    local_sem,
+):
+    tasks, bands, cols, quarter, mid, wide, piece = sizes
+    low, f32 = jnp.bfloat16, jnp.float32
+    at = Place(tasks, bands)
+    post = Post(send_sem, recv_sem)
+    task, band = at.task, at.band
+    my_rows = pl.ds(pl.multiple_of(task * quarter, quarter), quarter)
+    loads = [
+        pltpu.make_async_copy(source, target, local_sem.at[number])
+        for number, (source, target) in enumerate(
+            ((x_hbm, x), (wr_hbm, wr), (wd_hbm, wd), (we_hbm, we))
+        )
+    ]
+    for load in loads:
+        load.start()
+    at.meet(True, True)
+    pixels = x.shape[0]
+    band_rows = pixels // cols
+    mask = row_mask(widths_ref, band * band_rows, band_rows, cols)
+    count = count_pixels(widths_ref)
+    spread = mid // LANE
+
+    def across(value, lanes):
+        return jnp.concatenate([value] * (lanes // LANE), axis=1)
+
+    def put_sums(target, value, keep):
+        kept = value * keep
+        first = jnp.sum(kept, axis=0, keepdims=True)
+        second = jnp.sum(kept * value, axis=0, keepdims=True)
+        for number in range(spread):
+            lanes = slice(number * LANE, (number + 1) * LANE)
+            target[number : number + 1] = first[:, lanes]
+            target[spread + number : spread + number + 1] = second[:, lanes]
+
+    def get_sums(total):
+        return [
+            jnp.concatenate([total[base + k : base + k + 1] for k in range(spread)], axis=1)
+            for base in (0, spread)
+        ]
+
+    def put_norm(vectors, lanes, first, second, start):
+        width = first.shape[1]
+        inv = across(1.0 / count, width)
+        mean_value = first * inv
+        variance = second * inv - mean_value * mean_value
+        vectors[0:1, lanes] = mean_value
+        vectors[1:2, lanes] = lax.rsqrt(variance + NORM_EPS)
+        vectors[2:3, lanes] = gain_ref[:, start : start + width]
+        vectors[3:4, lanes] = shift_ref[:, start : start + width]
+        stats_out[0:1, start : start + width] = mean_value
+        stats_out[1:2, start : start + width] = variance * across(count / (count - 1.0), width)
+
+    def activate(hidden, vectors, keep):
+        normed = vectors[2:3] * ((hidden - vectors[0:1]) * vectors[1:2]) + vectors[3:4]
+        return (gelu_of(normed) * keep).astype(low)
+
+    mask_mid = across(mask, mid)
+    for load in loads[:2]:
+        load.wait()
+    h1[...] = dot_nn(x[...], wr[...])
+    put_sums(st1, h1[...], mask_mid)
+    first, second = get_sums(at.sum_over(post, "space", st1, st1_land))
+    put_norm(v1, slice(0, mid), first, second, 0)
+    rim[1] = activate(h1[...], v1, mask_mid)
+
+    has_above, has_below = band > 0, band < bands - 1
+    up = post.copy(rim.at[1], rim.at[2], {"space": lax.rem(band + bands - 1, bands)})
+    down = post.copy(rim.at[1], rim.at[0], {"space": lax.rem(band + 1, bands)})
+
+    @pl.when(has_above)
+    def _():
+        up.start()
+
+    @pl.when(has_below)
+    def _():
+        down.start()
+
+    @pl.when(jnp.logical_not(has_above))
+    def _():
+        rim[0] = jnp.zeros(rim.shape[1:], low)
+
+    @pl.when(jnp.logical_not(has_below))
+    def _():
+        rim[2] = jnp.zeros(rim.shape[1:], low)
+
+    loads[2].wait()
+    halves = [slice(start, start + piece) for start in range(0, mid, piece)]
+
+    def tap_sum(row_taps, lanes):
+        total = None
+        for col_tap in range(3):
+            part = None
+            for row_tap in row_taps:
+                term = dot_nn(rim[row_tap], wd[3 * row_tap + col_tap, :, lanes])
+                part = term if part is None else part + term
+            part = shift_pixels(part, CONV_DILATION * (col_tap - 1), cols)
+            total = part if total is None else total + part
+        return total
+
+    for lanes in halves:
+        h2[:, lanes] = tap_sum((1,), lanes)
+
+    @pl.when(has_below)
+    def _():
+        up.wait_recv()
+
+    @pl.when(has_above)
+    def _():
+        down.wait_recv()
+
+    for lanes in halves:
+        h2[:, lanes] += tap_sum((0, 2), lanes)
+
+    put_sums(st2, h2[...], mask_mid)
+    first, second = get_sums(at.sum_over(post, "space", st2, st2_land))
+    put_norm(v2, slice(0, mid), first, second, mid)
+    a2[...] = activate(h2[...], v2, mask_mid)
+
+    loads[3].wait()
+    mask_piece = across(mask, piece)
+    per_row = st3.shape[1] // piece
+    half = st3.shape[0] // 2
+
+    def expand_step(number, carry):
+        lanes = pl.ds(pl.multiple_of(number * piece, piece), piece)
+        value = dot_nn(a2[...], we[:, lanes])
+        h3[:, lanes] = value
+        kept = value * mask_piece
+        row = number // per_row
+        spot = pl.ds(pl.multiple_of(lax.rem(number, per_row) * piece, piece), piece)
+        st3[pl.ds(row, 1), spot] = jnp.sum(kept, axis=0, keepdims=True)
+        st3[pl.ds(half + row, 1), spot] = jnp.sum(kept * value, axis=0, keepdims=True)
+        return carry
+
+    lax.fori_loop(0, bands, expand_step, 0)
+    begun = at.sum_begin(post, "space", st3, st3_land)
+    h3q[...] = h3[my_rows]
+    total = at.sum_end(begun)
+    lanes_in = st3.shape[1]
+    for row in range(half):
+        put_norm(
+            v3,
+            slice(row * lanes_in, (row + 1) * lanes_in),
+            total[row : row + 1],
+            total[half + row : half + row + 1],
+            2 * mid + row * lanes_in,
+        )
+
+    mask_own[...] = mask
+    mask_quarter = across(mask_own[my_rows], piece)
+
+    def shared_of(number):
+        lanes = pl.ds(pl.multiple_of(number * piece, piece), piece)
+        hat = (h3q[:, lanes] - v3[0:1, lanes]) * v3[1:2, lanes]
+        before = v3[2:3, lanes] * hat + v3[3:4, lanes] + x[my_rows, lanes].astype(f32)
+        return (gelu_of(before) * mask_quarter).astype(low)
+
+    slices_in = []
+    for other in at.other_bands:
+        blocks[other] = shared_of(other)
+        slices_in.append(
+            post.push(blocks.at[other], sh_out.at[band, my_rows], {"space": other})
+        )
+    sh_out[band, my_rows] = shared_of(band)
+
+    def to_tasks(number):
+        block = sh_out.at[number, my_rows]
+        return [post.push(block, block, {"task": other}) for other in at.other_tasks]
+
+    quarters_in = to_tasks(band)
+    for step, made in enumerate(slices_in, start=1):
+        made.wait_recv()
+        quarters_in += to_tasks(lax.rem(band + bands - step, bands))
+    for made in quarters_in:
+        made.wait_recv()
+    post.close()
+
+    @pl.when(has_above)
+    def _():
+        up.wait_send()
+
+    @pl.when(has_below)
+    def _():
+        down.wait_send()
+
+
+def trunk(tasks, bands, cols, collective, x, widths, gain, shift, wr, wd, we):
+    low, f32 = jnp.bfloat16, jnp.float32
+    pixels, wide = x.shape
+    mid = wr.shape[1]
+    quarter, piece = pixels // tasks, wide // bands
+    in_vmem = pl.BlockSpec(memory_space=pltpu.VMEM)
+    anywhere = pl.BlockSpec(memory_space=pl.ANY)
+    shape = jax.ShapeDtypeStruct
+    narrow_stats = [
+        pltpu.VMEM((2 * mid // LANE, LANE), f32),
+        pltpu.VMEM((bands, 2 * mid // LANE, LANE), f32),
+    ]
+    return pl.pallas_call(
+        functools.partial(trunk_kernel, (tasks, bands, cols, quarter, mid, wide, piece)),
+        name="trunk",
+        out_shape=(
+            shape((bands, pixels, piece), low),
+            shape((3, pixels, mid), low),
+            shape((pixels, mid), f32),
+            shape((pixels, mid), f32),
+            shape((pixels, mid), low),
+            shape((quarter, wide), f32),
+            shape((8, mid), f32),
+            shape((8, mid), f32),
+            shape((8, wide), f32),
+            shape((2, 2 * mid + wide), f32),
+        ),
+        in_specs=[anywhere, pl.BlockSpec(memory_space=pltpu.SMEM), in_vmem, in_vmem]
+        + [anywhere] * 3,
+        out_specs=(in_vmem,) * 10,
+        scratch_shapes=[
+            pltpu.VMEM(x.shape, low),
+            pltpu.VMEM(wr.shape, low),
+            pltpu.VMEM(wd.shape, low),
+            pltpu.VMEM(we.shape, low),
+            pltpu.VMEM((pixels, wide), f32),
+            pltpu.VMEM((bands, quarter, piece), low),
+            pltpu.VMEM((pixels, LANE), f32),
+        ]
+        + narrow_stats
+        + narrow_stats
+        + [
+            pltpu.VMEM((8, wide // 4), f32),
+            pltpu.VMEM((bands, 8, wide // 4), f32),
+            pltpu.SemaphoreType.DMA((64,)),
+            pltpu.SemaphoreType.DMA((64,)),
+            pltpu.SemaphoreType.DMA((4,)),
+        ],
+        compiler_params=pltpu.CompilerParams(
+            collective_id=collective, has_side_effects=True, vmem_limit_bytes=54 << 20
+        ),
+    )(x, widths, gain, shift, wr, wd, we)
+
+
+def finish_kernel(
+    places,
+    tap_ref,
+    ho_in,
+    ig_in,
+    rg_in,
+    dg_in,
+    eg_in,
+    pg_ref,
+    s3_ref,
+    s2_ref,
+    s1_ref,
+    both_ref,
+    proj_ref,
+    ho_out,
+    ig_out,
+    rg_out,
+    dg_out,
+    eg_out,
+    branch_out,
+    rate_out,
+    pg_out,
+    tg_out,
+    ts_out,
+    hg_out,
+    hs_out,
+    branch,
+    rate,
+    sems,
+):
+    f32 = jnp.float32
+    width = tap_ref.shape[2]
+    copies = [
+        pltpu.make_async_copy(source, target, sems.at[number])
+        for number, (source, target) in enumerate(
+            (
+                (ho_in, ho_out),
+                (ig_in, ig_out),
+                (rg_in, rg_out),
+                (dg_in, dg_out),
+                (eg_in, eg_out),
+            )
+        )
+    ]
+    for copy in copies:
+        copy.start()
+    per_level = len(places) // 3
+    for level in range(3):
+        for number in range(level * per_level, (level + 1) * per_level):
+            lanes = slice(number * width, (number + 1) * width)
+            if places[number] is None:
+                rate[:, lanes] = jnp.zeros((rate.shape[0], width), f32)
+            else:
+                rate[:, lanes] = tap_ref[places[number]].astype(f32)
+        lanes = slice(level * per_level * width, (level + 1) * per_level * width)
+        copy = pltpu.make_async_copy(
+            rate.at[:, lanes], rate_out.at[:, lanes], sems.at[len(copies)]
+        )
+        copy.start()
+        copies.append(copy)
+    count = tap_ref.shape[0]
+    branch[:, :width] = tap_ref[count - 2].astype(f32)
+    branch[:, width:] = tap_ref[count - 1].astype(f32)
+    copy = pltpu.make_async_copy(branch, branch_out, sems.at[len(copies)])
+    copy.start()
+    copies.append(copy)
+    pg_out[...] = pg_ref[...].astype(f32)
+    rows = s1_ref.shape[0] // 2
+    ts_out[0:rows] = s1_ref[0:rows]
+    tg_out[0:rows] = s1_ref[rows : 2 * rows]
+    ts_out[rows : 2 * rows] = s2_ref[0:rows]
+    tg_out[rows : 2 * rows] = s2_ref[rows : 2 * rows]
+    half, lanes_in = s3_ref.shape[0] // 2, s3_ref.shape[1]
+    for row in range(half):
+        for part in range(lanes_in // LANE):
+            target = 2 * rows + row * (lanes_in // LANE) + part
+            lanes = slice(part * LANE, (part + 1) * LANE)
+            ts_out[target : target + 1] = s3_ref[row : row + 1, lanes]
+            tg_out[target : target + 1] = s3_ref[half + row : half + row + 1, lanes]
+    spread = width // LANE
+    hs_out[0 : 4 * spread] = both_ref[0 : 4 * spread]
+    hg_out[0 : 4 * spread] = both_ref[4 * spread : 8 * spread]
+    hs_out[4 * spread : 5 * spread] = proj_ref[0:spread]
+    hg_out[4 * spread : 5 * spread] = proj_ref[spread : 2 * spread]
+    for copy in copies:
+        copy.wait()
+
+
+def finish(places, taps, ho, ig, rg, dg, eg, pg, s3, s2, s1, both, proj):
+    f32 = jnp.float32
+    in_vmem = pl.BlockSpec(memory_space=pltpu.VMEM)
+    anywhere = pl.BlockSpec(memory_space=pl.ANY)
+    shape = jax.ShapeDtypeStruct
+    depth, width = taps.shape[1:]
+    rows = (s1.size + s2.size + s3.size) // 2 // LANE
+    head_rows = 5 * width // LANE
+    return pl.pallas_call(
+        functools.partial(finish_kernel, places),
+        name="finish",
+        out_shape=(
+            shape(ho.shape, ho.dtype),
+            shape(ig.shape, ig.dtype),
+            shape(rg.shape, rg.dtype),
+            shape(dg.shape, dg.dtype),
+            shape(eg.shape, eg.dtype),
+            shape((depth, 2 * width), f32),
+            shape((depth, len(places) * width), f32),
+            shape(pg.shape, f32),
+            shape((rows, LANE), f32),
+            shape((rows, LANE), f32),
+            shape((head_rows, LANE), f32),
+            shape((head_rows, LANE), f32),
+        ),
+        in_specs=[in_vmem] + [anywhere] * 5 + [in_vmem] * 6,
+        out_specs=(anywhere,) * 7 + (in_vmem,) * 5,
+        scratch_shapes=[
+            pltpu.VMEM((depth, 2 * width), f32),
+            pltpu.VMEM((depth, len(places) * width), f32),
+            pltpu.SemaphoreType.DMA((9,)),
+        ],
+        compiler_params=pltpu.CompilerParams(vmem_limit_bytes=40 << 20),
+    )(taps, ho, ig, rg, dg, eg, pg, s3, s2, s1, both, proj)
 
 
 def live_taps(rows, cols):
@@ -2044,137 +2221,47 @@
     head_shift,
     head_cot,
 ):
-    links = Links()
-    bands, tasks = links.bands, links.tasks
-    low = jnp.bfloat16
-    wide = jnp.float32
-    band_rows, cols_count, in_width = features.shape
-    rows_count = band_rows * bands
-    pixels = band_rows * cols_count
-    all_pixels = pixels * bands
-    middle_width = w_reduce.shape[1]
+    bands, tasks = lax.axis_size("space"), lax.axis_size("task")
+    band_rows, cols, in_width = features.shape
+    rows = band_rows * bands
+    pixels = band_rows * cols
     head_width = proj_weight.shape[2]
-    slice_width = in_width // bands
-    band = lax.axis_index("space")
-    task = lax.axis_index("task")
-    widths = lax.dynamic_slice_in_dim(row_width, band * band_rows, band_rows)
-
-    def mask_of(some_widths):
-        return (
-            (jnp.arange(cols_count)[None, :] < some_widths[:, None]).astype(wide).reshape(-1, 1)
-        )
-
-    valid_mask = mask_of(widths)
-    all_mask = mask_of(row_width)
-    pixel_count = jnp.sum(row_width).astype(wide)
     inputs = features.reshape(pixels, in_width)
-    gains = [
-        trunk_gain[:middle_width],
-        trunk_gain[middle_width : 2 * middle_width],
-        trunk_gain[2 * middle_width :],
-    ]
-    shifts = [
-        trunk_shift[:middle_width],
-        trunk_shift[middle_width : 2 * middle_width],
-        trunk_shift[2 * middle_width :],
-    ]
-
-    def norm(hidden, totals, gain_vec, shift_vec):
-        mean_value, variance, inv_std = norm_scale(totals, pixel_count)
-        scaled = (hidden - mean_value) * inv_std
-        return gain_vec * scaled + shift_vec, scaled, inv_std, mean_value, variance
-
-    hidden_one = jnp.dot(inputs, w_reduce, preferred_element_type=wide)
-    stats_one = norm(
-        hidden_one, links.sums(masked_sums(hidden_one, valid_mask), "sums_one"), gains[0], shifts[0]
-    )
-    first_active = (jax.nn.gelu(stats_one[0]) * valid_mask).astype(low)
-    rim = band_rim(first_active.reshape(band_rows, cols_count, middle_width))
-    patches = trunk_taps(rim, CONV_DILATION, band_rows, cols_count, False)
-    hidden_two = jnp.einsum("pti,ito->po", patches, w_dilated, preferred_element_type=wide)
-    stats_two = norm(
-        hidden_two, links.sums(masked_sums(hidden_two, valid_mask), "sums_two"), gains[1], shifts[1]
-    )
-    active_two = (jax.nn.gelu(stats_two[0]) * valid_mask).astype(low)
-    hidden_three = jnp.dot(active_two, w_expand, preferred_element_type=wide)
-    stats_three = norm(
-        hidden_three,
-        links.sums(masked_sums(hidden_three, valid_mask), "sums_three"),
-        gains[2],
-        shifts[2],
-    )
-    before_act = stats_three[0] + inputs.astype(wide)
-    shared = (jax.nn.gelu(before_act) * valid_mask).astype(low)
-
-    shared_slice = links.swap(
-        shared.reshape(pixels, bands, slice_width).transpose(1, 0, 2), "swap_shared"
-    ).reshape(all_pixels, slice_width)
-    pixel_sum = jnp.sum(shared_slice.astype(wide), axis=0)
-    branch_local = branch_weight[0]
-    inv_block = jnp.broadcast_to(1.0 / pixel_count, (8, LANE))
-    links.used += 1
-    taps, (
-        head_result,
-        shared_grad,
-        tap_grads,
-        proj_term,
-        pool_rows,
-        both_sums,
-        proj_sums,
-    ) = head(
+    dilated = w_dilated.transpose(1, 0, 2)
+    shared, rim, h1, h2, a2, h3q, v1, v2, v3, batch_stats = trunk(
         tasks,
         bands,
-        cols_count,
-        rows_count,
-        links.used - 1,
-        shared_slice.reshape(bands, pixels, slice_width),
-        jnp.broadcast_to(all_mask, (all_pixels, LANE)),
-        inv_block,
+        cols,
+        0,
+        inputs,
+        row_width,
+        trunk_gain.reshape(1, -1),
+        trunk_shift.reshape(1, -1),
+        w_reduce,
+        dilated,
+        w_expand,
+    )
+    taps, (head_out, shared_grad, tap_grads, proj_term, both_sums, proj_sums) = head(
+        tasks,
+        bands,
+        cols,
+        rows,
+        1,
+        shared,
+        row_width,
         head_gain,
         head_shift,
         head_cot.reshape(pixels, head_width),
-        branch_local,
+        branch_weight[0],
         proj_weight[0],
         rate_weight[0],
     )
-    pool_weight_grad = pixel_sum[:, None] * pool_rows[0:1] / pixel_count
-    branch_grad = jnp.concatenate([tap_grads[len(taps)].astype(wide), pool_weight_grad], axis=1)
-    place_of = {tap[:3]: number for number, tap in enumerate(taps)}
-    nothing = jnp.zeros((slice_width, head_width), wide)
-    rate_grad = jnp.concatenate(
-        [
-            tap_grads[place_of[level, row_tap, col_tap]].astype(wide)
-            if (level, row_tap, col_tap) in place_of
-            else nothing
-            for level in (1, 2, 3)
-            for row_tap in range(3)
-            for col_tap in range(3)
-        ],
-        axis=1,
-    )
-    head_sums = [
-        jnp.concatenate([both, proj])
-        for both, proj in zip(
-            both_sums.reshape(-1)[: 8 * head_width].reshape(2, -1),
-            proj_sums.reshape(-1)[: 2 * head_width].reshape(2, -1),
-        )
-    ]
-
-    def vectors(stats, number):
-        return jnp.concatenate(
-            [
-                jnp.stack([stats[3], stats[2], gains[number], shifts[number]]),
-                jnp.zeros((4, stats[3].size), wide),
-            ]
-        )
-
-    links.used += 1
     (
         weight_rows,
         input_grad,
-        w_reduce_grad,
+        reduce_grad,
         dilated_grad,
-        w_expand_grad,
+        expand_grad,
         sums_three,
         sums_two,
         sums_one,
@@ -2182,52 +2269,74 @@
     ) = trunk_back(
         tasks,
         bands,
-        cols_count,
-        links.used - 1,
+        cols,
+        2,
         shared_grad,
-        hidden_three,
+        h3q,
         inputs,
-        vectors(stats_three, 2),
-        hidden_two,
-        vectors(stats_two, 1),
-        hidden_one,
-        vectors(stats_one, 0),
-        rim.reshape(3, pixels, middle_width),
-        active_two,
-        jnp.broadcast_to(valid_mask, (pixels, LANE)),
-        inv_block,
+        v3,
+        h2,
+        v2,
+        h1,
+        v1,
+        rim,
+        a2,
+        row_width,
         w_expand,
-        w_dilated.transpose(1, 0, 2),
+        dilated,
         w_reduce,
         proj_term.reshape(bands, -1, head_width),
     )
-    proj_grad = proj_grad.reshape(-1, head_width)
-    task_weight = weight_rows[:tasks, 0]
-    w_dilated_grad = dilated_grad.transpose(1, 0, 2)
-    sums_three, sums_two, sums_one = (
-        value.reshape(2, -1) for value in (sums_three, sums_two, sums_one)
-    )
-    means = jnp.concatenate([stats_one[3], stats_two[3], stats_three[3]])
-    variances = (
-        jnp.concatenate([stats_one[4], stats_two[4], stats_three[4]])
-        * pixel_count
-        / (pixel_count - 1.0)
+    place_of = {tap[:3]: number for number, tap in enumerate(taps)}
+    places = tuple(
+        place_of.get((level, row_tap, col_tap))
+        for level in (1, 2, 3)
+        for row_tap in range(3)
+        for col_tap in range(3)
+    )
+    (
+        head_out,
+        input_grad,
+        reduce_grad,
+        dilated_grad,
+        expand_grad,
+        branch_grad,
+        rate_grad,
+        proj_grad,
+        trunk_gains,
+        trunk_shifts,
+        head_gains,
+        head_shifts,
+    ) = finish(
+        places,
+        tap_grads,
+        head_out,
+        input_grad,
+        reduce_grad,
+        dilated_grad,
+        expand_grad,
+        proj_grad.reshape(-1, head_width),
+        sums_three,
+        sums_two,
+        sums_one,
+        both_sums,
+        proj_sums,
     )
     return (
-        head_result.reshape(1, band_rows, cols_count, head_width),
-        input_grad.reshape(band_rows, cols_count, in_width),
-        w_reduce_grad,
-        w_dilated_grad,
-        w_expand_grad,
-        jnp.concatenate([sums_one[1], sums_two[1], sums_three[1]]),
-        jnp.concatenate([sums_one[0], sums_two[0], sums_three[0]]),
-        jnp.stack([means, variances]),
+        head_out.reshape(1, band_rows, cols, head_width),
+        input_grad.reshape(features.shape),
+        reduce_grad,
+        dilated_grad.transpose(1, 0, 2),
+        expand_grad,
+        trunk_gains.reshape(-1),
+        trunk_shifts.reshape(-1),
+        batch_stats,
         branch_grad[None],
         rate_grad[None],
         proj_grad[None],
-        head_sums[1][None],
-        head_sums[0][None],
-        task_weight,
+        head_gains.reshape(1, -1),
+        head_shifts.reshape(1, -1),
+        weight_rows[:tasks, 0],
     )
 
 

time: 346 us -> 264 us (0.76)
  Pallas kernels: 286 us -> 255 us
  other arithmetic: 19.4 us -> 0 us
  local copies, waits for them, and re-layouts: 24.8 us -> 7.19 us
  starting transfers between devices: 5.56 us -> 0 us
  matrix products: 4.82 us -> 0 us
    pallas_call x1, Pallas kernels: 122 us -> 104 us  [trunk_back(): pl.pallas_call(functools.partial(trunk_back_kernel, (tasks, bands, cols,...]
    pallas_call x1, Pallas kernels: 117 us -> 103 us  [head(): pl.pallas_call(functools.partial(head_kernel, (tasks, bands, cols, pixels...]
    unnamed x16 -> x0, other arithmetic: 12 us -> none
    ppermute x2 -> x0, starting transfers between devices: 5.56 us -> none  [the longest x1 3.26 us: with_halo(): lax.ppermute(lax.slice_in_dim(block, block.shape[dim] - width, None, axis...]
    unnamed x60 -> x43, local copies, waits for them, and re-layouts: 11.1 us -> 5.96 us
    dot_general x3 -> x0, matrix products: 4.82 us -> none  [the longest x1 2.66 us: per_device_slices(): hidden_one = jnp.dot(inputs, w_reduce, preferred_element_type=wide)]
    broadcast_in_dim x6 -> x0, local copies, waits for them, and re-layouts: 3.9 us -> none  [the longest x1 1.3 us: per_device_slices(): jnp.broadcast_to(all_mask, (all_pixels, LANE))]
    pallas_call x4 -> x2, Pallas kernels: 46.2 us -> 47.2 us  [the longest x1 42 us: trunk(): pl.pallas_call(functools.partial(trunk_kernel, (tasks, bands, cols, quart...]
  transfers between devices with their start and end apart: 2 -> 0, of which waited for: 2 -> 0; matrix products, arithmetic and copies ran while one was open for 0% -> 0% of each run, Pallas kernels for 0% -> 0%
where the time goes in v3:
time: 264 us; the launch traced here: 263 us
  Pallas kernels  255 us (97%)
  local copies, waits for them, and re-layouts  7.19 us (3%)
    pallas_call x1, Pallas kernels, trunk_back(): pl.pallas_call(functools.partial(trunk_back_kernel, (tasks, bands, cols,...  104 us
    pallas_call x1, Pallas kernels, head(): pl.pallas_call(functools.partial(head_kernel, (tasks, bands, cols, pixels...  103 us
    pallas_call x1, Pallas kernels, trunk(): pl.pallas_call(functools.partial(trunk_kernel, (tasks, bands, cols, quart...  42 us
    unnamed x43, local copies, waits for them, and re-layouts  5.96 us

profile of v3, /device:TPU:13, one launch (start us, length us, event | category | flops | bytes accessed | tf_op | source)
XLA Modules:
  0.0 262.7 jit_solution(8201700919771862313)
XLA Ops:
  0.6 0.0 copy-start.4
  0.7 0.0 copy-start.7
  0.7 0.0 copy-start.12
  0.7 0.0 copy-start.13
  0.7 0.0 copy-start.17
  0.7 0.0 copy-start.18
  0.7 0.0 copy-start.19
  0.7 0.0 copy-start.1
  0.7 0.0 copy-start.2
  0.7 0.0 copy-start.3
  0.7 42.0 %trunk.1 = (bf16[8,256,256]{2,1,0:T(8,128)(2,1)}, bf16[3,256,512]{2,1,0:T(8,128)(2,1)}, f32[256,512]{1,0:T(8,128)}, f32[256,512]{1,0:T(8,128)}, bf16[256,512]{1,...) custom-call(bf16[256,2048]{1,0:T(8,128)(2,1)} %bitcast.28, ...), custom_call_target="tpu_custom_call" | custom-call | tf_op jit(solution)/shard_map/trunk/pallas_call | solution.py:2032
  42.8 0.0 copy-done.4
  42.8 1.2 copy-done.5
  44.1 0.0 copy-start.16
  44.1 103.3 %head.1 = (bf16[256,256]{1,0:T(8,128)(2,1)S(1)}, bf16[8,256,256]{2,1,0:T(8,128)(2,1)S(1)}, bf16[17,256,256]{2,1,0:T(8,128)(2,1)S(1)}, bf16[1280,256]{1,0:T(8,128...) custom-call(bf16[8,256,256]{2,1,0:T(8,128)(2,1)S(1)} %copy-done.5, s32[16]{0:T(128)S(1)} %copy-done.19, ...), custom_call_target="tpu_custom_call" | custom-call | tf_op jit(solution)/shard_map/head/pallas_call | solution.py:1784
  147.5 1.0 copy-done.8
  148.5 1.0 copy-done.9
  149.6 1.0 copy-done.10
  150.6 0.9 copy-done.11
  151.6 104.0 %trunk_back.1 = (f32[8,128]{1,0:T(8,128)S(1)}, bf16[256,2048]{1,0:T(8,128)(2,1)S(1)}, f32[256,512]{1,0:T(8,128)S(1)}, f32[9,64,512]{2,1,0:T(8,128)S(1)}, f32[64,...) custom-call(bf16[8,256,256]{2,1,0:T(8,128)(2,1)S(1)} %get-tuple-elem, ...), custom_call_target="tpu_custom_call" | custom-call | tf_op jit(solution)/shard_map/trunk_back/pallas_call | solution.py:1176
  255.6 0.6 slice_reduce_fusion
  256.2 5.3 %finish.1 = (bf16[256,256]{1,0:T(8,128)(2,1)}, bf16[256,2048]{1,0:T(8,128)(2,1)}, f32[256,512]{1,0:T(8,128)}, f32[9,64,512]{2,1,0:T(8,128)}, f32[64,2048]{1,0:T(...) custom-call(bf16[17,256,256]{2,1,0:T(8,128)(2,1)S(1)} %get-tuple-ele, ...), custom_call_target="tpu_custom_call" | custom-call | tf_op jit(solution)/shard_map/finish/pallas_call | solution.py:2170
  261.4 0.6 copy_bitcast_fusion
  262.1 0.6 copy.32
  (25 shorter events, 0.0 us)
Async XLA Ops:
  0.6 42.1 %copy-start.4 = (bf16[1,256,6912]{2,1,0:T(8,128)(2,1)S(1)}, bf16[1,256,6912]{2,1,0:T(8,128)(2,1)}, u32[]{:S(2)}) copy-start(bf16[1,256,6912]{2,1,0:T(8,128)(2,1)} %param.21) | copy-start | bytes 10616836
  0.7 42.1 %copy-start.7 = (bf16[1,1280,256]{2,1,0:T(8,128)(2,1)S(1)}, bf16[1,1280,256]{2,1,0:T(8,128)(2,1)}, u32[]{:S(2)}) copy-start(bf16[1,1280,256]{2,1,0:T(8,128)(2,1)} %param.22) | copy-start | bytes 1966084
  0.7 42.1 %copy-start.12 = (bf16[1,256,512]{2,1,0:T(8,128)(2,1)S(1)}, bf16[1,256,512]{2,1,0:T(8,128)(2,1)}, u32[]{:S(2)}) copy-start(bf16[1,256,512]{2,1,0:T(8,128)(2,1)} %param.20) | copy-start | bytes 786436
  0.7 42.1 %copy-start.13 = (bf16[1,2,128,256]{3,2,1,0:T(8,128)(2,1)S(1)}, bf16[1,2,128,256]{3,2,1,0:T(8,128)(2,1)}, u32[]{:S(2)}) copy-start(bf16[1,2,128,256]{3,2,1,0:T(8,128)(2,1)} %param.25) | copy-start | bytes 393220
  0.7 42.1 %copy-start.17 = (f32[1,1280]{1,0:T(1,128)S(1)}, f32[1,1280]{1,0:T(1,128)}, u32[]{:S(2)}) copy-start(f32[1,1280]{1,0:T(1,128)} %gain_ref.1) | copy-start | bytes 15364
  0.7 42.1 %copy-start.18 = (f32[1,1280]{1,0:T(1,128)S(1)}, f32[1,1280]{1,0:T(1,128)}, u32[]{:S(2)}) copy-start(f32[1,1280]{1,0:T(1,128)} %shift_ref.1) | copy-start | bytes 15364
  0.7 42.1 %copy-start.19 = (s32[16]{0:T(128)S(1)}, s32[16]{0:T(128)}, u32[]{:S(2)}) copy-start(s32[16]{0:T(128)} %widths_ref.5) | copy-start | bytes 196
  0.7 146.7 %copy-start.1 = (bf16[2048,512]{1,0:T(8,128)(2,1)S(1)}, bf16[2048,512]{1,0:T(8,128)(2,1)}, u32[]{:S(2)}) copy-start(bf16[2048,512]{1,0:T(8,128)(2,1)} %wr_hbm.3) | copy-start | bytes 6291460
  0.7 146.7 %copy-start.2 = (bf16[512,2048]{1,0:T(8,128)(2,1)S(1)}, bf16[512,2048]{1,0:T(8,128)(2,1)}, u32[]{:S(2)}) copy-start(bf16[512,2048]{1,0:T(8,128)(2,1)} %we_hbm.3) | copy-start | bytes 6291460
  0.7 146.7 %copy-start.3 = (bf16[2,128,2048]{2,1,0:T(8,128)(2,1)S(1)}, bf16[2,128,2048]{2,1,0:T(8,128)(2,1)}, u32[]{:S(2)}) copy-start(bf16[2,128,2048]{2,1,0:T(8,128)(2,1)} %param.13) | copy-start | bytes 3145732
  42.8 1.2 copy-start.5
  44.1 103.4 %copy-start = (bf16[512,9,512]{2,0,1:T(8,128)(2,1)S(1)}, bf16[512,9,512]{2,0,1:T(8,128)(2,1)}, u32[]{:S(2)}) copy-start(bf16[512,9,512]{2,0,1:T(8,128)(2,1)} %param.16) | copy-start | bytes 14155780
  44.1 103.4 %copy-start.6 = (bf16[3,256,512]{2,1,0:T(8,128)(2,1)S(1)}, bf16[3,256,512]{2,1,0:T(8,128)(2,1)}, u32[]{:S(2)}) copy-start(bf16[3,256,512]{2,1,0:T(8,128)(2,1)} %get-tuple-element.61.a1_ref) | copy-start | bytes 2359300
  44.1 103.4 %copy-start.14 = (f32[8,2048]{1,0:T(8,128)S(1)}, f32[8,2048]{1,0:T(8,128)}, u32[]{:S(2)}) copy-start(f32[8,2048]{1,0:T(8,128)} %get-tuple-element.56.v3_ref) | copy-start | bytes 196612
  44.1 103.4 %copy-start.15 = (f32[8,512]{1,0:T(8,128)S(1)}, f32[8,512]{1,0:T(8,128)}, u32[]{:S(2)}) copy-start(f32[8,512]{1,0:T(8,128)} %get-tuple-element.60.v1_ref) | copy-start | bytes 49156
  44.1 103.4 %copy-start.16 = (f32[8,512]{1,0:T(8,128)S(1)}, f32[8,512]{1,0:T(8,128)}, u32[]{:S(2)}) copy-start(f32[8,512]{1,0:T(8,128)} %get-tuple-element.58.v2_ref) | copy-start | bytes 49156
  147.5 1.0 copy-start.8
  148.5 1.0 copy-start.9
  149.6 1.0 copy-start.10
  150.6 0.9 copy-start.11
  256.2 5.9 %copy-start.20 = (f32[2,3072]{1,0:T(2,128)S(1)}, f32[2,3072]{1,0:T(2,128)}, u32[]{:S(2)}) copy-start(f32[2,3072]{1,0:T(2,128)} %get-tuple-element.111) | copy-start | bytes 73732

commit v4 on v3

--- a/solution.py
+++ b/solution.py
@@ -524,16 +524,16 @@
         self.other_tasks = [(1 - high) * 2 + 1 - low, high * 2 + 1 - low, (1 - high) * 2 + low]
         self.other_bands = [lax.rem(self.band + step, bands) for step in range(1, bands)]
 
-    def meet(self, with_tasks, with_bands):
+    def greet(self):
         barrier = pltpu.get_barrier_semaphore()
-        greeted = []
-        if with_tasks:
-            greeted += [{"task": task} for task in self.other_tasks]
-        if with_bands:
-            greeted += [{"space": band} for band in self.other_bands]
+        greeted = [{"task": task} for task in self.other_tasks]
+        greeted += [{"space": band} for band in self.other_bands]
         for device in greeted:
             pl.semaphore_signal(barrier, inc=1, device_id=device, device_id_type=MESH_ID)
-        pl.semaphore_wait(barrier, len(greeted))
+
+    def meet(self):
+        barrier = pltpu.get_barrier_semaphore()
+        pl.semaphore_wait(barrier, len(self.other_tasks) + len(self.other_bands))
 
     def sum_begin(self, post, axis, own_ref, land_ref):
         mine = self.task if axis == "task" else self.band
@@ -557,21 +557,30 @@
 
 def trunk_back_kernel(
     sizes,
-    sg_ref,
-    h3q,
-    x_ref,
-    v3_ref,
-    h2_ref,
-    v2_ref,
-    h1_ref,
-    v1_ref,
-    a1_ref,
-    a2_ref,
+    xg_hbm,
+    h3_hbm,
+    x_hbm,
+    v3_hbm,
+    h2_hbm,
+    v2_hbm,
+    h1_hbm,
+    v1_hbm,
+    act_hbm,
+    a2_hbm,
     widths_ref,
     we_hbm,
     wd_hbm,
     wr_hbm,
-    pt_ref,
+    ps_hbm,
+    tw_hbm,
+    ig_hbm,
+    rg_hbm,
+    dg_hbm,
+    eg_hbm,
+    s3_hbm,
+    s2_hbm,
+    s1_hbm,
+    pg_hbm,
     tw_out,
     ig_out,
     rg_out,
@@ -584,9 +593,19 @@
     we,
     wd,
     wr,
+    xg,
+    x_ref,
+    v3_ref,
+    v2_ref,
+    v1_ref,
+    act_ref,
+    ps_ref,
+    h3q,
+    h2_ref,
+    h1_ref,
+    a2_ref,
     mask_ref,
     xq,
-    xg,
     gram_own,
     gram_land,
     gram_mid,
@@ -614,16 +633,14 @@
     st1_land,
     l1,
     xt,
-    a1t,
     a2t,
     e_term,
     e_twin,
     e_land,
     e_share,
     e_tasks,
-    d_term,
-    d_twin,
-    d_land,
+    l2c,
+    d_sum,
     d_share,
     d_tasks,
     r_term,
@@ -631,12 +648,11 @@
     r_land,
     r_share,
     r_tasks,
-    p_twin,
-    p_land,
     p_all,
     send_sem,
     recv_sem,
     local_sem,
+    out_sem,
 ):
     tasks, bands, cols, quarter, mid, wide, piece = sizes
     low = jnp.bfloat16
@@ -645,55 +661,46 @@
     post = Post(send_sem, recv_sem)
     task, band = at.task, at.band
     my_rows = pl.ds(pl.multiple_of(task * quarter, quarter), quarter)
-    loads = [
-        pltpu.make_async_copy(x_ref.at[my_rows], xq, local_sem.at[0]),
-        pltpu.make_async_copy(we_hbm, we, local_sem.at[1]),
-        pltpu.make_async_copy(wd_hbm, wd, local_sem.at[2]),
-        pltpu.make_async_copy(wr_hbm, wr, local_sem.at[3]),
-    ]
-    for load in loads:
+    arrays = {
+        "xg": (xg_hbm, xg),
+        "a2": (a2_hbm, a2_ref),
+        "x": (x_hbm, x_ref),
+        "xq": (x_hbm.at[my_rows], xq),
+        "h3": (h3_hbm, h3q),
+        "v3": (v3_hbm, v3_ref),
+        "ps": (ps_hbm, ps_ref),
+        "we": (we_hbm, we),
+        "h2": (h2_hbm, h2_ref),
+        "v2": (v2_hbm, v2_ref),
+        "wd": (wd_hbm, wd),
+        "h1": (h1_hbm, h1_ref),
+        "v1": (v1_hbm, v1_ref),
+        "act": (act_hbm, act_ref),
+        "wr": (wr_hbm, wr),
+    }
+    loads = {
+        name: pltpu.make_async_copy(source, target, local_sem.at[number])
+        for number, (name, (source, target)) in enumerate(arrays.items())
+    }
+
+    writes = []
+
+    def write(source, target):
+        copy = pltpu.make_async_copy(source, target, out_sem.at[len(writes)])
+        copy.start()
+        writes.append(copy)
+
+    def loaded(*names):
+        for name in names:
+            loads[name].wait()
+
+    for load in loads.values():
         load.start()
-    at.meet(True, True)
-
-    grads_in = []
-    for other in at.other_tasks:
-        theirs = pl.ds(pl.multiple_of(other * quarter, quarter), quarter)
-        grads_in.append(post.push(sg_ref.at[:, theirs], xg.at[task], {"task": other}))
-    own_copy = pltpu.make_async_copy(sg_ref.at[:, my_rows], xg.at[task], local_sem.at[4])
-    own_copy.start()
-
-    p_pair = [
-        post.push(pt_ref.at[2 * number + 1 - at.core], p_twin.at[number], at.twin)
-        for number in range(at.chips)
-    ]
-
+    at.greet()
     band_rows = x_ref.shape[0] // cols
     mask_ref[...] = row_mask(widths_ref, band * band_rows, band_rows, cols)
 
-    for number in range(3):
-        a1t[number] = a1_ref[number].T
-    a2t[...] = a2_ref[...].T
-
-    def turn_inputs(number, carry):
-        lanes = pl.ds(pl.multiple_of(number * piece, piece), piece)
-        xt[lanes, :] = x_ref[:, lanes].T
-        return carry
-
-    lax.fori_loop(0, wide // piece, turn_inputs, 0)
-    for made in p_pair:
-        made.wait_recv()
-    p_in = []
-    for step in range(1, at.chips):
-        other = lax.rem(at.chip + step, at.chips)
-        both = pt_ref[2 * other + at.core].astype(f32) + p_twin[other].astype(f32)
-        p_twin[other] = both.astype(low)
-        p_in.append(
-            post.push(p_twin.at[other], p_land.at[at.chip], {"space": other * 2 + at.core})
-        )
-    own_copy.wait()
-    for made in grads_in:
-        made.wait_recv()
-
+    loaded("xg")
     pairs = [(a, b) for a in range(tasks) for b in range(a, tasks)]
 
     def gram_step(number, totals):
@@ -713,24 +720,21 @@
     gram_own[...] = jnp.zeros_like(gram_own)
     for number, total in enumerate(totals):
         gram_own[number : number + 1] = jnp.sum(total, axis=0, keepdims=True)
-    p_total = pt_ref[band].astype(f32) + p_twin[at.chip].astype(f32)
-    for made in p_in:
-        made.wait_recv()
-    for step in range(1, at.chips):
-        p_total = p_total + p_land[lax.rem(at.chip + step, at.chips)].astype(f32)
-    p_all[pl.ds(band, 1)] = p_total.astype(low)[None]
-    p_block = p_all.at[band]
-    p_near = post.push(p_block, p_block, at.twin)
-    p_far = [
-        post.push(
-            p_block,
-            p_block,
-            {"space": lax.rem(at.chip + step, at.chips) * 2 + at.core},
-        )
-        for step in range(1, at.chips)
-    ]
-    gram_mid[...] = at.sum_over(post, "task", gram_own, gram_land)
-    gram_sum = at.sum_over(post, "space", gram_mid, gram_land_b)
+    at.meet()
+    begun = at.sum_begin(post, "task", gram_own, gram_land)
+    loaded("a2")
+    a2t[...] = a2_ref[...].T
+    gram_mid[...] = at.sum_end(begun)
+    begun = at.sum_begin(post, "space", gram_mid, gram_land_b)
+
+    loaded("x")
+    def turn_inputs(number, carry):
+        lanes = pl.ds(pl.multiple_of(number * piece, piece), piece)
+        xt[lanes, :] = x_ref[:, lanes].T
+        return carry
+
+    lax.fori_loop(0, wide // piece, turn_inputs, 0)
+    gram_sum = at.sum_end(begun)
     gram_sum = jnp.broadcast_to(jnp.sum(gram_sum, axis=1, keepdims=True), gram_sum.shape)
     gram = [[None] * tasks for _ in range(tasks)]
     for number, (a, b) in enumerate(pairs):
@@ -775,7 +779,7 @@
         comb[other] = mixed(other)
         comb_in.append(post.push(comb.at[other], comb_land.at[band], {"space": other}))
     comb_land[pl.ds(band, 1)] = mixed(band)[None]
-    loads[0].wait()
+    loaded("xq", "h3", "v3")
     for made in comb_in:
         made.wait_recv()
 
@@ -825,7 +829,18 @@
             post.push(l3.at[pl.ds(other * per_task, per_task)], l3x.at[task], {"task": other})
         )
     l3x[pl.ds(task, 1)] = l3[pl.ds(task * per_task, per_task)][None]
-    loads[1].wait()
+    loaded("ps", "we")
+    p_all[pl.ds(band, 1)] = ps_ref[...][None]
+    p_block = p_all.at[band]
+    p_near = post.push(p_block, p_block, at.twin)
+    p_far = [
+        post.push(
+            p_block,
+            p_block,
+            {"space": lax.rem(at.chip + step, at.chips) * 2 + at.core},
+        )
+        for step in range(1, at.chips)
+    ]
 
     def expand_step(number, total):
         lanes = pl.ds(pl.multiple_of(number * piece, piece), piece)
@@ -835,6 +850,7 @@
 
     mask_mid = jnp.concatenate([mask_quarter] * (mid // LANE), axis=1)
     inv_mid = jnp.concatenate([inv_count] * (mid // LANE), axis=1)
+    loaded("h2", "v2")
     hat = (h2_ref[my_rows] - v2_ref[0:1]) * v2_ref[1:2]
     grad = gelu_slope(v2_ref[2:3] * hat + v2_ref[3:4]) * ag2 * mask_mid
     spread = mid // LANE
@@ -946,7 +962,7 @@
         made.wait_recv()
         block = p_all.at[lax.rem(at.chip + at.chips - step, at.chips) * 2 + at.core]
         p_passed.append(post.push(block, block, at.twin))
-    loads[2].wait()
+    loaded("wd")
     halves = [slice(start, start + piece) for start in range(0, mid, piece)]
     for lanes in halves:
         total = None
@@ -957,18 +973,6 @@
             total = part if total is None else total + part
         ag1[:, lanes] = total
 
-    share_d = l2[:, my_lanes].astype(f32)
-    for col_tap in range(3):
-        moved = shift_pixels(share_d, -CONV_DILATION * (col_tap - 1), cols).astype(low)
-        for row_tap in range(3):
-            part = dot_nn(a1t[row_tap], moved).astype(low)
-            per_band = part.shape[0] // bands
-            for target in range(bands):
-                d_term[target % 2, target // 2, 3 * row_tap + col_tap] = part[
-                    target * per_band : (target + 1) * per_band
-                ]
-    d_pair = to_twin(d_term, d_twin)
-
     @pl.when(has_below)
     def _():
         up.wait_recv()
@@ -987,6 +991,7 @@
             total = part if total is None else total + part
         ag1[:, lanes] += total
 
+    loaded("h1", "v1")
     pixels = ag1.shape[0]
     chunk = pixels // 8
 
@@ -1008,10 +1013,19 @@
     first, second = lax.fori_loop(0, 8, first_step, (nothing, nothing))
     put_sums(st1, first, second)
     begun = at.sum_begin(post, "space", st1, st1_land)
-    both_cores(d_pair, d_term, d_twin)
+    l2c[pl.ds(band, 1)] = l2[:, my_lanes][None]
+    l2_block = l2c.at[band]
+    d_far = [
+        post.push(
+            l2_block,
+            l2_block,
+            {"space": lax.rem(at.chip + step, at.chips) * 2 + at.core},
+        )
+        for step in range(1, at.chips)
+    ]
+    d_near = [post.push(l2_block, l2_block, at.twin)]
     e_share[...] = settle(e_in, e_term, e_twin, e_land)
     s1_out[...] = at.sum_end(begun)
-    d_in = along(d_twin, d_land)
     shift_grad, gain_grad = get_sums(s1_out[...])
     shift_grad, gain_grad = shift_grad * inv_mid, gain_grad * inv_mid
 
@@ -1040,7 +1054,12 @@
     both_cores(r_pair, r_term, r_twin)
     r_in = along(r_twin, r_land)
 
-    loads[3].wait()
+    for step, made in enumerate(d_far, start=1):
+        made.wait_recv()
+        block = l2c.at[lax.rem(at.chip + at.chips - step, at.chips) * 2 + at.core]
+        d_near.append(post.push(block, block, at.twin))
+
+    loaded("wr", "act")
     for made in gate_in:
         made.wait_recv()
 
@@ -1051,26 +1070,51 @@
         return carry
 
     lax.fori_loop(0, bands, input_step, 0)
-    d_share[...] = settle(d_in, d_term, d_twin, d_land)
+    write(ig_out, ig_hbm)
+    for source, target in ((tw_out, tw_hbm), (s3_out, s3_hbm), (s2_out, s2_hbm), (s1_out, s1_hbm)):
+        write(source, target)
+    for made in d_near:
+        made.wait_recv()
+    d_sum[...] = jnp.zeros_like(d_sum)
+
+    def dilated_step(number, carry):
+        left = jnp.concatenate([act_ref[number + row_tap] for row_tap in range(3)], axis=0)
+        right = l2c[number].astype(f32)
+        for col_tap in range(3):
+            moved = shift_pixels(right, -CONV_DILATION * (col_tap - 1), cols).astype(low)
+            d_sum[col_tap] += dot_nn(left, moved)
+        return carry
+
+    lax.fori_loop(0, bands, dilated_step, 0)
+    part = d_share.shape[1]
+    for row_tap in range(3):
+        for col_tap in range(3):
+            d_share[3 * row_tap + col_tap] = d_sum[
+                col_tap, row_tap * part : (row_tap + 1) * part
+            ].astype(low)
     d_back = to_tasks(d_share, d_tasks)
     r_share[...] = settle(r_in, r_term, r_twin, r_land)
     r_back = to_tasks(r_share, r_tasks)
     for made in [p_near] + p_passed:
         made.wait_recv()
     pg_out[...] = p_all[...]
+    write(pg_out, pg_hbm)
     for made in e_back:
         made.wait_recv()
     broad = wide // tasks
     for a in range(tasks):
         eg_out[:, a * broad : (a + 1) * broad] = e_tasks[a].astype(f32)
+    write(eg_out, eg_hbm)
     for made in d_back:
         made.wait_recv()
     for a in range(tasks):
         dg_out[:, :, a * narrow : (a + 1) * narrow] = d_tasks[a].astype(f32)
+    write(dg_out, dg_hbm)
     for made in r_back:
         made.wait_recv()
     for a in range(tasks):
         rg_out[:, a * narrow : (a + 1) * narrow] = r_tasks[a].astype(f32)
+    write(rg_out, rg_hbm)
     post.close()
 
     @pl.when(has_above)
@@ -1080,10 +1124,12 @@
     @pl.when(has_below)
     def _():
         down.wait_send()
+    for copy in writes:
+        copy.wait()
 
 
 def trunk_back(
-    tasks, bands, cols, collective, sg, h3, x, v3, h2, v2, h1, v1, a1, a2, widths, we, wd, wr, pt
+    tasks, bands, cols, collective, xg, h3, x, v3, h2, v2, h1, v1, act, a2, widths, we, wd, wr, ps
 ):
     low, f32 = jnp.bfloat16, jnp.float32
     pixels, wide = x.shape
@@ -1093,7 +1139,6 @@
     narrow, broad = mid // tasks, wide // tasks
     chips = bands // 2
     part = mid // bands
-    in_vmem = pl.BlockSpec(memory_space=pltpu.VMEM)
     anywhere = pl.BlockSpec(memory_space=pl.ANY)
     shape = jax.ShapeDtypeStruct
 
@@ -1120,9 +1165,19 @@
             pltpu.VMEM(we.shape, low),
             pltpu.VMEM(wd.shape, low),
             pltpu.VMEM(wr.shape, low),
+            pltpu.VMEM(xg.shape, low),
+            pltpu.VMEM(x.shape, low),
+            pltpu.VMEM(v3.shape, f32),
+            pltpu.VMEM(v2.shape, f32),
+            pltpu.VMEM(v1.shape, f32),
+            pltpu.VMEM(act.shape, low),
+            pltpu.VMEM(ps.shape, low),
+            pltpu.VMEM(h3.shape, f32),
+            pltpu.VMEM(h2.shape, f32),
+            pltpu.VMEM(h1.shape, f32),
+            pltpu.VMEM(a2.shape, low),
             pltpu.VMEM((pixels, LANE), f32),
             pltpu.VMEM((quarter, wide), low),
-            pltpu.VMEM((tasks, bands, quarter, piece), low),
         ]
         + stats(16, LANE)
         + [
@@ -1147,19 +1202,22 @@
             pltpu.VMEM((bands, 2 * mid // LANE, LANE), f32),
             pltpu.VMEM((pixels, mid), low),
             pltpu.VMEM((wide, pixels), low),
-            pltpu.VMEM((3, mid, pixels), low),
             pltpu.VMEM((mid, pixels), low),
         ]
         + terms(part, broad)
-        + terms(9, part, narrow)
+        + [
+            pltpu.VMEM((bands, pixels, narrow), low),
+            pltpu.VMEM((3, 3 * part, narrow), f32),
+            pltpu.VMEM((9, part, narrow), low),
+            pltpu.VMEM((tasks, 9, part, narrow), low),
+        ]
         + terms(piece, narrow)
         + [
-            pltpu.VMEM((chips,) + pt.shape[1:], low),
-            pltpu.VMEM((chips,) + pt.shape[1:], low),
-            pltpu.VMEM(pt.shape, low),
+            pltpu.VMEM((bands,) + ps.shape, low),
             pltpu.SemaphoreType.DMA((96,)),
             pltpu.SemaphoreType.DMA((96,)),
-            pltpu.SemaphoreType.DMA((6,)),
+            pltpu.SemaphoreType.DMA((15,)),
+            pltpu.SemaphoreType.DMA((9,)),
         ]
     )
     out_shapes = (
@@ -1171,26 +1229,28 @@
         shape((8, stat_wide), f32),
         shape((2 * mid // LANE, LANE), f32),
         shape((2 * mid // LANE, LANE), f32),
-        shape(pt.shape, low),
+        shape((bands,) + ps.shape, low),
     )
     return pl.pallas_call(
         functools.partial(trunk_back_kernel, (tasks, bands, cols, quarter, mid, wide, piece)),
         name="trunk_back",
         out_shape=out_shapes,
-        in_specs=[in_vmem] * 10
+        in_specs=[anywhere] * 10
         + [pl.BlockSpec(memory_space=pltpu.SMEM)]
-        + [anywhere] * 3
-        + [in_vmem],
-        out_specs=(in_vmem,) * 9,
-        scratch_shapes=scratch,
+        + [anywhere] * 4,
+        out_specs=(anywhere,) * len(out_shapes),
+        scratch_shapes=[pltpu.VMEM(out.shape, out.dtype) for out in out_shapes] + scratch,
         compiler_params=pltpu.CompilerParams(
-            collective_id=collective, has_side_effects=True, vmem_limit_bytes=27 << 20
+            collective_id=collective, has_side_effects=True, vmem_limit_bytes=60 << 20
         ),
-    )(sg, h3, x, v3, h2, v2, h1, v1, a1, a2, widths, we, wd, wr, pt)
-
-
-def head_kernel(
+    )(xg, h3, x, v3, h2, v2, h1, v1, act, a2, widths, we, wd, wr, ps)
+
+
+def head_phase(
+    at,
+    post,
     plan,
+    rate_loads,
     sh_ref,
     widths_ref,
     gain_ref,
@@ -1198,11 +1258,10 @@
     cot_ref,
     bw_ref,
     pw_ref,
-    rate_hbm,
     head_out,
-    sg_out,
+    xg_out,
     grads_out,
-    proj_out,
+    proj_share,
     both_sums_out,
     proj_sums_out,
     rate,
@@ -1229,28 +1288,19 @@
     moved,
     grads,
     back,
-    send_sem,
-    recv_sem,
-    rate_sem,
+    sg,
+    proj_term,
+    p_twin,
+    p_land,
 ):
     tasks, bands, cols, pixels, width, taps, extras = plan
     low, f32 = jnp.bfloat16, jnp.float32
-    at = Place(tasks, bands)
-    post = Post(send_sem, recv_sem)
+    send_sem, recv_sem = post.send_sem, post.recv_sem
     chips, chip, core, band = at.chips, at.chip, at.core, at.band
     last = chips - 1
     group = 2 * pixels
     number_of = {tap[:3]: number for number, tap in enumerate(taps)}
-    loads = []
-    for number, (level, row_tap, col_tap, _, _) in enumerate(taps):
-        start = (9 * (level - 1) + 3 * row_tap + col_tap) * width
-        load = pltpu.make_async_copy(
-            rate_hbm.at[:, start : start + width], rate.at[number], rate_sem.at[number]
-        )
-        load.start()
-        loads.append(load)
-    at.meet(False, True)
-    for load in loads:
+    for load in rate_loads:
         load.wait()
 
     def rows_of(ref, number):
@@ -1275,20 +1325,25 @@
     for level, target, source, row_tap in extras:
         extra[level - 1, target] += forward_taps(rows_of(sh_ref, source), level, row_tap)
 
+    first_twin = post.used
+    post.used += chips
+
     def twin_term(number):
         return pltpu.make_async_remote_copy(
             term.at[number, 1 - core],
             twin_land.at[number],
-            send_sem.at[number],
-            recv_sem.at[number],
+            send_sem.at[first_twin + number],
+            recv_sem.at[first_twin + number],
             device_id=at.twin,
             device_id_type=MESH_ID,
         )
 
-    post.used = chips
+
+    side = chip // (chips // 2)
 
     def forward_group(step, carry):
-        number = lax.rem(step, 2) * (last - step // 2) + (1 - lax.rem(step, 2)) * (step // 2)
+        near = lax.rem(step, 2) * (step // 2) + (1 - lax.rem(step, 2)) * (last - step // 2)
+        number = near * (1 - side) + (last - near) * side
         source = rows_of(sh_ref, number)
 
         def put(branch, value):
@@ -1305,7 +1360,7 @@
         twin_term(number).start()
         return carry
 
-    lax.fori_loop(0, 2, forward_group, 0)
+    lax.fori_loop(0, 1, forward_group, 0)
 
     def hop(source, landing, device_chip, number):
         return pltpu.make_async_remote_copy(
@@ -1370,7 +1425,7 @@
     def _():
         start_off(0, go_left(0))
 
-    lax.fori_loop(2, chips, forward_group, 0)
+    lax.fori_loop(1, chips, forward_group, 0)
 
     def pass_right(number):
         there = (chip < number) if number < last else ((chip < number) & (chip > 0))
@@ -1532,7 +1587,7 @@
         column * (pool_grad.astype(f32) * inv_count)
     ).astype(low)
 
-    def both_step(branch, carry):
+    def make_both(branch):
         _, inv_std = scale_of(st_both_sum, branch, 4 + branch)
         shift_grad = get_rows(both_sums_out, branch) * inv_count
         gain_grad = get_rows(both_sums_out, 4 + branch) * inv_count
@@ -1541,88 +1596,169 @@
             * (gain_ref[:, lanes_of(branch)] * inv_std)
             * (upstream[branch] - shift_grad - pre[branch] * gain_grad)
         ).astype(low)
-        return carry
-
-    lax.fori_loop(0, 4, both_step, 0)
-
+
+    moved_levels = sorted({entry[0] for entry in extras})
+    slots = moved_levels + [branch for branch in range(4) if branch not in moved_levels]
     all_right = post.used
-    all_left = all_right + chips
-    all_twin = all_left + chips
-
-    def send_right(step):
-        block = both_all.at[lax.rem(chip - step + 1 + chips, chips) * 2 + core]
-        return hop(block, block, next_chip, all_right + step)
-
-    def send_left(step):
-        block = both_all.at[lax.rem(chip + step - 1, chips) * 2 + core]
-        return hop(block, block, prev_chip, all_left + step)
-
-    def hand_over(number):
-        block = both_all.at[number * 2 + core]
+    all_left = all_right + 4 * chips
+    all_twin = all_left + 4 * chips
+
+    def block_of(number, slot):
+        return both_all.at[number * 2 + core, slots[slot]]
+
+    def send_right(step, slot):
+        block = block_of(lax.rem(chip - step + 1 + chips, chips), slot)
+        return hop(block, block, next_chip, all_right + 4 * step + slot)
+
+    def send_left(step, slot):
+        block = block_of(lax.rem(chip + step - 1, chips), slot)
+        return hop(block, block, prev_chip, all_left + 4 * step + slot)
+
+    def hand_over(number, slot):
+        block = block_of(number, slot)
         return pltpu.make_async_remote_copy(
             block,
             block,
-            send_sem.at[all_twin + number],
-            recv_sem.at[all_twin + number],
+            send_sem.at[all_twin + 4 * number + slot],
+            recv_sem.at[all_twin + 4 * number + slot],
             device_id=at.twin,
             device_id_type=MESH_ID,
         )
 
-    def from_left(step):
-        block = both_all.at[lax.rem(chip - step + chips, chips) * 2 + core]
-        return hop(block, block, next_chip, all_right + step)
-
-    def from_right(step):
-        block = both_all.at[lax.rem(chip + step, chips) * 2 + core]
-        return hop(block, block, prev_chip, all_left + step)
-
-    @pl.when(chip < last)
-    def _():
-        send_right(1).start()
-
-    @pl.when(chip > 0)
-    def _():
-        send_left(1).start()
-
-    hand_over(chip).start()
+    def from_left(step, slot):
+        block = block_of(lax.rem(chip - step + chips, chips), slot)
+        return hop(block, block, next_chip, all_right + 4 * step + slot)
+
+    def from_right(step, slot):
+        block = block_of(lax.rem(chip + step, chips), slot)
+        return hop(block, block, prev_chip, all_left + 4 * step + slot)
+
+    for slot in range(4):
+        make_both(slots[slot])
+
+        @pl.when(chip < last)
+        def _():
+            send_right(1, slot).start()
+
+        @pl.when(chip > 0)
+        def _():
+            send_left(1, slot).start()
+
+        hand_over(chip, slot).start()
 
     def proj_step(branch, carry):
-        proj_out[lanes_of(branch), :] = dot_nn(joined[branch].T, proj_low).astype(low)
+        proj_term[lanes_of(branch), :] = dot_nn(joined[branch].T, proj_low).astype(low)
         return carry
 
     lax.fori_loop(0, 5, proj_step, 0)
+    rows_p = proj_share.shape[0]
+
+    def proj_rows(number):
+        return pl.ds(pl.multiple_of(number * rows_p, rows_p), rows_p)
+
+    post.used = all_twin + 4 * chips
+    p_pair = [
+        post.push(proj_term.at[proj_rows(2 * number + 1 - core)], p_twin.at[number], at.twin)
+        for number in range(chips)
+    ]
     grads[...] = jnp.zeros_like(grads)
     pool_row = dot_nt(
         jnp.broadcast_to(pool_grad, (16, width)), bw_ref[:, width:]
     )[0:1] * inv_count
-    moved_levels = sorted({entry[0] for entry in extras})
-
-    def back_group(step, carry):
-        number = group_at(step)
-        hand_over(number).wait_recv()
-        columns = turned[:, pl.ds(pl.multiple_of(number * group, group), group)]
-
-        def both_of(branch):
-            return jnp.concatenate(
+    quarter = pixels // tasks
+    my_rows = pl.ds(pl.multiple_of(at.task * quarter, quarter), quarter)
+    late = sorted({entry[2] for entry in extras})
+    first_task = post.used
+    post.used += chips * len(at.other_tasks)
+
+    def to_task(number, turn):
+        other = at.other_tasks[turn]
+        theirs = pl.ds(pl.multiple_of(other * quarter, quarter), quarter)
+        two = pl.ds(2 * number, 2)
+        spot = first_task + number * len(at.other_tasks) + turn
+        return pltpu.make_async_remote_copy(
+            sg.at[two, theirs],
+            xg_out.at[at.task, two],
+            send_sem.at[spot],
+            recv_sem.at[spot],
+            device_id={"task": other},
+            device_id_type=MESH_ID,
+        )
+
+    def finish_group(number, total):
+        keep = row_mask(widths_ref, number * 2 * band_rows, 2 * band_rows, cols)
+        keep = jnp.concatenate([keep] * spread, axis=1)
+        value = (total + keep * pool_row).astype(low)
+        sg[2 * number] = value[:pixels]
+        sg[2 * number + 1] = value[pixels:]
+        for turn in range(len(at.other_tasks)):
+            to_task(number, turn).start()
+        for half in range(2):
+            xg_out[at.task, 2 * number + half] = sg[2 * number + half, my_rows]
+
+    def back_slot(slot):
+        branch = slots[slot]
+
+        def step_of(step, carry):
+            number = group_at(step)
+            hand_over(number, slot).wait_recv()
+            columns = turned[:, pl.ds(pl.multiple_of(number * group, group), group)]
+            part = jnp.concatenate(
                 [both_all[2 * number, branch], both_all[2 * number + 1, branch]], axis=0
             )
-
-        part = both_of(0)
-        total = dot_nt(part, bw_ref[:, :width])
-        grads[len(taps)] += dot_nn(columns, part)
-        for level in (1, 2, 3):
-            image = both_of(level).astype(f32)
+            if branch == 0:
+                total = dot_nt(part, bw_ref[:, :width])
+                grads[len(taps)] += dot_nn(columns, part)
+            else:
+                total = None
+                image = part.astype(f32)
+                for col_tap in range(3):
+                    tap = number_of.get((branch, 1, col_tap))
+                    if tap is None:
+                        continue
+                    part = shift_pixels(image, -right_of(branch, col_tap), cols).astype(low)
+                    if branch in moved_levels:
+                        moved[moved_levels.index(branch), number, col_tap] = part
+                    term_now = dot_nt(part, rate[tap])
+                    total = term_now if total is None else total + term_now
+                    grads[tap] += dot_nn(columns, part)
+            if slot == 0:
+                back[number] = total
+            else:
+                back[number] += total
+            if slot == 3:
+                ready = number >= 0
+                for entry in late:
+                    ready = ready & (number != entry)
+
+                @pl.when(ready)
+                def _():
+                    finish_group(number, back[number])
+
+            return carry
+
+        return step_of
+
+    def far_taps():
+        for level, target, source, row_tap in extras:
+            columns = turned[:, source * group : (source + 1) * group]
+            total = back[source]
             for col_tap in range(3):
-                tap = number_of.get((level, 1, col_tap))
+                tap = number_of.get((level, row_tap, col_tap))
                 if tap is None:
                     continue
-                part = shift_pixels(image, -right_of(level, col_tap), cols).astype(low)
-                if level in moved_levels:
-                    moved[moved_levels.index(level), number, col_tap] = part
+                part = moved[moved_levels.index(level), target, col_tap]
                 total = total + dot_nt(part, rate[tap])
                 grads[tap] += dot_nn(columns, part)
-        back[number] = total
-        return carry
+            back[source] = total
+
+    def finish_late(early):
+        for number in late:
+            near_enough = (chip - number < last) & (number - chip < last)
+
+            @pl.when(near_enough if early else jnp.logical_not(near_enough))
+            def _():
+                finish_group(number, back[number])
 
     mirror = chip // 2
     near = chip * (1 - mirror) + (last - chip) * mirror
@@ -1631,56 +1767,53 @@
         place = step + near * (1 - 2 * step) * ((last - step) // 2)
         return place * (1 - mirror) + (last - place) * mirror
 
-    lax.fori_loop(0, 1, back_group, 0)
+    for slot in range(4):
+        lax.fori_loop(0, 1, back_slot(slot), 0)
     done = 1
     for step in range(1, chips):
-        @pl.when(chip >= step)
-        def _():
-            from_left(step).wait_recv()
-            if step < last:
-
-                @pl.when(chip < last)
-                def _():
-                    send_right(step + 1).start()
-
-            hand_over(lax.rem(chip - step + chips, chips)).start()
-
-        @pl.when(chip + step <= last)
-        def _():
-            from_right(step).wait_recv()
-            if step < last:
-
-                @pl.when(chip > 0)
-                def _():
-                    send_left(step + 1).start()
-
-            hand_over(lax.rem(chip + step, chips)).start()
-
         upto = chips if step == last else step + 1 + near
-        lax.fori_loop(done, upto, back_group, 0)
+        for slot in range(4):
+
+            @pl.when(chip >= step)
+            def _():
+                from_left(step, slot).wait_recv()
+                if step < last:
+
+                    @pl.when(chip < last)
+                    def _():
+                        send_right(step + 1, slot).start()
+
+                hand_over(lax.rem(chip - step + chips, chips), slot).start()
+
+            @pl.when(chip + step <= last)
+            def _():
+                from_right(step, slot).wait_recv()
+                if step < last:
+
+                    @pl.when(chip > 0)
+                    def _():
+                        send_left(step + 1, slot).start()
+
+                hand_over(lax.rem(chip + step, chips), slot).start()
+
+            lax.fori_loop(done, upto, back_slot(slot), 0)
+            if step == last and slot == len(moved_levels) - 1:
+                far_taps()
+                finish_late(True)
         done = upto
 
-    for level, target, source, row_tap in extras:
-        columns = turned[:, source * group : (source + 1) * group]
-        total = back[source]
-        for col_tap in range(3):
-            tap = number_of.get((level, row_tap, col_tap))
-            if tap is None:
-                continue
-            part = moved[moved_levels.index(level), target, col_tap]
-            total = total + dot_nt(part, rate[tap])
-            grads[tap] += dot_nn(columns, part)
-        back[source] = total
-
-    def finish_group(number, carry):
-        keep = row_mask(widths_ref, number * 2 * band_rows, 2 * band_rows, cols)
-        keep = jnp.concatenate([keep] * spread, axis=1)
-        value = (back[number] + keep * pool_row).astype(low)
-        sg_out[2 * number] = value[:pixels]
-        sg_out[2 * number + 1] = value[pixels:]
-        return carry
-
-    lax.fori_loop(0, chips, finish_group, 0)
+    for made in p_pair:
+        made.wait_recv()
+    p_in = []
+    for step in range(1, chips):
+        other = lax.rem(chip + step, chips)
+        both = proj_term[proj_rows(2 * other + core)].astype(f32) + p_twin[other].astype(f32)
+        p_twin[other] = both.astype(low)
+        p_in.append(
+            post.push(p_twin.at[other], p_land.at[chip], {"space": other * 2 + core})
+        )
+
+    finish_late(False)
 
     def finish_tap(number, carry):
         grads_out[number] = grads[number].astype(low)
@@ -1688,11 +1821,26 @@
 
     lax.fori_loop(0, len(taps) + 1, finish_tap, 0)
 
+    p_total = proj_term[proj_rows(band)].astype(f32) + p_twin[chip].astype(f32)
+    for made in p_in:
+        made.wait_recv()
+    for step in range(1, chips):
+        p_total = p_total + p_land[lax.rem(chip + step, chips)].astype(f32)
+    proj_share[...] = p_total.astype(low)
+
+    def tasks_in(number, carry):
+        for turn in range(len(at.other_tasks)):
+            to_task(number, turn).wait()
+        return carry
+
+    lax.fori_loop(0, chips, tasks_in, 0)
+
     post.close()
 
     def twin_left(number, carry):
         twin_term(number).wait_send()
-        hand_over(number).wait_send()
+        for slot in range(4):
+            hand_over(number, slot).wait_send()
         return carry
 
     lax.fori_loop(0, chips, twin_left, 0)
@@ -1711,16 +1859,338 @@
 
         @pl.when((chip < last) & (chip - step + 1 >= 0))
         def _():
-            send_right(step).wait_send()
+            for slot in range(4):
+                send_right(step, slot).wait_send()
 
         @pl.when((chip > 0) & (chip + step - 1 <= last))
         def _():
-            send_left(step).wait_send()
-
-
-def head(tasks, bands, cols, rows, collective, sh, widths, gain, shift, cot, bw, pw, rate):
+            for slot in range(4):
+                send_left(step, slot).wait_send()
+
+
+def trunk_phase(
+    at,
+    post,
+    sizes,
+    when_loaded,
+    x_hbm,
+    widths_ref,
+    gain_ref,
+    shift_ref,
+    wr_hbm,
+    wd_hbm,
+    we_hbm,
+    sh_out,
+    act,
+    h1,
+    h2,
+    a2,
+    h3q,
+    v1,
+    v2,
+    v3,
+    stats_out,
+    x,
+    wr,
+    wd,
+    we,
+    rim,
+    turned,
+    h3,
+    blocks,
+    mask_own,
+    st1,
+    st1_land,
+    st2,
+    st2_land,
+    st3,
+    st3_land,
+    local_sem,
+):
+    tasks, bands, cols, quarter, mid, wide, piece = sizes
     low, f32 = jnp.bfloat16, jnp.float32
-    pixels, width = sh.shape[1], pw.shape[1]
+    task, band = at.task, at.band
+    my_rows = pl.ds(pl.multiple_of(task * quarter, quarter), quarter)
+    loads = [
+        pltpu.make_async_copy(source, target, local_sem.at[number])
+        for number, (source, target) in enumerate(
+            ((x_hbm, x), (wr_hbm, wr), (wd_hbm, wd), (we_hbm, we))
+        )
+    ]
+    for load in loads[:2]:
+        load.start()
+    at.greet()
+    pixels = x.shape[0]
+    band_rows = pixels // cols
+    mask = row_mask(widths_ref, band * band_rows, band_rows, cols)
+    count = count_pixels(widths_ref)
+    spread = mid // LANE
+
+    def across(value, lanes):
+        return jnp.concatenate([value] * (lanes // LANE), axis=1)
+
+    def put_sums(target, value, keep):
+        kept = value * keep
+        first = jnp.sum(kept, axis=0, keepdims=True)
+        second = jnp.sum(kept * value, axis=0, keepdims=True)
+        for number in range(spread):
+            lanes = slice(number * LANE, (number + 1) * LANE)
+            target[number : number + 1] = first[:, lanes]
+            target[spread + number : spread + number + 1] = second[:, lanes]
+
+    def get_sums(total):
+        return [
+            jnp.concatenate([total[base + k : base + k + 1] for k in range(spread)], axis=1)
+            for base in (0, spread)
+        ]
+
+    def put_norm(vectors, lanes, first, second, start):
+        width = first.shape[1]
+        inv = across(1.0 / count, width)
+        mean_value = first * inv
+        variance = second * inv - mean_value * mean_value
+        vectors[0:1, lanes] = mean_value
+        vectors[1:2, lanes] = lax.rsqrt(variance + NORM_EPS)
+        vectors[2:3, lanes] = gain_ref[:, start : start + width]
+        vectors[3:4, lanes] = shift_ref[:, start : start + width]
+        stats_out[0:1, start : start + width] = mean_value
+        stats_out[1:2, start : start + width] = variance * across(count / (count - 1.0), width)
+
+    def activate(hidden, vectors, keep):
+        normed = vectors[2:3] * ((hidden - vectors[0:1]) * vectors[1:2]) + vectors[3:4]
+        return (gelu_of(normed) * keep).astype(low)
+
+    mask_mid = across(mask, mid)
+    for load in loads[:2]:
+        load.wait()
+    for load in loads[2:]:
+        load.start()
+    when_loaded()
+    h1[...] = dot_nn(x[...], wr[...])
+    at.meet()
+    put_sums(st1, h1[...], mask_mid)
+    first, second = get_sums(at.sum_over(post, "space", st1, st1_land))
+    put_norm(v1, slice(0, mid), first, second, 0)
+    rim[1] = activate(h1[...], v1, mask_mid)
+
+    has_above, has_below = band > 0, band < bands - 1
+    up = post.copy(rim.at[1], rim.at[2], {"space": lax.rem(band + bands - 1, bands)})
+    down = post.copy(rim.at[1], rim.at[0], {"space": lax.rem(band + 1, bands)})
+
+    @pl.when(has_above)
+    def _():
+        up.start()
+
+    @pl.when(has_below)
+    def _():
+        down.start()
+
+    @pl.when(jnp.logical_not(has_above))
+    def _():
+        rim[0] = jnp.zeros(rim.shape[1:], low)
+
+    @pl.when(jnp.logical_not(has_below))
+    def _():
+        rim[2] = jnp.zeros(rim.shape[1:], low)
+
+    loads[2].wait()
+    halves = [slice(start, start + piece) for start in range(0, mid, piece)]
+
+    def tap_sum(row_taps, lanes):
+        total = None
+        for col_tap in range(3):
+            part = None
+            for row_tap in row_taps:
+                term = dot_nn(rim[row_tap], wd[3 * row_tap + col_tap, :, lanes])
+                part = term if part is None else part + term
+            part = shift_pixels(part, CONV_DILATION * (col_tap - 1), cols)
+            total = part if total is None else total + part
+        return total
+
+    for lanes in halves:
+        h2[:, lanes] = tap_sum((1,), lanes)
+
+    turned[...] = rim[1].T
+
+    @pl.when(has_below)
+    def _():
+        up.wait_recv()
+
+    @pl.when(has_above)
+    def _():
+        down.wait_recv()
+
+    for lanes in halves:
+        h2[:, lanes] += tap_sum((0, 2), lanes)
+
+    put_sums(st2, h2[...], mask_mid)
+    first, second = get_sums(at.sum_over(post, "space", st2, st2_land))
+    put_norm(v2, slice(0, mid), first, second, mid)
+    a2[...] = activate(h2[...], v2, mask_mid)
+
+    loads[3].wait()
+    mask_piece = across(mask, piece)
+    per_row = st3.shape[1] // piece
+    half = st3.shape[0] // 2
+
+    def expand_step(number, carry):
+        lanes = pl.ds(pl.multiple_of(number * piece, piece), piece)
+        value = dot_nn(a2[...], we[:, lanes])
+        h3[:, lanes] = value
+        kept = value * mask_piece
+        row = number // per_row
+        spot = pl.ds(pl.multiple_of(lax.rem(number, per_row) * piece, piece), piece)
+        st3[pl.ds(row, 1), spot] = jnp.sum(kept, axis=0, keepdims=True)
+        st3[pl.ds(half + row, 1), spot] = jnp.sum(kept * value, axis=0, keepdims=True)
+        return carry
+
+    lax.fori_loop(0, bands, expand_step, 0)
+    begun = at.sum_begin(post, "space", st3, st3_land)
+    h3q[...] = h3[my_rows]
+    total = at.sum_end(begun)
+    lanes_in = st3.shape[1]
+    for row in range(half):
+        put_norm(
+            v3,
+            slice(row * lanes_in, (row + 1) * lanes_in),
+            total[row : row + 1],
+            total[half + row : half + row + 1],
+            2 * mid + row * lanes_in,
+        )
+
+    mask_own[...] = mask
+    mask_quarter = across(mask_own[my_rows], piece)
+
+    def shared_of(number):
+        lanes = pl.ds(pl.multiple_of(number * piece, piece), piece)
+        hat = (h3q[:, lanes] - v3[0:1, lanes]) * v3[1:2, lanes]
+        before = v3[2:3, lanes] * hat + v3[3:4, lanes] + x[my_rows, lanes].astype(f32)
+        return (gelu_of(before) * mask_quarter).astype(low)
+
+    slices_in = []
+    for other in at.other_bands:
+        blocks[other] = shared_of(other)
+        slices_in.append(
+            post.push(blocks.at[other], sh_out.at[band, my_rows], {"space": other})
+        )
+    sh_out[band, my_rows] = shared_of(band)
+
+    part = mid // bands
+
+    def part_of(number):
+        return turned.at[pl.ds(pl.multiple_of(number * part, part), part)]
+
+    act[0] = jnp.zeros(act.shape[1:], low)
+    act[bands + 1] = jnp.zeros(act.shape[1:], low)
+    act[band + 1] = part_of(band)[...]
+    parts_in = [
+        post.push(part_of(other), act.at[band + 1], {"space": other}) for other in at.other_bands
+    ]
+
+    def to_tasks(number):
+        block = sh_out.at[number, my_rows]
+        return [post.push(block, block, {"task": other}) for other in at.other_tasks]
+
+    quarters_in = to_tasks(band)
+    for step, made in enumerate(slices_in, start=1):
+        made.wait_recv()
+        quarters_in += to_tasks(lax.rem(band + bands - step, bands))
+    for made in quarters_in + parts_in:
+        made.wait_recv()
+
+    @pl.when(has_above)
+    def _():
+        up.wait_send()
+
+    @pl.when(has_below)
+    def _():
+        down.wait_send()
+
+
+def front_kernel(sizes, plan, counts, *refs):
+    refs = list(refs)
+
+    def take(count):
+        taken = refs[:count]
+        del refs[:count]
+        return taken
+
+    x_hbm, widths, gain, shift, wr_hbm, wd_hbm, we_hbm = take(7)
+    head_gain, head_shift, cot, bw, pw, rate_hbm = take(6)
+    trunk_hbm, head_hbm = take(9), take(6)
+    trunk_outs, head_outs = take(9), take(6)
+    (shared,), trunk_scratch, head_scratch = take(1), take(counts[0]), take(counts[1])
+    send_sem, recv_sem, local_sem, rate_sem, out_sem = refs
+    tasks, bands, width, taps = sizes[0], sizes[1], plan[4], plan[5]
+    at = Place(tasks, bands)
+    post = Post(send_sem, recv_sem)
+    rate = head_scratch[0]
+    rate_loads = []
+    for number, (level, row_tap, col_tap, _, _) in enumerate(taps):
+        start = (9 * (level - 1) + 3 * row_tap + col_tap) * width
+        rate_loads.append(
+            pltpu.make_async_copy(
+                rate_hbm.at[:, start : start + width], rate.at[number], rate_sem.at[number]
+            )
+        )
+
+    def when_loaded():
+        for load in rate_loads:
+            load.start()
+
+    trunk_phase(
+        at,
+        post,
+        sizes,
+        when_loaded,
+        x_hbm,
+        widths,
+        gain,
+        shift,
+        wr_hbm,
+        wd_hbm,
+        we_hbm,
+        shared,
+        *trunk_outs,
+        *trunk_scratch,
+        local_sem,
+    )
+    writes = []
+
+    def write(sources, targets):
+        for source, target in zip(sources, targets):
+            copy = pltpu.make_async_copy(source, target, out_sem.at[len(writes)])
+            copy.start()
+            writes.append(copy)
+
+    write(trunk_outs, trunk_hbm)
+    head_phase(
+        at,
+        post,
+        plan,
+        rate_loads,
+        shared,
+        widths,
+        head_gain,
+        head_shift,
+        cot,
+        bw,
+        pw,
+        *head_outs,
+        *head_scratch,
+    )
+    write(head_outs, head_hbm)
+    for copy in writes:
+        copy.wait()
+
+
+def front(tasks, bands, cols, rows, collective, x, widths, gain, shift, wr, wd, we, *head_in):
+    low, f32 = jnp.bfloat16, jnp.float32
+    head_gain, head_shift, cot, bw, pw, rate = head_in
+    pixels, wide = x.shape
+    mid = wr.shape[1]
+    quarter, piece = pixels // tasks, wide // bands
+    width = pw.shape[1]
     chips = bands // 2
     group_rows = rows // chips
     taps = live_taps(rows, cols)
@@ -1741,13 +2211,29 @@
     block = (pixels, width)
     both_rows, proj_rows = -(-9 * width // LANE // 8) * 8, 8
 
-    def stats(count):
-        return [pltpu.VMEM((count, LANE), f32), pltpu.VMEM((bands, count, LANE), f32)]
-
-    scratch = (
+    def stats(count, lanes=LANE):
+        return [pltpu.VMEM((count, lanes), f32), pltpu.VMEM((bands, count, lanes), f32)]
+
+    trunk_scratch = (
         [
-            pltpu.VMEM((len(taps), sh.shape[2], width), low),
-            pltpu.VMEM((sh.shape[2], bands * pixels), low),
+            pltpu.VMEM(x.shape, low),
+            pltpu.VMEM(wr.shape, low),
+            pltpu.VMEM(wd.shape, low),
+            pltpu.VMEM(we.shape, low),
+            pltpu.VMEM((3, pixels, mid), low),
+            pltpu.VMEM((mid, pixels), low),
+            pltpu.VMEM((pixels, wide), f32),
+            pltpu.VMEM((bands, quarter, piece), low),
+            pltpu.VMEM((pixels, LANE), f32),
+        ]
+        + stats(2 * mid // LANE)
+        + stats(2 * mid // LANE)
+        + stats(8, wide // 4)
+    )
+    head_scratch = (
+        [
+            pltpu.VMEM((len(taps), piece, width), low),
+            pltpu.VMEM((piece, bands * pixels), low),
             pltpu.VMEM((levels, chips, 2 * pixels, width), f32),
             pltpu.VMEM((chips, 2, 4) + block, low),
             pltpu.VMEM((chips, 4) + block, low),
@@ -1766,330 +2252,81 @@
         + [
             pltpu.VMEM((bands, 4) + block, low),
             pltpu.VMEM((levels, chips, 3, 2 * pixels, width), low),
-            pltpu.VMEM((len(taps) + 1, sh.shape[2], width), f32),
+            pltpu.VMEM((len(taps) + 1, piece, width), f32),
             pltpu.VMEM((chips, 2 * pixels, width), f32),
-            pltpu.SemaphoreType.DMA((80,)),
-            pltpu.SemaphoreType.DMA((80,)),
-            pltpu.SemaphoreType.DMA((len(taps),)),
+            pltpu.VMEM((bands, pixels, piece), low),
+            pltpu.VMEM(pw.shape, low),
+            pltpu.VMEM((chips, pw.shape[0] // bands, width), low),
+            pltpu.VMEM((chips, pw.shape[0] // bands, width), low),
         ]
     )
+    sizes = (tasks, bands, cols, quarter, mid, wide, piece)
+    plan = (tasks, bands, cols, pixels, width, tuple(taps), tuple(extras))
     out_shapes = (
+        shape((bands + 2, mid // bands, pixels), low),
+        shape((pixels, mid), f32),
+        shape((pixels, mid), f32),
+        shape((pixels, mid), low),
+        shape((quarter, wide), f32),
+        shape((8, mid), f32),
+        shape((8, mid), f32),
+        shape((8, wide), f32),
+        shape((2, 2 * mid + wide), f32),
         shape(block, low),
-        shape(sh.shape, low),
-        shape((len(taps) + 2, sh.shape[2], width), low),
-        shape(pw.shape, low),
+        shape((tasks, bands, quarter, piece), low),
+        shape((len(taps) + 2, piece, width), low),
+        shape((pw.shape[0] // bands, width), low),
         shape((both_rows, LANE), f32),
         shape((proj_rows, LANE), f32),
     )
     return taps, pl.pallas_call(
-        functools.partial(
-            head_kernel, (tasks, bands, cols, pixels, width, tuple(taps), tuple(extras))
-        ),
-        name="head",
+        functools.partial(front_kernel, sizes, plan, (len(trunk_scratch), len(head_scratch))),
+        name="front",
         out_shape=out_shapes,
-        in_specs=[in_vmem, pl.BlockSpec(memory_space=pltpu.SMEM)] + [in_vmem] * 5 + [anywhere],
-        out_specs=(in_vmem,) * 6,
-        scratch_shapes=scratch,
-        compiler_params=pltpu.CompilerParams(
-            collective_id=collective, has_side_effects=True, vmem_limit_bytes=36 << 20
-        ),
-    )(sh, widths, gain, shift, cot, bw, pw, rate)
-
-
-def trunk_kernel(
-    sizes,
-    x_hbm,
-    widths_ref,
-    gain_ref,
-    shift_ref,
-    wr_hbm,
-    wd_hbm,
-    we_hbm,
-    sh_out,
-    rim,
-    h1,
-    h2,
-    a2,
-    h3q,
-    v1,
-    v2,
-    v3,
-    stats_out,
-    x,
-    wr,
-    wd,
-    we,
-    h3,
-    blocks,
-    mask_own,
-    st1,
-    st1_land,
-    st2,
-    st2_land,
-    st3,
-    st3_land,
-    send_sem,
-    recv_sem,
-    local_sem,
-):
-    tasks, bands, cols, quarter, mid, wide, piece = sizes
-    low, f32 = jnp.bfloat16, jnp.float32
-    at = Place(tasks, bands)
-    post = Post(send_sem, recv_sem)
-    task, band = at.task, at.band
-    my_rows = pl.ds(pl.multiple_of(task * quarter, quarter), quarter)
-    loads = [
-        pltpu.make_async_copy(source, target, local_sem.at[number])
-        for number, (source, target) in enumerate(
-            ((x_hbm, x), (wr_hbm, wr), (wd_hbm, wd), (we_hbm, we))
-        )
-    ]
-    for load in loads:
-        load.start()
-    at.meet(True, True)
-    pixels = x.shape[0]
-    band_rows = pixels // cols
-    mask = row_mask(widths_ref, band * band_rows, band_rows, cols)
-    count = count_pixels(widths_ref)
-    spread = mid // LANE
-
-    def across(value, lanes):
-        return jnp.concatenate([value] * (lanes // LANE), axis=1)
-
-    def put_sums(target, value, keep):
-        kept = value * keep
-        first = jnp.sum(kept, axis=0, keepdims=True)
-        second = jnp.sum(kept * value, axis=0, keepdims=True)
-        for number in range(spread):
-            lanes = slice(number * LANE, (number + 1) * LANE)
-            target[number : number + 1] = first[:, lanes]
-            target[spread + number : spread + number + 1] = second[:, lanes]
-
-    def get_sums(total):
-        return [
-            jnp.concatenate([total[base + k : base + k + 1] for k in range(spread)], axis=1)
-            for base in (0, spread)
-        ]
-
-    def put_norm(vectors, lanes, first, second, start):
-        width = first.shape[1]
-        inv = across(1.0 / count, width)
-        mean_value = first * inv
-        variance = second * inv - mean_value * mean_value
-        vectors[0:1, lanes] = mean_value
-        vectors[1:2, lanes] = lax.rsqrt(variance + NORM_EPS)
-        vectors[2:3, lanes] = gain_ref[:, start : start + width]
-        vectors[3:4, lanes] = shift_ref[:, start : start + width]
-        stats_out[0:1, start : start + width] = mean_value
-        stats_out[1:2, start : start + width] = variance * across(count / (count - 1.0), width)
-
-    def activate(hidden, vectors, keep):
-        normed = vectors[2:3] * ((hidden - vectors[0:1]) * vectors[1:2]) + vectors[3:4]
-        return (gelu_of(normed) * keep).astype(low)
-
-    mask_mid = across(mask, mid)
-    for load in loads[:2]:
-        load.wait()
-    h1[...] = dot_nn(x[...], wr[...])
-    put_sums(st1, h1[...], mask_mid)
-    first, second = get_sums(at.sum_over(post, "space", st1, st1_land))
-    put_norm(v1, slice(0, mid), first, second, 0)
-    rim[1] = activate(h1[...], v1, mask_mid)
-
-    has_above, has_below = band > 0, band < bands - 1
-    up = post.copy(rim.at[1], rim.at[2], {"space": lax.rem(band + bands - 1, bands)})
-    down = post.copy(rim.at[1], rim.at[0], {"space": lax.rem(band + 1, bands)})
-
-    @pl.when(has_above)
-    def _():
-        up.start()
-
-    @pl.when(has_below)
-    def _():
-        down.start()
-
-    @pl.when(jnp.logical_not(has_above))
-    def _():
-        rim[0] = jnp.zeros(rim.shape[1:], low)
-
-    @pl.when(jnp.logical_not(has_below))
-    def _():
-        rim[2] = jnp.zeros(rim.shape[1:], low)
-
-    loads[2].wait()
-    halves = [slice(start, start + piece) for start in range(0, mid, piece)]
-
-    def tap_sum(row_taps, lanes):
-        total = None
-        for col_tap in range(3):
-            part = None
-            for row_tap in row_taps:
-                term = dot_nn(rim[row_tap], wd[3 * row_tap + col_tap, :, lanes])
-                part = term if part is None else part + term
-            part = shift_pixels(part, CONV_DILATION * (col_tap - 1), cols)
-            total = part if total is None else total + part
-        return total
-
-    for lanes in halves:
-        h2[:, lanes] = tap_sum((1,), lanes)
-
-    @pl.when(has_below)
-    def _():
-        up.wait_recv()
-
-    @pl.when(has_above)
-    def _():
-        down.wait_recv()
-
-    for lanes in halves:
-        h2[:, lanes] += tap_sum((0, 2), lanes)
-
-    put_sums(st2, h2[...], mask_mid)
-    first, second = get_sums(at.sum_over(post, "space", st2, st2_land))
-    put_norm(v2, slice(0, mid), first, second, mid)
-    a2[...] = activate(h2[...], v2, mask_mid)
-
-    loads[3].wait()
-    mask_piece = across(mask, piece)
-    per_row = st3.shape[1] // piece
-    half = st3.shape[0] // 2
-
-    def expand_step(number, carry):
-        lanes = pl.ds(pl.multiple_of(number * piece, piece), piece)
-        value = dot_nn(a2[...], we[:, lanes])
-        h3[:, lanes] = value
-        kept = value * mask_piece
-        row = number // per_row
-        spot = pl.ds(pl.multiple_of(lax.rem(number, per_row) * piece, piece), piece)
-        st3[pl.ds(row, 1), spot] = jnp.sum(kept, axis=0, keepdims=True)
-        st3[pl.ds(half + row, 1), spot] = jnp.sum(kept * value, axis=0, keepdims=True)
-        return carry
-
-    lax.fori_loop(0, bands, expand_step, 0)
-    begun = at.sum_begin(post, "space", st3, st3_land)
-    h3q[...] = h3[my_rows]
-    total = at.sum_end(begun)
-    lanes_in = st3.shape[1]
-    for row in range(half):
-        put_norm(
-            v3,
-            slice(row * lanes_in, (row + 1) * lanes_in),
-            total[row : row + 1],
-            total[half + row : half + row + 1],
-            2 * mid + row * lanes_in,
-        )
-
-    mask_own[...] = mask
-    mask_quarter = across(mask_own[my_rows], piece)
-
-    def shared_of(number):
-        lanes = pl.ds(pl.multiple_of(number * piece, piece), piece)
-        hat = (h3q[:, lanes] - v3[0:1, lanes]) * v3[1:2, lanes]
-        before = v3[2:3, lanes] * hat + v3[3:4, lanes] + x[my_rows, lanes].astype(f32)
-        return (gelu_of(before) * mask_quarter).astype(low)
-
-    slices_in = []
-    for other in at.other_bands:
-        blocks[other] = shared_of(other)
-        slices_in.append(
-            post.push(blocks.at[other], sh_out.at[band, my_rows], {"space": other})
-        )
-    sh_out[band, my_rows] = shared_of(band)
-
-    def to_tasks(number):
-        block = sh_out.at[number, my_rows]
-        return [post.push(block, block, {"task": other}) for other in at.other_tasks]
-
-    quarters_in = to_tasks(band)
-    for step, made in enumerate(slices_in, start=1):
-        made.wait_recv()
-        quarters_in += to_tasks(lax.rem(band + bands - step, bands))
-    for made in quarters_in:
-        made.wait_recv()
-    post.close()
-
-    @pl.when(has_above)
-    def _():
-        up.wait_send()
-
-    @pl.when(has_below)
-    def _():
-        down.wait_send()
-
-
-def trunk(tasks, bands, cols, collective, x, widths, gain, shift, wr, wd, we):
-    low, f32 = jnp.bfloat16, jnp.float32
-    pixels, wide = x.shape
-    mid = wr.shape[1]
-    quarter, piece = pixels // tasks, wide // bands
-    in_vmem = pl.BlockSpec(memory_space=pltpu.VMEM)
-    anywhere = pl.BlockSpec(memory_space=pl.ANY)
-    shape = jax.ShapeDtypeStruct
-    narrow_stats = [
-        pltpu.VMEM((2 * mid // LANE, LANE), f32),
-        pltpu.VMEM((bands, 2 * mid // LANE, LANE), f32),
-    ]
-    return pl.pallas_call(
-        functools.partial(trunk_kernel, (tasks, bands, cols, quarter, mid, wide, piece)),
-        name="trunk",
-        out_shape=(
-            shape((bands, pixels, piece), low),
-            shape((3, pixels, mid), low),
-            shape((pixels, mid), f32),
-            shape((pixels, mid), f32),
-            shape((pixels, mid), low),
-            shape((quarter, wide), f32),
-            shape((8, mid), f32),
-            shape((8, mid), f32),
-            shape((8, wide), f32),
-            shape((2, 2 * mid + wide), f32),
-        ),
         in_specs=[anywhere, pl.BlockSpec(memory_space=pltpu.SMEM), in_vmem, in_vmem]
-        + [anywhere] * 3,
-        out_specs=(in_vmem,) * 10,
-        scratch_shapes=[
-            pltpu.VMEM(x.shape, low),
-            pltpu.VMEM(wr.shape, low),
-            pltpu.VMEM(wd.shape, low),
-            pltpu.VMEM(we.shape, low),
-            pltpu.VMEM((pixels, wide), f32),
-            pltpu.VMEM((bands, quarter, piece), low),
-            pltpu.VMEM((pixels, LANE), f32),
-        ]
-        + narrow_stats
-        + narrow_stats
+        + [anywhere] * 3
+        + [in_vmem] * 5
+        + [anywhere],
+        out_specs=(anywhere,) * len(out_shapes),
+        scratch_shapes=[pltpu.VMEM(out.shape, out.dtype) for out in out_shapes]
+        + [pltpu.VMEM((bands, pixels, piece), low)]
+        + trunk_scratch
+        + head_scratch
         + [
-            pltpu.VMEM((8, wide // 4), f32),
-            pltpu.VMEM((bands, 8, wide // 4), f32),
-            pltpu.SemaphoreType.DMA((64,)),
-            pltpu.SemaphoreType.DMA((64,)),
+            pltpu.SemaphoreType.DMA((192,)),
+            pltpu.SemaphoreType.DMA((192,)),
             pltpu.SemaphoreType.DMA((4,)),
+            pltpu.SemaphoreType.DMA((len(taps),)),
+            pltpu.SemaphoreType.DMA((len(out_shapes),)),
         ],
         compiler_params=pltpu.CompilerParams(
-            collective_id=collective, has_side_effects=True, vmem_limit_bytes=54 << 20
+            collective_id=collective, has_side_effects=True, vmem_limit_bytes=60 << 20
         ),
-    )(x, widths, gain, shift, wr, wd, we)
+    )(x, widths, gain, shift, wr, wd, we, *head_in)
 
 
 def finish_kernel(
     places,
-    tap_ref,
+    tap_hbm,
     ho_in,
     ig_in,
     rg_in,
     dg_in,
     eg_in,
-    pg_ref,
-    s3_ref,
-    s2_ref,
-    s1_ref,
-    both_ref,
-    proj_ref,
+    bs_in,
+    tw_hbm,
+    pg_hbm,
+    s3_hbm,
+    s2_hbm,
+    s1_hbm,
+    both_hbm,
+    proj_hbm,
     ho_out,
     ig_out,
     rg_out,
     dg_out,
     eg_out,
+    bs_out,
     branch_out,
     rate_out,
     pg_out,
@@ -2097,27 +2334,65 @@
     ts_out,
     hg_out,
     hs_out,
+    tw_out,
+    tap_ref,
+    tw_ref,
+    pg_ref,
+    s3_ref,
+    s2_ref,
+    s1_ref,
+    both_ref,
+    proj_ref,
+    ho_buf,
+    ig_buf,
+    rg_buf,
+    dg_buf,
+    eg_buf,
+    bs_buf,
     branch,
     rate,
     sems,
+    load_sems,
 ):
     f32 = jnp.float32
     width = tap_ref.shape[2]
-    copies = [
-        pltpu.make_async_copy(source, target, sems.at[number])
+    loads = [
+        pltpu.make_async_copy(source, target, load_sems.at[number])
         for number, (source, target) in enumerate(
             (
-                (ho_in, ho_out),
-                (ig_in, ig_out),
-                (rg_in, rg_out),
-                (dg_in, dg_out),
-                (eg_in, eg_out),
+                (tap_hbm, tap_ref),
+                (pg_hbm, pg_ref),
+                (tw_hbm, tw_ref),
+                (s3_hbm, s3_ref),
+                (s2_hbm, s2_ref),
+                (s1_hbm, s1_ref),
+                (both_hbm, both_ref),
+                (proj_hbm, proj_ref),
             )
         )
     ]
-    for copy in copies:
+    for load in loads:
+        load.start()
+    passed = [
+        (ho_in, ho_buf, ho_out),
+        (ig_in, ig_buf, ig_out),
+        (rg_in, rg_buf, rg_out),
+        (dg_in, dg_buf, dg_out),
+        (eg_in, eg_buf, eg_out),
+        (bs_in, bs_buf, bs_out),
+    ]
+    passes = [
+        (
+            pltpu.make_async_copy(source, buffer, load_sems.at[len(loads) + number]),
+            pltpu.make_async_copy(buffer, target, sems.at[number]),
+        )
+        for number, (source, buffer, target) in enumerate(passed)
+    ]
+    for copy, _ in passes:
         copy.start()
+    copies = [copy for _, copy in passes]
     per_level = len(places) // 3
+    loads[0].wait()
     for level in range(3):
         for number in range(level * per_level, (level + 1) * per_level):
             lanes = slice(number * width, (number + 1) * width)
@@ -2131,12 +2406,17 @@
         )
         copy.start()
         copies.append(copy)
+    for arrival, copy in passes:
+        arrival.wait()
+        copy.start()
     count = tap_ref.shape[0]
     branch[:, :width] = tap_ref[count - 2].astype(f32)
     branch[:, width:] = tap_ref[count - 1].astype(f32)
     copy = pltpu.make_async_copy(branch, branch_out, sems.at[len(copies)])
     copy.start()
     copies.append(copy)
+    for load in loads[1:]:
+        load.wait()
     pg_out[...] = pg_ref[...].astype(f32)
     rows = s1_ref.shape[0] // 2
     ts_out[0:rows] = s1_ref[0:rows]
@@ -2151,22 +2431,31 @@
             ts_out[target : target + 1] = s3_ref[row : row + 1, lanes]
             tg_out[target : target + 1] = s3_ref[half + row : half + row + 1, lanes]
     spread = width // LANE
-    hs_out[0 : 4 * spread] = both_ref[0 : 4 * spread]
-    hg_out[0 : 4 * spread] = both_ref[4 * spread : 8 * spread]
-    hs_out[4 * spread : 5 * spread] = proj_ref[0:spread]
-    hg_out[4 * spread : 5 * spread] = proj_ref[spread : 2 * spread]
+    for row in range(4 * spread):
+        lanes = slice(row * LANE, (row + 1) * LANE)
+        hs_out[:, lanes] = both_ref[row : row + 1]
+        hg_out[:, lanes] = both_ref[4 * spread + row : 4 * spread + row + 1]
+    for row in range(spread):
+        lanes = slice((4 * spread + row) * LANE, (4 * spread + row + 1) * LANE)
+        hs_out[:, lanes] = proj_ref[row : row + 1]
+        hg_out[:, lanes] = proj_ref[spread + row : spread + row + 1]
+    tasks = tw_out.shape[1]
+    place = lax.broadcasted_iota(jnp.int32, (1, LANE), 1)
+    weights = jnp.zeros((1, LANE), f32)
+    for number in range(tasks):
+        weights = jnp.where(place == number, tw_ref[number : number + 1], weights)
+    tw_out[...] = weights[:, :tasks]
     for copy in copies:
         copy.wait()
 
 
-def finish(places, taps, ho, ig, rg, dg, eg, pg, s3, s2, s1, both, proj):
+def finish(places, tasks, taps, ho, ig, rg, dg, eg, bs, tw, pg, s3, s2, s1, both, proj):
     f32 = jnp.float32
     in_vmem = pl.BlockSpec(memory_space=pltpu.VMEM)
     anywhere = pl.BlockSpec(memory_space=pl.ANY)
     shape = jax.ShapeDtypeStruct
     depth, width = taps.shape[1:]
     rows = (s1.size + s2.size + s3.size) // 2 // LANE
-    head_rows = 5 * width // LANE
     return pl.pallas_call(
         functools.partial(finish_kernel, places),
         name="finish",
@@ -2176,23 +2465,29 @@
             shape(rg.shape, rg.dtype),
             shape(dg.shape, dg.dtype),
             shape(eg.shape, eg.dtype),
+            shape(bs.shape, bs.dtype),
             shape((depth, 2 * width), f32),
             shape((depth, len(places) * width), f32),
             shape(pg.shape, f32),
             shape((rows, LANE), f32),
             shape((rows, LANE), f32),
-            shape((head_rows, LANE), f32),
-            shape((head_rows, LANE), f32),
+            shape((1, 5 * width), f32),
+            shape((1, 5 * width), f32),
+            shape((1, tasks), f32),
         ),
-        in_specs=[in_vmem] + [anywhere] * 5 + [in_vmem] * 6,
-        out_specs=(anywhere,) * 7 + (in_vmem,) * 5,
+        in_specs=[anywhere] * 14,
+        out_specs=(anywhere,) * 8 + (in_vmem,) * 6,
         scratch_shapes=[
+            pltpu.VMEM(value.shape, value.dtype) for value in (taps, tw, pg, s3, s2, s1, both, proj, ho, ig, rg, dg, eg, bs)
+        ]
+        + [
             pltpu.VMEM((depth, 2 * width), f32),
             pltpu.VMEM((depth, len(places) * width), f32),
-            pltpu.SemaphoreType.DMA((9,)),
+            pltpu.SemaphoreType.DMA((10,)),
+            pltpu.SemaphoreType.DMA((14,)),
         ],
-        compiler_params=pltpu.CompilerParams(vmem_limit_bytes=40 << 20),
-    )(taps, ho, ig, rg, dg, eg, pg, s3, s2, s1, both, proj)
+        compiler_params=pltpu.CompilerParams(vmem_limit_bytes=60 << 20),
+    )(taps, ho, ig, rg, dg, eg, bs, tw, pg, s3, s2, s1, both, proj)
 
 
 def live_taps(rows, cols):
@@ -2228,10 +2523,27 @@
     head_width = proj_weight.shape[2]
     inputs = features.reshape(pixels, in_width)
     dilated = w_dilated.transpose(1, 0, 2)
-    shared, rim, h1, h2, a2, h3q, v1, v2, v3, batch_stats = trunk(
+    taps, (
+        act,
+        h1,
+        h2,
+        a2,
+        h3q,
+        v1,
+        v2,
+        v3,
+        batch_stats,
+        head_out,
+        task_grads,
+        tap_grads,
+        proj_share,
+        both_sums,
+        proj_sums,
+    ) = front(
         tasks,
         bands,
         cols,
+        rows,
         0,
         inputs,
         row_width,
@@ -2240,15 +2552,6 @@
         w_reduce,
         dilated,
         w_expand,
-    )
-    taps, (head_out, shared_grad, tap_grads, proj_term, both_sums, proj_sums) = head(
-        tasks,
-        bands,
-        cols,
-        rows,
-        1,
-        shared,
-        row_width,
         head_gain,
         head_shift,
         head_cot.reshape(pixels, head_width),
@@ -2270,8 +2573,8 @@
         tasks,
         bands,
         cols,
-        2,
-        shared_grad,
+        1,
+        task_grads,
         h3q,
         inputs,
         v3,
@@ -2279,13 +2582,13 @@
         v2,
         h1,
         v1,
-        rim,
+        act,
         a2,
         row_width,
         w_expand,
         dilated,
         w_reduce,
-        proj_term.reshape(bands, -1, head_width),
+        proj_share,
     )
     place_of = {tap[:3]: number for number, tap in enumerate(taps)}
     places = tuple(
@@ -2300,6 +2603,7 @@
         reduce_grad,
         dilated_grad,
         expand_grad,
+        batch_stats,
         branch_grad,
         rate_grad,
         proj_grad,
@@ -2307,14 +2611,18 @@
         trunk_shifts,
         head_gains,
         head_shifts,
+        task_weight,
     ) = finish(
         places,
+        tasks,
         tap_grads,
         head_out,
         input_grad,
         reduce_grad,
         dilated_grad,
         expand_grad,
+        batch_stats,
+        weight_rows,
         proj_grad.reshape(-1, head_width),
         sums_three,
         sums_two,
@@ -2334,9 +2642,9 @@
         branch_grad[None],
         rate_grad[None],
         proj_grad[None],
-        head_gains.reshape(1, -1),
-        head_shifts.reshape(1, -1),
-        weight_rows[:tasks, 0],
+        head_gains,
+        head_shifts,
+        task_weight.reshape(-1),
     )
 
 

time: 264 us -> 237 us (0.90)
  Pallas kernels: 255 us -> 233 us
  local copies, waits for them, and re-layouts: 7.19 us -> 0 us
    pallas_call x1, Pallas kernels: 104 us -> 71.4 us  [trunk_back(): pl.pallas_call(functools.partial(trunk_back_kernel, (tasks, bands, cols,...]
    pallas_call x2 -> x1, Pallas kernels: 145 us -> 154 us  [front(): pl.pallas_call(functools.partial(front_kernel, sizes, plan, (len(trunk_sc...]
    unnamed x43 -> x0, local copies, waits for them, and re-layouts: 5.96 us -> none
where the time goes in v4:
time: 237 us; the launch traced here: 234 us
  Pallas kernels  233 us (98%)
    pallas_call x1, Pallas kernels, front(): pl.pallas_call(functools.partial(front_kernel, sizes, plan, (len(trunk_sc...  154 us
    pallas_call x1, Pallas kernels, trunk_back(): pl.pallas_call(functools.partial(trunk_back_kernel, (tasks, bands, cols,...  71.4 us
    pallas_call x1, Pallas kernels, finish(): pl.pallas_call(functools.partial(finish_kernel, places), name='finish', o...  7.17 us

profile of v4, /device:TPU:13, one launch (start us, length us, event | category | flops | bytes accessed | tf_op | source)
XLA Modules:
  0.0 233.5 jit_solution(18137389022329757656)
XLA Ops:
  0.7 154.2 %front.1 = (bf16[10,64,256]{2,1,0:T(8,128)(2,1)}, f32[256,512]{1,0:T(8,128)}, f32[256,512]{1,0:T(8,128)}, bf16[256,512]{1,0:T(8,128)(2,1)}, f32[64,2048]{1,0:T(8...) custom-call(bf16[256,2048]{1,0:T(8,128)(2,1)} %bitcast.20, ...), custom_call_target="tpu_custom_call" | custom-call | tf_op jit(solution)/shard_map/front/pallas_call | solution.py:2282
  154.8 71.4 %trunk_back.1 = (f32[8,128]{1,0:T(8,128)}, bf16[256,2048]{1,0:T(8,128)(2,1)}, f32[256,512]{1,0:T(8,128)}, f32[9,64,512]{2,1,0:T(8,128)}, f32[64,2048]{1,0:T(8,12...) custom-call(bf16[4,8,64,256]{3,2,1,0:T(8,128)(2,1)} %get-tuple-element.54.xg_hbm, ...), custom_call_target="tpu_custom_call" | custom-call | tf_op jit(solution)/shard_map/trunk_back/pallas_call | solution.py:1234
  226.2 7.2 %finish.1 = (bf16[256,256]{1,0:T(8,128)(2,1)}, bf16[256,2048]{1,0:T(8,128)(2,1)}, f32[256,512]{1,0:T(8,128)}, f32[9,64,512]{2,1,0:T(8,128)}, f32[64,2048]{1,0:T(...) custom-call(bf16[17,256,256]{2,1,0:T(8,128)(2,1)} %get-tuple-element, ...), custom_call_target="tpu_custom_call" | custom-call | tf_op jit(solution)/shard_map/finish/pallas_call | solution.py:2459

commit v5 on v4

--- a/solution.py
+++ b/solution.py
@@ -430,6 +430,7 @@
 LANE = 128
 
 
+FAR_LAG = 3
 GELU_A = 0.7978845608028654
 GELU_B = 0.044715
 
@@ -444,6 +445,14 @@
     return 0.5 * (1.0 + bend) + 0.5 * value * (1.0 - bend * bend) * (
         GELU_A * (1.0 + 3.0 * GELU_B * square)
     )
+
+
+def gelu_both(value):
+    square = value * value
+    bend = jnp.tanh(GELU_A * value * (1.0 + GELU_B * square))
+    lift = 0.5 * (1.0 + bend)
+    slope = lift + 0.5 * value * (1.0 - bend * bend) * (GELU_A * (1.0 + 3.0 * GELU_B * square))
+    return value * lift, slope
 
 
 def dot_nn(left_side, right_side):
@@ -510,6 +519,7 @@
     def close(self):
         for made in self.sent:
             made.wait_send()
+        self.sent = []
 
 
 class Place:
@@ -555,23 +565,27 @@
         return self.sum_end(self.sum_begin(post, axis, own_ref, land_ref))
 
 
-def trunk_back_kernel(
+def back_phase(
+    at,
+    post,
     sizes,
-    xg_hbm,
-    h3_hbm,
+    local_sem,
+    xg,
+    h3q,
+    v3_ref,
+    h2_ref,
+    v2_ref,
+    h1_ref,
+    v1_ref,
+    act_ref,
+    a2_ref,
+    ps_ref,
     x_hbm,
-    v3_hbm,
-    h2_hbm,
-    v2_hbm,
-    h1_hbm,
-    v1_hbm,
-    act_hbm,
-    a2_hbm,
     widths_ref,
     we_hbm,
     wd_hbm,
     wr_hbm,
-    ps_hbm,
+    write,
     tw_hbm,
     ig_hbm,
     rg_hbm,
@@ -593,19 +607,8 @@
     we,
     wd,
     wr,
-    xg,
     x_ref,
-    v3_ref,
-    v2_ref,
-    v1_ref,
-    act_ref,
-    ps_ref,
-    h3q,
-    h2_ref,
-    h1_ref,
-    a2_ref,
     mask_ref,
-    xq,
     gram_own,
     gram_land,
     gram_mid,
@@ -649,33 +652,16 @@
     r_share,
     r_tasks,
     p_all,
-    send_sem,
-    recv_sem,
-    local_sem,
-    out_sem,
 ):
     tasks, bands, cols, quarter, mid, wide, piece = sizes
     low = jnp.bfloat16
     f32 = jnp.float32
-    at = Place(tasks, bands)
-    post = Post(send_sem, recv_sem)
     task, band = at.task, at.band
     my_rows = pl.ds(pl.multiple_of(task * quarter, quarter), quarter)
     arrays = {
-        "xg": (xg_hbm, xg),
-        "a2": (a2_hbm, a2_ref),
         "x": (x_hbm, x_ref),
-        "xq": (x_hbm.at[my_rows], xq),
-        "h3": (h3_hbm, h3q),
-        "v3": (v3_hbm, v3_ref),
-        "ps": (ps_hbm, ps_ref),
         "we": (we_hbm, we),
-        "h2": (h2_hbm, h2_ref),
-        "v2": (v2_hbm, v2_ref),
         "wd": (wd_hbm, wd),
-        "h1": (h1_hbm, h1_ref),
-        "v1": (v1_hbm, v1_ref),
-        "act": (act_hbm, act_ref),
         "wr": (wr_hbm, wr),
     }
     loads = {
@@ -683,24 +669,15 @@
         for number, (name, (source, target)) in enumerate(arrays.items())
     }
 
-    writes = []
-
-    def write(source, target):
-        copy = pltpu.make_async_copy(source, target, out_sem.at[len(writes)])
-        copy.start()
-        writes.append(copy)
-
     def loaded(*names):
         for name in names:
             loads[name].wait()
 
     for load in loads.values():
         load.start()
-    at.greet()
     band_rows = x_ref.shape[0] // cols
     mask_ref[...] = row_mask(widths_ref, band * band_rows, band_rows, cols)
 
-    loaded("xg")
     pairs = [(a, b) for a in range(tasks) for b in range(a, tasks)]
 
     def gram_step(number, totals):
@@ -720,9 +697,7 @@
     gram_own[...] = jnp.zeros_like(gram_own)
     for number, total in enumerate(totals):
         gram_own[number : number + 1] = jnp.sum(total, axis=0, keepdims=True)
-    at.meet()
     begun = at.sum_begin(post, "task", gram_own, gram_land)
-    loaded("a2")
     a2t[...] = a2_ref[...].T
     gram_mid[...] = at.sum_end(begun)
     begun = at.sum_begin(post, "space", gram_mid, gram_land_b)
@@ -779,7 +754,6 @@
         comb[other] = mixed(other)
         comb_in.append(post.push(comb.at[other], comb_land.at[band], {"space": other}))
     comb_land[pl.ds(band, 1)] = mixed(band)[None]
-    loaded("xq", "h3", "v3")
     for made in comb_in:
         made.wait_recv()
 
@@ -793,7 +767,7 @@
     def gate_step(number, carry):
         lanes = pl.ds(pl.multiple_of(number * piece, piece), piece)
         hat = (h3q[:, lanes] - v3_ref[0:1, lanes]) * v3_ref[1:2, lanes]
-        before = v3_ref[2:3, lanes] * hat + v3_ref[3:4, lanes] + xq[:, lanes].astype(f32)
+        before = v3_ref[2:3, lanes] * hat + v3_ref[3:4, lanes] + x_ref[my_rows, lanes].astype(f32)
         grad = gelu_slope(before) * comb_land[number].astype(f32) * mask_piece
         gate[number] = grad
         scaled[number] = hat
@@ -829,7 +803,7 @@
             post.push(l3.at[pl.ds(other * per_task, per_task)], l3x.at[task], {"task": other})
         )
     l3x[pl.ds(task, 1)] = l3[pl.ds(task * per_task, per_task)][None]
-    loaded("ps", "we")
+    loaded("we")
     p_all[pl.ds(band, 1)] = ps_ref[...][None]
     p_block = p_all.at[band]
     p_near = post.push(p_block, p_block, at.twin)
@@ -850,7 +824,6 @@
 
     mask_mid = jnp.concatenate([mask_quarter] * (mid // LANE), axis=1)
     inv_mid = jnp.concatenate([inv_count] * (mid // LANE), axis=1)
-    loaded("h2", "v2")
     hat = (h2_ref[my_rows] - v2_ref[0:1]) * v2_ref[1:2]
     grad = gelu_slope(v2_ref[2:3] * hat + v2_ref[3:4]) * ag2 * mask_mid
     spread = mid // LANE
@@ -991,7 +964,6 @@
             total = part if total is None else total + part
         ag1[:, lanes] += total
 
-    loaded("h1", "v1")
     pixels = ag1.shape[0]
     chunk = pixels // 8
 
@@ -1059,7 +1031,7 @@
         block = l2c.at[lax.rem(at.chip + at.chips - step, at.chips) * 2 + at.core]
         d_near.append(post.push(block, block, at.twin))
 
-    loaded("wr", "act")
+    loaded("wr")
     for made in gate_in:
         made.wait_recv()
 
@@ -1124,126 +1096,6 @@
     @pl.when(has_below)
     def _():
         down.wait_send()
-    for copy in writes:
-        copy.wait()
-
-
-def trunk_back(
-    tasks, bands, cols, collective, xg, h3, x, v3, h2, v2, h1, v1, act, a2, widths, we, wd, wr, ps
-):
-    low, f32 = jnp.bfloat16, jnp.float32
-    pixels, wide = x.shape
-    mid = a2.shape[1]
-    quarter = pixels // tasks
-    piece = wide // bands
-    narrow, broad = mid // tasks, wide // tasks
-    chips = bands // 2
-    part = mid // bands
-    anywhere = pl.BlockSpec(memory_space=pl.ANY)
-    shape = jax.ShapeDtypeStruct
-
-    def stats(rows, lanes):
-        return [
-            pltpu.VMEM((rows, lanes), f32),
-            pltpu.VMEM((tasks, rows, lanes), f32),
-            pltpu.VMEM((rows, lanes), f32),
-            pltpu.VMEM((bands, rows, lanes), f32),
-        ]
-
-    def terms(*dims):
-        return [
-            pltpu.VMEM((2, chips) + dims, low),
-            pltpu.VMEM((chips,) + dims, low),
-            pltpu.VMEM((chips,) + dims, low),
-            pltpu.VMEM(dims, low),
-            pltpu.VMEM((tasks,) + dims, low),
-        ]
-
-    stat_wide = 2 * wide // 8
-    scratch = (
-        [
-            pltpu.VMEM(we.shape, low),
-            pltpu.VMEM(wd.shape, low),
-            pltpu.VMEM(wr.shape, low),
-            pltpu.VMEM(xg.shape, low),
-            pltpu.VMEM(x.shape, low),
-            pltpu.VMEM(v3.shape, f32),
-            pltpu.VMEM(v2.shape, f32),
-            pltpu.VMEM(v1.shape, f32),
-            pltpu.VMEM(act.shape, low),
-            pltpu.VMEM(ps.shape, low),
-            pltpu.VMEM(h3.shape, f32),
-            pltpu.VMEM(h2.shape, f32),
-            pltpu.VMEM(h1.shape, f32),
-            pltpu.VMEM(a2.shape, low),
-            pltpu.VMEM((pixels, LANE), f32),
-            pltpu.VMEM((quarter, wide), low),
-        ]
-        + stats(16, LANE)
-        + [
-            pltpu.VMEM((bands, quarter, piece), low),
-            pltpu.VMEM((bands, quarter, piece), low),
-            pltpu.VMEM((bands, quarter, piece), f32),
-            pltpu.VMEM((bands, quarter, piece), f32),
-            pltpu.VMEM((bands, quarter, piece), low),
-            pltpu.VMEM((tasks, bands, quarter, piece), low),
-        ]
-        + stats(8, stat_wide)
-        + [
-            pltpu.VMEM((bands, quarter, piece), low),
-            pltpu.VMEM((tasks, bands // tasks, quarter, piece), low),
-        ]
-        + stats(2 * mid // LANE, LANE)
-        + [
-            pltpu.VMEM((pixels, mid), low),
-            pltpu.VMEM((2, pixels, mid), low),
-            pltpu.VMEM((pixels, mid), f32),
-            pltpu.VMEM((2 * mid // LANE, LANE), f32),
-            pltpu.VMEM((bands, 2 * mid // LANE, LANE), f32),
-            pltpu.VMEM((pixels, mid), low),
-            pltpu.VMEM((wide, pixels), low),
-            pltpu.VMEM((mid, pixels), low),
-        ]
-        + terms(part, broad)
-        + [
-            pltpu.VMEM((bands, pixels, narrow), low),
-            pltpu.VMEM((3, 3 * part, narrow), f32),
-            pltpu.VMEM((9, part, narrow), low),
-            pltpu.VMEM((tasks, 9, part, narrow), low),
-        ]
-        + terms(piece, narrow)
-        + [
-            pltpu.VMEM((bands,) + ps.shape, low),
-            pltpu.SemaphoreType.DMA((96,)),
-            pltpu.SemaphoreType.DMA((96,)),
-            pltpu.SemaphoreType.DMA((15,)),
-            pltpu.SemaphoreType.DMA((9,)),
-        ]
-    )
-    out_shapes = (
-        shape((8, LANE), f32),
-        shape((pixels, wide), low),
-        shape((piece, mid), f32),
-        shape((9, part, mid), f32),
-        shape((part, wide), f32),
-        shape((8, stat_wide), f32),
-        shape((2 * mid // LANE, LANE), f32),
-        shape((2 * mid // LANE, LANE), f32),
-        shape((bands,) + ps.shape, low),
-    )
-    return pl.pallas_call(
-        functools.partial(trunk_back_kernel, (tasks, bands, cols, quarter, mid, wide, piece)),
-        name="trunk_back",
-        out_shape=out_shapes,
-        in_specs=[anywhere] * 10
-        + [pl.BlockSpec(memory_space=pltpu.SMEM)]
-        + [anywhere] * 4,
-        out_specs=(anywhere,) * len(out_shapes),
-        scratch_shapes=[pltpu.VMEM(out.shape, out.dtype) for out in out_shapes] + scratch,
-        compiler_params=pltpu.CompilerParams(
-            collective_id=collective, has_side_effects=True, vmem_limit_bytes=60 << 20
-        ),
-    )(xg, h3, x, v3, h2, v2, h1, v1, act, a2, widths, we, wd, wr, ps)
 
 
 def head_phase(
@@ -1274,6 +1126,13 @@
     pre,
     joined,
     upstream,
+    cot,
+    out_rows,
+    masks,
+    projected,
+    proj_up,
+    proj_low,
+    pixel_sum,
     st_both,
     st_both_sum,
     st_both_land,
@@ -1297,9 +1156,56 @@
     low, f32 = jnp.bfloat16, jnp.float32
     send_sem, recv_sem = post.send_sem, post.recv_sem
     chips, chip, core, band = at.chips, at.chip, at.core, at.band
-    last = chips - 1
+    last, half = chips - 1, chips // 2
     group = 2 * pixels
+    band_rows = pixels // cols
+    spread = width // LANE
     number_of = {tap[:3]: number for number, tap in enumerate(taps)}
+    moved_levels = sorted({entry[0] for entry in extras})
+    late = sorted({entry[2] for entry in extras})
+    slots = moved_levels + [branch for branch in range(4) if branch not in moved_levels]
+    side = chip // half
+    is_end = (chip == 0) | (chip == last)
+    next_chip = lax.rem(chip + 1, chips)
+    prev_chip = lax.rem(chip + last, chips)
+    own = side * (half - 1)
+
+    def reserve(count):
+        first = post.used
+        post.used += count
+        return first
+
+    def hop(source, landing, device_chip, number):
+        return pltpu.make_async_remote_copy(
+            source,
+            landing,
+            send_sem.at[number],
+            recv_sem.at[number],
+            device_id={"space": device_chip * 2 + core},
+            device_id_type=MESH_ID,
+        )
+
+    def to_twin(source, landing, number):
+        return pltpu.make_async_remote_copy(
+            source,
+            landing,
+            send_sem.at[number],
+            recv_sem.at[number],
+            device_id=at.twin,
+            device_id_type=MESH_ID,
+        )
+
+    first_cot = reserve(half)
+
+    def send_cot(number):
+        return hop(cot_ref, cot.at[number], side * last, first_cot + number)
+
+    cot[pl.ds(own, 1)] = cot_ref[...][None]
+
+    @pl.when(jnp.logical_not(is_end))
+    def _():
+        send_cot(chip - side * half).start()
+
     for load in rate_loads:
         load.wait()
 
@@ -1323,153 +1229,141 @@
 
     extra[...] = jnp.zeros_like(extra)
     for level, target, source, row_tap in extras:
-        extra[level - 1, target] += forward_taps(rows_of(sh_ref, source), level, row_tap)
-
-    first_twin = post.used
-    post.used += chips
-
-    def twin_term(number):
-        return pltpu.make_async_remote_copy(
-            term.at[number, 1 - core],
-            twin_land.at[number],
-            send_sem.at[first_twin + number],
-            recv_sem.at[first_twin + number],
-            device_id=at.twin,
-            device_id_type=MESH_ID,
-        )
-
-
-    side = chip // (chips // 2)
+        extra[moved_levels.index(level), target // last] += forward_taps(
+            rows_of(sh_ref, source), level, row_tap
+        )
+
+    first_twin = reserve(4 * chips)
+
+    def twin_term(number, branch):
+        return to_twin(
+            term.at[number, 1 - core, branch],
+            twin_land.at[number, branch],
+            first_twin + 4 * number + branch,
+        )
 
     def forward_group(step, carry):
-        near = lax.rem(step, 2) * (step // 2) + (1 - lax.rem(step, 2)) * (last - step // 2)
-        number = near * (1 - side) + (last - near) * side
+        number = lax.rem(step + half * (1 - side), chips)
+        at_rim = jnp.where(lax.rem(number, last) == 0, 1.0, 0.0)
         source = rows_of(sh_ref, number)
-
-        def put(branch, value):
+        for branch in slots:
+            if branch == 0:
+                value = dot_nn(source, bw_ref[:, :width])
+            else:
+                value = forward_taps(source, branch, 1)
+                if branch in moved_levels:
+                    value = value + at_rim * extra[moved_levels.index(branch), number // last]
             value = value.astype(low)
             term[number, 0, branch] = value[:pixels]
             term[number, 1, branch] = value[pixels:]
-
-        put(0, dot_nn(source, bw_ref[:, :width]))
-        for level in (1, 2, 3):
-            total = forward_taps(source, level, 1)
-            if any(level == entry[0] for entry in extras):
-                total = total + extra[level - 1, number]
-            put(level, total)
-        twin_term(number).start()
+            twin_term(number, branch).start()
         return carry
 
-    lax.fori_loop(0, 1, forward_group, 0)
-
-    def hop(source, landing, device_chip, number):
-        return pltpu.make_async_remote_copy(
-            source,
-            landing,
-            send_sem.at[number],
-            recv_sem.at[number],
-            device_id={"space": device_chip * 2 + core},
-            device_id_type=MESH_ID,
-        )
-
-    base_right, base_left = post.used, post.used + chips
-    post.used += 2 * chips
-    next_chip = lax.rem(chip + 1, chips)
-    prev_chip = lax.rem(chip + last, chips)
-
-    def go_right(number):
-        return hop(twin_land.at[number], right_land.at[number], next_chip, base_right + number)
-
-    def go_left(number):
-        return hop(twin_land.at[number], left_land.at[number], prev_chip, base_left + number)
-
-    def start_off(number, copy):
-        twin_term(number).wait_recv()
-
-        def add(branch, carry):
-            twin_land[number, branch] = (
-                term[number, core, branch].astype(f32) + twin_land[number, branch].astype(f32)
-            ).astype(low)
-            return carry
-
-        lax.fori_loop(0, 4, add, 0)
+    first_right, first_left = reserve(8 * half), reserve(8 * half)
+    portion = pixels // 2
+
+    def rows_at(part):
+        return pl.ds(part * portion, portion)
+
+    def go_right(number, branch, part):
+        return hop(
+            twin_land.at[half + number, branch, rows_at(part)],
+            right_land.at[number, branch, rows_at(part)],
+            next_chip,
+            first_right + 8 * number + 2 * branch + part,
+        )
+
+    def go_left(number, branch, part):
+        return hop(
+            twin_land.at[number, branch, rows_at(part)],
+            left_land.at[number, branch, rows_at(part)],
+            prev_chip,
+            first_left + 8 * number + 2 * branch + part,
+        )
+
+    def both_cores(number, branch):
+        twin_term(number, branch).wait_recv()
+        return term[number, core, branch].astype(f32) + twin_land[number, branch].astype(f32)
+
+    def start_off(number, copy_of):
+        for branch in slots:
+            twin_land[number, branch] = both_cores(number, branch).astype(low)
+            for part in range(2):
+                copy_of(branch, part).start()
+
+    for number in range(half):
+        lax.fori_loop(number, number + 1, forward_group, 0)
+
+        @pl.when(chip == 0)
+        def _():
+            start_off(half + number, functools.partial(go_right, number))
+
+        @pl.when(chip == last)
+        def _():
+            start_off(number, functools.partial(go_left, number))
+
+    lax.fori_loop(half, chips, forward_group, 0)
+
+    def pass_on(number, branch, part, copy, landing):
+        if part == 0:
+            twin_term(number, branch).wait_recv()
+        copy.wait_recv()
+        rows = rows_at(part)
+        twin_land[number, branch, rows] = (
+            term[number, core, branch, rows].astype(f32)
+            + twin_land[number, branch, rows].astype(f32)
+            + landing[rows].astype(f32)
+        ).astype(low)
         copy.start()
 
-    def pass_on(number, copy, landing, has_incoming):
-
-        @pl.when(jnp.logical_not(has_incoming))
-        def _():
-            start_off(number, copy)
-
-        @pl.when(has_incoming)
-        def _():
-            twin_term(number).wait_recv()
-            copy.wait_recv()
-
-            def add(branch, carry):
-                twin_land[number, branch] = (
-                    term[number, core, branch].astype(f32)
-                    + twin_land[number, branch].astype(f32)
-                    + landing[number, branch].astype(f32)
-                ).astype(low)
-                return carry
-
-            lax.fori_loop(0, 4, add, 0)
-            copy.start()
-
-    @pl.when(chip == 0)
+    def pass_right(number, branch, part):
+        landing = right_land.at[number, branch]
+        pass_on(half + number, branch, part, go_right(number, branch, part), landing)
+
+    def pass_left(number, branch, part):
+        landing = left_land.at[number, branch]
+        pass_on(number, branch, part, go_left(number, branch, part), landing)
+
+    order = [
+        (number, branch, part) for number in range(half) for branch in slots for part in range(2)
+    ]
+
+    def pass_both(near, far):
+        for step in range(len(order) + FAR_LAG):
+            if step < len(order):
+                near(*order[step])
+            if step >= FAR_LAG:
+                far(*order[step - FAR_LAG])
+
+    @pl.when(jnp.logical_not(is_end) & (side == 0))
     def _():
-        start_off(last, go_right(last))
-
-    @pl.when(chip == last)
+        pass_both(pass_right, pass_left)
+
+    @pl.when(jnp.logical_not(is_end) & (side == 1))
     def _():
-        start_off(0, go_left(0))
-
-    lax.fori_loop(1, chips, forward_group, 0)
-
-    def pass_right(number):
-        there = (chip < number) if number < last else ((chip < number) & (chip > 0))
-
-        @pl.when(there)
-        def _():
-            pass_on(number, go_right(number), right_land, chip > 0)
-
-    def pass_left(number):
-        there = (chip > number) if number > 0 else ((chip > number) & (chip < last))
-
-        @pl.when(there)
-        def _():
-            pass_on(number, go_left(number), left_land, chip < last)
+        pass_both(pass_left, pass_right)
+
+    pixel_sum[...] = jnp.zeros_like(pixel_sum)
 
     def turn_group(number, carry):
         source = rows_of(sh_ref, number)
         turned[:, pl.ds(pl.multiple_of(number * group, group), group)] = source.T
-        return carry + jnp.sum(source.astype(f32), axis=0, keepdims=True)
-
-    pixel_sum = lax.fori_loop(0, chips, turn_group, jnp.zeros((1, width), f32))
-
-    @pl.when(chip < chips // 2)
-    def _():
-        for number in range(last):
-            pass_right(last - number)
-            pass_left(number)
-
-    @pl.when(chip >= chips // 2)
-    def _():
-        for number in range(last):
-            pass_left(number)
-            pass_right(last - number)
-
-    band_rows = pixels // cols
-    mask_own = row_mask(widths_ref, band * band_rows, band_rows, cols)
-    mask_own = jnp.concatenate([mask_own] * (width // LANE), axis=1)
-    inv_count = jnp.concatenate([1.0 / count_pixels(widths_ref)] * (width // LANE), axis=1)
-    spread = width // LANE
+        pixel_sum[0:1] += jnp.sum(source.astype(f32), axis=0, keepdims=True)
+        return carry
+
+    lax.fori_loop(0, chips, turn_group, 0)
+    inv_count = jnp.concatenate([1.0 / count_pixels(widths_ref)] * spread, axis=1)
 
     def put_rows(target, number, value):
         for part in range(spread):
             target[pl.ds(number * spread + part, 1), :] = value[:, part * LANE : (part + 1) * LANE]
 
+    def add_rows(target, number, value):
+        for part in range(spread):
+            target[pl.ds(number * spread + part, 1), :] += value[
+                :, part * LANE : (part + 1) * LANE
+            ]
+
     def get_rows(target, number):
         return jnp.concatenate(
             [target[pl.ds(number * spread + part, 1), :] for part in range(spread)], axis=1
@@ -1478,42 +1372,42 @@
     def column_sum(value):
         return jnp.sum(value, axis=0, keepdims=True)
 
-    twin_term(chip).wait_recv()
-
-    @pl.when(chip > 0)
-    def _():
-        go_right(chip).wait_recv()
-
-    @pl.when(chip < last)
-    def _():
-        go_left(chip).wait_recv()
+    def mask_of(number):
+        return jnp.concatenate([masks[number]] * spread, axis=1)
+
+    for target in (st_both, st_proj, st_pback, st_back):
+        target[...] = jnp.zeros_like(target)
+    for number in range(half):
+        masks[number] = row_mask(
+            widths_ref, (2 * (side * half + number) + core) * band_rows, band_rows, cols
+        )
+
+    def settle(copy_of, landing):
+        def step_of(step, carry):
+            number, branch = step // 4, lax.rem(step, 4)
+            total = both_cores(side * half + number, branch)
+            for part in range(2):
+                copy_of(number, branch, part).wait_recv()
+            value = total + landing[number, branch].astype(f32)
+            pre[number, branch] = value
+            kept = value * mask_of(number)
+            add_rows(st_both, branch, column_sum(kept))
+            add_rows(st_both, 4 + branch, column_sum(kept * value))
+            return carry
+
+        lax.fori_loop(0, 4 * half, step_of, 0)
 
     @pl.when(chip == 0)
     def _():
-        right_land[0] = jnp.zeros(right_land.shape[1:], low)
+        settle(go_left, left_land)
 
     @pl.when(chip == last)
     def _():
-        left_land[last] = jnp.zeros(left_land.shape[1:], low)
-
-    st_both[...] = jnp.zeros_like(st_both)
-
-    def settle(branch, carry):
-        value = (
-            term[chip, core, branch].astype(f32)
-            + twin_land[chip, branch].astype(f32)
-            + right_land[chip, branch].astype(f32)
-            + left_land[chip, branch].astype(f32)
-        )
-        pre[branch] = value
-        kept = value * mask_own
-        put_rows(st_both, branch, column_sum(kept))
-        put_rows(st_both, 4 + branch, column_sum(kept * value))
-        return carry
-
-    lax.fori_loop(0, 4, settle, 0)
-    high = pixel_sum.astype(low)
-    rest = pixel_sum - high.astype(f32)
+        settle(go_right, right_land)
+
+    sums_now = pixel_sum[0:1]
+    high = sums_now.astype(low)
+    rest = sums_now - high.astype(f32)
     middle = rest.astype(low)
     tail = (rest - middle.astype(f32)).astype(low)
     pieces = jnp.concatenate(
@@ -1532,144 +1426,216 @@
         variance = get_rows(target, second) * inv_count - mean_value * mean_value
         return mean_value, lax.rsqrt(variance + NORM_EPS)
 
-    def activate(branch, projected):
+    def at_ends(body, count):
+        @pl.when(is_end)
+        def _():
+            lax.fori_loop(0, count, body, 0)
+
+    pool_lanes = slice(4 * width, 5 * width)
+
+    def pool_step(number, carry):
+        joined[number, 4] = (
+            gelu_of(pooled).astype(low).astype(f32) * mask_of(number)
+        ).astype(low)
+        projected[number] = dot_nn(joined[number, 4], pw_ref[pool_lanes, :])
+        return carry
+
+    at_ends(pool_step, half)
+
+    def activate(step, carry):
+        number, branch = step // 4, lax.rem(step, 4)
         mean_value, inv_std = scale_of(st_both_sum, branch, 4 + branch)
-        hat = (pre[branch] - mean_value) * inv_std
-        pre[branch] = hat
+        hat = (pre[number, branch] - mean_value) * inv_std
+        pre[number, branch] = hat
         normed = gain_ref[:, lanes_of(branch)] * hat + shift_ref[:, lanes_of(branch)]
-        active = (gelu_of(normed) * mask_own).astype(low)
-        joined[branch] = active
-        return projected + dot_nn(active, pw_ref[lanes_of(branch), :])
-
-    joined[4] = (gelu_of(pooled).astype(low).astype(f32) * mask_own).astype(low)
-    projected = dot_nn(joined[4], pw_ref[4 * width : 5 * width, :])
-    projected = lax.fori_loop(0, 4, activate, projected)
-    kept = projected * mask_own
-    st_proj[...] = jnp.zeros_like(st_proj)
-    put_rows(st_proj, 0, column_sum(kept))
-    put_rows(st_proj, 1, column_sum(kept * projected))
+        active, slope = gelu_both(normed)
+        keep = mask_of(number)
+        active = (active * keep).astype(low)
+        upstream[number, branch] = slope * keep
+        joined[number, branch] = active
+        projected[number] += dot_nn(active, pw_ref[lanes_of(branch), :])
+        return carry
+
+    at_ends(activate, 4 * half)
+
+    def project_sums(number, carry):
+        value = projected[number]
+        kept = value * mask_of(number)
+        add_rows(st_proj, 0, column_sum(kept))
+        add_rows(st_proj, 1, column_sum(kept * value))
+        return carry
+
+    at_ends(project_sums, half)
     st_proj_sum[...] = at.sum_over(post, "space", st_proj, st_proj_land)
-    mean_value, inv_std = scale_of(st_proj_sum, 0, 1)
-    hat = (projected - mean_value) * inv_std
-    gain_proj = gain_ref[:, 4 * width : 5 * width]
-    normed = gain_proj * hat + shift_ref[:, 4 * width : 5 * width]
-    proj_up = gelu_slope(normed) * cot_ref[...].astype(f32) * mask_own
-    st_pback[...] = jnp.zeros_like(st_pback)
-    put_rows(st_pback, 0, column_sum(proj_up))
-    put_rows(st_pback, 1, column_sum(proj_up * hat))
+    proj_mean, proj_inv = scale_of(st_proj_sum, 0, 1)
+    gain_proj = gain_ref[:, pool_lanes]
+
+    def proj_back(number, carry):
+        hat = (projected[number] - proj_mean) * proj_inv
+        projected[number] = hat
+        normed = gain_proj * hat + shift_ref[:, pool_lanes]
+        keep = mask_of(number)
+        active, slope = gelu_both(normed)
+        up = slope * cot[number].astype(f32) * keep
+        proj_up[number] = up
+        add_rows(st_pback, 0, column_sum(up))
+        add_rows(st_pback, 1, column_sum(up * hat))
+        out_rows[number] = (active * keep).astype(low)
+        return carry
+
+    @pl.when(is_end)
+    def _():
+        for number in range(half):
+
+            @pl.when(own != number)
+            def _():
+                send_cot(number).wait_recv()
+
+    at_ends(proj_back, half)
     proj_sums_out[...] = at.sum_over(post, "space", st_pback, st_pback_land)
-    head_out[...] = (gelu_of(normed) * mask_own).astype(low)
-    shift_grad, gain_grad = get_rows(proj_sums_out, 0), get_rows(proj_sums_out, 1)
-    proj_low = (
-        mask_own
-        * (gain_proj * inv_std)
-        * (proj_up - shift_grad * inv_count - hat * (gain_grad * inv_count))
-    ).astype(low)
-    st_back[...] = jnp.zeros_like(st_back)
-
-    def back_step(branch, carry):
-        joined_grad = dot_nt(proj_low, pw_ref[lanes_of(branch), :])
-        hat = pre[branch]
-        normed = gain_ref[:, lanes_of(branch)] * hat + shift_ref[:, lanes_of(branch)]
-        up = gelu_slope(normed) * joined_grad * mask_own
-        upstream[branch] = up
-        put_rows(st_back, branch, column_sum(up))
-        put_rows(st_back, 4 + branch, column_sum(up * hat))
+    shift_proj, gain_grad_proj = get_rows(proj_sums_out, 0), get_rows(proj_sums_out, 1)
+
+    def proj_finish(number, carry):
+        keep = mask_of(number)
+        proj_low[number] = (
+            keep
+            * (gain_proj * proj_inv)
+            * (
+                proj_up[number]
+                - shift_proj * inv_count
+                - projected[number] * (gain_grad_proj * inv_count)
+            )
+        ).astype(low)
+        add_rows(
+            st_back, 8, column_sum(dot_nt(proj_low[number], pw_ref[pool_lanes, :]) * keep)
+        )
         return carry
 
-    lax.fori_loop(0, 4, back_step, 0)
-    pool_total = column_sum(dot_nt(proj_low, pw_ref[4 * width : 5 * width, :]) * mask_own)
-    put_rows(st_back, 8, pool_total)
+    at_ends(proj_finish, half)
+
+    def back_step(step, carry):
+        number, branch = step // 4, lax.rem(step, 4)
+        joined_grad = dot_nt(proj_low[number], pw_ref[lanes_of(branch), :])
+        hat = pre[number, branch]
+        up = upstream[number, branch] * joined_grad
+        upstream[number, branch] = up
+        add_rows(st_back, branch, column_sum(up))
+        add_rows(st_back, 4 + branch, column_sum(up * hat))
+        return carry
+
+    at_ends(back_step, 4 * half)
     both_sums_out[...] = at.sum_over(post, "space", st_back, st_back_land)
     pool_grad = (gelu_slope(pooled) * get_rows(both_sums_out, 8)).astype(low)
-    column = jnp.broadcast_to(pixel_sum, (8, width)).T[:, 0:1]
-    grads_out[len(taps) + 1] = (
-        column * (pool_grad.astype(f32) * inv_count)
-    ).astype(low)
-
-    def make_both(branch):
+
+    order = [(number, branch) for branch in moved_levels for number in range(half)]
+    order += [
+        (number, branch)
+        for number in range(half)
+        for branch in slots
+        if branch not in moved_levels
+    ]
+    first_right_all, first_left_all = reserve(8 * half), reserve(8 * half)
+    first_twin_all, first_out = reserve(8 * chips), reserve(half)
+
+    def block_of(number, branch, part):
+        return both_all.at[number * 2 + core, branch, rows_at(part)]
+
+    def along_right(number, branch, part):
+        block = block_of(number, branch, part)
+        return hop(block, block, next_chip, first_right_all + 8 * number + 2 * branch + part)
+
+    def along_left(number, branch, part):
+        block = block_of(half + number, branch, part)
+        return hop(block, block, prev_chip, first_left_all + 8 * number + 2 * branch + part)
+
+    def hand_over(number, branch, part):
+        block = block_of(number, branch, part)
+        return to_twin(block, block, first_twin_all + 8 * number + 2 * branch + part)
+
+    def make_both(number, branch):
         _, inv_std = scale_of(st_both_sum, branch, 4 + branch)
         shift_grad = get_rows(both_sums_out, branch) * inv_count
         gain_grad = get_rows(both_sums_out, 4 + branch) * inv_count
-        both_all[band, branch] = (
-            mask_own
+        mine = side * half + number
+        both_all[2 * mine + core, branch] = (
+            mask_of(number)
             * (gain_ref[:, lanes_of(branch)] * inv_std)
-            * (upstream[branch] - shift_grad - pre[branch] * gain_grad)
+            * (upstream[number, branch] - shift_grad - pre[number, branch] * gain_grad)
         ).astype(low)
 
-    moved_levels = sorted({entry[0] for entry in extras})
-    slots = moved_levels + [branch for branch in range(4) if branch not in moved_levels]
-    all_right = post.used
-    all_left = all_right + 4 * chips
-    all_twin = all_left + 4 * chips
-
-    def block_of(number, slot):
-        return both_all.at[number * 2 + core, slots[slot]]
-
-    def send_right(step, slot):
-        block = block_of(lax.rem(chip - step + 1 + chips, chips), slot)
-        return hop(block, block, next_chip, all_right + 4 * step + slot)
-
-    def send_left(step, slot):
-        block = block_of(lax.rem(chip + step - 1, chips), slot)
-        return hop(block, block, prev_chip, all_left + 4 * step + slot)
-
-    def hand_over(number, slot):
-        block = block_of(number, slot)
-        return pltpu.make_async_remote_copy(
-            block,
-            block,
-            send_sem.at[all_twin + 4 * number + slot],
-            recv_sem.at[all_twin + 4 * number + slot],
-            device_id=at.twin,
-            device_id_type=MESH_ID,
-        )
-
-    def from_left(step, slot):
-        block = block_of(lax.rem(chip - step + chips, chips), slot)
-        return hop(block, block, next_chip, all_right + 4 * step + slot)
-
-    def from_right(step, slot):
-        block = block_of(lax.rem(chip + step, chips), slot)
-        return hop(block, block, prev_chip, all_left + 4 * step + slot)
-
-    for slot in range(4):
-        make_both(slots[slot])
-
-        @pl.when(chip < last)
-        def _():
-            send_right(1, slot).start()
-
-        @pl.when(chip > 0)
-        def _():
-            send_left(1, slot).start()
-
-        hand_over(chip, slot).start()
+        for part in range(2):
+
+            @pl.when(chip == 0)
+            def _():
+                along_right(number, branch, part).start()
+
+            @pl.when(chip == last)
+            def _():
+                along_left(number, branch, part).start()
+
+            hand_over(mine, branch, part).start()
+
+    def send_out(number):
+        return hop(out_rows.at[number], head_out, side * half + number, first_out + number)
+
+    @pl.when(is_end)
+    def _():
+        for number, branch in order:
+            make_both(number, branch)
+        for number in range(half):
+
+            @pl.when(own != number)
+            def _():
+                send_out(number).start()
+
+        head_out[...] = out_rows[own]
 
     def proj_step(branch, carry):
-        proj_term[lanes_of(branch), :] = dot_nn(joined[branch].T, proj_low).astype(low)
+        total = dot_nn(joined[0, branch].T, proj_low[0])
+        for number in range(1, half):
+            total = total + dot_nn(joined[number, branch].T, proj_low[number])
+        proj_term[lanes_of(branch), :] = total.astype(low)
         return carry
 
-    lax.fori_loop(0, 5, proj_step, 0)
+    at_ends(proj_step, 5)
+
     rows_p = proj_share.shape[0]
 
     def proj_rows(number):
         return pl.ds(pl.multiple_of(number * rows_p, rows_p), rows_p)
 
-    post.used = all_twin + 4 * chips
-    p_pair = [
-        post.push(proj_term.at[proj_rows(2 * number + 1 - core)], p_twin.at[number], at.twin)
-        for number in range(chips)
-    ]
+    first_pair, first_p = reserve(chips), reserve(2 * chips)
+
+    def p_pair(number):
+        return to_twin(
+            proj_term.at[proj_rows(2 * number + 1 - core)], p_twin.at[number], first_pair + number
+        )
+
+    def p_hop(end, number):
+        return hop(p_twin.at[number], p_land.at[end], number, first_p + end * chips + number)
+
+    @pl.when(is_end)
+    def _():
+        for number in range(chips):
+            p_pair(number).start()
+
+    def send_projection():
+        for number in range(chips):
+            p_pair(number).wait_recv()
+            both = proj_term[proj_rows(2 * number + core)].astype(f32)
+            p_twin[number] = (both + p_twin[number].astype(f32)).astype(low)
+
+            @pl.when(chip != number)
+            def _():
+                p_hop(side, number).start()
+
     grads[...] = jnp.zeros_like(grads)
     pool_row = dot_nt(
         jnp.broadcast_to(pool_grad, (16, width)), bw_ref[:, width:]
     )[0:1] * inv_count
     quarter = pixels // tasks
     my_rows = pl.ds(pl.multiple_of(at.task * quarter, quarter), quarter)
-    late = sorted({entry[2] for entry in extras})
-    first_task = post.used
-    post.used += chips * len(at.other_tasks)
+    first_task = reserve(chips * len(at.other_tasks))
 
     def to_task(number, turn):
         other = at.other_tasks[turn]
@@ -1685,59 +1651,44 @@
             device_id_type=MESH_ID,
         )
 
-    def finish_group(number, total):
+    def finish_group(number):
         keep = row_mask(widths_ref, number * 2 * band_rows, 2 * band_rows, cols)
         keep = jnp.concatenate([keep] * spread, axis=1)
-        value = (total + keep * pool_row).astype(low)
+        value = (back[number] + keep * pool_row).astype(low)
         sg[2 * number] = value[:pixels]
         sg[2 * number + 1] = value[pixels:]
         for turn in range(len(at.other_tasks)):
             to_task(number, turn).start()
-        for half in range(2):
-            xg_out[at.task, 2 * number + half] = sg[2 * number + half, my_rows]
-
-    def back_slot(slot):
-        branch = slots[slot]
-
-        def step_of(step, carry):
-            number = group_at(step)
-            hand_over(number, slot).wait_recv()
-            columns = turned[:, pl.ds(pl.multiple_of(number * group, group), group)]
-            part = jnp.concatenate(
-                [both_all[2 * number, branch], both_all[2 * number + 1, branch]], axis=0
-            )
-            if branch == 0:
-                total = dot_nt(part, bw_ref[:, :width])
-                grads[len(taps)] += dot_nn(columns, part)
-            else:
-                total = None
-                image = part.astype(f32)
-                for col_tap in range(3):
-                    tap = number_of.get((branch, 1, col_tap))
-                    if tap is None:
-                        continue
-                    part = shift_pixels(image, -right_of(branch, col_tap), cols).astype(low)
-                    if branch in moved_levels:
-                        moved[moved_levels.index(branch), number, col_tap] = part
-                    term_now = dot_nt(part, rate[tap])
-                    total = term_now if total is None else total + term_now
-                    grads[tap] += dot_nn(columns, part)
-            if slot == 0:
-                back[number] = total
-            else:
-                back[number] += total
-            if slot == 3:
-                ready = number >= 0
-                for entry in late:
-                    ready = ready & (number != entry)
-
-                @pl.when(ready)
-                def _():
-                    finish_group(number, back[number])
-
-            return carry
-
-        return step_of
+        for part in range(2):
+            xg_out[at.task, 2 * number + part] = sg[2 * number + part, my_rows]
+
+    def back_part(number, branch):
+        for part in range(2):
+            hand_over(number, branch, part).wait_recv()
+        columns = turned[:, number * group : (number + 1) * group]
+        part = jnp.concatenate(
+            [both_all[2 * number, branch], both_all[2 * number + 1, branch]], axis=0
+        )
+        if branch == 0:
+            total = dot_nt(part, bw_ref[:, :width])
+            grads[len(taps)] += dot_nn(columns, part)
+        else:
+            total = None
+            image = part.astype(f32)
+            for col_tap in range(3):
+                tap = number_of.get((branch, 1, col_tap))
+                if tap is None:
+                    continue
+                part = shift_pixels(image, -right_of(branch, col_tap), cols).astype(low)
+                if branch in moved_levels and number in late:
+                    moved[moved_levels.index(branch), number // last, col_tap] = part
+                now = dot_nt(part, rate[tap])
+                total = now if total is None else total + now
+                grads[tap] += dot_nn(columns, part)
+        if branch == slots[0]:
+            back[number] = total
+        else:
+            back[number] += total
 
     def far_taps():
         for level, target, source, row_tap in extras:
@@ -1747,86 +1698,86 @@
                 tap = number_of.get((level, row_tap, col_tap))
                 if tap is None:
                     continue
-                part = moved[moved_levels.index(level), target, col_tap]
+                part = moved[moved_levels.index(level), target // last, col_tap]
                 total = total + dot_nt(part, rate[tap])
                 grads[tap] += dot_nn(columns, part)
             back[source] = total
 
-    def finish_late(early):
-        for number in late:
-            near_enough = (chip - number < last) & (number - chip < last)
-
-            @pl.when(near_enough if early else jnp.logical_not(near_enough))
+    def take_right(number, branch, part):
+        along_right(number, branch, part).wait_recv()
+
+        @pl.when(chip < last)
+        def _():
+            along_right(number, branch, part).start()
+
+        hand_over(number, branch, part).start()
+
+    def take_left(number, branch, part):
+        along_left(number, branch, part).wait_recv()
+
+        @pl.when(chip > 0)
+        def _():
+            along_left(number, branch, part).start()
+
+        hand_over(half + number, branch, part).start()
+
+    parts = [entry + (part,) for entry in order for part in range(2)]
+    for step in range(len(parts) + FAR_LAG + 1):
+        if step < len(parts):
+
+            @pl.when(jnp.logical_not(is_end) & (side == 0))
             def _():
-                finish_group(number, back[number])
-
-    mirror = chip // 2
-    near = chip * (1 - mirror) + (last - chip) * mirror
-
-    def group_at(step):
-        place = step + near * (1 - 2 * step) * ((last - step) // 2)
-        return place * (1 - mirror) + (last - place) * mirror
-
-    for slot in range(4):
-        lax.fori_loop(0, 1, back_slot(slot), 0)
-    done = 1
-    for step in range(1, chips):
-        upto = chips if step == last else step + 1 + near
-        for slot in range(4):
-
-            @pl.when(chip >= step)
+                take_right(*parts[step])
+
+            @pl.when(jnp.logical_not(is_end) & (side == 1))
             def _():
-                from_left(step, slot).wait_recv()
-                if step < last:
-
-                    @pl.when(chip < last)
-                    def _():
-                        send_right(step + 1, slot).start()
-
-                hand_over(lax.rem(chip - step + chips, chips), slot).start()
-
-            @pl.when(chip + step <= last)
+                take_left(*parts[step])
+
+        if FAR_LAG <= step < len(parts) + FAR_LAG:
+
+            @pl.when(side == 0)
             def _():
-                from_right(step, slot).wait_recv()
-                if step < last:
-
-                    @pl.when(chip > 0)
-                    def _():
-                        send_left(step + 1, slot).start()
-
-                hand_over(lax.rem(chip + step, chips), slot).start()
-
-            lax.fori_loop(done, upto, back_slot(slot), 0)
-            if step == last and slot == len(moved_levels) - 1:
+                take_left(*parts[step - FAR_LAG])
+
+            @pl.when(side == 1)
+            def _():
+                take_right(*parts[step - FAR_LAG])
+
+        if step == len(parts) + FAR_LAG:
+
+            @pl.when(is_end)
+            def _():
+                send_projection()
+
+        done = step - FAR_LAG - 2
+        if done >= 0 and done % 2 == 0:
+            number, branch = order[done // 2]
+            back_part(number, branch)
+            back_part(half + number, branch)
+            if done // 2 + 1 == half * len(moved_levels):
                 far_taps()
-                finish_late(True)
-        done = upto
-
-    for made in p_pair:
-        made.wait_recv()
-    p_in = []
-    for step in range(1, chips):
-        other = lax.rem(chip + step, chips)
-        both = proj_term[proj_rows(2 * other + core)].astype(f32) + p_twin[other].astype(f32)
-        p_twin[other] = both.astype(low)
-        p_in.append(
-            post.push(p_twin.at[other], p_land.at[chip], {"space": other * 2 + core})
-        )
-
-    finish_late(False)
+            if branch == slots[3]:
+                finish_group(number)
+                finish_group(half + number)
+    column = jnp.broadcast_to(pixel_sum[0:1], (8, width)).T[:, 0:1]
+    grads_out[len(taps) + 1] = (column * (pool_grad.astype(f32) * inv_count)).astype(low)
 
     def finish_tap(number, carry):
         grads_out[number] = grads[number].astype(low)
         return carry
 
     lax.fori_loop(0, len(taps) + 1, finish_tap, 0)
-
-    p_total = proj_term[proj_rows(band)].astype(f32) + p_twin[chip].astype(f32)
-    for made in p_in:
-        made.wait_recv()
-    for step in range(1, chips):
-        p_total = p_total + p_land[lax.rem(chip + step, chips)].astype(f32)
-    proj_share[...] = p_total.astype(low)
+    for end in range(2):
+
+        @pl.when(chip == end * last)
+        def _():
+            p_land[end] = p_twin[end * last]
+
+        @pl.when(chip != end * last)
+        def _():
+            p_hop(end, chip).wait_recv()
+
+    proj_share[...] = (p_land[0].astype(f32) + p_land[1].astype(f32)).astype(low)
 
     def tasks_in(number, carry):
         for turn in range(len(at.other_tasks)):
@@ -1835,37 +1786,54 @@
 
     lax.fori_loop(0, chips, tasks_in, 0)
 
+    @pl.when(jnp.logical_not(is_end))
+    def _():
+        send_out(chip - side * half).wait_recv()
+        send_cot(chip - side * half).wait_send()
+
     post.close()
 
     def twin_left(number, carry):
-        twin_term(number).wait_send()
-        for slot in range(4):
-            hand_over(number, slot).wait_send()
+        for branch in range(4):
+            twin_term(number, branch).wait_send()
+            for part in range(2):
+                hand_over(number, branch, part).wait_send()
         return carry
 
     lax.fori_loop(0, chips, twin_left, 0)
-    for number in range(last):
-        to_right, to_left = last - number, number
-
-        @pl.when(chip < to_right)
-        def _():
-            go_right(to_right).wait_send()
-
-        @pl.when(chip > to_left)
-        def _():
-            go_left(to_left).wait_send()
-
-    for step in range(1, chips):
-
-        @pl.when((chip < last) & (chip - step + 1 >= 0))
-        def _():
-            for slot in range(4):
-                send_right(step, slot).wait_send()
-
-        @pl.when((chip > 0) & (chip + step - 1 <= last))
-        def _():
-            for slot in range(4):
-                send_left(step, slot).wait_send()
+
+    def line_left(number, carry):
+        for branch in range(4):
+            for part in range(2):
+
+                @pl.when(chip < last)
+                def _():
+                    go_right(number, branch, part).wait_send()
+                    along_right(number, branch, part).wait_send()
+
+                @pl.when(chip > 0)
+                def _():
+                    go_left(number, branch, part).wait_send()
+                    along_left(number, branch, part).wait_send()
+
+        return carry
+
+    lax.fori_loop(0, half, line_left, 0)
+
+    @pl.when(is_end)
+    def _():
+        for number in range(half):
+
+            @pl.when(own != number)
+            def _():
+                send_out(number).wait_send()
+
+        for number in range(chips):
+            p_pair(number).wait_send()
+
+            @pl.when(chip != number)
+            def _():
+                p_hop(side, number).wait_send()
 
 
 def trunk_phase(
@@ -2097,6 +2065,7 @@
         quarters_in += to_tasks(lax.rem(band + bands - step, bands))
     for made in quarters_in + parts_in:
         made.wait_recv()
+    post.close()
 
     @pl.when(has_above)
     def _():
@@ -2107,7 +2076,21 @@
         down.wait_send()
 
 
-def front_kernel(sizes, plan, counts, *refs):
+class Held:
+    def __init__(self, shape, dtype, passing=False):
+        self.memory = pltpu.VMEM(shape, dtype)
+        self.passing = passing
+
+
+def with_phase(entries, refs, body):
+    def run(*passing):
+        passing, kept = list(passing), list(refs)
+        body([(passing if entry.passing else kept).pop(0) for entry in entries])
+
+    pl.run_scoped(run, *[entry.memory for entry in entries if entry.passing])
+
+
+def whole_kernel(sizes, plan, phases, counts, *refs):
     refs = list(refs)
 
     def take(count):
@@ -2117,14 +2100,23 @@
 
     x_hbm, widths, gain, shift, wr_hbm, wd_hbm, we_hbm = take(7)
     head_gain, head_shift, cot, bw, pw, rate_hbm = take(6)
-    trunk_hbm, head_hbm = take(9), take(6)
-    trunk_outs, head_outs = take(9), take(6)
-    (shared,), trunk_scratch, head_scratch = take(1), take(counts[0]), take(counts[1])
+    stats_hbm, head_hbm, grads_hbm, both_hbm, proj_hbm = take(5)
+    back_hbm = take(counts[2])
+    trunk_outs, head_outs = take(counts[0]), take(counts[1])
+    (shared,) = take(1)
+    kept = [take(sum(not entry.passing for entry in entries)) for entries in phases]
     send_sem, recv_sem, local_sem, rate_sem, out_sem = refs
     tasks, bands, width, taps = sizes[0], sizes[1], plan[4], plan[5]
     at = Place(tasks, bands)
     post = Post(send_sem, recv_sem)
-    rate = head_scratch[0]
+    writes = []
+
+    def write(source, target):
+        copy = pltpu.make_async_copy(source, target, out_sem.at[len(writes)])
+        copy.start()
+        writes.append(copy)
+
+    rate = kept[1][0]
     rate_loads = []
     for number, (level, row_tap, col_tap, _, _) in enumerate(taps):
         start = (9 * (level - 1) + 3 * row_tap + col_tap) * width
@@ -2138,53 +2130,90 @@
         for load in rate_loads:
             load.start()
 
-    trunk_phase(
-        at,
-        post,
-        sizes,
-        when_loaded,
-        x_hbm,
-        widths,
-        gain,
-        shift,
-        wr_hbm,
-        wd_hbm,
-        we_hbm,
-        shared,
-        *trunk_outs,
-        *trunk_scratch,
-        local_sem,
-    )
-    writes = []
-
-    def write(sources, targets):
-        for source, target in zip(sources, targets):
-            copy = pltpu.make_async_copy(source, target, out_sem.at[len(writes)])
-            copy.start()
-            writes.append(copy)
-
-    write(trunk_outs, trunk_hbm)
-    head_phase(
-        at,
-        post,
-        plan,
-        rate_loads,
-        shared,
-        widths,
-        head_gain,
-        head_shift,
-        cot,
-        bw,
-        pw,
-        *head_outs,
-        *head_scratch,
-    )
-    write(head_outs, head_hbm)
+    def run_trunk(scratch):
+        trunk_phase(
+            at,
+            post,
+            sizes,
+            when_loaded,
+            x_hbm,
+            widths,
+            gain,
+            shift,
+            wr_hbm,
+            wd_hbm,
+            we_hbm,
+            shared,
+            *trunk_outs,
+            *scratch,
+            local_sem,
+        )
+
+    def run_head(scratch):
+        head_phase(
+            at,
+            post,
+            plan,
+            rate_loads,
+            shared,
+            widths,
+            head_gain,
+            head_shift,
+            cot,
+            bw,
+            pw,
+            *head_outs,
+            *scratch,
+        )
+
+    with_phase(phases[0], kept[0], run_trunk)
+    act, h1, h2, a2, h3q, v1, v2, v3, stats = trunk_outs
+    write(stats, stats_hbm)
+    with_phase(phases[1], kept[1], run_head)
+    head_out, xg, grads_out, proj_share, both_sums, proj_sums = head_outs
+    for source, target in (
+        (head_out, head_hbm),
+        (grads_out, grads_hbm),
+        (both_sums, both_hbm),
+        (proj_sums, proj_hbm),
+    ):
+        write(source, target)
+
+    def run_back(scratch):
+        back_phase(
+            at,
+            post,
+            sizes,
+            local_sem,
+            xg,
+            h3q,
+            v3,
+            h2,
+            v2,
+            h1,
+            v1,
+            act,
+            a2,
+            proj_share,
+            x_hbm,
+            widths,
+            we_hbm,
+            wd_hbm,
+            wr_hbm,
+            write,
+            *back_hbm,
+            *scratch,
+        )
+        while len(writes) > before:
+            writes.pop().wait()
+
+    before = len(writes)
+    with_phase(phases[2], kept[2], run_back)
     for copy in writes:
         copy.wait()
 
 
-def front(tasks, bands, cols, rows, collective, x, widths, gain, shift, wr, wd, we, *head_in):
+def whole(tasks, bands, cols, rows, collective, x, widths, gain, shift, wr, wd, we, *head_in):
     low, f32 = jnp.bfloat16, jnp.float32
     head_gain, head_shift, cot, bw, pw, rate = head_in
     pixels, wide = x.shape
@@ -2204,66 +2233,154 @@
                     for target in range(chips)
                     if 0 <= target + away < chips
                 ]
-    levels = max([entry[0] for entry in extras], default=1)
+    levels = max(len({entry[0] for entry in extras}), 1)
     in_vmem = pl.BlockSpec(memory_space=pltpu.VMEM)
     anywhere = pl.BlockSpec(memory_space=pl.ANY)
     shape = jax.ShapeDtypeStruct
     block = (pixels, width)
     both_rows, proj_rows = -(-9 * width // LANE // 8) * 8, 8
 
-    def stats(count, lanes=LANE):
-        return [pltpu.VMEM((count, lanes), f32), pltpu.VMEM((bands, count, lanes), f32)]
+    part, narrow, broad = mid // bands, mid // tasks, wide // tasks
+    half = chips // 2
+    pool_rows = pw.shape[0] // bands
+    mid_rows, stat_wide = 2 * mid // LANE, wide // 4
+
+    def kept(dims, dtype=low):
+        return Held(tuple(dims), dtype)
+
+    def passing(dims, dtype=low):
+        return Held(tuple(dims), dtype, True)
+
+    def over_bands(count, lanes=LANE):
+        return [kept((count, lanes), f32), kept((bands, count, lanes), f32)]
+
+    def over_all(count, lanes=LANE):
+        return [kept((count, lanes), f32), kept((tasks, count, lanes), f32)] + over_bands(
+            count, lanes
+        )
+
+    def terms(*dims):
+        return [
+            kept((2, chips) + dims),
+            kept((chips,) + dims),
+            kept((chips,) + dims),
+            kept(dims),
+            kept((tasks,) + dims),
+        ]
 
     trunk_scratch = (
         [
-            pltpu.VMEM(x.shape, low),
-            pltpu.VMEM(wr.shape, low),
-            pltpu.VMEM(wd.shape, low),
-            pltpu.VMEM(we.shape, low),
-            pltpu.VMEM((3, pixels, mid), low),
-            pltpu.VMEM((mid, pixels), low),
-            pltpu.VMEM((pixels, wide), f32),
-            pltpu.VMEM((bands, quarter, piece), low),
-            pltpu.VMEM((pixels, LANE), f32),
+            passing(x.shape),
+            passing(wr.shape),
+            passing(wd.shape),
+            passing(we.shape),
+            kept((3, pixels, mid)),
+            kept((mid, pixels)),
+            passing((pixels, wide), f32),
+            kept((bands, quarter, piece)),
+            passing((pixels, LANE), f32),
         ]
-        + stats(2 * mid // LANE)
-        + stats(2 * mid // LANE)
-        + stats(8, wide // 4)
+        + over_bands(mid_rows)
+        + over_bands(mid_rows)
+        + over_bands(8, stat_wide)
     )
     head_scratch = (
         [
-            pltpu.VMEM((len(taps), piece, width), low),
-            pltpu.VMEM((piece, bands * pixels), low),
-            pltpu.VMEM((levels, chips, 2 * pixels, width), f32),
-            pltpu.VMEM((chips, 2, 4) + block, low),
-            pltpu.VMEM((chips, 4) + block, low),
-            pltpu.VMEM((chips, 4) + block, low),
-            pltpu.VMEM((chips, 4) + block, low),
-            pltpu.VMEM((4,) + block, f32),
-            pltpu.VMEM((5,) + block, low),
-            pltpu.VMEM((4,) + block, f32),
+            kept((len(taps), piece, width)),
+            passing((piece, bands * pixels)),
+            passing((levels, 2, 2 * pixels, width), f32),
+            passing((chips, 2, 4) + block),
+            kept((chips, 4) + block),
+            kept((half, 4) + block),
+            kept((half, 4) + block),
+            passing((half, 4) + block, f32),
+            passing((half, 5) + block),
+            passing((half, 4) + block, f32),
+            kept((half,) + block),
+            passing((half,) + block),
+            passing((half, pixels, LANE), f32),
+            passing((half,) + block, f32),
+            passing((half,) + block, f32),
+            passing((half,) + block),
+            passing((8, piece), f32),
+            kept((both_rows, LANE), f32),
         ]
-        + [pltpu.VMEM((both_rows, LANE), f32)]
-        + stats(both_rows)
-        + [pltpu.VMEM((proj_rows, LANE), f32)]
-        + stats(proj_rows)
-        + stats(proj_rows)
-        + stats(both_rows)
+        + over_bands(both_rows)
+        + [kept((proj_rows, LANE), f32)]
+        + over_bands(proj_rows)
+        + over_bands(proj_rows)
+        + over_bands(both_rows)
         + [
-            pltpu.VMEM((bands, 4) + block, low),
-            pltpu.VMEM((levels, chips, 3, 2 * pixels, width), low),
-            pltpu.VMEM((len(taps) + 1, piece, width), f32),
-            pltpu.VMEM((chips, 2 * pixels, width), f32),
-            pltpu.VMEM((bands, pixels, piece), low),
-            pltpu.VMEM(pw.shape, low),
-            pltpu.VMEM((chips, pw.shape[0] // bands, width), low),
-            pltpu.VMEM((chips, pw.shape[0] // bands, width), low),
+            kept((bands, 4) + block),
+            passing((levels, 2, 3, 2 * pixels, width)),
+            passing((len(taps) + 1, piece, width), f32),
+            passing((chips, 2 * pixels, width), f32),
+            passing((bands, pixels, piece)),
+            passing(pw.shape),
+            kept((chips, pool_rows, width)),
+            kept((2, pool_rows, width)),
         ]
+    )
+    back_outs = (
+        shape((8, LANE), f32),
+        shape((pixels, wide), low),
+        shape((piece, mid), f32),
+        shape((9, part, mid), f32),
+        shape((part, wide), f32),
+        shape((8, stat_wide), f32),
+        shape((mid_rows, LANE), f32),
+        shape((mid_rows, LANE), f32),
+        shape((bands, pool_rows, width), low),
+    )
+    back_scratch = (
+        [kept(out.shape, out.dtype) for out in back_outs]
+        + [
+            passing(we.shape),
+            passing(wd.shape),
+            passing(wr.shape),
+            passing(x.shape),
+            passing((pixels, LANE), f32),
+        ]
+        + over_all(16)
+        + [
+            kept((bands, quarter, piece)),
+            kept((bands, quarter, piece)),
+            passing((bands, quarter, piece), f32),
+            passing((bands, quarter, piece), f32),
+            kept((bands, quarter, piece)),
+            kept((tasks, bands, quarter, piece)),
+        ]
+        + over_all(8, stat_wide)
+        + [
+            kept((bands, quarter, piece)),
+            kept((tasks, bands // tasks, quarter, piece)),
+        ]
+        + over_all(mid_rows)
+        + [
+            kept((pixels, mid)),
+            kept((2, pixels, mid)),
+            passing((pixels, mid), f32),
+        ]
+        + over_bands(mid_rows)
+        + [
+            passing((pixels, mid)),
+            passing((wide, pixels)),
+            passing((mid, pixels)),
+        ]
+        + terms(part, broad)
+        + [
+            kept((bands, pixels, narrow)),
+            passing((3, 3 * part, narrow), f32),
+            kept((9, part, narrow)),
+            kept((tasks, 9, part, narrow)),
+        ]
+        + terms(piece, narrow)
+        + [kept((bands, pool_rows, width))]
     )
     sizes = (tasks, bands, cols, quarter, mid, wide, piece)
     plan = (tasks, bands, cols, pixels, width, tuple(taps), tuple(extras))
-    out_shapes = (
-        shape((bands + 2, mid // bands, pixels), low),
+    trunk_outs = (
+        shape((bands + 2, part, pixels), low),
         shape((pixels, mid), f32),
         shape((pixels, mid), f32),
         shape((pixels, mid), low),
@@ -2272,29 +2389,35 @@
         shape((8, mid), f32),
         shape((8, wide), f32),
         shape((2, 2 * mid + wide), f32),
+    )
+    head_outs = (
         shape(block, low),
         shape((tasks, bands, quarter, piece), low),
         shape((len(taps) + 2, piece, width), low),
-        shape((pw.shape[0] // bands, width), low),
+        shape((pool_rows, width), low),
         shape((both_rows, LANE), f32),
         shape((proj_rows, LANE), f32),
     )
+    out_shapes = (trunk_outs[8], head_outs[0], head_outs[2], head_outs[4], head_outs[5])
+    out_shapes += back_outs
+    phases = (trunk_scratch, head_scratch, back_scratch)
     return taps, pl.pallas_call(
-        functools.partial(front_kernel, sizes, plan, (len(trunk_scratch), len(head_scratch))),
-        name="front",
+        functools.partial(
+            whole_kernel, sizes, plan, phases, (len(trunk_outs), len(head_outs), len(back_outs))
+        ),
+        name="whole",
         out_shape=out_shapes,
         in_specs=[anywhere, pl.BlockSpec(memory_space=pltpu.SMEM), in_vmem, in_vmem]
         + [anywhere] * 3
         + [in_vmem] * 5
         + [anywhere],
         out_specs=(anywhere,) * len(out_shapes),
-        scratch_shapes=[pltpu.VMEM(out.shape, out.dtype) for out in out_shapes]
+        scratch_shapes=[pltpu.VMEM(out.shape, out.dtype) for out in trunk_outs + head_outs]
         + [pltpu.VMEM((bands, pixels, piece), low)]
-        + trunk_scratch
-        + head_scratch
+        + [entry.memory for entries in phases for entry in entries if not entry.passing]
         + [
-            pltpu.SemaphoreType.DMA((192,)),
-            pltpu.SemaphoreType.DMA((192,)),
+            pltpu.SemaphoreType.DMA((352,)),
+            pltpu.SemaphoreType.DMA((352,)),
             pltpu.SemaphoreType.DMA((4,)),
             pltpu.SemaphoreType.DMA((len(taps),)),
             pltpu.SemaphoreType.DMA((len(out_shapes),)),
@@ -2524,22 +2647,21 @@
     inputs = features.reshape(pixels, in_width)
     dilated = w_dilated.transpose(1, 0, 2)
     taps, (
-        act,
-        h1,
-        h2,
-        a2,
-        h3q,
-        v1,
-        v2,
-        v3,
         batch_stats,
         head_out,
-        task_grads,
         tap_grads,
-        proj_share,
         both_sums,
         proj_sums,
-    ) = front(
+        weight_rows,
+        input_grad,
+        reduce_grad,
+        dilated_grad,
+        expand_grad,
+        sums_three,
+        sums_two,
+        sums_one,
+        proj_grad,
+    ) = whole(
         tasks,
         bands,
         cols,
@@ -2558,37 +2680,6 @@
         branch_weight[0],
         proj_weight[0],
         rate_weight[0],
-    )
-    (
-        weight_rows,
-        input_grad,
-        reduce_grad,
-        dilated_grad,
-        expand_grad,
-        sums_three,
-        sums_two,
-        sums_one,
-        proj_grad,
-    ) = trunk_back(
-        tasks,
-        bands,
-        cols,
-        1,
-        task_grads,
-        h3q,
-        inputs,
-        v3,
-        h2,
-        v2,
-        h1,
-        v1,
-        act,
-        a2,
-        row_width,
-        w_expand,
-        dilated,
-        w_reduce,
-        proj_share,
     )
     place_of = {tap[:3]: number for number, tap in enumerate(taps)}
     places = tuple(

time: 237 us -> 226 us (0.954)
  Pallas kernels: 233 us -> 221 us
    pallas_call x2 -> x1, Pallas kernels: 226 us -> 214 us  [whole(): pl.pallas_call(functools.partial(whole_kernel, sizes, plan, phases, (len(...]
where the time goes in v5:
time: 226 us; the launch traced here: 222 us
  Pallas kernels  221 us (98%)
    pallas_call x1, Pallas kernels, whole(): pl.pallas_call(functools.partial(whole_kernel, sizes, plan, phases, (len(...  214 us
    pallas_call x1, Pallas kernels, finish(): pl.pallas_call(functools.partial(finish_kernel, places), name='finish', o...  7.17 us

profile of v5, /device:TPU:13, one launch (start us, length us, event | category | flops | bytes accessed | tf_op | source)
XLA Modules:
  0.0 222.3 jit_solution(2207778470315537589)
XLA Ops:
  0.7 214.3 %whole.1 = (f32[2,3072]{1,0:T(2,128)}, bf16[256,256]{1,0:T(8,128)(2,1)}, bf16[17,256,256]{2,1,0:T(8,128)(2,1)}, f32[24,128]{1,0:T(8,128)}, f32[8,128]{1,0:T(8,12...) custom-call(bf16[256,2048]{1,0:T(8,128)(2,1)} %bitcast.20, ...), custom_call_target="tpu_custom_call" | custom-call | tf_op jit(solution)/shard_map/whole/pallas_call | solution.py:2404
  214.9 7.2 %finish.1 = (bf16[256,256]{1,0:T(8,128)(2,1)}, bf16[256,2048]{1,0:T(8,128)(2,1)}, f32[256,512]{1,0:T(8,128)}, f32[9,64,512]{2,1,0:T(8,128)}, f32[64,2048]{1,0:T(...) custom-call(bf16[17,256,256]{2,1,0:T(8,128)(2,1)} %get-tuple-element, ...), custom_call_target="tpu_custom_call" | custom-call | tf_op jit(solution)/shard_map/finish/pallas_call | solution.py:2582

commit v6 on v5

--- a/solution.py
+++ b/solution.py
@@ -430,7 +430,8 @@
 LANE = 128
 
 
-FAR_LAG = 3
+FAR_LAG = 2
+SEND_LAG = 0
 GELU_A = 0.7978845608028654
 GELU_B = 0.044715
 
@@ -1143,6 +1144,9 @@
     st_pback_land,
     st_back,
     st_back_land,
+    st_rim_sum,
+    st_rim,
+    st_rim_land,
     both_all,
     moved,
     grads,
@@ -1200,14 +1204,13 @@
     def send_cot(number):
         return hop(cot_ref, cot.at[number], side * last, first_cot + number)
 
+    for load in rate_loads:
+        load.wait()
     cot[pl.ds(own, 1)] = cot_ref[...][None]
 
     @pl.when(jnp.logical_not(is_end))
     def _():
         send_cot(chip - side * half).start()
-
-    for load in rate_loads:
-        load.wait()
 
     def rows_of(ref, number):
         return jnp.concatenate([ref[2 * number], ref[2 * number + 1]], axis=0)
@@ -1375,7 +1378,7 @@
     def mask_of(number):
         return jnp.concatenate([masks[number]] * spread, axis=1)
 
-    for target in (st_both, st_proj, st_pback, st_back):
+    for target in (st_both, st_proj, st_pback, st_back, st_rim):
         target[...] = jnp.zeros_like(target)
     for number in range(half):
         masks[number] = row_mask(
@@ -1506,26 +1509,37 @@
                 - projected[number] * (gain_grad_proj * inv_count)
             )
         ).astype(low)
-        add_rows(
-            st_back, 8, column_sum(dot_nt(proj_low[number], pw_ref[pool_lanes, :]) * keep)
-        )
         return carry
 
+    def pool_back(number, carry):
+        joined_grad = dot_nt(proj_low[number], pw_ref[pool_lanes, :])
+        add_rows(st_back, 8, column_sum(joined_grad * mask_of(number)))
+        return carry
+
+    def back_step(branch):
+        def step_of(number, carry):
+            joined_grad = dot_nt(proj_low[number], pw_ref[lanes_of(branch), :])
+            hat = pre[number, branch]
+            up = upstream[number, branch] * joined_grad
+            upstream[number, branch] = up
+            shift_sum, gain_sum = column_sum(up), column_sum(up * hat)
+            add_rows(st_back, branch, shift_sum)
+            add_rows(st_back, 4 + branch, gain_sum)
+            if branch == slots[0]:
+                add_rows(st_rim, 0, shift_sum)
+                add_rows(st_rim, 1, gain_sum)
+            return carry
+
+        return step_of
+
     at_ends(proj_finish, half)
-
-    def back_step(step, carry):
-        number, branch = step // 4, lax.rem(step, 4)
-        joined_grad = dot_nt(proj_low[number], pw_ref[lanes_of(branch), :])
-        hat = pre[number, branch]
-        up = upstream[number, branch] * joined_grad
-        upstream[number, branch] = up
-        add_rows(st_back, branch, column_sum(up))
-        add_rows(st_back, 4 + branch, column_sum(up * hat))
-        return carry
-
-    at_ends(back_step, 4 * half)
-    both_sums_out[...] = at.sum_over(post, "space", st_back, st_back_land)
-    pool_grad = (gelu_slope(pooled) * get_rows(both_sums_out, 8)).astype(low)
+    at_ends(back_step(slots[0]), half)
+    begun_rim = at.sum_begin(post, "space", st_rim, st_rim_land)
+    at_ends(pool_back, half)
+    for branch in slots[1:]:
+        at_ends(back_step(branch), half)
+    begun_back = at.sum_begin(post, "space", st_back, st_back_land)
+    st_rim_sum[...] = at.sum_end(begun_rim)
 
     order = [(number, branch) for branch in moved_levels for number in range(half)]
     order += [
@@ -1554,34 +1568,52 @@
 
     def make_both(number, branch):
         _, inv_std = scale_of(st_both_sum, branch, 4 + branch)
-        shift_grad = get_rows(both_sums_out, branch) * inv_count
-        gain_grad = get_rows(both_sums_out, 4 + branch) * inv_count
-        mine = side * half + number
-        both_all[2 * mine + core, branch] = (
+        if branch == slots[0]:
+            sums = get_rows(st_rim_sum, 0), get_rows(st_rim_sum, 1)
+        else:
+            sums = get_rows(both_sums_out, branch), get_rows(both_sums_out, 4 + branch)
+        shift_grad, gain_grad = sums[0] * inv_count, sums[1] * inv_count
+        both_all[2 * (side * half + number) + core, branch] = (
             mask_of(number)
             * (gain_ref[:, lanes_of(branch)] * inv_std)
             * (upstream[number, branch] - shift_grad - pre[number, branch] * gain_grad)
         ).astype(low)
 
-        for part in range(2):
+    parts = [(number, branch, part) for number, branch in order for part in range(2)]
+    by_halves = [entry for entry in order[half:] if entry[0] == half - 1]
+    parts = parts[: -2 * len(by_halves)]
+    parts += [entry + (part,) for part in range(2) for entry in by_halves]
+
+    def send_out(number):
+        return hop(out_rows.at[number], head_out, side * half + number, first_out + number)
+
+    def send_parts(some):
+        made = set()
+        for number, branch, part in some:
+            if (number, branch) not in made:
+                make_both(number, branch)
+                made.add((number, branch))
 
             @pl.when(chip == 0)
             def _():
                 along_right(number, branch, part).start()
+                hand_over(number, branch, part).start()
 
             @pl.when(chip == last)
             def _():
-                along_left(number, branch, part).start()
-
-            hand_over(mine, branch, part).start()
-
-    def send_out(number):
-        return hop(out_rows.at[number], head_out, side * half + number, first_out + number)
+                along_left(number, branch, 1 - part).start()
+                hand_over(half + number, branch, 1 - part).start()
 
     @pl.when(is_end)
     def _():
-        for number, branch in order:
-            make_both(number, branch)
+        send_parts([entry for entry in parts if entry[1] == slots[0]])
+
+    both_sums_out[...] = at.sum_end(begun_back)
+    pool_grad = (gelu_slope(pooled) * get_rows(both_sums_out, 8)).astype(low)
+
+    @pl.when(is_end)
+    def _():
+        send_parts([entry for entry in parts if entry[1] != slots[0]])
         for number in range(half):
 
             @pl.when(own != number)
@@ -1651,44 +1683,64 @@
             device_id_type=MESH_ID,
         )
 
-    def finish_group(number):
-        keep = row_mask(widths_ref, number * 2 * band_rows, 2 * band_rows, cols)
-        keep = jnp.concatenate([keep] * spread, axis=1)
-        value = (back[number] + keep * pool_row).astype(low)
-        sg[2 * number] = value[:pixels]
-        sg[2 * number + 1] = value[pixels:]
-        for turn in range(len(at.other_tasks)):
-            to_task(number, turn).start()
-        for part in range(2):
-            xg_out[at.task, 2 * number + part] = sg[2 * number + part, my_rows]
-
-    def back_part(number, branch):
-        for part in range(2):
-            hand_over(number, branch, part).wait_recv()
-        columns = turned[:, number * group : (number + 1) * group]
-        part = jnp.concatenate(
-            [both_all[2 * number, branch], both_all[2 * number + 1, branch]], axis=0
+    def finish_group(number, part=None):
+        some = band_rows if part is None else band_rows // 2
+        for place in range(2):
+            first = (2 * number + place) * band_rows + (0 if part is None else part * some)
+            keep = row_mask(widths_ref, first, some, cols)
+            keep = jnp.concatenate([keep] * spread, axis=1)
+            start = 0 if part is None else part * portion
+            rows = slice(start, start + some * cols)
+            value = back[number, place * pixels + start : place * pixels + start + some * cols]
+            sg[2 * number + place, rows] = (value + keep * pool_row).astype(low)
+
+        def there(task):
+            return task >= 0 if part is None else task // (tasks // 2) == part
+
+        for turn, other in enumerate(at.other_tasks):
+
+            @pl.when(there(other))
+            def _():
+                to_task(number, turn).start()
+
+        @pl.when(there(at.task))
+        def _():
+            for place in range(2):
+                xg_out[at.task, 2 * number + place] = sg[2 * number + place, my_rows]
+
+    def back_part(number, branch, part=None):
+        for piece in range(2) if part is None else (part,):
+            hand_over(number, branch, piece).wait_recv()
+        rows = slice(0, pixels) if part is None else slice(part * portion, (part + 1) * portion)
+        count = rows.stop - rows.start
+        starts = [(2 * number + place) * pixels + rows.start for place in range(2)]
+        columns = jnp.concatenate([turned[:, start : start + count] for start in starts], axis=1)
+        image = jnp.concatenate(
+            [both_all[2 * number, branch, rows], both_all[2 * number + 1, branch, rows]], axis=0
         )
         if branch == 0:
-            total = dot_nt(part, bw_ref[:, :width])
-            grads[len(taps)] += dot_nn(columns, part)
+            total = dot_nt(image, bw_ref[:, :width])
+            grads[len(taps)] += dot_nn(columns, image)
         else:
             total = None
-            image = part.astype(f32)
+            image = image.astype(f32)
             for col_tap in range(3):
                 tap = number_of.get((branch, 1, col_tap))
                 if tap is None:
                     continue
-                part = shift_pixels(image, -right_of(branch, col_tap), cols).astype(low)
+                moved_now = shift_pixels(image, -right_of(branch, col_tap), cols).astype(low)
                 if branch in moved_levels and number in late:
-                    moved[moved_levels.index(branch), number // last, col_tap] = part
-                now = dot_nt(part, rate[tap])
+                    moved[moved_levels.index(branch), number // last, col_tap] = moved_now
+                now = dot_nt(moved_now, rate[tap])
                 total = now if total is None else total + now
-                grads[tap] += dot_nn(columns, part)
-        if branch == slots[0]:
-            back[number] = total
-        else:
-            back[number] += total
+                grads[tap] += dot_nn(columns, moved_now)
+        for place in range(2):
+            target = slice(place * pixels + rows.start, place * pixels + rows.stop)
+            share = total[place * count : (place + 1) * count]
+            if branch == slots[0]:
+                back[number, target] = share
+            else:
+                back[number, target] += share
 
     def far_taps():
         for level, target, source, row_tap in extras:
@@ -1721,44 +1773,54 @@
 
         hand_over(half + number, branch, part).start()
 
-    parts = [entry + (part,) for entry in order for part in range(2)]
     for step in range(len(parts) + FAR_LAG + 1):
         if step < len(parts):
+            number, branch, part = parts[step]
 
             @pl.when(jnp.logical_not(is_end) & (side == 0))
             def _():
-                take_right(*parts[step])
+                take_right(number, branch, part)
 
             @pl.when(jnp.logical_not(is_end) & (side == 1))
             def _():
-                take_left(*parts[step])
+                take_left(number, branch, 1 - part)
 
         if FAR_LAG <= step < len(parts) + FAR_LAG:
+            number, branch, part = parts[step - FAR_LAG]
 
             @pl.when(side == 0)
             def _():
-                take_left(*parts[step - FAR_LAG])
+                take_left(number, branch, 1 - part)
 
             @pl.when(side == 1)
             def _():
-                take_right(*parts[step - FAR_LAG])
-
-        if step == len(parts) + FAR_LAG:
+                take_right(number, branch, part)
+
+        if step == len(parts) + SEND_LAG:
 
             @pl.when(is_end)
             def _():
                 send_projection()
 
-        done = step - FAR_LAG - 2
-        if done >= 0 and done % 2 == 0:
-            number, branch = order[done // 2]
+        done = step - FAR_LAG - 1
+        if done < 0:
+            continue
+        number, branch, part = parts[done]
+        if (number, branch) in by_halves:
+            back_part(number, branch, part)
+            back_part(half + number, branch, 1 - part)
+            if (number, branch) == by_halves[-1]:
+                finish_group(number, part)
+                finish_group(half + number, 1 - part)
+        elif part == 1:
             back_part(number, branch)
             back_part(half + number, branch)
-            if done // 2 + 1 == half * len(moved_levels):
+            if (number, branch) == order[half - 1]:
                 far_taps()
             if branch == slots[3]:
                 finish_group(number)
                 finish_group(half + number)
+
     column = jnp.broadcast_to(pixel_sum[0:1], (8, width)).T[:, 0:1]
     grads_out[len(taps) + 1] = (column * (pool_grad.astype(f32) * inv_count)).astype(low)
 
@@ -1841,6 +1903,7 @@
     post,
     sizes,
     when_loaded,
+    norm_loads,
     x_hbm,
     widths_ref,
     gain_ref,
@@ -1933,11 +1996,14 @@
         load.wait()
     for load in loads[2:]:
         load.start()
-    when_loaded()
     h1[...] = dot_nn(x[...], wr[...])
     at.meet()
     put_sums(st1, h1[...], mask_mid)
-    first, second = get_sums(at.sum_over(post, "space", st1, st1_land))
+    begun = at.sum_begin(post, "space", st1, st1_land)
+    for load in norm_loads:
+        load.wait()
+    first, second = get_sums(at.sum_end(begun))
+    when_loaded()
     put_norm(v1, slice(0, mid), first, second, 0)
     rim[1] = activate(h1[...], v1, mask_mid)
 
@@ -2098,14 +2164,17 @@
         del refs[:count]
         return taken
 
-    x_hbm, widths, gain, shift, wr_hbm, wd_hbm, we_hbm = take(7)
-    head_gain, head_shift, cot, bw, pw, rate_hbm = take(6)
+    x_hbm, widths, gain_hbm, shift_hbm, wr_hbm, wd_hbm, we_hbm = take(7)
+    head_hbm_in = take(5)
+    (rate_hbm,) = take(1)
     stats_hbm, head_hbm, grads_hbm, both_hbm, proj_hbm = take(5)
     back_hbm = take(counts[2])
     trunk_outs, head_outs = take(counts[0]), take(counts[1])
+    gain, shift, *head_in = take(7)
+    head_gain, head_shift, cot, bw, pw = head_in
     (shared,) = take(1)
     kept = [take(sum(not entry.passing for entry in entries)) for entries in phases]
-    send_sem, recv_sem, local_sem, rate_sem, out_sem = refs
+    send_sem, recv_sem, local_sem, rate_sem, out_sem, in_sem = refs
     tasks, bands, width, taps = sizes[0], sizes[1], plan[4], plan[5]
     at = Place(tasks, bands)
     post = Post(send_sem, recv_sem)
@@ -2126,6 +2195,17 @@
             )
         )
 
+    norm_loads = [
+        pltpu.make_async_copy(source, target, in_sem.at[number])
+        for number, (source, target) in enumerate(((gain_hbm, gain), (shift_hbm, shift)))
+    ]
+    for load in norm_loads:
+        load.start()
+    rate_loads += [
+        pltpu.make_async_copy(source, target, in_sem.at[2 + number])
+        for number, (source, target) in enumerate(zip(head_hbm_in, head_in))
+    ]
+
     def when_loaded():
         for load in rate_loads:
             load.start()
@@ -2136,6 +2216,7 @@
             post,
             sizes,
             when_loaded,
+            norm_loads,
             x_hbm,
             widths,
             gain,
@@ -2234,7 +2315,6 @@
                     if 0 <= target + away < chips
                 ]
     levels = max(len({entry[0] for entry in extras}), 1)
-    in_vmem = pl.BlockSpec(memory_space=pltpu.VMEM)
     anywhere = pl.BlockSpec(memory_space=pl.ANY)
     shape = jax.ShapeDtypeStruct
     block = (pixels, width)
@@ -2310,6 +2390,8 @@
         + over_bands(proj_rows)
         + over_bands(proj_rows)
         + over_bands(both_rows)
+        + [kept((proj_rows, LANE), f32)]
+        + over_bands(proj_rows)
         + [
             kept((bands, 4) + block),
             passing((levels, 2, 3, 2 * pixels, width)),
@@ -2407,12 +2489,13 @@
         ),
         name="whole",
         out_shape=out_shapes,
-        in_specs=[anywhere, pl.BlockSpec(memory_space=pltpu.SMEM), in_vmem, in_vmem]
-        + [anywhere] * 3
-        + [in_vmem] * 5
-        + [anywhere],
+        in_specs=[anywhere, pl.BlockSpec(memory_space=pltpu.SMEM)] + [anywhere] * 11,
         out_specs=(anywhere,) * len(out_shapes),
         scratch_shapes=[pltpu.VMEM(out.shape, out.dtype) for out in trunk_outs + head_outs]
+        + [
+            pltpu.VMEM(value.shape, value.dtype)
+            for value in (gain, shift, head_gain, head_shift, cot, bw, pw)
+        ]
         + [pltpu.VMEM((bands, pixels, piece), low)]
         + [entry.memory for entries in phases for entry in entries if not entry.passing]
         + [
@@ -2421,6 +2504,7 @@
             pltpu.SemaphoreType.DMA((4,)),
             pltpu.SemaphoreType.DMA((len(taps),)),
             pltpu.SemaphoreType.DMA((len(out_shapes),)),
+            pltpu.SemaphoreType.DMA((7,)),
         ],
         compiler_params=pltpu.CompilerParams(
             collective_id=collective, has_side_effects=True, vmem_limit_bytes=60 << 20

time: 226 us -> 220 us (0.973)
  Pallas kernels: 221 us -> 217 us
    pallas_call x1, Pallas kernels: 214 us -> 210 us  [whole(): pl.pallas_call(functools.partial(whole_kernel, sizes, plan, phases, (len(...]
where the time goes in v6:
time: 220 us; the launch traced here: 218 us
  Pallas kernels  217 us (99%)
    pallas_call x1, Pallas kernels, whole(): pl.pallas_call(functools.partial(whole_kernel, sizes, plan, phases, (len(...  210 us
    pallas_call x1, Pallas kernels, finish(): pl.pallas_call(functools.partial(finish_kernel, places), name='finish', o...  7.17 us

profile of v6, /device:TPU:13, one launch (start us, length us, event | category | flops | bytes accessed | tf_op | source)
XLA Modules:
  0.0 217.6 jit_solution(2354224244948128374)
XLA Ops:
  0.7 209.6 %whole.1 = (f32[2,3072]{1,0:T(2,128)}, bf16[256,256]{1,0:T(8,128)(2,1)}, bf16[17,256,256]{2,1,0:T(8,128)(2,1)}, f32[24,128]{1,0:T(8,128)}, f32[8,128]{1,0:T(8,12...) custom-call(bf16[256,2048]{1,0:T(8,128)(2,1)} %bitcast.20, ...), custom_call_target="tpu_custom_call" | custom-call | tf_op jit(solution)/shard_map/whole/pallas_call | solution.py:2486
  210.2 7.2 %finish.1 = (bf16[256,256]{1,0:T(8,128)(2,1)}, bf16[256,2048]{1,0:T(8,128)(2,1)}, f32[256,512]{1,0:T(8,128)}, f32[9,64,512]{2,1,0:T(8,128)}, f32[64,2048]{1,0:T(...) custom-call(bf16[17,256,256]{2,1,0:T(8,128)(2,1)} %get-tuple-element, ...), custom_call_target="tpu_custom_call" | custom-call | tf_op jit(solution)/shard_map/finish/pallas_call | solution.py:2666

commit v7 on v6

--- a/solution.py
+++ b/solution.py
@@ -1942,14 +1942,24 @@
     low, f32 = jnp.bfloat16, jnp.float32
     task, band = at.task, at.band
     my_rows = pl.ds(pl.multiple_of(task * quarter, quarter), quarter)
+    depth = x.shape[1] // 4
+    pieces = []
+    for number in range(4):
+        some = slice(number * depth, (number + 1) * depth)
+        pieces.append(
+            (
+                some,
+                pltpu.make_async_copy(x_hbm.at[:, some], x.at[:, some], local_sem.at[2 * number]),
+                pltpu.make_async_copy(wr_hbm.at[some], wr.at[some], local_sem.at[2 * number + 1]),
+            )
+        )
+    for _, of_x, of_weight in pieces:
+        of_x.start()
+        of_weight.start()
     loads = [
-        pltpu.make_async_copy(source, target, local_sem.at[number])
-        for number, (source, target) in enumerate(
-            ((x_hbm, x), (wr_hbm, wr), (wd_hbm, wd), (we_hbm, we))
-        )
+        pltpu.make_async_copy(wd_hbm, wd, local_sem.at[8]),
+        pltpu.make_async_copy(we_hbm, we, local_sem.at[9]),
     ]
-    for load in loads[:2]:
-        load.start()
     at.greet()
     pixels = x.shape[0]
     band_rows = pixels // cols
@@ -1992,11 +2002,16 @@
         return (gelu_of(normed) * keep).astype(low)
 
     mask_mid = across(mask, mid)
-    for load in loads[:2]:
-        load.wait()
-    for load in loads[2:]:
+    for number, (some, of_x, of_weight) in enumerate(pieces):
+        of_x.wait()
+        of_weight.wait()
+        term = dot_nn(x[:, some], wr[some])
+        if number == 0:
+            h1[...] = term
+        else:
+            h1[...] += term
+    for load in loads:
         load.start()
-    h1[...] = dot_nn(x[...], wr[...])
     at.meet()
     put_sums(st1, h1[...], mask_mid)
     begun = at.sum_begin(post, "space", st1, st1_land)
@@ -2027,7 +2042,7 @@
     def _():
         rim[2] = jnp.zeros(rim.shape[1:], low)
 
-    loads[2].wait()
+    loads[0].wait()
     halves = [slice(start, start + piece) for start in range(0, mid, piece)]
 
     def tap_sum(row_taps, lanes):
@@ -2062,7 +2077,7 @@
     put_norm(v2, slice(0, mid), first, second, mid)
     a2[...] = activate(h2[...], v2, mask_mid)
 
-    loads[3].wait()
+    loads[1].wait()
     mask_piece = across(mask, piece)
     per_row = st3.shape[1] // piece
     half = st3.shape[0] // 2
@@ -2501,7 +2516,7 @@
         + [
             pltpu.SemaphoreType.DMA((352,)),
             pltpu.SemaphoreType.DMA((352,)),
-            pltpu.SemaphoreType.DMA((4,)),
+            pltpu.SemaphoreType.DMA((10,)),
             pltpu.SemaphoreType.DMA((len(taps),)),
             pltpu.SemaphoreType.DMA((len(out_shapes),)),
             pltpu.SemaphoreType.DMA((7,)),
@@ -2536,12 +2551,12 @@
     bs_out,
     branch_out,
     rate_out,
-    pg_out,
-    tg_out,
-    ts_out,
-    hg_out,
-    hs_out,
-    tw_out,
+    pg_hbm_out,
+    tg_hbm_out,
+    ts_hbm_out,
+    hg_hbm_out,
+    hs_hbm_out,
+    tw_hbm_out,
     tap_ref,
     tw_ref,
     pg_ref,
@@ -2558,6 +2573,12 @@
     bs_buf,
     branch,
     rate,
+    pg_out,
+    tg_out,
+    ts_out,
+    hg_out,
+    hs_out,
+    tw_out,
     sems,
     load_sems,
 ):
@@ -2599,13 +2620,16 @@
         copy.start()
     copies = [copy for _, copy in passes]
     per_level = len(places) // 3
+    for number, place in enumerate(places):
+        if place is None:
+            rate[:, number * width : (number + 1) * width] = jnp.zeros(
+                (rate.shape[0], width), f32
+            )
     loads[0].wait()
     for level in range(3):
         for number in range(level * per_level, (level + 1) * per_level):
             lanes = slice(number * width, (number + 1) * width)
-            if places[number] is None:
-                rate[:, lanes] = jnp.zeros((rate.shape[0], width), f32)
-            else:
+            if places[number] is not None:
                 rate[:, lanes] = tap_ref[places[number]].astype(f32)
         lanes = slice(level * per_level * width, (level + 1) * per_level * width)
         copy = pltpu.make_async_copy(
@@ -2622,9 +2646,13 @@
     copy = pltpu.make_async_copy(branch, branch_out, sems.at[len(copies)])
     copy.start()
     copies.append(copy)
-    for load in loads[1:]:
+    loads[1].wait()
+    pg_out[...] = pg_ref[...].astype(f32)
+    copy = pltpu.make_async_copy(pg_out, pg_hbm_out, sems.at[len(copies)])
+    copy.start()
+    copies.append(copy)
+    for load in loads[2:]:
         load.wait()
-    pg_out[...] = pg_ref[...].astype(f32)
     rows = s1_ref.shape[0] // 2
     ts_out[0:rows] = s1_ref[0:rows]
     tg_out[0:rows] = s1_ref[rows : 2 * rows]
@@ -2652,45 +2680,59 @@
     for number in range(tasks):
         weights = jnp.where(place == number, tw_ref[number : number + 1], weights)
     tw_out[...] = weights[:, :tasks]
+    for source, target in (
+        (tg_out, tg_hbm_out),
+        (ts_out, ts_hbm_out),
+        (hg_out, hg_hbm_out),
+        (hs_out, hs_hbm_out),
+        (tw_out, tw_hbm_out),
+    ):
+        copy = pltpu.make_async_copy(source, target, sems.at[len(copies)])
+        copy.start()
+        copies.append(copy)
     for copy in copies:
         copy.wait()
 
 
 def finish(places, tasks, taps, ho, ig, rg, dg, eg, bs, tw, pg, s3, s2, s1, both, proj):
     f32 = jnp.float32
-    in_vmem = pl.BlockSpec(memory_space=pltpu.VMEM)
     anywhere = pl.BlockSpec(memory_space=pl.ANY)
     shape = jax.ShapeDtypeStruct
     depth, width = taps.shape[1:]
     rows = (s1.size + s2.size + s3.size) // 2 // LANE
+    out_shapes = (
+        shape(ho.shape, ho.dtype),
+        shape(ig.shape, ig.dtype),
+        shape(rg.shape, rg.dtype),
+        shape(dg.shape, dg.dtype),
+        shape(eg.shape, eg.dtype),
+        shape(bs.shape, bs.dtype),
+        shape((depth, 2 * width), f32),
+        shape((depth, len(places) * width), f32),
+        shape(pg.shape, f32),
+        shape((rows, LANE), f32),
+        shape((rows, LANE), f32),
+        shape((1, 5 * width), f32),
+        shape((1, 5 * width), f32),
+        shape((1, tasks), f32),
+        )
+    small = out_shapes[8:]
     return pl.pallas_call(
         functools.partial(finish_kernel, places),
         name="finish",
-        out_shape=(
-            shape(ho.shape, ho.dtype),
-            shape(ig.shape, ig.dtype),
-            shape(rg.shape, rg.dtype),
-            shape(dg.shape, dg.dtype),
-            shape(eg.shape, eg.dtype),
-            shape(bs.shape, bs.dtype),
-            shape((depth, 2 * width), f32),
-            shape((depth, len(places) * width), f32),
-            shape(pg.shape, f32),
-            shape((rows, LANE), f32),
-            shape((rows, LANE), f32),
-            shape((1, 5 * width), f32),
-            shape((1, 5 * width), f32),
-            shape((1, tasks), f32),
-        ),
+        out_shape=out_shapes,
         in_specs=[anywhere] * 14,
-        out_specs=(anywhere,) * 8 + (in_vmem,) * 6,
+        out_specs=(anywhere,) * 14,
         scratch_shapes=[
             pltpu.VMEM(value.shape, value.dtype) for value in (taps, tw, pg, s3, s2, s1, both, proj, ho, ig, rg, dg, eg, bs)
         ]
         + [
             pltpu.VMEM((depth, 2 * width), f32),
             pltpu.VMEM((depth, len(places) * width), f32),
-            pltpu.SemaphoreType.DMA((10,)),
+        ]
+        + [pltpu.VMEM(out.shape, out.dtype) for out in small]
+        + [
+            pltpu.SemaphoreType.DMA((16,)),
             pltpu.SemaphoreType.DMA((14,)),
         ],
         compiler_params=pltpu.CompilerParams(vmem_limit_bytes=60 << 20),
@@ -2824,7 +2866,12 @@
 
 
 def solution(mesh):
-    body = per_device_slices if mesh.shape["space"] == 8 else per_device
+    def body(features, *others):
+        small = mesh.shape["space"] == 8 and mesh.shape["task"] == 4
+        if small and features.shape[:2] == (2, 128):
+            return per_device_slices(features, *others)
+        return per_device(features, *others)
+
     return jax.shard_map(
         body,
         mesh=mesh,

time: 220 us -> 219 us (level)
  no operation moved by 1% of the time
where the time goes in v7:
time: 219 us; the launch traced here: 217 us
  Pallas kernels  216 us (99%)
    pallas_call x1, Pallas kernels, whole(): pl.pallas_call(functools.partial(whole_kernel, sizes, plan, phases, (len(...  209 us
    pallas_call x1, Pallas kernels, finish(): pl.pallas_call(functools.partial(finish_kernel, places), name='finish', o...  6.58 us

profile of v7, /device:TPU:13, one launch (start us, length us, event | category | flops | bytes accessed | tf_op | source)
XLA Modules:
  0.0 216.6 jit_solution(2541152773586775894)
XLA Ops:
  0.7 209.1 %whole.1 = (f32[2,3072]{1,0:T(2,128)}, bf16[256,256]{1,0:T(8,128)(2,1)}, bf16[17,256,256]{2,1,0:T(8,128)(2,1)}, f32[24,128]{1,0:T(8,128)}, f32[8,128]{1,0:T(8,12...) custom-call(bf16[256,2048]{1,0:T(8,128)(2,1)} %bitcast.20, ...), custom_call_target="tpu_custom_call" | custom-call | tf_op jit(solution)/shard_map/whole/pallas_call | solution.py:2501
  209.8 6.6 %finish.1 = (bf16[256,256]{1,0:T(8,128)(2,1)}, bf16[256,2048]{1,0:T(8,128)(2,1)}, f32[256,512]{1,0:T(8,128)}, f32[9,64,512]{2,1,0:T(8,128)}, f32[64,2048]{1,0:T(...) custom-call(bf16[17,256,256]{2,1,0:T(8,128)(2,1)} %get-tuple-element, ...), custom_call_target="tpu_custom_call" | custom-call | tf_op jit(solution)/shard_map/finish/pallas_call | solution.py:2720

commit v8 on v7

--- a/solution.py
+++ b/solution.py
@@ -571,6 +571,7 @@
     post,
     sizes,
     local_sem,
+    part_copy,
     xg,
     h3q,
     v3_ref,
@@ -1046,6 +1047,8 @@
     write(ig_out, ig_hbm)
     for source, target in ((tw_out, tw_hbm), (s3_out, s3_hbm), (s2_out, s2_hbm), (s1_out, s1_hbm)):
         write(source, target)
+    for step in range(bands - 1):
+        part_copy(step).wait()
     for made in d_near:
         made.wait_recv()
     d_sum[...] = jnp.zeros_like(d_sum)
@@ -1904,6 +1907,7 @@
     sizes,
     when_loaded,
     norm_loads,
+    part_copy,
     x_hbm,
     widths_ref,
     gain_ref,
@@ -2132,9 +2136,8 @@
     act[0] = jnp.zeros(act.shape[1:], low)
     act[bands + 1] = jnp.zeros(act.shape[1:], low)
     act[band + 1] = part_of(band)[...]
-    parts_in = [
-        post.push(part_of(other), act.at[band + 1], {"space": other}) for other in at.other_bands
-    ]
+    for step in range(bands - 1):
+        part_copy(step).start()
 
     def to_tasks(number):
         block = sh_out.at[number, my_rows]
@@ -2144,7 +2147,7 @@
     for step, made in enumerate(slices_in, start=1):
         made.wait_recv()
         quarters_in += to_tasks(lax.rem(band + bands - step, bands))
-    for made in quarters_in + parts_in:
+    for made in quarters_in:
         made.wait_recv()
     post.close()
 
@@ -2200,6 +2203,21 @@
         copy.start()
         writes.append(copy)
 
+    part = sizes[4] // bands
+    first_part = post.used
+    post.used += bands
+
+    def part_copy(step):
+        other = at.other_bands[step]
+        return pltpu.make_async_remote_copy(
+            kept[0][1].at[pl.ds(pl.multiple_of(other * part, part), part)],
+            trunk_outs[0].at[at.band + 1],
+            send_sem.at[first_part + step],
+            recv_sem.at[first_part + step],
+            device_id={"space": other},
+            device_id_type=MESH_ID,
+        )
+
     rate = kept[1][0]
     rate_loads = []
     for number, (level, row_tap, col_tap, _, _) in enumerate(taps):
@@ -2232,6 +2250,7 @@
             sizes,
             when_loaded,
             norm_loads,
+            part_copy,
             x_hbm,
             widths,
             gain,
@@ -2281,6 +2300,7 @@
             post,
             sizes,
             local_sem,
+            part_copy,
             xg,
             h3q,
             v3,

time: 219 us -> 219 us (level)
  no operation moved by 1% of the time
where the time goes in v8:
time: 219 us; the launch traced here: 217 us
  Pallas kernels  216 us (99%)
    pallas_call x1, Pallas kernels, whole(): pl.pallas_call(functools.partial(whole_kernel, sizes, plan, phases, (len(...  209 us
    pallas_call x1, Pallas kernels, finish(): pl.pallas_call(functools.partial(finish_kernel, places), name='finish', o...  6.58 us

profile of v8, /device:TPU:13, one launch (start us, length us, event | category | flops | bytes accessed | tf_op | source)
XLA Modules:
  0.0 216.7 jit_solution(2121514990999403542)
XLA Ops:
  0.7 209.3 %whole.1 = (f32[2,3072]{1,0:T(2,128)}, bf16[256,256]{1,0:T(8,128)(2,1)}, bf16[17,256,256]{2,1,0:T(8,128)(2,1)}, f32[24,128]{1,0:T(8,128)}, f32[8,128]{1,0:T(8,12...) custom-call(bf16[256,2048]{1,0:T(8,128)(2,1)} %bitcast.20, ...), custom_call_target="tpu_custom_call" | custom-call | tf_op jit(solution)/shard_map/whole/pallas_call | solution.py:2521
  210.0 6.6 %finish.1 = (bf16[256,256]{1,0:T(8,128)(2,1)}, bf16[256,2048]{1,0:T(8,128)(2,1)}, f32[256,512]{1,0:T(8,128)}, f32[9,64,512]{2,1,0:T(8,128)}, f32[64,2048]{1,0:T(...) custom-call(bf16[17,256,256]{2,1,0:T(8,128)(2,1)} %get-tuple-element, ...), custom_call_target="tpu_custom_call" | custom-call | tf_op jit(solution)/shard_map/finish/pallas_call | solution.py:2740
